TPU v7x, 32 devices: a whole 2x2x4 slice. The times are simulated.
32 devices in a mesh: seq: 8 (over z, x), mp: 4 (over y, core).
Axes of the slice: x: 2, y: 2, z: 4, core: 2. Of those that a mesh axis runs over, the one named last changes fastest.
Arguments:
- inputs: bfloat16 [1024, 4, 8192], P('mp', None, 'seq'), may hold values from -12 to 12
- valid: int32 [4, 8192], P(None, 'seq'), may hold values from 0 to 1, as said below
- cotangent: bfloat16 [1024, 4, 8192], P('mp', None, 'seq'), may hold values from -6 to 6
- first_gain: float32 [1024], P('mp'), may hold values from 0.25 to 1.75
- step_size: float32 [1024], P('mp'), may hold values from 0.001 to 0.1
- decay_rate: float32 [1024, 32], P('mp'), may hold values from 0.2 to 1
- frequency: float32 [1024, 32], P('mp'), may hold values from 0 to 50
- readout_real: float32 [1024, 32], P('mp'), may hold values from -3 to 3
- readout_imag: float32 [1024, 32], P('mp'), may hold values from -3 to 3
- skip_weight: float32 [1024], P('mp'), may hold values from -4 to 4
- gated_weight: bfloat16 [1024, 2, 1024], P(None, None, 'mp'), may hold values from -0.1875 to 0.1875
- gated_bias: float32 [2, 1024], P(None, 'mp'), may hold values from -2 to 2
- second_gain: float32 [1024], P('mp'), may hold values from 0.25 to 1.75
- expand_weight: bfloat16 [1024, 4096], P(None, 'mp'), may hold values from -0.1875 to 0.1875
- expand_bias: float32 [4096], P('mp'), may hold values from -2 to 2
- shrink_weight: bfloat16 [4096, 1024], P('mp'), may hold values from -0.09375 to 0.09375
- shrink_bias: float32 [1024], P('mp'), may hold values from -2 to 2
Outputs:
- result: bfloat16 [1024, 4, 8192], P('mp', None, 'seq')
- grad_inputs: float32 [1024, 4, 8192], P('mp', None, 'seq')
- grad_first_gain: float32 [1024], P('mp')
- grad_step_size: float32 [1024], P('mp')
- grad_decay_rate: float32 [1024, 32], P('mp')
- grad_frequency: float32 [1024, 32], P('mp')
- grad_readout_real: float32 [1024, 32], P('mp')
- grad_readout_imag: float32 [1024, 32], P('mp')
- grad_skip_weight: float32 [1024], P('mp')
- grad_gated_weight: float32 [1024, 2, 1024], P(None, None, 'mp')
- grad_gated_bias: float32 [2, 1024], P(None, 'mp')
- grad_second_gain: float32 [1024], P('mp')
- grad_expand_weight: float32 [1024, 4096], P(None, 'mp')
- grad_expand_bias: float32 [4096], P('mp')
- grad_shrink_weight: float32 [4096, 1024], P('mp')
- grad_shrink_bias: float32 [1024], P('mp')
- rms_input: float32 [], replicated
- rms_branch: float32 [], replicated
- rms_feed: float32 [], replicated
Inputs may be any that keep to these rules, and one draw needn't show every extreme that they name: In each context the valid tokens are the first ones up to the context's length and the rest are invalid; every length is at least 6144, and one context, drawn from the seed, is valid at every position.
All inputs are finite; a program needn't handle non-finite values.
Results may differ from a plain program's by a relative error of at most 0.0081.
Values may be sent and summed in bfloat16 or wider, within the bound.
No kernel may reach another device: no remote copies, remote signals or barrier semaphores. Data moves between devices by JAX's collectives and lax.ppermute only.
A program may use at most 256 MiB of HBM per device.

v0:
```python
import jax
import jax.numpy as jnp
from jax import lax
from jax.sharding import PartitionSpec as P

D = 1024
L = 8192


highest = lax.Precision.HIGHEST
epsilon = 1e-05


def kernel_block(step_size, decay_rate, frequency, readout_real, readout_imag):
    real_part = -decay_rate
    scaled_real = step_size[:, None] * real_part
    scaled_imag = step_size[:, None] * frequency
    growth = jnp.exp(scaled_real)
    minus_real = growth * jnp.cos(scaled_imag) - 1.0
    minus_imag = growth * jnp.sin(scaled_imag)
    modulus = real_part * real_part + frequency * frequency
    ratio_real = (minus_real * real_part + minus_imag * frequency) / modulus
    ratio_imag = (minus_imag * real_part - minus_real * frequency) / modulus
    coeff_real = readout_real * ratio_real - readout_imag * ratio_imag
    coeff_imag = readout_real * ratio_imag + readout_imag * ratio_real
    positions = jnp.arange(L, dtype=jnp.float32)
    envelope = jnp.exp(scaled_real[:, :, None] * positions)
    angles = scaled_imag[:, :, None] * positions
    waves = coeff_real[:, :, None] * jnp.cos(angles) - coeff_imag[:, :, None] * jnp.sin(angles)
    return 2.0 * jnp.sum(envelope * waves, axis=1)


def unit_table(extent):
    indices = jnp.arange(extent, dtype=jnp.int32)
    angles = (indices[:, None] * indices[None, :] % extent).astype(jnp.float32) * (
        2.0 * jnp.pi / extent
    )
    return (jnp.cos(angles), -jnp.sin(angles))


def tables(points):
    q_size = 2
    while q_size * q_size * 4 <= points:
        q_size = q_size * 2
    p_size = points // q_size
    q_real, q_imag = unit_table(q_size)
    p_real, p_imag = unit_table(p_size)
    row_index = jnp.arange(q_size, dtype=jnp.int32)[:, None]
    col_index = jnp.arange(p_size, dtype=jnp.int32)[None, :]
    angles = (row_index * col_index % points).astype(jnp.float32) * (2.0 * jnp.pi / points)
    return (q_real, q_imag, p_real, p_imag, jnp.cos(angles), -jnp.sin(angles))


def spectrum(signal_in, transform):
    q_real, q_imag, p_real, p_imag, twist_real, twist_imag = transform
    q_size = q_real.shape[0]
    p_size = p_real.shape[0]
    blocked = signal_in.reshape(signal_in.shape[:-1] + (q_size // 2, p_size))
    section_real = jnp.einsum(
        "kq,...qp->...kp", q_real[:, : q_size // 2], blocked, precision=highest
    )
    section_imag = jnp.einsum(
        "kq,...qp->...kp", q_imag[:, : q_size // 2], blocked, precision=highest
    )
    turned_real = section_real * twist_real - section_imag * twist_imag
    turned_imag = section_real * twist_imag + section_imag * twist_real
    spec_real = jnp.einsum("...kn,nm->...km", turned_real, p_real, precision=highest) - jnp.einsum(
        "...kn,nm->...km", turned_imag, p_imag, precision=highest
    )
    spec_imag = jnp.einsum("...kn,nm->...km", turned_real, p_imag, precision=highest) + jnp.einsum(
        "...kn,nm->...km", turned_imag, p_real, precision=highest
    )
    return (spec_real, spec_imag)


def signal(spec_real, spec_imag, transform):
    q_real, q_imag, p_real, p_imag, twist_real, twist_imag = transform
    q_size = q_real.shape[0]
    p_size = p_real.shape[0]
    back_real = jnp.einsum("...km,mn->...kn", spec_real, p_real, precision=highest) + jnp.einsum(
        "...km,mn->...kn", spec_imag, p_imag, precision=highest
    )
    back_imag = jnp.einsum("...km,mn->...kn", spec_imag, p_real, precision=highest) - jnp.einsum(
        "...km,mn->...kn", spec_real, p_imag, precision=highest
    )
    turned_real = back_real * twist_real + back_imag * twist_imag
    turned_imag = back_imag * twist_real - back_real * twist_imag
    output = jnp.einsum(
        "nk,...kp->...np", q_real[: q_size // 2], turned_real, precision=highest
    ) + jnp.einsum("nk,...kp->...np", q_imag[: q_size // 2], turned_imag, precision=highest)
    output = output / (q_size * p_size)
    return output.reshape(output.shape[:-2] + (q_size // 2 * p_size,))


def contract(left, right, left_dim, right_dim):
    return lax.dot_general(
        left, right, (((left_dim,), (right_dim,)), ((), ())), preferred_element_type=jnp.float32
    )


def token_total(values):
    return lax.psum(values, "mp")


def feature_rows(values):
    return lax.all_gather(values, "mp", axis=0, tiled=True)


def feature_sums(weight, row_dim, right_side):
    return lax.psum_scatter(
        contract(weight, right_side, 1 - row_dim, 0), "mp", scatter_dimension=0, tiled=True
    )


def to_positions(values):
    return lax.all_to_all(values, "seq", split_axis=2, concat_axis=0, tiled=True)


def shards(
    inputs,
    valid,
    cotangent,
    first_gain,
    step_size,
    decay_rate,
    frequency,
    readout_real,
    readout_imag,
    skip_weight,
    gated_weight,
    gated_bias,
    second_gain,
    expand_weight,
    expand_bias,
    shrink_weight,
    shrink_bias,
):
    mp_count = lax.axis_size("mp")
    features, contexts, local_len = inputs.shape
    tokens = contexts * local_len
    channels = features // lax.axis_size("seq")
    offset_own = lax.axis_index("seq") * channels

    def own_rows(values):
        return lax.dynamic_slice_in_dim(values, offset_own, channels, 0)

    def padded(values):
        zeros = jnp.zeros((features,) + values.shape[1:], jnp.float32)
        return lax.dynamic_update_slice_in_dim(zeros, values, offset_own, 0)

    residual = inputs.astype(jnp.float32)
    valid_f = valid.astype(jnp.float32)
    square_one = jnp.sum(residual * residual, axis=0)
    scale_one = lax.rsqrt(token_total(square_one) / D + epsilon)
    normed_one = (residual * scale_one * first_gain[:, None, None]).astype(jnp.bfloat16)
    local_params = (
        own_rows(step_size),
        own_rows(decay_rate),
        own_rows(frequency),
        own_rows(readout_real),
        own_rows(readout_imag),
    )
    skip_own = own_rows(skip_weight)
    transform = tables(2 * L)
    kernel = kernel_block(*local_params)
    kern_real, kern_imag = spectrum(kernel, transform)
    channel_block = lax.all_to_all(normed_one, "seq", split_axis=0, concat_axis=2, tiled=True)
    signal_in = channel_block.astype(jnp.float32)
    spec_real, spec_imag = spectrum(signal_in, transform)
    prod_real = spec_real * kern_real[:, None] - spec_imag * kern_imag[:, None]
    prod_imag = spec_real * kern_imag[:, None] + spec_imag * kern_real[:, None]
    mixed_chan = signal(prod_real, prod_imag, transform) + skip_own[:, None, None] * signal_in
    mixed = to_positions(mixed_chan.astype(jnp.bfloat16))
    mixed_f = mixed.astype(jnp.float32)
    lifted_one = jax.nn.gelu(mixed_f).astype(jnp.bfloat16)
    full_one = feature_rows(lifted_one).reshape(D, tokens)
    gated_flat = gated_weight.reshape(D, 2 * features)
    projected = contract(gated_flat, full_one, 0, 0) + gated_bias.reshape(2 * features, 1)
    projected = projected.reshape(2, features, contexts, local_len)
    value_part = projected[0]
    opening = jax.nn.sigmoid(projected[1])
    branch = value_part * opening
    hidden = residual + branch
    square_two = jnp.sum(hidden * hidden, axis=0)
    scale_two = lax.rsqrt(token_total(square_two) / D + epsilon)
    normed_two = (hidden * scale_two * second_gain[:, None, None]).astype(jnp.bfloat16)
    full_two = feature_rows(normed_two).reshape(D, tokens)
    expanded = contract(expand_weight, full_two, 0, 0) + expand_bias[:, None]
    lifted_three = jax.nn.gelu(expanded).astype(jnp.bfloat16)
    feed_out = (
        feature_sums(shrink_weight, 1, lifted_three).reshape(features, contexts, local_len)
        + shrink_bias[:, None, None]
    )
    result = (hidden + feed_out).astype(jnp.bfloat16)
    stat_terms = (
        jnp.sum(valid_f * square_one),
        jnp.sum(valid_f * jnp.sum(branch * branch, axis=0)),
        jnp.sum(valid_f * jnp.sum(feed_out * feed_out, axis=0)),
        jnp.sum(valid_f) / mp_count,
    )
    totals = lax.psum((stat_terms[0], stat_terms[1], stat_terms[2], stat_terms[3]), ("seq", "mp"))
    upstream = cotangent.astype(jnp.float32) * valid_f[None]
    grad_shrink_bias = jnp.sum(upstream, axis=(1, 2))
    full_up = feature_rows(upstream.astype(jnp.bfloat16)).reshape(D, tokens)
    grad_shrink = contract(lifted_three, full_up, 1, 1)
    grad_lifted_three = contract(shrink_weight, full_up, 1, 0)
    gelu_out, gelu_back = jax.vjp(jax.nn.gelu, expanded)
    grad_expanded = gelu_back(grad_lifted_three)[0].astype(jnp.bfloat16)
    grad_expand_bias = jnp.sum(grad_expanded.astype(jnp.float32), axis=1)
    grad_expand = contract(full_two, grad_expanded, 1, 1)
    grad_normed_two = feature_sums(expand_weight, 0, grad_expanded).reshape(
        features, contexts, local_len
    )
    grad_second_gain = jnp.sum(grad_normed_two * hidden * scale_two, axis=(1, 2))
    inner_two = grad_normed_two * second_gain[:, None, None]
    dot_two = token_total(jnp.sum(inner_two * hidden, axis=0))
    grad_hidden = (
        scale_two * inner_two
        - hidden * (scale_two * scale_two * scale_two) * dot_two / D
        + upstream
    )
    ffn_grads = (grad_expand, grad_expand_bias, grad_shrink, grad_shrink_bias, grad_second_gain)
    grad_value = grad_hidden * opening
    grad_gate = grad_hidden * value_part * opening * (1.0 - opening)
    grad_projected = (
        jnp.stack([grad_value, grad_gate]).astype(jnp.bfloat16).reshape(2 * features, tokens)
    )
    grad_gated_bias = jnp.sum(grad_projected.astype(jnp.float32), axis=1).reshape(2, features)
    grad_gated = contract(full_one, grad_projected, 1, 1).reshape(D, 2, features)
    grad_lifted_one = feature_sums(gated_flat, 0, grad_projected).reshape(
        features, contexts, local_len
    )
    act_out, act_back = jax.vjp(jax.nn.gelu, mixed_f)
    grad_mixed = act_back(grad_lifted_one)[0].astype(jnp.bfloat16)
    grad_chan = lax.all_to_all(grad_mixed, "seq", split_axis=0, concat_axis=2, tiled=True)
    grad_signal = grad_chan.astype(jnp.float32)
    kept_f = channel_block.astype(jnp.float32)
    grad_spec_real, grad_spec_imag = spectrum(grad_signal, transform)
    kept_spec_real, kept_spec_imag = spectrum(kept_f, transform)
    back_real = grad_spec_real * kern_real[:, None] + grad_spec_imag * kern_imag[:, None]
    back_imag = grad_spec_imag * kern_real[:, None] - grad_spec_real * kern_imag[:, None]
    grad_input_chan = (
        signal(back_real, back_imag, transform) + skip_own[:, None, None] * grad_signal
    )
    corr_real = jnp.sum(grad_spec_real * kept_spec_real + grad_spec_imag * kept_spec_imag, axis=1)
    corr_imag = jnp.sum(grad_spec_imag * kept_spec_real - grad_spec_real * kept_spec_imag, axis=1)
    grad_kernel = signal(corr_real, corr_imag, transform)
    grad_skip_own = jnp.sum(grad_signal * kept_f, axis=(1, 2))
    kernel_out, kernel_back = jax.vjp(kernel_block, *local_params)
    kernel_grads = kernel_back(grad_kernel)
    grad_normed_one = to_positions(grad_input_chan.astype(jnp.bfloat16)).astype(jnp.float32)
    grad_first_gain = jnp.sum(grad_normed_one * residual * scale_one, axis=(1, 2))
    inner_one = grad_normed_one * first_gain[:, None, None]
    dot_one = token_total(jnp.sum(inner_one * residual, axis=0))
    grad_inputs = (
        scale_one * inner_one
        - residual * (scale_one * scale_one * scale_one) * dot_one / D
        + grad_hidden
    )
    mixer_grads = (
        grad_first_gain,
        padded(kernel_grads[0]),
        padded(kernel_grads[1]),
        padded(kernel_grads[2]),
        padded(kernel_grads[3]),
        padded(kernel_grads[4]),
        padded(grad_skip_own),
        grad_gated,
        grad_gated_bias,
    )
    summed = lax.psum(
        (
            ffn_grads[0],
            ffn_grads[1],
            ffn_grads[2],
            ffn_grads[3],
            ffn_grads[4],
            mixer_grads[0],
            mixer_grads[1],
            mixer_grads[2],
            mixer_grads[3],
            mixer_grads[4],
            mixer_grads[5],
            mixer_grads[6],
            mixer_grads[7],
            mixer_grads[8],
        ),
        "seq",
    )
    ffn_grads = summed[:5]
    mixer_grads = summed[5:]
    count = totals[3]
    rms_input = jnp.sqrt(totals[0] / (count * D))
    rms_branch = jnp.sqrt(totals[1] / (count * D))
    rms_feed = jnp.sqrt(totals[2] / (count * D))
    return (
        result,
        grad_inputs,
        mixer_grads[0],
        mixer_grads[1],
        mixer_grads[2],
        mixer_grads[3],
        mixer_grads[4],
        mixer_grads[5],
        mixer_grads[6],
        mixer_grads[7],
        mixer_grads[8],
        ffn_grads[4],
        ffn_grads[0],
        ffn_grads[1],
        ffn_grads[2],
        ffn_grads[3],
        rms_input,
        rms_branch,
        rms_feed,
    )


def solution(mesh):
    placed = (
        P("mp", None, "seq"),
        P(None, "seq"),
        P("mp", None, "seq"),
        P("mp"),
        P("mp"),
        P("mp", None),
        P("mp", None),
        P("mp", None),
        P("mp", None),
        P("mp"),
        P(None, None, "mp"),
        P(None, "mp"),
        P("mp"),
        P(None, "mp"),
        P("mp"),
        P("mp", None),
        P("mp"),
    )
    return jax.shard_map(
        shards,
        mesh=mesh,
        in_specs=placed,
        out_specs=(
            P("mp", None, "seq"),
            P("mp", None, "seq"),
            P("mp"),
            P("mp"),
            P("mp", None),
            P("mp", None),
            P("mp", None),
            P("mp", None),
            P("mp"),
            P(None, None, "mp"),
            P(None, "mp"),
            P("mp"),
            P(None, "mp"),
            P("mp"),
            P("mp", None),
            P("mp"),
            P(),
            P(),
            P(),
        ),
        check_vma=False,
    )
```

profile of v0, /device:TPU:0, one launch (start us, length us, event | category | flops | bytes accessed | tf_op | source)
XLA Modules:
  0.0 2116.7 jit_solution(5908528952199066219)
XLA Ops:
  9.6 12.7 psum.154
  29.0 5.8 all-to-all-start
  36.4 131.1 %multiply_reduce_fusion.4 = f32[32,8192]{1,0:T(8,128)S(1)} fusion(f32[32,32]{1,0:T(8,128)S(1)} %multiply_add_fusion.14, f32[32,32]{1,0:T(8,128)S(1)} %get-tuple-element.197, f32[32,32]{1,0:T(8,128)S(1)} %get-tuple-element.193, f32[32,32]{1,0:T(8,128)S(1)} %get-tuple-element.209), kind=kLoop, calls=%fused_computation.4 | loop fusion | flops 58458112 | bytes 1064960 | tf_op jit(solution)/shard_map/reduce_sum | solution.py:30
  207.6 6.5 fusion.183
  218.9 16.5 fusion.84
  235.4 16.7 fusion.86
  252.0 19.1 convolution_add_fusion.1
  271.2 23.7 %convolution_subtract_fusion.1 = f32[32,4,128,128]{3,2,1,0:T(8,128)} fusion(f32[32,4,128,128]{3,2,1,0:T(8,128)} %fusion.86, f32[32,4,128,128]{3,2,1,0:T(8,128)} %copy-done.7, f32[32,4,128,128]{3,2,1,0:T(8,128)} %copy-done.8, f32[128,128]{0,1:T(8,128)S(1)} %get-tuple-element.219, f32[128,128]{0,1:T(8,128)S(1)} %get-tuple-element.220), kind=kOutput, calls=%fused_computation.147 | convolution fusion | flops 3229859840 | bytes 33685504 | tf_op jit(solution)/shard_map/...kn,nm->...km/dot_general | solution.py:67
  294.9 13.4 fusion.124
  308.3 13.7 fusion.126
  322.0 13.4 fusion.127
  335.3 13.9 fusion.125
  354.1 16.6 fusion.27
  370.8 18.1 multiply_bitcast_fusion.1
  394.3 7.2 fusion.63
  401.5 10.9 copy.597
  412.4 11.2 reshape.295
  423.6 52.4 %all_to_all.48 = bf16[8,2,65536]{2,1,0:T(2,128)(2,1)} all-to-all(bf16[8,2,65536]{2,1,0:T(2,128)(2,1)} %reshape.295), channel_id=1, replica_groups=mesh['seq'=8,'mp'=4] {'seq'}, dimensions={0} | all-to-all | bytes 4194304 | tf_op jit(solution)/shard_map/all_to_all | solution.py:116
  476.0 8.7 reshape.296
  484.8 13.4 copy.598
  505.9 56.2 %all-gather.4.cloned.1.call-done = bf16[1024,4,1024]{2,1,0:T(4,128)(2,1)} async-done(((bf16[256,4,1024]{2,1,0:T(4,128)(2,1)}), bf16[1024,4,1024]{2,1,0:T(4,128)(2,1)}) %all-gather.4.cloned.1.call-update) | async-done | bytes 8388624 | tf_op jit(solution)/shard_map/all_gather | solution.py:106
  562.1 12.3 copy.765
  574.4 7.4 add_bitcast_fusion
  597.1 7.8 multiply_reduce_fusion.10
  604.9 10.2 psum.155
  627.0 53.6 %all-gather.6.cloned.1.call-done = bf16[1024,4,1024]{2,1,0:T(4,128)(2,1)} async-done(((bf16[256,4,1024]{2,1,0:T(4,128)(2,1)}), bf16[1024,4,1024]{2,1,0:T(4,128)(2,1)}) %all-gather.6.cloned.1.call-update) | async-done | bytes 8388624 | tf_op jit(solution)/shard_map/all_gather | solution.py:106
  680.6 13.2 copy.768
  693.8 19.8 fusion.14
  716.8 11.8 convolution_bitcast_fusion.2
  728.9 12.2 all-gather.8.cloned.1.call-done
  741.1 14.0 copy.769
  755.0 29.9 %convert_reduce_fusion = (f32[1024]{0:T(1024)}, bf16[1024,4096]{0,1:T(8,128)(2,1)}) fusion(f32[4096,1024]{1,0:T(8,128)} %get-tuple-element.215, f32[1024]{0:T(1024)S(1)} %copy-done.99, bf16[1024,4096]{1,0:T(8,128)(2,1)} %bitcast.367, bf16[1024,1024]{1,0:T(8,128)(2,1)S(1)} %copy-done.98), kind=kOutput, calls=%fused_computation.28 | convolution fusion | flops 8686402560 | bytes 35659776 | tf_op jit(solution)/shard_map/dot_general | solution.py:96
  785.0 14.8 convolution_bitcast_fusion.1
  799.9 69.8 %reduce-scatter.4.cloned.1.call-done = f32[256,4096]{0,1:T(8,128)} async-done(((f32[1024,4096]{0,1:T(8,128)}), f32[256,4096]{0,1:T(8,128)}) %reduce-scatter.4.cloned.1.call-update) | async-done | bytes 4194320 | tf_op jit(solution)/shard_map/reduce_scatter | solution.py:110
  875.1 123.3 %reduce-scatter.6.cloned.1.call-done = f32[256,4096]{0,1:T(8,128)} async-done(((f32[1024,4096]{0,1:T(8,128)}), f32[256,4096]{0,1:T(8,128)}) %reduce-scatter.6.cloned.1.call-update) | async-done | bytes 4194320 | tf_op jit(solution)/shard_map/reduce_scatter | solution.py:110
  1003.9 5.7 multiply_reduce_fusion.7
  1009.6 10.3 psum.156
  1019.9 9.3 multiply_convert_fusion.1
  1038.0 8.5 convolution_bitcast_fusion
  1046.5 14.9 reshape.291
  1061.5 18.1 fusion.319
  1079.5 15.7 fusion.318
  1109.3 10.7 fusion.55
  1120.0 53.8 %reduce-scatter.8.cloned.1.call-done = f32[256,4096]{0,1:T(8,128)} async-done(((f32[1024,4096]{0,1:T(8,128)}), f32[256,4096]{0,1:T(8,128)}) %reduce-scatter.8.cloned.1.call-update) | async-done | bytes 4194320 | tf_op jit(solution)/shard_map/reduce_scatter | solution.py:110
  1197.1 118.0 %all-reduce = (f32[]{:T(128)}, f32[]{:T(128)}, f32[]{:T(128)}, f32[]{:T(128)}) all-reduce(f32[]{:T(128)} %get-tuple-element.165, f32[]{:T(128)S(6)} %div.76, f32[]{:T(128)} %get-tuple-element.167, f32[]{:T(128)} %get-tuple-element.164), channel_id=1, replica_groups=mesh['seq'=8,'mp'=4] {'seq','mp'}, use_global_device_ids=true, to_apply=%region_41.42 | all-reduce | flops 4 | bytes 32 | tf_op jit(solution)/shard_map/psum | solution.py:201
  1323.8 229.5 %all-reduce.8.cloned.1.call-done = (f32[1024,2,256]{2,0,1:T(8,128)}, f32[1024,1024]{1,0:T(8,128)}, f32[1024,1024]{1,0:T(8,128)}) async-done(((f32[1024,2,256]{2,0,1:T(8,128)}, f32[1024,1024]{1,0:T(8,128)}, f32[1024,1024]{1,0:T(8,128)}), (f32[1024,2,256]{2,0,1:T(8,128)}, f32[1024,1024]{1,0:T(8,128)}, f32[1024,1024]{1,0:T(8,128)})) %all-reduce.8.cloned.1.call-update) | async-done | bytes 10485776 | tf_op jit(solution)/shard_map/psum | solution.py:271
  1576.8 16.3 fusion.90
  1593.1 16.6 fusion.92
  1609.7 18.5 convolution_add_fusion
  1628.1 28.1 %subtract_reduce_fusion = (f32[32,128,128]{2,1,0:T(8,128)}, f32[32,128,128]{2,1,0:T(8,128)}, f32[32,4,128,128]{3,2,1,0:T(8,128)}) fusion(f32[32,4,128,128]{3,2,1,0:T(8,128)} %copy-done.2, f32[32,4,128,128]{3,2,1,0:T(8,128)} %convolution_add_fusion, f32[32,4,128,128]{3,2,1,0:T(8,128)} %convolution_subtract_fusion.1, f32[32,4,128,128]{3,2,1,0:T(8,128)} %fusion.92, ...), kind=kOutput, calls=%fused_computation.51 | convolution fusion | flops 3245588480 | bytes 63045632 | tf_op jit(solution)/shard_map/...kn,nm->...km/dot_general | solution.py:67
  1656.2 14.8 fusion.128
  1671.0 11.3 fusion.130
  1682.3 11.1 fusion.131
  1693.4 11.1 fusion.129
  1725.3 16.6 fusion.19
  1742.0 18.5 multiply_bitcast_fusion
  1766.1 5.9 fusion.59
  1772.0 8.4 copy.638
  1780.4 11.2 reshape.297
  1796.3 171.4 %multiply_reduce_fusion = (f32[32,32]{1,0:T(8,128)S(1)}, f32[32,32]{1,0:T(8,128)S(1)}, f32[32,32]{1,0:T(8,128)S(1)}, f32[32,32]{1,0:T(8,128)S(1)}) fusion(f32[32,8192]{1,0:T(8,128)S(1)} %bitcast.383, f32[32,32]{1,0:T(8,128)S(1)} %copy-done.80, f32[32,32]{1,0:T(8,128)S(1)} %copy-done.72, f32[32,32]{1,0:T(8,128)S(1)} %copy-done.76, f32[32,32]{1,0:T(8,128)S(1)} %copy-done.78), kind=kLoop, calls=%fused_computation | loop fusion | flops 192933888 | bytes 1081344 | tf_op jit(solution)/shard_map/transpose(jvp())/reduce_sum | solution.py:27
  1974.3 9.0 reshape.298
  1983.4 13.5 copy.639
  2001.6 11.2 psum.157
  2022.8 63.5 %all-reduce.6.cloned.1.call-done = (f32[256]{0:T(256)}, f32[256]{0:T(256)}, f32[256,32]{0,1:T(8,128)}, f32[256,32]{0,1:T(8,128)}, f32[256,32]{0,1:T(8,128)}, /*i...) async-done(((f32[256]{0:T(256)}, f32[256]{0:T(256)}, f32[256,32]{0,1:T(8,128)}, ...) | async-done | bytes 142352 | tf_op jit(solution)/shard_map/psum | solution.py:271
  (347 shorter events, 261.1 us)
Async XLA Ops:
  7.2 686.6 %copy-start = (bf16[1024,1024]{1,0:T(8,128)(2,1)S(1)}, bf16[1024,1024]{1,0:T(8,128)(2,1)}, u32[]{:S(2)}) copy-start(bf16[1024,1024]{1,0:T(8,128)(2,1)} %param.30) | copy-start | bytes 6291460
  9.6 19.4 copy-start.59
  29.0 164.8 %all-to-all-start = ((bf16[256,4,1024]{2,1,0:T(4,128)(2,1)}), bf16[256,4,1024]{2,1,0:T(4,128)(2,1)}, u32[]{:S(2)}, u32[]{:S(2)}) async-start(bf16[256,4,1024]{2,1,0:T(4,128)(2,1)} %copy.561), calls=%async_computation | async-start | bytes 4194304 | tf_op jit(solution)/shard_map/all_to_all | solution.py:167
  34.8 527.4 %all-gather.4.cloned.1.call-start = ((), (), s32[]{:S(2)}) async-start(), calls=%async_computation.7 | async-start | bytes 10485760 | tf_op jit(solution)/shard_map/all_gather | solution.py:106
  34.9 132.6 %copy-start.83 = (f32[32]{0:T(128)}, f32[32]{0:T(128)S(1)}, u32[]{:S(2)}) copy-start(f32[32]{0:T(128)S(1)} %dynamic_slice.18) | copy-start | bytes 388
  35.1 132.5 %copy-start.55 = (f32[32,32]{1,0:T(8,128)}, f32[32,32]{1,0:T(8,128)S(1)}, u32[]{:S(2)}) copy-start(f32[32,32]{1,0:T(8,128)S(1)} %copy.761) | copy-start | bytes 12292
  35.1 132.4 %copy-start.51 = (f32[32,32]{1,0:T(8,128)}, f32[32,32]{1,0:T(8,128)S(1)}, u32[]{:S(2)}) copy-start(f32[32,32]{1,0:T(8,128)S(1)} %copy.760) | copy-start | bytes 12292
  35.3 132.2 %copy-start.57 = (f32[32,32]{1,0:T(8,128)}, f32[32,32]{1,0:T(8,128)S(1)}, u32[]{:S(2)}) copy-start(f32[32,32]{1,0:T(8,128)S(1)} %copy.763) | copy-start | bytes 12292
  35.4 132.2 %copy-start.45 = (f32[32,32]{1,0:T(8,128)}, f32[32,32]{1,0:T(8,128)S(1)}, u32[]{:S(2)}) copy-start(f32[32,32]{1,0:T(8,128)S(1)} %copy.762) | copy-start | bytes 12292
  35.5 132.0 %copy-start.71 = (f32[32,32]{1,0:T(8,128)}, f32[32,32]{1,0:T(8,128)S(1)}, u32[]{:S(2)}) copy-start(f32[32,32]{1,0:T(8,128)S(1)} %get-tuple-element.197) | copy-start | bytes 12292
  35.8 131.8 %copy-start.75 = (f32[32,32]{1,0:T(8,128)}, f32[32,32]{1,0:T(8,128)S(1)}, u32[]{:S(2)}) copy-start(f32[32,32]{1,0:T(8,128)S(1)} %get-tuple-element.193) | copy-start | bytes 12292
  35.8 131.8 %copy-start.77 = (f32[32,32]{1,0:T(8,128)}, f32[32,32]{1,0:T(8,128)S(1)}, u32[]{:S(2)}) copy-start(f32[32,32]{1,0:T(8,128)S(1)} %get-tuple-element.209) | copy-start | bytes 12292
  35.8 131.8 %copy-start.79 = (f32[32,32]{1,0:T(8,128)}, f32[32,32]{1,0:T(8,128)S(1)}, u32[]{:S(2)}) copy-start(f32[32,32]{1,0:T(8,128)S(1)} %multiply_add_fusion.14) | copy-start | bytes 12292
  36.4 131.2 %copy-start.101 = (f32[256]{0:T(256)S(1)}, f32[256]{0:T(256)}, u32[]{:S(2)}) copy-start(f32[256]{0:T(256)} %param.26) | copy-start | bytes 3076
  167.7 226.7 %copy-start.92 = (f32[32]{0:T(128)}, f32[32]{0:T(128)S(1)}, u32[]{:S(2)}) copy-start(f32[32]{0:T(128)S(1)} %dynamic_slice.23) | copy-start | bytes 388
  168.2 202.5 %copy-start.36 = (f32[128,128]{0,1:T(8,128)}, f32[128,128]{0,1:T(8,128)S(1)}, u32[]{:S(2)}) copy-start(f32[128,128]{0,1:T(8,128)S(1)} %fusion.194) | copy-start | bytes 196612
  168.5 185.7 %copy-start.39 = (f32[128,128]{0,1:T(8,128)}, f32[128,128]{0,1:T(8,128)S(1)}, u32[]{:S(2)}) copy-start(f32[128,128]{0,1:T(8,128)S(1)} %sine_negate_fusion.1) | copy-start | bytes 196612
  168.8 202.0 %copy-start.23 = (f32[128,128]{0,1:T(8,128)}, f32[128,128]{0,1:T(8,128)S(1)}, u32[]{:S(2)}) copy-start(f32[128,128]{0,1:T(8,128)S(1)} %get-tuple-element.219) | copy-start | bytes 196612
  168.8 202.0 %copy-start.26 = (f32[128,128]{0,1:T(8,128)}, f32[128,128]{0,1:T(8,128)S(1)}, u32[]{:S(2)}) copy-start(f32[128,128]{0,1:T(8,128)S(1)} %get-tuple-element.220) | copy-start | bytes 196612
  214.1 21.3 %copy-start.7 = (f32[32,4,128,128]{3,2,1,0:T(8,128)}, f32[32,4,128,128]{3,2,1,0:T(8,128)S(1)}, u32[]{:S(2)}) copy-start(f32[32,4,128,128]{3,2,1,0:T(8,128)S(1)} %fusion.183) | copy-start | bytes 25165828
  218.9 16.5 copy-start.8
  271.2 64.2 %copy-start.2 = (f32[32,4,128,128]{3,2,1,0:T(8,128)}, f32[32,4,128,128]{3,2,1,0:T(8,128)S(1)}, u32[]{:S(2)}) copy-start(f32[32,4,128,128]{3,2,1,0:T(8,128)S(1)} %convolution_add_fusion.1) | copy-start | bytes 25165828
  271.2 23.8 %copy-start.9 = (f32[32,128,128]{2,1,0:T(8,128)S(1)}, f32[32,128,128]{2,1,0:T(8,128)}, u32[]{:S(2)}) copy-start(f32[32,128,128]{2,1,0:T(8,128)} %convolution_add_fusion.3) | copy-start | bytes 6291460
  271.2 23.8 %copy-start.11 = (f32[32,128,128]{2,1,0:T(8,128)S(1)}, f32[32,128,128]{2,1,0:T(8,128)}, u32[]{:S(2)}) copy-start(f32[32,128,128]{2,1,0:T(8,128)} %convolution_subtract_fusion.3) | copy-start | bytes 6291460
  504.6 176.0 %all-gather.6.cloned.1.call-start = ((), (), s32[]{:S(2)}) async-start(), calls=%async_computation.8 | async-start | bytes 10485760 | tf_op jit(solution)/shard_map/all_gather | solution.py:106
  562.1 12.3 copy-start.43
  597.1 18.1 copy-start.82
  621.1 120.0 %all-gather.8.cloned.1.call-start = ((), (), s32[]{:S(2)}) async-start(), calls=%async_computation.10 | async-start | bytes 10485760 | tf_op jit(solution)/shard_map/all_gather | solution.py:106
  626.5 243.2 %reduce-scatter.4.cloned.1.call-start = ((), (), s32[]{:S(2)}) async-start(), calls=%async_computation.9 | async-start | bytes 20971520 | tf_op jit(solution)/shard_map/reduce_scatter | solution.py:110
  680.6 13.2 copy-start.99
  693.8 23.0 %copy-start.97 = (bf16[1024,1024]{1,0:T(8,128)(2,1)S(1)}, bf16[1024,1024]{1,0:T(8,128)(2,1)}, u32[]{:S(2)}) copy-start(bf16[1024,1024]{1,0:T(8,128)(2,1)} %param.32) | copy-start | bytes 6291460
  728.6 269.8 %reduce-scatter.6.cloned.1.call-start = ((), (), s32[]{:S(2)}) async-start(), calls=%async_computation.11 | async-start | bytes 20971520 | tf_op jit(solution)/shard_map/reduce_scatter | solution.py:110
  741.1 14.0 copy-start.98
  799.8 374.1 %reduce-scatter.8.cloned.1.call-start = ((), (), s32[]{:S(2)}) async-start(), calls=%async_computation.12 | async-start | bytes 20971520 | tf_op jit(solution)/shard_map/reduce_scatter | solution.py:110
  1003.8 16.1 copy-start.34
  1003.9 16.1 copy-start.89
  1031.6 67.6 %copy-start.19 = (bf16[256,4,1024]{2,0,1:T(8,128)(2,1)}, bf16[256,4,1024]{2,0,1:T(8,128)(2,1)S(1)}, u32[]{:S(2)}) copy-start(bf16[256,4,1024]{2,0,1:T(8,128)(2,1)S(1)} %multiply_convert_fusion) | copy-start | bytes 6291460
  1046.5 506.8 %all-reduce.8.cloned.1.call-start = ((), (), s32[]{:S(2)}) async-start(), calls=%async_computation.14 | async-start | bytes 20971520 | tf_op jit(solution)/shard_map/psum | solution.py:271
  1187.2 370.6 %all-to-all-start.2 = ((bf16[256,4,1024]{2,1,0:T(4,128)(2,1)}), bf16[256,4,1024]{2,1,0:T(4,128)(2,1)S(1)}, u32[]{:S(2)}, u32[]{:S(2)}) async-start(bf16[256,4,1024]{2,1,0:T(4,128)(2,1)} %copy.614), calls=%async_computation.5 | async-start | bytes 4194304 | tf_op jit(solution)/shard_map/all_to_all | solution.py:235
  1571.9 37.7 %copy-start.5 = (f32[32,4,128,128]{3,2,1,0:T(8,128)}, f32[32,4,128,128]{3,2,1,0:T(8,128)S(1)}, u32[]{:S(2)}) copy-start(f32[32,4,128,128]{3,2,1,0:T(8,128)S(1)} %fusion.181) | copy-start | bytes 25165828
  1576.8 16.3 copy-start.6
  1628.1 28.1 %copy-start.10 = (f32[32,128,128]{2,1,0:T(8,128)S(1)}, f32[32,128,128]{2,1,0:T(8,128)}, u32[]{:S(2)}) copy-start(f32[32,128,128]{2,1,0:T(8,128)} %convolution_add_fusion.3) | copy-start | bytes 6291460
  1628.1 28.1 %copy-start.12 = (f32[32,128,128]{2,1,0:T(8,128)S(1)}, f32[32,128,128]{2,1,0:T(8,128)}, u32[]{:S(2)}) copy-start(f32[32,128,128]{2,1,0:T(8,128)} %convolution_subtract_fusion.3) | copy-start | bytes 6291460
  1656.2 14.8 copy-start.3
  1656.2 14.8 copy-start.4
  1791.6 182.6 %all-to-all-start.3 = ((bf16[8,2,65536]{2,1,0:T(2,128)(2,1)}), bf16[8,2,65536]{2,1,0:T(2,128)(2,1)}, u32[]{:S(2)}, u32[]{:S(2)}) async-start(bf16[8,2,65536]{2,1,0:T(2,128)(2,1)} %reshape.297), calls=%async_computation.6 | async-start | bytes 4194304 | tf_op jit(solution)/shard_map/all_to_all | solution.py:116
  1796.1 290.2 %all-reduce.6.cloned.1.call-start = ((), (), s32[]{:S(2)}) async-start(), calls=%async_computation.13 | async-start | bytes 284672 | tf_op jit(solution)/shard_map/psum | solution.py:271
  1796.2 171.5 %copy-start.46 = (f32[32,32]{1,0:T(8,128)S(1)}, f32[32,32]{1,0:T(8,128)}, u32[]{:S(2)}) copy-start(f32[32,32]{1,0:T(8,128)} %copy-done.45) | copy-start | bytes 12292
  1796.2 171.5 %copy-start.50 = (f32[32,32]{1,0:T(8,128)S(1)}, f32[32,32]{1,0:T(8,128)}, u32[]{:S(2)}) copy-start(f32[32,32]{1,0:T(8,128)} %copy-done.49) | copy-start | bytes 12292
  1796.3 171.5 %copy-start.52 = (f32[32,32]{1,0:T(8,128)S(1)}, f32[32,32]{1,0:T(8,128)}, u32[]{:S(2)}) copy-start(f32[32,32]{1,0:T(8,128)} %copy-done.51) | copy-start | bytes 12292
  1796.3 171.5 %copy-start.54 = (f32[32,32]{1,0:T(8,128)S(1)}, f32[32,32]{1,0:T(8,128)}, u32[]{:S(2)}) copy-start(f32[32,32]{1,0:T(8,128)} %copy-done.53) | copy-start | bytes 12292
  1796.3 171.5 %copy-start.56 = (f32[32,32]{1,0:T(8,128)S(1)}, f32[32,32]{1,0:T(8,128)}, u32[]{:S(2)}) copy-start(f32[32,32]{1,0:T(8,128)} %copy-done.55) | copy-start | bytes 12292
  1796.3 171.5 %copy-start.58 = (f32[32,32]{1,0:T(8,128)S(1)}, f32[32,32]{1,0:T(8,128)}, u32[]{:S(2)}) copy-start(f32[32,32]{1,0:T(8,128)} %copy-done.57) | copy-start | bytes 12292
  1796.3 171.5 %copy-start.62 = (f32[32,32]{1,0:T(8,128)S(1)}, f32[32,32]{1,0:T(8,128)}, u32[]{:S(2)}) copy-start(f32[32,32]{1,0:T(8,128)} %copy-done.61) | copy-start | bytes 12292
  1796.3 171.5 %copy-start.64 = (f32[32,32]{1,0:T(8,128)S(1)}, f32[32,32]{1,0:T(8,128)}, u32[]{:S(2)}) copy-start(f32[32,32]{1,0:T(8,128)} %copy-done.63) | copy-start | bytes 12292
  1796.3 171.5 %copy-start.84 = (f32[32]{0:T(128)S(1)}, f32[32]{0:T(128)}, u32[]{:S(2)}) copy-start(f32[32]{0:T(128)} %copy-done.83) | copy-start | bytes 388
  1796.3 172.1 %copy-start.18 = (bf16[256,4,1024]{2,1,0:T(4,128)(2,1)S(1)}, bf16[256,4,1024]{2,1,0:T(4,128)(2,1)}, u32[]{:S(2)}) copy-start(bf16[256,4,1024]{2,1,0:T(4,128)(2,1)} %copy-done.17) | copy-start | bytes 6291460
  1972.7 10.6 copy-start.95
  1973.0 10.2 copy-start.66
  1973.4 9.9 copy-start.67
  1983.3 13.6 copy-start.14
  1983.3 13.6 copy-start.48
  1983.3 13.6 copy-start.81
  1996.9 15.9 copy-start.69
  (52 other events, 263.1 us)
Sparse Core Ops, SparseCore 0:
  504.8 57.3 all-gather.3
  621.2 59.3 all-gather.5
  682.8 58.2 all-gather.7
  743.5 126.1 reduce-scatter.3
  872.3 126.0 reduce-scatter.5
  1046.6 127.2 reduce-scatter.7
  1179.1 374.1 all-reduce.7
  2012.9 73.3 all-reduce.5
where the time goes:
time: 2130 us; the launch traced here: 2120 us
  waiting for transfers between devices  662 us (31%)
  matrix products  525 us (25%)
  other arithmetic  393 us (18%)
  local copies, waits for them, and re-layouts  283 us (13%)
  blocking collectives  215 us (10%)
  between operations  22.8 us (1%)
    psum x2, waiting for transfers between devices, shards(): lax.psum((ffn_grads[0], ffn_grads[1], ffn_grads[2], ffn_grads[3], ffn_gra...  293 us
    reduce_scatter x3, waiting for transfers between devices, feature_sums(): lax.psum_scatter(contract(weight, right_side, 1 - row_dim, 0), 'mp', scat...  247 us
    reduce_sum x1, other arithmetic, kernel_block(): envelope = jnp.exp(scaled_real[:, :, None] * positions)  171 us
    dot_general x9, matrix products, contract(): lax.dot_general(left, right, (((left_dim,), (right_dim,)), ((), ())), pre...  137 us
    reduce_sum x1, other arithmetic, kernel_block(): return 2.0 * jnp.sum(envelope * waves, axis=1)  131 us
    unnamed x242, local copies, waits for them, and re-layouts  124 us
    all_gather x3, waiting for transfers between devices, feature_rows(): return lax.all_gather(values, 'mp', axis=0, tiled=True)  122 us
    psum x1, blocking collectives, shards(): lax.psum((stat_terms[0], stat_terms[1], stat_terms[2], stat_terms[3]), ('...  118 us
  transfers between devices with their start and end apart: 11, of which 8 were waited for; matrix products, arithmetic and copies ran while one was open for 27% of the time, Pallas kernels for 0%

commit v1 on v0

v1 whole, which is shorter than its diff:
```python
import functools

import jax
import jax.numpy as jnp
from jax import lax
from jax.experimental import pallas as pl
from jax.experimental.pallas import tpu as pltpu
from jax.sharding import PartitionSpec as P

D = 1024
epsilon = 1e-05
CHUNK = 128
f32 = jnp.float32
bf16 = jnp.bfloat16


def contract(left, right, left_dim, right_dim):
    return lax.dot_general(
        left, right, (((left_dim,), (right_dim,)), ((), ())), preferred_element_type=f32
    )


def nt(left, right):
    return lax.dot_general(left, right, (((1,), (1,)), ((), ())), preferred_element_type=f32)


def nn(left, right):
    return lax.dot_general(left, right, (((1,), (0,)), ((), ())), preferred_element_type=f32)


def tn(left, right):
    return lax.dot_general(left, right, (((0,), (0,)), ((), ())), preferred_element_type=f32)


def gelu_pair(v):
    k0 = 0.7978845608028654
    k1 = 0.044715
    square = v * v
    t = jnp.tanh(k0 * v * (1.0 + k1 * square))
    half = 0.5 * (1.0 + t)
    return v * half, half + 0.5 * v * (1.0 - t * t) * k0 * (1.0 + 3.0 * k1 * square)


def cmul(a, b):
    return (a[0] * b[0] - a[1] * b[1], a[0] * b[1] + a[1] * b[0])


def cadd(a, b):
    return (a[0] + b[0], a[1] + b[1])


def discretized(step, decay, freq):
    return step[:, None] * (-decay), step[:, None] * freq


def coefficients(step, decay, freq, out_real, out_imag):
    a_real, a_imag = -decay, freq
    w_real, w_imag = discretized(step, decay, freq)
    growth = jnp.exp(w_real)
    minus_real = growth * jnp.cos(w_imag) - 1.0
    minus_imag = growth * jnp.sin(w_imag)
    modulus = a_real * a_real + a_imag * a_imag
    ratio_real = (minus_real * a_real + minus_imag * a_imag) / modulus
    ratio_imag = (minus_imag * a_real - minus_real * a_imag) / modulus
    return (
        out_real * ratio_real - out_imag * ratio_imag,
        out_real * ratio_imag + out_imag * ratio_real,
    )


def power(w, exponent):
    envelope = jnp.exp(w[0] * exponent)
    return envelope * jnp.cos(w[1] * exponent), envelope * jnp.sin(w[1] * exponent)


def states_kernel(u_ref, e2_ref, q_ref):
    for i in range(u_ref.shape[0]):
        q_ref[i] = nt(u_ref[i], e2_ref[i])


def toeplitz(taps):
    size = taps.shape[-1]
    rolled = pltpu.roll(
        jnp.broadcast_to(taps, (size, size)), 0, 1, stride=1, stride_axis=0
    )
    rows = lax.broadcasted_iota(jnp.int32, (size, size), 0)
    lanes = lax.broadcasted_iota(jnp.int32, (size, size), 1)
    return jnp.where(lanes >= rows, rolled, 0.0).astype(bf16)


def mix_kernel(u_ref, x_ref, e1_ref, taps_ref, skip_ref, mixed_ref, lifted_ref):
    for i in range(u_ref.shape[0]):
        u = u_ref[i]
        y = nn(u, toeplitz(taps_ref[i : i + 1, :]))
        y = y + nn(x_ref[i].astype(bf16), e1_ref[i])
        mixed = (y + skip_ref[i : i + 1, :] * u.astype(f32)).astype(bf16)
        mixed_ref[i] = mixed
        lifted_ref[i] = gelu_pair(mixed.astype(f32))[0].astype(bf16)


def adjoint_kernel(g_ref, u_ref, e1_ref, e2_ref, p_ref, pa_ref, qp_ref, diag_ref, skip_ref):
    size = g_ref.shape[2]
    rows = g_ref.shape[1]
    lanes = lax.broadcasted_iota(jnp.int32, (rows, size), 1).astype(f32)
    row_id = lax.broadcasted_iota(jnp.int32, (size, size), 0)
    lane_id = lax.broadcasted_iota(jnp.int32, (size, size), 1)
    keep = lane_id <= row_id
    flip = jnp.where(lane_id + row_id == size - 1, 1.0, 0.0).astype(bf16)
    for i in range(g_ref.shape[0]):
        g = g_ref[i]
        u = u_ref[i]
        gf = g.astype(f32)
        uf = u.astype(f32)
        p_ref[i] = nt(g, e1_ref[i])
        pa_ref[i] = nt((gf * lanes).astype(bf16), e1_ref[i])
        qp_ref[i] = nt((uf * lanes).astype(bf16), e2_ref[i])
        outer = tn(nn(u, flip).astype(bf16), g)
        rolled = pltpu.roll(outer, 1, 1, stride=1, stride_axis=0)
        diag_ref[i : i + 1, :] = jnp.sum(jnp.where(keep, rolled, 0.0), axis=0, keepdims=True)
        skip_ref[i : i + 1, :] = jnp.sum(gf * uf, axis=0, keepdims=True)


def back_kernel(g_ref, x_ref, e2_ref, taps_ref, skip_ref, out_ref):
    for i in range(g_ref.shape[0]):
        g = g_ref[i]
        y = nt(g, toeplitz(taps_ref[i : i + 1, :]))
        y = y + nn(x_ref[i].astype(bf16), e2_ref[i])
        out_ref[i] = (y + skip_ref[i : i + 1, :] * g.astype(f32)).astype(bf16)


def by_channel(kernel, block, args, outs, flops):
    channels = args[0].shape[0]
    block = min(block, channels)

    def spec(shape):
        rest = len(shape) - 1
        return pl.BlockSpec((block,) + tuple(shape[1:]), lambda i: (i,) + (0,) * rest)

    moved = sum(a.size * a.dtype.itemsize for a in args) + sum(
        o.size * o.dtype.itemsize for o in outs
    )
    return pl.pallas_call(
        kernel,
        grid=(channels // block,),
        in_specs=[spec(a.shape) for a in args],
        out_specs=[spec(o.shape) for o in outs],
        out_shape=outs,
        compiler_params=pltpu.CompilerParams(vmem_limit_bytes=40 * 1024 * 1024),
        cost_estimate=pl.CostEstimate(flops=flops, bytes_accessed=moved, transcendentals=0),
    )(*args)


def swap(values, axis, bit):
    size = lax.axis_size(axis)
    return lax.ppermute(values, axis, [(i, i ^ bit) for i in range(size)])


def take(values, index):
    return lax.dynamic_index_in_dim(values, index, 0, keepdims=False)


def scattered_sum(blocks, axis):
    size = lax.axis_size(axis)
    me = lax.axis_index(axis)
    bit = 1
    while bit < size:
        pairs = blocks.reshape((blocks.shape[0] // 2, 2) + blocks.shape[1:]).swapaxes(0, 1)
        mine = (me // bit) % 2
        there = swap(take(pairs, 1 - mine), axis, bit)
        blocks = (take(pairs, mine).astype(f32) + there.astype(f32)).astype(bf16)
        bit *= 2
    return blocks[0]


def gathered(block, axis):
    size = lax.axis_size(axis)
    me = lax.axis_index(axis)
    blocks = block[None]
    bit = size // 2
    while bit >= 1:
        there = swap(blocks, axis, bit)
        mine = (me // bit) % 2
        first = jnp.where(mine == 0, blocks, there)
        second = jnp.where(mine == 0, there, blocks)
        blocks = jnp.stack([first, second], axis=1).reshape((-1,) + block.shape)
        bit //= 2
    return blocks


def axis_total(values, axis):
    bit = 1
    while bit < lax.axis_size(axis):
        values = jax.tree.map(lambda v: v + swap(v, axis, bit), values)
        bit *= 2
    return values


def weight_total(terms):
    shape = terms.shape[1:]
    seq, mp = lax.axis_size("seq"), lax.axis_size("mp")
    parts = terms.reshape(mp, seq, -1, shape[-1])
    parts = scattered_sum(parts.swapaxes(0, 1), "seq")
    part = scattered_sum(parts, "mp")
    return gathered(part, "seq").reshape(shape).astype(f32)


def shards(
    inputs,
    valid,
    cotangent,
    first_gain,
    step_size,
    decay_rate,
    frequency,
    readout_real,
    readout_imag,
    skip_weight,
    gated_weight,
    gated_bias,
    second_gain,
    expand_weight,
    expand_bias,
    shrink_weight,
    shrink_bias,
):
    mp = lax.axis_size("mp")
    seq = lax.axis_size("seq")
    mp_me = lax.axis_index("mp")
    seq_me = lax.axis_index("seq")
    features, contexts, local = inputs.shape
    chunk = min(CHUNK, local)
    chunks = local // chunk
    rows = contexts * chunks
    modes = decay_rate.shape[1]
    own_contexts = contexts // mp
    tokens = own_contexts * local

    def exchanged(values):
        moved = lax.all_to_all(values, "mp", 0, 0, tiled=True)
        moved = moved.reshape(mp, own_contexts, features, local).swapaxes(1, 2)
        return moved.reshape(mp * features, tokens)

    def returned(values):
        moved = values.reshape(mp, features, own_contexts, local).swapaxes(1, 2)
        moved = moved.reshape(mp * own_contexts, features, local)
        return lax.all_to_all(moved, "mp", 0, 0, tiled=True)

    def to_rows(values):
        return values.reshape(features, rows, chunk)

    def rows_to_tokens(values):
        return exchanged(values.reshape(features, contexts, local).swapaxes(0, 1))

    def tokens_to_rows(values):
        return to_rows(returned(values).swapaxes(0, 1))

    whole_gated = lax.all_gather(gated_weight, "mp", axis=0)
    whole_expand = lax.all_gather(expand_weight, "mp", axis=0)
    whole_shrink = lax.all_gather(shrink_weight, "mp", axis=0)
    small = lax.all_gather(
        jnp.concatenate(
            [gated_bias.reshape(-1), second_gain, expand_bias, shrink_bias]
        ),
        "mp",
        axis=0,
    )
    cut = [0, 2 * features]
    cut += [cut[-1] + features]
    cut += [cut[-1] + expand_bias.shape[0]]
    whole_gated_bias = small[:, : cut[1]].reshape(mp, 2, features).swapaxes(0, 1).reshape(2, D)
    whole_gain_two = small[:, cut[1] : cut[2]].reshape(D)
    whole_expand_bias = small[:, cut[2] : cut[3]].reshape(-1)
    whole_shrink_bias = small[:, cut[3] :].reshape(D)
    gated_flat = whole_gated.transpose(2, 1, 0, 3).reshape(2, D, D)
    expand_flat = whole_expand.swapaxes(0, 1).reshape(D, -1)
    shrink_flat = whole_shrink.reshape(-1, D)

    residual = to_rows(inputs).astype(f32)
    square_one = axis_total(jnp.sum(residual * residual, axis=0), "mp")
    scale_one = lax.rsqrt(square_one / D + epsilon)
    normed_one = (residual * scale_one * first_gain[:, None, None]).astype(bf16)

    w = discretized(step_size, decay_rate, frequency)
    coeff = coefficients(step_size, decay_rate, frequency, readout_real, readout_imag)
    places = jnp.arange(chunk, dtype=f32)
    wide = (w[0][:, :, None], w[1][:, :, None])
    ahead = power(wide, places + 1.0)
    behind = power(wide, chunk - 1.0 - places)
    level = power(wide, places)
    taps = 2.0 * jnp.sum(
        coeff[0][:, :, None] * level[0] - coeff[1][:, :, None] * level[1], axis=1
    )
    table_one = jnp.concatenate(ahead, axis=1).astype(bf16)
    table_two = jnp.concatenate(behind, axis=1).astype(bf16)
    z_chunk = power(w, float(chunk))
    z_chunks = [power(w, float(chunk * i)) for i in range(chunks + 1)]
    double = (2.0 * coeff[0], 2.0 * coeff[1])

    def halves(values):
        values = values.reshape(features, contexts, chunks, 2 * modes)
        return values[..., :modes], values[..., modes:]

    def per_mode(pair):
        return pair[0][:, None], pair[1][:, None]

    def scan(terms, backward):
        order = range(chunks - 1, -1, -1) if backward else range(chunks)
        state = (jnp.zeros((features, contexts, modes), f32),) * 2
        before = [None] * chunks
        for i in order:
            before[i] = state
            state = cadd(
                cmul(per_mode(z_chunk), state), (terms[0][:, :, i], terms[1][:, :, i])
            )
        return before, state

    def incoming(end, backward):
        gathered_ends = lax.all_gather(jnp.stack(end), "seq", axis=0)
        total = (jnp.zeros_like(end[0]),) * 2
        for k in range(seq):
            gap = (k - seq_me - 1) if backward else (seq_me - 1 - k)
            factor = power(w, jnp.maximum(gap, 0).astype(f32) * local)
            keep = (gap >= 0).astype(f32)
            factor = (keep * factor[0], keep * factor[1])
            total = cadd(total, cmul(per_mode(factor), (gathered_ends[k, 0], gathered_ends[k, 1])))
        return total

    def spread(before, into, backward):
        states = []
        for i in range(chunks):
            gap = chunks - 1 - i if backward else i
            states.append(cadd(before[i], cmul(per_mode(z_chunks[gap]), into)))
        return (
            jnp.stack([s[0] for s in states], axis=2),
            jnp.stack([s[1] for s in states], axis=2),
        )

    def scaled(states):
        pair = cmul((double[0][:, None, None], double[1][:, None, None]), states)
        return jnp.concatenate([pair[0], -pair[1]], axis=-1).reshape(features, rows, 2 * modes)

    def out(shape, dtype):
        return jax.ShapeDtypeStruct(shape, dtype)

    block = 16
    state_shape = out((features, rows, 2 * modes), f32)
    row_shape = out((features, rows, chunk), bf16)
    skip_wide = jnp.broadcast_to(skip_weight[:, None], (features, chunk))
    (terms,) = by_channel(
        states_kernel, block, (normed_one, table_two), [state_shape], features * rows * 16384
    )
    before, end = scan(halves(terms), False)
    states = spread(before, incoming(end, False), False)
    mixed, lifted_one = by_channel(
        mix_kernel,
        block,
        (normed_one, scaled(states), table_one, taps, skip_wide),
        [row_shape, row_shape],
        features * rows * 65536,
    )

    whole_residual = exchanged(inputs.swapaxes(0, 1)).astype(f32)
    own_valid = lax.dynamic_slice_in_dim(valid, mp_me * own_contexts, own_contexts, 0)
    own_valid = own_valid.reshape(tokens).astype(f32)
    upstream = exchanged(cotangent.swapaxes(0, 1)) * own_valid.astype(bf16)
    upstream_f = upstream.astype(f32)
    whole_one = rows_to_tokens(lifted_one)
    value_part = contract(gated_flat[0], whole_one, 0, 0) + whole_gated_bias[0][:, None]
    gate_part = contract(gated_flat[1], whole_one, 0, 0) + whole_gated_bias[1][:, None]
    opening = jax.nn.sigmoid(gate_part)
    branch = value_part * opening
    hidden = whole_residual + branch
    scale_two = lax.rsqrt(jnp.sum(hidden * hidden, axis=0) / D + epsilon)
    normed_two = (hidden * scale_two * whole_gain_two[:, None]).astype(bf16)
    expanded = contract(expand_flat, normed_two, 0, 0) + whole_expand_bias[:, None]
    lifted_three = gelu_pair(expanded)[0].astype(bf16)
    feed = contract(shrink_flat, lifted_three, 0, 0) + whole_shrink_bias[:, None]
    result = returned((hidden + feed).astype(bf16)).swapaxes(0, 1)

    grad_shrink = contract(lifted_three, upstream, 1, 1)
    grad_shrink_bias = jnp.sum(upstream_f, axis=1)
    grad_lifted_three = contract(shrink_flat, upstream, 1, 0)
    grad_expanded = (grad_lifted_three * gelu_pair(expanded)[1]).astype(bf16)
    grad_expand_bias = jnp.sum(grad_expanded.astype(f32), axis=1)
    grad_expand = contract(normed_two, grad_expanded, 1, 1)
    grad_normed_two = contract(expand_flat, grad_expanded, 1, 0)
    grad_second_gain = jnp.sum(grad_normed_two * hidden * scale_two, axis=1)
    inner_two = grad_normed_two * whole_gain_two[:, None]
    dot_two = jnp.sum(inner_two * hidden, axis=0)
    grad_hidden = (
        scale_two * inner_two
        - hidden * (scale_two * scale_two * scale_two) * dot_two / D
        + upstream_f
    )
    grad_value = (grad_hidden * opening).astype(bf16)
    grad_gate = (grad_hidden * value_part * opening * (1.0 - opening)).astype(bf16)
    grad_gated_bias = jnp.stack(
        [jnp.sum(grad_value.astype(f32), axis=1), jnp.sum(grad_gate.astype(f32), axis=1)]
    )
    grad_gated = (
        contract(whole_one, grad_value, 1, 1),
        contract(whole_one, grad_gate, 1, 1),
    )
    grad_lifted_one = contract(gated_flat[0], grad_value, 1, 0) + contract(
        gated_flat[1], grad_gate, 1, 0
    )
    own_lifted_one = tokens_to_rows(grad_lifted_one.astype(bf16)).astype(f32)
    own_hidden = tokens_to_rows(grad_hidden.astype(bf16)).astype(f32)

    grad_mixed = (own_lifted_one * gelu_pair(mixed.astype(f32))[1]).astype(bf16)
    line_shape = out((features, chunk), f32)
    adj, adj_a, state_p, diagonal, skip_terms = by_channel(
        adjoint_kernel,
        block,
        (grad_mixed, normed_one, table_one, table_two),
        [state_shape, state_shape, state_shape, line_shape, line_shape],
        features * rows * 131072,
    )
    adj_terms = halves(adj)
    adj_before, adj_end = scan(adj_terms, True)
    adjoint = spread(adj_before, incoming(adj_end, True), True)
    (grad_normed_rows,) = by_channel(
        back_kernel,
        block,
        (grad_mixed, scaled(adjoint), table_two, taps, skip_wide),
        [row_shape],
        features * rows * 65536,
    )
    intra = (level[0] * diagonal[:, None], level[1] * diagonal[:, None])
    sum_a = [
        jnp.sum(p, axis=(1, 2)) + jnp.sum(q, axis=2)
        for p, q in zip(cmul(adj_terms, states), intra)
    ]
    wide_chunk = (z_chunk[0][:, None, None], z_chunk[1][:, None, None])
    here = cadd(adj_terms, cmul(wide_chunk, adjoint))
    crossing = cmul(here, states)
    part_a = cmul(halves(adj_a), states)
    part_p = cmul(halves(state_p), adjoint)
    sum_b = [
        jnp.sum(float(chunk) * c + a - p, axis=(1, 2)) + jnp.sum(q * places, axis=2)
        for c, a, p, q in zip(crossing, part_a, part_p, intra)
    ]
    grad_skip = jnp.sum(skip_terms, axis=1)

    grad_normed_one = grad_normed_rows.astype(f32)
    inner_one = grad_normed_one * first_gain[:, None, None]
    grad_first_gain = jnp.sum(grad_normed_one * residual * scale_one, axis=(1, 2))
    dot_one = axis_total(jnp.sum(inner_one * residual, axis=0), "mp")
    grad_inputs = (
        scale_one * inner_one
        - residual * (scale_one * scale_one * scale_one) * dot_one / D
        + own_hidden
    ).reshape(features, contexts, local)

    hidden_all = expand_flat.shape[1]
    hidden_own = hidden_all // mp
    grad_shrink = weight_total(grad_shrink.reshape(mp, hidden_own, D).astype(bf16))
    grad_expand = weight_total(
        grad_expand.astype(bf16).reshape(D, mp, hidden_own).swapaxes(0, 1)
    )
    grad_gated = weight_total(
        jnp.stack(grad_gated, axis=1)
        .astype(bf16)
        .reshape(2 * D, mp, features)
        .swapaxes(0, 1)
    ).reshape(D, 2, features)
    stats = jnp.stack(
        [
            jnp.sum(own_valid * jnp.sum(whole_residual * whole_residual, axis=0)),
            jnp.sum(own_valid * jnp.sum(branch * branch, axis=0)),
            jnp.sum(own_valid * jnp.sum(feed * feed, axis=0)),
            jnp.sum(own_valid),
        ]
    )
    bias_terms = jnp.concatenate(
        [
            grad_gated_bias.reshape(2, mp, features).swapaxes(0, 1).reshape(mp, -1),
            grad_second_gain.reshape(mp, -1),
            grad_expand_bias.reshape(mp, -1),
            grad_shrink_bias.reshape(mp, -1),
            jnp.broadcast_to(stats, (mp, 4)),
        ],
        axis=1,
    )
    bias_own = lax.dynamic_index_in_dim(axis_total(bias_terms, "mp"), mp_me, 0, keepdims=False)
    bias_own, grad_first_gain, grad_skip, sum_a, sum_b = axis_total(
        (bias_own, grad_first_gain, grad_skip, sum_a, sum_b), "seq"
    )

    def form(step, decay, freq, out_real, out_imag):
        c = coefficients(step, decay, freq, out_real, out_imag)
        moved = cmul(coeff, discretized(step, decay, freq))
        return 2.0 * jnp.sum(
            c[0] * sum_a[0] - c[1] * sum_a[1] + moved[0] * sum_b[0] - moved[1] * sum_b[1]
        )

    kernel_grads = jax.grad(form, argnums=(0, 1, 2, 3, 4))(
        step_size, decay_rate, frequency, readout_real, readout_imag
    )
    totals = bias_own[cut[3] + features :]
    count = totals[3]
    rms = jnp.sqrt(totals[:3] / (count * D))
    return (
        result,
        grad_inputs,
        grad_first_gain,
        *kernel_grads,
        grad_skip,
        grad_gated,
        bias_own[: cut[1]].reshape(2, features),
        bias_own[cut[1] : cut[2]],
        grad_expand,
        bias_own[cut[2] : cut[3]],
        grad_shrink,
        bias_own[cut[3] : cut[3] + features],
        rms[0],
        rms[1],
        rms[2],
    )


def solution(mesh):
    placed = (
        P("mp", None, "seq"),
        P(None, "seq"),
        P("mp", None, "seq"),
        P("mp"),
        P("mp"),
        P("mp", None),
        P("mp", None),
        P("mp", None),
        P("mp", None),
        P("mp"),
        P(None, None, "mp"),
        P(None, "mp"),
        P("mp"),
        P(None, "mp"),
        P("mp"),
        P("mp", None),
        P("mp"),
    )
    return jax.shard_map(
        shards,
        mesh=mesh,
        in_specs=placed,
        out_specs=(
            P("mp", None, "seq"),
            P("mp", None, "seq"),
            P("mp"),
            P("mp"),
            P("mp", None),
            P("mp", None),
            P("mp", None),
            P("mp", None),
            P("mp"),
            P(None, None, "mp"),
            P(None, "mp"),
            P("mp"),
            P(None, "mp"),
            P("mp"),
            P("mp", None),
            P("mp"),
            P(),
            P(),
            P(),
        ),
        check_vma=False,
    )
```

time: 2130 us -> 1200 us (0.56)
  matrix products: 525 us -> 142 us
  waiting for transfers between devices: 662 us -> 311 us
  other arithmetic: 393 us -> 199 us
  blocking collectives: 215 us -> 24.6 us
  Pallas kernels: 0 us -> 81.9 us
  starting transfers between devices: 16.9 us -> 82.8 us
  local copies, waits for them, and re-layouts: 283 us -> 328 us
    dot_general x36 -> x0, matrix products: 388 us -> none  [the longest x3 56.9 us: spectrum(): jnp.einsum('...kn,nm->...km', turned_imag, p_imag, precision=highest)]
    psum x2 -> x0, waiting for transfers between devices: 293 us -> none  [shards(): lax.psum((ffn_grads[0], ffn_grads[1], ffn_grads[2], ffn_grads[3], ffn_gra...]
    reduce_sum x11 -> x10, other arithmetic: 332 us -> 46.1 us  [the longest x1 24 us: shards(): jnp.sum(q * places, axis=2)]
    reduce_scatter x3 -> x0, waiting for transfers between devices: 247 us -> none  [feature_sums(): lax.psum_scatter(contract(weight, right_side, 1 - row_dim, 0), 'mp', scat...]
    ppermute x0 -> x51, waiting for transfers between devices: none -> 236 us  [swap(): return lax.ppermute(values, axis, [(i, i ^ bit) for i in range(size)])]
    psum x5 -> x0, blocking collectives: 162 us -> none  [the longest x1 118 us: shards(): lax.psum((stat_terms[0], stat_terms[1], stat_terms[2], stat_terms[3]), ('...]
    slice x0 -> x15, local copies, waits for them, and re-layouts: none -> 85.9 us  [the longest x2 52.6 us: scan(): terms[1][:, :, i]]
    pallas_call x0 -> x4, Pallas kernels: none -> 81.9 us  [by_channel(): pl.pallas_call(kernel, grid=(channels // block,), in_specs=[spec(a.shape)...]
  transfers between devices with their start and end apart: 11 -> 62, of which waited for: 8 -> 19; matrix products, arithmetic and copies ran while one was open for 27% -> 43% of each run, Pallas kernels for 0% -> 7%
where the time goes in v1:
time: 1200 us; the launch traced here: 1190 us
  local copies, waits for them, and re-layouts  328 us (27%)
  waiting for transfers between devices  311 us (26%)
  other arithmetic  199 us (17%)
  matrix products  142 us (12%)
  starting transfers between devices  82.8 us (7%)
  Pallas kernels  81.9 us (7%)
  blocking collectives  24.6 us (2%)
  between operations  18 us (2%)
    ppermute x51, waiting for transfers between devices, swap(): return lax.ppermute(values, axis, [(i, i ^ bit) for i in range(size)])  236 us
    dot_general x12, matrix products, contract(): lax.dot_general(left, right, (((left_dim,), (right_dim,)), ((), ())), pre...  142 us
    unnamed x430, local copies, waits for them, and re-layouts  94.1 us
    pallas_call x4, Pallas kernels, by_channel(): pl.pallas_call(kernel, grid=(channels // block,), in_specs=[spec(a.shape)...  81.9 us
    ppermute x51, starting transfers between devices, swap(): return lax.ppermute(values, axis, [(i, i ^ bit) for i in range(size)])  55.1 us
    slice x2, local copies, waits for them, and re-layouts, scan(): terms[1][:, :, i]  52.6 us
    another operation x1, other arithmetic  50.1 us
    all_to_all x3, waiting for transfers between devices, exchanged(): moved = lax.all_to_all(values, 'mp', 0, 0, tiled=True)  30.6 us
  transfers between devices with their start and end apart: 62, of which 19 were waited for; matrix products, arithmetic and copies ran while one was open for 43% of the time, Pallas kernels for 7%

profile of v1, /device:TPU:0, one launch (start us, length us, event | category | flops | bytes accessed | tf_op | source)
XLA Modules:
  0.0 1187.6 jit_solution(524077674682171892)
XLA Ops:
  18.5 50.1 %fusion.32 = (bf16[256,32,128]{2,1,0:T(8,128)(2,1)}, bf16[256,32,128]{2,1,0:T(8,128)(2,1)}, f32[256,128]{1,0:T(8,128)}, bf16[256,32,128]{2,1,0:T(8,128)(2,1)S(1)}, bf16[256,32,128]{2,1,0:T(8,128)(2,1)S(1)}) fusion(f32[128]{0:T(128)S(1)} %get-tuple-element.350, f32[256,32]{1,0:T(8,128)S(1)} %copy.1087, f32[256,32]{1,0:T(8,128)S(1)} %copy.1086, ...), kind=kLoop, calls=%fused_computation.53 | loop fusion | flops 20938752 | bytes 8651776 | tf_op jit(solution)/shard_map/convert.22
  85.3 13.2 %fusion.82 = (f32[256,4,1,32]{3,2,1,0:T(1,128)}, f32[256,4,1,32]{3,2,1,0:T(1,128)}, f32[256,4,1,32]{3,2,1,0:T(1,128)}, f32[256,4,1,32]{3,2,1,0:T(1,128)}, f32[25...) fusion(f32[256,4,8,64]{3,2,1,0:T(8,128)S(1)} %bitcast.802), kind=kLoop, calls=%fused_computation.468 | loop fusion | bytes 4194304 | tf_op jit(solution)/shard_map/slice | solution.py:313
  127.9 4.6 all-to-all-start.3
  134.7 24.6 %all-gather.2 = f32[8192]{0:T(1024)S(1)} all-gather(f32[2048]{0:T(1024)S(1)} %pad_maximum_fusion.10), channel_id=4, replica_groups=mesh['seq'=8,'mp'=4] {'mp'}, dimensions={0}, use_global_device_ids=true | all-gather | bytes 40960 | tf_op jit(solution)/shard_map/all_gather | solution.py:260
  160.1 5.6 pad_maximum_fusion.2.e1_ref
  178.7 4.8 all-to-all-start
  194.7 5.0 fusion.50
  201.4 11.9 %shard_map.313 = (bf16[256,32,128]{2,1,0:T(8,128)(2,1)S(1)}, bf16[256,32,128]{2,1,0:T(8,128)(2,1)S(1)}) custom-call(bf16[256,32,128]{2,1,0:T(8,128)(2,1)S(1)} %copy-done.4, f32[256,32,64]{2,1,0:T(8,128)S(1)} %pad_maximum_fusion.1.x_ref, bf16[256,64,128]{2,1,0:T(8,128)(2,1)} %pad_maximum_fusion.2.e1_ref, f32[256,128]{1,0:T(8,128)S(1)} %broadcast_multiply_fusion.1.taps_ref, ...), custom_call_target="tpu_custom_call" | custom-call | flops 536870912 | bytes 12845056 | tf_op jit(solution)/shard_map/pallas_call | solution.py:142
  220.2 6.7 all-to-all-done
  226.9 4.9 all-to-all-start.1
  251.9 23.9 %all-to-all-done.1 = bf16[4,256,1024]{2,1,0:T(8,128)(2,1)} async-done(((bf16[4,256,1024]{2,1,0:T(8,128)(2,1)}), bf16[4,256,1024]{2,1,0:T(8,128)(2,1)}, u32[]{:S(2)}, u32[]{:S(2)}) %all-to-all-start.1) | async-done | bytes 2097184 | tf_op jit(solution)/shard_map/all_to_all | solution.py:239
  275.8 4.7 fusion.87
  280.6 9.3 multiply_reduce_fusion.5
  289.8 14.4 %all-gather.16.cloned.1.call-done = bf16[4096,1024]{1,0:T(8,128)(2,1)} async-done(((bf16[1024,1024]{1,0:T(8,128)(2,1)}), bf16[4096,1024]{1,0:T(8,128)(2,1)}) %all-gather.16.cloned.1.call-update) | async-done | bytes 8388624 | tf_op jit(solution)/shard_map/all_gather | solution.py:258
  304.2 11.6 copy.1113
  315.9 23.2 %fusion.3 = (bf16[4096,1024]{0,1:T(8,128)(2,1)}, f32[1024,4096]{1,0:T(8,128)}) fusion(f32[4096]{0:T(1024)S(1)} %bitcast.852, bf16[1024,4096]{0,1:T(8,128)(2,1)} %bitcast.823, f32[1024,1024]{1,0:T(8,128)} %get-tuple-element.148, f32[1024]{0:T(1024)S(1)} %bitcast.856, f32[1024]{0:T(1024)S(1)} %get-tuple-element.339), kind=kOutput, calls=%fused_computation.8 | convolution fusion | flops 8635023360 | bytes 37773312 | tf_op jit(solution)/shard_map/dot_general | solution.py:18
  339.1 24.9 %all-gather.18.cloned.1.call-done = bf16[4096,1024]{1,0:T(8,128)(2,1)} async-done(((bf16[1024,1024]{1,0:T(8,128)(2,1)}), bf16[4096,1024]{1,0:T(8,128)(2,1)}) %all-gather.18.cloned.1.call-update) | async-done | bytes 8388624 | tf_op jit(solution)/shard_map/all_gather | solution.py:259
  364.0 22.6 %convert_reduce_fusion = (f32[4096]{0:T(1024)S(1)}, bf16[4096,1024]{0,1:T(8,128)(2,1)}) fusion(f32[1024,4096]{1,0:T(8,128)} %get-tuple-element.345, f32[4096]{0:T(1024)S(1)} %bitcast.853, bf16[1024,1024]{1,0:T(8,128)(2,1)S(1)} %bitcast.839, bf16[4096,1024]{1,0:T(8,128)(2,1)} %all-gather.18.cloned.1.call-done), kind=kOutput, calls=%fused_computation.13 | convolution fusion | flops 8678010880 | bytes 35684352 | tf_op jit(solution)/shard_map/dot_general | solution.py:18
  386.6 16.2 %fusion.44 = (f32[1024]{0:T(1024)S(1)}, f32[1024]{0:T(1024)S(1)}, f32[1024,1024]{0,1:T(8,128)}) fusion(f32[1024,1024]{1,0:T(8,128)} %get-tuple-element.148, f32[1024]{0:T(1024)S(1)} %get-tuple-element.339, f32[1024]{0:T(1024)S(1)} %bitcast.857, bf16[4096,1024]{0,1:T(8,128)(2,1)} %get-tuple-element.348, bf16[1024,4096]{0,1:T(8,128)(2,1)} %bitcast.824), kind=kOutput, calls=%fused_computation.79 | convolution fusion | flops 8596224000 | bytes 25182208 | tf_op jit(solution)/shard_map/dot_general | solution.py:18
  402.8 14.6 %convolution_convert_fusion = bf16[1024,4096]{1,0:T(8,128)(2,1)} fusion(bf16[4096,1024]{0,1:T(8,128)(2,1)} %get-tuple-element.348, f32[1024,1024]{1,0:T(8,128)} %get-tuple-element.148, f32[1024]{0:T(1024)S(1)} %bitcast.858, f32[1024]{0:T(1024)S(1)} %get-tuple-element.339), kind=kOutput, calls=%fused_computation.20 | convolution fusion | flops 8597274624 | bytes 20979712 | tf_op jit(solution)/shard_map/dot_general | solution.py:18
  417.5 12.0 %copy.1168 = bf16[4096,1024]{1,0:T(8,128)(2,1)} copy(bf16[4096,1024]{0,1:T(8,128)(2,1)} %get-tuple-element.344) | data formatting | bytes 16777216 | tf_op jit(solution)/shard_map/dot_general | solution.py:18
  429.5 20.0 %fusion.46 = (f32[1024]{0:T(1024)S(1)}, bf16[1024,1024]{1,0:T(8,128)(2,1)}, f32[1024]{0:T(1024)S(1)}, bf16[1024,1024]{1,0:T(8,128)(2,1)}, f32[1024,1024]{1,0:T(8,128)}) fusion(f32[1024]{0:T(1024)S(1)} %bitcast.855, f32[1024,1024]{1,0:T(8,128)} %get-tuple-element.148, f32[1024,1024]{0,1:T(8,128)} %get-tuple-element.343, ...), kind=kOutput, calls=%fused_computation.83 | convolution fusion | flops 8608806912 | bytes 39876608 | tf_op jit(solution)/shard_map/dot_general | solution.py:18
  449.4 8.5 convert_reduce_fusion.2
  461.5 5.4 convert_bitcast_fusion.2
  477.2 15.1 %convolution_convert_fusion.1 = bf16[4,1024,1024]{2,1,0:T(8,128)(2,1)} fusion(bf16[4,1024,1024]{2,1,0:T(8,128)(2,1)} %bitcast.821, bf16[1024,1024,1]{1,0,2:T(8,128)(2,1)} %bitcast.838), kind=kOutput, calls=%fused_computation.21 | convolution fusion | flops 8594128896 | bytes 18874368 | tf_op jit(solution)/shard_map/dot_general | solution.py:18
  500.9 8.5 copy.1154
  509.4 7.8 convert_element_type.462
  523.5 8.0 copy.1222
  531.5 8.2 copy.1159
  539.7 8.2 copy.1163
  550.9 5.1 dynamic-slice_bitcast_fusion
  566.4 4.5 all-to-all-start.5
  571.4 4.7 copy.1116
  576.2 6.0 reshape.5546
  582.2 4.5 fusion.21.g_ref
  586.7 56.5 %shard_map.314 = (f32[256,32,64]{2,1,0:T(8,128)S(1)}, f32[256,32,64]{2,1,0:T(8,128)S(1)}, f32[256,32,64]{2,1,0:T(8,128)}, f32[256,128]{1,0:T(8,128)S(1)}, f32[256,128]{1,0:T(8,128)S(1)}) custom-call(bf16[256,32,128]{2,1,0:T(8,128)(2,1)S(1)} %fusion.21.g_ref, bf16[256,32,128]{2,1,0:T(8,128)(2,1)S(1)} %copy-done.5, ...), custom_call_target="tpu_custom_call" | custom-call | flops 1073741824 | bytes 19136512 | tf_op jit(solution)/shard_map/pallas_call | solution.py:142
  647.8 39.4 %fusion.80 = (f32[256,4,1,32]{3,2,1,0:T(1,128)}, f32[256,4,1,32]{3,2,1,0:T(1,128)S(1)}, f32[256,4,1,32]{3,2,1,0:T(1,128)S(1)}, f32[256,4,1,32]{3,2,1,0:T(1,128)}...) fusion(f32[256,4,8,64]{3,2,1,0:T(8,128)} %bitcast.800), kind=kLoop, calls=%fused_computation.466 | loop fusion | bytes 4194304 | tf_op jit(solution)/shard_map/slice | solution.py:313
  710.6 8.0 fusion.77
  724.1 8.1 fusion.78
  732.2 24.0 %collective-permute-done.23 = bf16[2,4,256,256]{3,2,1,0:T(8,128)(2,1)S(1)} collective-permute-done((bf16[2,4,256,256]{3,2,1,0:T(8,128)(2,1)S(1)}, bf16[2,4,256,256]{3,2,1,0:T(8,128)(2,1)S(1)}, u32[]{:S(2)}, u32[]{:S(2)}) %collective-permute-start.23) | collective-permute-done | bytes 1048608 | tf_op jit(solution)/shard_map/ppermute | solution.py:155
  757.7 4.7 fusion.79
  762.4 4.8 all-to-all-start.2
  767.2 31.7 %collective-permute-done.24 = bf16[1,4,256,256]{3,2,1,0:T(8,128)(2,1)S(1)} collective-permute-done((bf16[1,4,256,256]{3,2,1,0:T(8,128)(2,1)S(1)}, bf16[1,4,256,256]{3,2,1,0:T(8,128)(2,1)S(1)}, u32[]{:S(2)}, u32[]{:S(2)}) %collective-permute-start.24) | collective-permute-done | bytes 524320 | tf_op jit(solution)/shard_map/ppermute | solution.py:155
  799.1 24.0 %multiply_reduce_fusion.2 = (f32[256,32]{1,0:T(8,128)S(1)}, f32[256,32]{1,0:T(8,128)S(1)}, f32[256,32]{1,0:T(8,128)S(1)}, f32[256,32]{1,0:T(8,128)S(1)}) fusion(f32[256,128]{1,0:T(8,128)S(1)} %get-tuple-element.31, f32[256,32]{1,0:T(8,128)S(1)} %copy-done.165, f32[256,32]{1,0:T(8,128)S(1)} %copy-done.167), kind=kLoop, calls=%fused_computation.109 | loop fusion | flops 12550144 | bytes 327680 | tf_op jit(solution)/shard_map/reduce_sum | solution.py:440
  828.8 4.7 copy.1167
  833.5 4.7 copy.1135
  838.2 5.5 reshape.5547
  865.5 4.7 copy.1209
  876.6 5.6 fusion.9
  886.1 5.6 fusion.8
  897.3 41.1 %collective-permute-done.28 = bf16[2,256,256]{2,1,0:T(8,128)(2,1)S(1)} collective-permute-done((bf16[2,256,256]{2,1,0:T(8,128)(2,1)S(1)}, bf16[2,256,256]{2,1,0:T(8,128)(2,1)S(1)}, u32[]{:S(2)}, u32[]{:S(2)}) %collective-permute-start.28) | collective-permute-done | bytes 262176 | tf_op jit(solution)/shard_map/ppermute | solution.py:155
  944.8 4.4 copy.1133
  949.2 4.5 copy.1134
  953.8 4.8 fusion.40
  961.5 9.4 shard_map.315
  992.4 59.4 %collective-permute-done.37 = bf16[1,4,128,1024]{3,2,1,0:T(8,128)(2,1)S(1)} collective-permute-done((bf16[1,4,128,1024]{3,2,1,0:T(8,128)(2,1)S(1)}, bf16[1,4,128,1024]{3,2,1,0:T(8,128)(2,1)S(1)}, u32[]{:S(2)}, u32[]{:S(2)}) %collective-permute-start.37) | collective-permute-done | bytes 1048608 | tf_op jit(solution)/shard_map/ppermute | solution.py:155
  1053.1 21.1 %collective-permute-done.45 = bf16[1,4,128,1024]{3,2,1,0:T(8,128)(2,1)S(1)} collective-permute-done((bf16[1,4,128,1024]{3,2,1,0:T(8,128)(2,1)S(1)}, bf16[1,4,128,1024]{3,2,1,0:T(8,128)(2,1)S(1)}, u32[]{:S(2)}, u32[]{:S(2)}) %collective-permute-start.45) | collective-permute-done | bytes 1048608 | tf_op jit(solution)/shard_map/ppermute | solution.py:155
  1098.3 4.6 fusion.23
  1103.0 5.3 reshape.5521
  1123.4 5.6 collective-permute-done.48
  1129.2 9.6 collective-permute-done.41
  1140.6 5.6 collective-permute-done.49
  1148.4 16.9 %collective-permute-done.42 = bf16[4,128,1024]{2,1,0:T(8,128)(2,1)S(1)} collective-permute-done((bf16[4,128,1024]{2,1,0:T(8,128)(2,1)S(1)}, bf16[4,128,1024]{2,1,0:T(8,128)(2,1)S(1)}, u32[]{:S(2)}, u32[]{:S(2)}) %collective-permute-start.42) | collective-permute-done | bytes 1048608 | tf_op jit(solution)/shard_map/ppermute | solution.py:155
  1168.1 10.0 collective-permute-done.50
  (717 shorter events, 311.8 us)
Async XLA Ops:
  7.2 164.2 %all-gather.12.cloned.1.call-start = ((), (), s32[]{:S(2)}) async-start(), calls=%async_computation.6 | async-start | bytes 2359296 | tf_op jit(solution)/shard_map/all_gather | solution.py:318
  10.0 58.7 %collective-permute-start = (f32[32,128]{1,0:T(8,128)S(1)}, f32[32,128]{1,0:T(8,128)S(1)}, u32[]{:S(2)}, u32[]{:S(2)}) collective-permute-start(f32[32,128]{1,0:T(8,128)S(1)} %reduce_sum.298), channel_id=1, source_target_pairs={{0,1},{1,0},{2,3},{3,2},{4,5},{5,4},{6,7},{7,6},{8,9},{9,8},{10,11... | collective-permute-start | bytes 49160 | tf_op jit(solution)/shard_map/ppermute | solution.py:155
  16.0 168.7 %copy-start.26 = (f32[256,32]{0,1:T(8,128)}, f32[256,32]{0,1:T(8,128)S(1)}, u32[]{:S(2)}) copy-start(f32[256,32]{0,1:T(8,128)S(1)} %get-tuple-element.308) | copy-start | bytes 98308
  16.0 168.7 %copy-start.28 = (f32[256,32]{0,1:T(8,128)}, f32[256,32]{0,1:T(8,128)S(1)}, u32[]{:S(2)}) copy-start(f32[256,32]{0,1:T(8,128)S(1)} %get-tuple-element.309) | copy-start | bytes 98308
  68.7 8.8 collective-permute-start.1
  121.6 120.2 %all-gather.14.cloned.1.call-start = ((), (), s32[]{:S(2)}) async-start(), calls=%async_computation.7 | async-start | bytes 5242880 | tf_op jit(solution)/shard_map/all_gather | solution.py:257
  122.9 181.3 %all-gather.16.cloned.1.call-start = ((), (), s32[]{:S(2)}) async-start(), calls=%async_computation.8 | async-start | bytes 10485760 | tf_op jit(solution)/shard_map/all_gather | solution.py:258
  123.6 240.3 %all-gather.18.cloned.1.call-start = ((), (), s32[]{:S(2)}) async-start(), calls=%async_computation.9 | async-start | bytes 10485760 | tf_op jit(solution)/shard_map/all_gather | solution.py:259
  127.9 50.7 %all-to-all-start.3 = ((bf16[4,256,1024]{2,1,0:T(8,128)(2,1)}), bf16[4,256,1024]{2,1,0:T(8,128)(2,1)}, u32[]{:S(2)}, u32[]{:S(2)}) async-start(bf16[4,256,1024]{2,1,0:T(8,128)(2,1)} %bitcast.825), calls=%async_computation.3 | async-start | bytes 4194304 | tf_op jit(solution)/shard_map/all_to_all | solution.py:239
  178.7 48.2 %all-to-all-start = ((bf16[4,256,1024]{2,1,0:T(8,128)(2,1)}), bf16[4,256,1024]{2,1,0:T(8,128)(2,1)}, u32[]{:S(2)}, u32[]{:S(2)}) async-start(bf16[4,256,1024]{2,1,0:T(8,128)(2,1)} %bitcast.798), calls=%async_computation | async-start | bytes 4194304 | tf_op jit(solution)/shard_map/all_to_all | solution.py:239
  226.9 48.9 %all-to-all-start.1 = ((bf16[4,256,1024]{2,1,0:T(8,128)(2,1)}), bf16[4,256,1024]{2,1,0:T(8,128)(2,1)}, u32[]{:S(2)}, u32[]{:S(2)}) async-start(bf16[4,256,1024]{2,1,0:T(8,128)(2,1)} %bitcast.797), calls=%async_computation.1 | async-start | bytes 4194304 | tf_op jit(solution)/shard_map/all_to_all | solution.py:239
  461.3 35.2 %collective-permute-start.30 = (f32[4,2052]{1,0:T(4,128)S(1)}, f32[4,2052]{1,0:T(4,128)S(1)}, u32[]{:S(2)}, u32[]{:S(2)}) collective-permute-start(f32[4,2052]{1,0:T(4,128)S(1)} %constant_dynamic-update-slice_fusion), channel_id=1, source_target_pairs={{0,1},{1,0},{2,3},{3,2},{4,5},{5,4},{6,7},{7,6},{8,9},{9,8},{10,11... | collective-permute-start | bytes 98504 | tf_op jit(solution)/shard_map/ppermute | solution.py:155
  473.4 93.0 %all-to-all-start.4 = ((bf16[4,256,1024]{2,1,0:T(8,128)(2,1)}), bf16[4,256,1024]{2,1,0:T(8,128)(2,1)S(1)}, u32[]{:S(2)}, u32[]{:S(2)}) async-start(bf16[4,256,1024]{2,1,0:T(8,128)(2,1)} %bitcast.844), calls=%async_computation.4 | async-start | bytes 4194304 | tf_op jit(solution)/shard_map/all_to_all | solution.py:246
  496.5 23.7 %collective-permute-start.31 = (f32[4,2052]{1,0:T(4,128)S(1)}, f32[4,2052]{1,0:T(4,128)S(1)}, u32[]{:S(2)}, u32[]{:S(2)}) collective-permute-start(f32[4,2052]{1,0:T(4,128)S(1)} %add.5059), channel_id=1, source_target_pairs={{0,2},{1,3},{2,0},{3,1},{4,6},{5,7},{6,4},{7,5},{8,10},{9,11},{10,... | collective-permute-start | bytes 98504 | tf_op jit(solution)/shard_map/ppermute | solution.py:155
  520.2 29.2 %collective-permute-start.32 = (f32[2052]{0:T(1024)S(1)}, f32[2052]{0:T(1024)S(1)}, u32[]{:S(2)}, u32[]{:S(2)}) collective-permute-start(f32[2052]{0:T(1024)S(1)} %fusion.66), channel_id=1, source_target_pairs={{0,4},{4,0},{8,12},{12,8},{16,20},{20,16},{24,28},{28,24},{1,5},{5... | collective-permute-start | bytes 24632 | tf_op jit(solution)/shard_map/ppermute | solution.py:155
  547.9 170.7 %collective-permute-start.22 = (bf16[4,4,256,256]{3,2,1,0:T(8,128)(2,1)}, bf16[4,4,256,256]{3,2,1,0:T(8,128)(2,1)}, u32[]{:S(2)}, u32[]{:S(2)}) collective-permute-start(bf16[4,4,256,256]{3,2,1,0:T(8,128)(2,1)} %dynamic-slice_bitcast_fusion.4), channel_id=1, source_target_pairs={{0,4},{4,0},{8,12},{12,8},{16,20},{20,16},{24,28},{28,24},{1,5},{5... | collective-permute-start | bytes 6291464 | tf_op jit(solution)/shard_map/ppermute | solution.py:155
  549.4 6.6 collective-permute-start.33
  556.0 6.8 collective-permute-start.34
  560.8 315.8 %collective-permute-start.35 = (bf16[4,4,128,1024]{3,2,1,0:T(8,128)(2,1)}, bf16[4,4,128,1024]{3,2,1,0:T(8,128)(2,1)}, u32[]{:S(2)}, u32[]{:S(2)}) collective-permute-start(bf16[4,4,128,1024]{3,2,1,0:T(8,128)(2,1)} %dynamic-slice_bitcast_fusion.1), channel_id=1, source_target_pairs={{0,4},{4,0},{8,12},{12,8},{16,20},{20,16},{24,28},{28,24},{1,5},{5... | collective-permute-start | bytes 12582920 | tf_op jit(solution)/shard_map/ppermute | solution.py:155
  561.3 324.8 %collective-permute-start.43 = (bf16[4,4,128,1024]{3,2,1,0:T(8,128)(2,1)}, bf16[4,4,128,1024]{3,2,1,0:T(8,128)(2,1)}, u32[]{:S(2)}, u32[]{:S(2)}) collective-permute-start(bf16[4,4,128,1024]{3,2,1,0:T(8,128)(2,1)} %dynamic-slice_bitcast_fusion), channel_id=1, source_target_pairs={{0,4},{4,0},{8,12},{12,8},{16,20},{20,16},{24,28},{28,24},{1,5},{5... | collective-permute-start | bytes 12582920 | tf_op jit(solution)/shard_map/ppermute | solution.py:155
  566.4 195.9 %all-to-all-start.5 = ((bf16[4,256,1024]{2,1,0:T(8,128)(2,1)}), bf16[4,256,1024]{2,1,0:T(8,128)(2,1)}, u32[]{:S(2)}, u32[]{:S(2)}) async-start(bf16[4,256,1024]{2,1,0:T(8,128)(2,1)} %bitcast.101), calls=%async_computation.5 | async-start | bytes 4194304 | tf_op jit(solution)/shard_map/all_to_all | solution.py:246
  570.9 369.8 %all-gather.20.cloned.1.call-start = ((), (), s32[]{:S(2)}) async-start(), calls=%async_computation.10 | async-start | bytes 2359296 | tf_op jit(solution)/shard_map/all_gather | solution.py:318
  647.2 176.0 %collective-permute-start.19 = (f32[256]{0:T(256)S(1)}, f32[256]{0:T(256)S(1)}, u32[]{:S(2)}, u32[]{:S(2)}) collective-permute-start(f32[256]{0:T(256)S(1)} %reduce_sum.316), channel_id=1, source_target_pairs={{0,4},{4,0},{8,12},{12,8},{16,20},{20,16},{24,28},{28,24},{1,5},{5... | collective-permute-start | bytes 3080 | tf_op jit(solution)/shard_map/ppermute | solution.py:155
  722.5 33.7 %collective-permute-start.23 = (bf16[2,4,256,256]{3,2,1,0:T(8,128)(2,1)S(1)}, bf16[2,4,256,256]{3,2,1,0:T(8,128)(2,1)S(1)}, u32[]{:S(2)}, u32[]{:S(2)}) collective-permute-start(bf16[2,4,256,256]{3,2,1,0:T(8,128)(2,1)S(1)} %dynamic-slice_bitcast_fusion.5), channel_id=1, source_target_pairs={{0,8},{4,12},{8,0},{12,4},{16,24},{20,28},{24,16},{28,20},{1,9},{5... | collective-permute-start | bytes 3145736 | tf_op jit(solution)/shard_map/ppermute | solution.py:155
  756.5 42.3 %collective-permute-start.24 = (bf16[1,4,256,256]{3,2,1,0:T(8,128)(2,1)S(1)}, bf16[1,4,256,256]{3,2,1,0:T(8,128)(2,1)S(1)}, u32[]{:S(2)}, u32[]{:S(2)}) collective-permute-start(bf16[1,4,256,256]{3,2,1,0:T(8,128)(2,1)S(1)} %constant_dynamic-slice_fusion.5), channel_id=1, source_target_pairs={{0,16},{4,20},{8,24},{12,28},{16,0},{20,4},{24,8},{28,12},{1,17},{... | collective-permute-start | bytes 1572872 | tf_op jit(solution)/shard_map/ppermute | solution.py:155
  762.4 66.5 %all-to-all-start.2 = ((bf16[4,256,1024]{2,1,0:T(8,128)(2,1)}), bf16[4,256,1024]{2,1,0:T(8,128)(2,1)}, u32[]{:S(2)}, u32[]{:S(2)}) async-start(bf16[4,256,1024]{2,1,0:T(8,128)(2,1)} %bitcast.837), calls=%async_computation.2 | async-start | bytes 4194304 | tf_op jit(solution)/shard_map/all_to_all | solution.py:246
  799.0 24.2 %collective-permute-start.25 = (bf16[2,256,256]{2,1,0:T(8,128)(2,1)S(1)}, bf16[2,256,256]{2,1,0:T(8,128)(2,1)S(1)}, u32[]{:S(2)}, u32[]{:S(2)}) collective-permute-start(bf16[2,256,256]{2,1,0:T(8,128)(2,1)S(1)} %dynamic-slice_bitcast_fusion.8), channel_id=1, source_target_pairs={{0,1},{1,0},{2,3},{3,2},{4,5},{5,4},{6,7},{7,6},{8,9},{9,8},{10,11... | collective-permute-start | bytes 786440 | tf_op jit(solution)/shard_map/ppermute | solution.py:155
  823.2 20.5 %collective-permute-start.20 = (f32[256]{0:T(256)S(1)}, f32[256]{0:T(256)S(1)}, u32[]{:S(2)}, u32[]{:S(2)}) collective-permute-start(f32[256]{0:T(256)S(1)} %add.5036), channel_id=1, source_target_pairs={{0,8},{4,12},{8,0},{12,4},{16,24},{20,28},{24,16},{28,20},{1,9},{5... | collective-permute-start | bytes 3080 | tf_op jit(solution)/shard_map/ppermute | solution.py:155
  823.4 51.8 %collective-permute-start.26 = (bf16[1,256,256]{2,1,0:T(8,128)(2,1)S(1)}, bf16[1,256,256]{2,1,0:T(8,128)(2,1)S(1)}, u32[]{:S(2)}, u32[]{:S(2)}) collective-permute-start(bf16[1,256,256]{2,1,0:T(8,128)(2,1)S(1)} %constant_dynamic-slice_fusion.4), channel_id=1, source_target_pairs={{0,2},{1,3},{2,0},{3,1},{4,6},{5,7},{6,4},{7,5},{8,10},{9,11},{10,... | collective-permute-start | bytes 393224 | tf_op jit(solution)/shard_map/ppermute | solution.py:155
  843.7 30.9 %collective-permute-start.21 = (f32[256]{0:T(256)S(1)}, f32[256]{0:T(256)S(1)}, u32[]{:S(2)}, u32[]{:S(2)}) collective-permute-start(f32[256]{0:T(256)S(1)} %add.5037), channel_id=1, source_target_pairs={{0,16},{4,20},{8,24},{12,28},{16,0},{20,4},{24,8},{28,12},{1,17},{... | collective-permute-start | bytes 3080 | tf_op jit(solution)/shard_map/ppermute | solution.py:155
  875.2 10.8 collective-permute-start.27
  884.0 95.4 %collective-permute-start.36 = (bf16[2,4,128,1024]{3,2,1,0:T(8,128)(2,1)}, bf16[2,4,128,1024]{3,2,1,0:T(8,128)(2,1)}, u32[]{:S(2)}, u32[]{:S(2)}) collective-permute-start(bf16[2,4,128,1024]{3,2,1,0:T(8,128)(2,1)} %dynamic-slice_bitcast_fusion.3), channel_id=1, source_target_pairs={{0,8},{4,12},{8,0},{12,4},{16,24},{20,28},{24,16},{28,20},{1,9},{5... | collective-permute-start | bytes 6291464 | tf_op jit(solution)/shard_map/ppermute | solution.py:155
  886.0 52.3 %collective-permute-start.28 = (bf16[2,256,256]{2,1,0:T(8,128)(2,1)S(1)}, bf16[2,256,256]{2,1,0:T(8,128)(2,1)S(1)}, u32[]{:S(2)}, u32[]{:S(2)}) collective-permute-start(bf16[2,256,256]{2,1,0:T(8,128)(2,1)S(1)} %maximum_bitcast_fusion.2), channel_id=1, source_target_pairs={{0,8},{4,12},{8,0},{12,4},{16,24},{20,28},{24,16},{28,20},{1,9},{5... | collective-permute-start | bytes 786440 | tf_op jit(solution)/shard_map/ppermute | solution.py:155
  895.3 87.2 %collective-permute-start.44 = (bf16[2,4,128,1024]{3,2,1,0:T(8,128)(2,1)}, bf16[2,4,128,1024]{3,2,1,0:T(8,128)(2,1)}, u32[]{:S(2)}, u32[]{:S(2)}) collective-permute-start(bf16[2,4,128,1024]{3,2,1,0:T(8,128)(2,1)} %dynamic-slice_bitcast_fusion.2), channel_id=1, source_target_pairs={{0,8},{4,12},{8,0},{12,4},{16,24},{20,28},{24,16},{28,20},{1,9},{5... | collective-permute-start | bytes 6291464 | tf_op jit(solution)/shard_map/ppermute | solution.py:155
  939.3 35.0 %collective-permute-start.29 = (bf16[4,256,256]{2,1,0:T(8,128)(2,1)}, bf16[4,256,256]{2,1,0:T(8,128)(2,1)}, u32[]{:S(2)}, u32[]{:S(2)}) collective-permute-start(bf16[4,256,256]{2,1,0:T(8,128)(2,1)} %bitcast.125), channel_id=1, source_target_pairs={{0,4},{4,0},{8,12},{12,8},{16,20},{20,16},{24,28},{28,24},{1,5},{5... | collective-permute-start | bytes 1572872 | tf_op jit(solution)/shard_map/ppermute | solution.py:155
  973.7 3.6 collective-permute-start.4
  975.6 16.2 %collective-permute-start.2 = (f32[32,128]{1,0:T(8,128)S(1)}, f32[32,128]{1,0:T(8,128)S(1)}, u32[]{:S(2)}, u32[]{:S(2)}) collective-permute-start(f32[32,128]{1,0:T(8,128)S(1)} %get-tuple-element.95), channel_id=1, source_target_pairs={{0,1},{1,0},{2,3},{3,2},{4,5},{5,4},{6,7},{7,6},{8,9},{9,8},{10,11... | collective-permute-start | bytes 49160 | tf_op jit(solution)/shard_map/ppermute | solution.py:155
  977.3 12.9 %collective-permute-start.5 = (f32[256]{0:T(256)S(1)}, f32[256]{0:T(256)S(1)}, u32[]{:S(2)}, u32[]{:S(2)}) collective-permute-start(f32[256]{0:T(256)S(1)} %add.5008), channel_id=1, source_target_pairs={{0,8},{4,12},{8,0},{12,4},{16,24},{20,28},{24,16},{28,20},{1,9},{5... | collective-permute-start | bytes 3080 | tf_op jit(solution)/shard_map/ppermute | solution.py:155
  982.2 69.6 %collective-permute-start.37 = (bf16[1,4,128,1024]{3,2,1,0:T(8,128)(2,1)S(1)}, bf16[1,4,128,1024]{3,2,1,0:T(8,128)(2,1)S(1)}, u32[]{:S(2)}, u32[]{:S(2)}) collective-permute-start(bf16[1,4,128,1024]{3,2,1,0:T(8,128)(2,1)S(1)} %constant_dynamic-slice_fusion.3), channel_id=1, source_target_pairs={{0,16},{4,20},{8,24},{12,28},{16,0},{20,4},{24,8},{28,12},{1,17},{... | collective-permute-start | bytes 3145736 | tf_op jit(solution)/shard_map/ppermute | solution.py:155
  985.4 88.8 %collective-permute-start.45 = (bf16[1,4,128,1024]{3,2,1,0:T(8,128)(2,1)S(1)}, bf16[1,4,128,1024]{3,2,1,0:T(8,128)(2,1)S(1)}, u32[]{:S(2)}, u32[]{:S(2)}) collective-permute-start(bf16[1,4,128,1024]{3,2,1,0:T(8,128)(2,1)S(1)} %constant_dynamic-slice_fusion.1), channel_id=1, source_target_pairs={{0,16},{4,20},{8,24},{12,28},{16,0},{20,4},{24,8},{28,12},{1,17},{... | collective-permute-start | bytes 3145736 | tf_op jit(solution)/shard_map/ppermute | solution.py:155
  989.6 87.3 %collective-permute-start.7 = (f32[256,32]{0,1:T(8,128)S(1)}, f32[256,32]{0,1:T(8,128)S(1)}, u32[]{:S(2)}, u32[]{:S(2)}) collective-permute-start(f32[256,32]{0,1:T(8,128)S(1)} %add.5018), channel_id=1, source_target_pairs={{0,4},{4,0},{8,12},{12,8},{16,20},{20,16},{24,28},{28,24},{1,5},{5... | collective-permute-start | bytes 98312 | tf_op jit(solution)/shard_map/ppermute | solution.py:155
  990.3 87.3 %collective-permute-start.10 = (f32[256,32]{0,1:T(8,128)S(1)}, f32[256,32]{0,1:T(8,128)S(1)}, u32[]{:S(2)}, u32[]{:S(2)}) collective-permute-start(f32[256,32]{0,1:T(8,128)S(1)} %add.5023), channel_id=1, source_target_pairs={{0,4},{4,0},{8,12},{12,8},{16,20},{20,16},{24,28},{28,24},{1,5},{5... | collective-permute-start | bytes 98312 | tf_op jit(solution)/shard_map/ppermute | solution.py:155
  991.8 91.4 %collective-permute-start.16 = (f32[256,32]{0,1:T(8,128)S(1)}, f32[256,32]{0,1:T(8,128)S(1)}, u32[]{:S(2)}, u32[]{:S(2)}) collective-permute-start(f32[256,32]{0,1:T(8,128)S(1)} %add.5032), channel_id=1, source_target_pairs={{0,4},{4,0},{8,12},{12,8},{16,20},{20,16},{24,28},{28,24},{1,5},{5... | collective-permute-start | bytes 98312 | tf_op jit(solution)/shard_map/ppermute | solution.py:155
  1051.8 23.7 %collective-permute-start.6 = (f32[256]{0:T(256)S(1)}, f32[256]{0:T(256)S(1)}, u32[]{:S(2)}, u32[]{:S(2)}) collective-permute-start(f32[256]{0:T(256)S(1)} %add.5009), channel_id=1, source_target_pairs={{0,16},{4,20},{8,24},{12,28},{16,0},{20,4},{24,8},{28,12},{1,17},{... | collective-permute-start | bytes 3080 | tf_op jit(solution)/shard_map/ppermute | solution.py:155
  1074.2 11.4 collective-permute-start.38
  1075.4 7.9 collective-permute-start.13
  1076.9 8.5 collective-permute-start.3
  1077.6 11.5 collective-permute-start.46
  1083.2 14.9 %collective-permute-start.8 = (f32[256,32]{0,1:T(8,128)S(1)}, f32[256,32]{0,1:T(8,128)S(1)}, u32[]{:S(2)}, u32[]{:S(2)}) collective-permute-start(f32[256,32]{0,1:T(8,128)S(1)} %add.5019), channel_id=1, source_target_pairs={{0,8},{4,12},{8,0},{12,4},{16,24},{20,28},{24,16},{28,20},{1,9},{5... | collective-permute-start | bytes 98312 | tf_op jit(solution)/shard_map/ppermute | solution.py:155
  1083.3 24.9 %collective-permute-start.11 = (f32[256,32]{0,1:T(8,128)S(1)}, f32[256,32]{0,1:T(8,128)S(1)}, u32[]{:S(2)}, u32[]{:S(2)}) collective-permute-start(f32[256,32]{0,1:T(8,128)S(1)} %add.5024), channel_id=1, source_target_pairs={{0,8},{4,12},{8,0},{12,4},{16,24},{20,28},{24,16},{28,20},{1,9},{5... | collective-permute-start | bytes 98312 | tf_op jit(solution)/shard_map/ppermute | solution.py:155
  1085.4 25.8 %collective-permute-start.17 = (f32[256,32]{0,1:T(8,128)S(1)}, f32[256,32]{0,1:T(8,128)S(1)}, u32[]{:S(2)}, u32[]{:S(2)}) collective-permute-start(f32[256,32]{0,1:T(8,128)S(1)} %add.5033), channel_id=1, source_target_pairs={{0,8},{4,12},{8,0},{12,4},{16,24},{20,28},{24,16},{28,20},{1,9},{5... | collective-permute-start | bytes 98312 | tf_op jit(solution)/shard_map/ppermute | solution.py:155
  1085.5 25.8 %collective-permute-start.14 = (f32[256,32]{0,1:T(8,128)S(1)}, f32[256,32]{0,1:T(8,128)S(1)}, u32[]{:S(2)}, u32[]{:S(2)}) collective-permute-start(f32[256,32]{0,1:T(8,128)S(1)} %add.5029), channel_id=1, source_target_pairs={{0,8},{4,12},{8,0},{12,4},{16,24},{20,28},{24,16},{28,20},{1,9},{5... | collective-permute-start | bytes 98312 | tf_op jit(solution)/shard_map/ppermute | solution.py:155
  1089.0 7.7 collective-permute-start.39
  1096.7 17.6 %collective-permute-start.47 = (bf16[1,128,1024]{2,1,0:T(8,128)(2,1)S(1)}, bf16[1,128,1024]{2,1,0:T(8,128)(2,1)S(1)}, u32[]{:S(2)}, u32[]{:S(2)}) collective-permute-start(bf16[1,128,1024]{2,1,0:T(8,128)(2,1)S(1)} %constant_dynamic-slice_fusion), channel_id=1, source_target_pairs={{0,2},{1,3},{2,0},{3,1},{4,6},{5,7},{6,4},{7,5},{8,10},{9,11},{10,... | collective-permute-start | bytes 786440 | tf_op jit(solution)/shard_map/ppermute | solution.py:155
  1098.2 16.3 %collective-permute-start.40 = (bf16[1,128,1024]{2,1,0:T(8,128)(2,1)S(1)}, bf16[1,128,1024]{2,1,0:T(8,128)(2,1)S(1)}, u32[]{:S(2)}, u32[]{:S(2)}) collective-permute-start(bf16[1,128,1024]{2,1,0:T(8,128)(2,1)S(1)} %add_convert_fusion.5), channel_id=1, source_target_pairs={{0,16},{4,20},{8,24},{12,28},{16,0},{20,4},{24,8},{28,12},{1,17},{... | collective-permute-start | bytes 786440 | tf_op jit(solution)/shard_map/ppermute | solution.py:155
  1108.2 31.5 %collective-permute-start.9 = (f32[256,32]{0,1:T(8,128)S(1)}, f32[256,32]{0,1:T(8,128)S(1)}, u32[]{:S(2)}, u32[]{:S(2)}) collective-permute-start(f32[256,32]{0,1:T(8,128)S(1)} %add.5020), channel_id=1, source_target_pairs={{0,16},{4,20},{8,24},{12,28},{16,0},{20,4},{24,8},{28,12},{1,17},{... | collective-permute-start | bytes 98312 | tf_op jit(solution)/shard_map/ppermute | solution.py:155
  1111.2 28.6 %collective-permute-start.12 = (f32[256,32]{0,1:T(8,128)S(1)}, f32[256,32]{0,1:T(8,128)S(1)}, u32[]{:S(2)}, u32[]{:S(2)}) collective-permute-start(f32[256,32]{0,1:T(8,128)S(1)} %add.5025), channel_id=1, source_target_pairs={{0,16},{4,20},{8,24},{12,28},{16,0},{20,4},{24,8},{28,12},{1,17},{... | collective-permute-start | bytes 98312 | tf_op jit(solution)/shard_map/ppermute | solution.py:155
  1111.3 9.9 collective-permute-start.18
  1114.3 8.4 collective-permute-start.15
  1114.5 14.5 %collective-permute-start.48 = (bf16[1,128,1024]{2,1,0:T(8,128)(2,1)S(1)}, bf16[1,128,1024]{2,1,0:T(8,128)(2,1)S(1)}, u32[]{:S(2)}, u32[]{:S(2)}) collective-permute-start(bf16[1,128,1024]{2,1,0:T(8,128)(2,1)S(1)} %add_convert_fusion.4), channel_id=1, source_target_pairs={{0,16},{4,20},{8,24},{12,28},{16,0},{20,4},{24,8},{28,12},{1,17},{... | collective-permute-start | bytes 786440 | tf_op jit(solution)/shard_map/ppermute | solution.py:155
  1121.3 17.6 %collective-permute-start.41 = (bf16[2,128,1024]{2,1,0:T(8,128)(2,1)S(1)}, bf16[2,128,1024]{2,1,0:T(8,128)(2,1)S(1)}, u32[]{:S(2)}, u32[]{:S(2)}) collective-permute-start(bf16[2,128,1024]{2,1,0:T(8,128)(2,1)S(1)} %maximum_bitcast_fusion), channel_id=1, source_target_pairs={{0,8},{4,12},{8,0},{12,4},{16,24},{20,28},{24,16},{28,20},{1,9},{5... | collective-permute-start | bytes 1572872 | tf_op jit(solution)/shard_map/ppermute | solution.py:155
  1129.1 17.0 %collective-permute-start.49 = (bf16[2,128,1024]{2,1,0:T(8,128)(2,1)S(1)}, bf16[2,128,1024]{2,1,0:T(8,128)(2,1)S(1)}, u32[]{:S(2)}, u32[]{:S(2)}) collective-permute-start(bf16[2,128,1024]{2,1,0:T(8,128)(2,1)S(1)} %maximum_bitcast_fusion.1), channel_id=1, source_target_pairs={{0,8},{4,12},{8,0},{12,4},{16,24},{20,28},{24,16},{28,20},{1,9},{5... | collective-permute-start | bytes 1572872 | tf_op jit(solution)/shard_map/ppermute | solution.py:155
  1139.1 26.2 %collective-permute-start.42 = (bf16[4,128,1024]{2,1,0:T(8,128)(2,1)S(1)}, bf16[4,128,1024]{2,1,0:T(8,128)(2,1)S(1)}, u32[]{:S(2)}, u32[]{:S(2)}) collective-permute-start(bf16[4,128,1024]{2,1,0:T(8,128)(2,1)S(1)} %bitcast.826), channel_id=1, source_target_pairs={{0,4},{4,0},{8,12},{12,8},{16,20},{20,16},{24,28},{28,24},{1,5},{5... | collective-permute-start | bytes 3145736 | tf_op jit(solution)/shard_map/ppermute | solution.py:155
  1146.4 31.6 %collective-permute-start.50 = (bf16[4,128,1024]{2,1,0:T(8,128)(2,1)S(1)}, bf16[4,128,1024]{2,1,0:T(8,128)(2,1)S(1)}, u32[]{:S(2)}, u32[]{:S(2)}) collective-permute-start(bf16[4,128,1024]{2,1,0:T(8,128)(2,1)S(1)} %bitcast.827), channel_id=1, source_target_pairs={{0,4},{4,0},{8,12},{12,8},{16,20},{20,16},{24,28},{28,24},{1,5},{5... | collective-permute-start | bytes 3145736 | tf_op jit(solution)/shard_map/ppermute | solution.py:155
  (187 other events, 2901.0 us)
Sparse Core Ops, SparseCore 0:
  121.8 49.5 all-gather.11
  172.9 50.7 all-gather.13
  225.3 78.8 all-gather.15
  305.6 58.2 all-gather.17
  724.2 72.4 all-gather.19

commit v2 on v1

v2 whole, which is shorter than its diff:
```python
import functools

import jax
import jax.numpy as jnp
from jax import lax
from jax.experimental import pallas as pl
from jax.experimental.pallas import tpu as pltpu
from jax.sharding import PartitionSpec as P

D = 1024
epsilon = 1e-05
CHUNK = 128
f32 = jnp.float32
bf16 = jnp.bfloat16


def contract(left, right, left_dim, right_dim):
    return lax.dot_general(
        left, right, (((left_dim,), (right_dim,)), ((), ())), preferred_element_type=f32
    )


def nt(left, right):
    return lax.dot_general(left, right, (((1,), (1,)), ((), ())), preferred_element_type=f32)


def nn(left, right):
    return lax.dot_general(left, right, (((1,), (0,)), ((), ())), preferred_element_type=f32)


def tn(left, right):
    return lax.dot_general(left, right, (((0,), (0,)), ((), ())), preferred_element_type=f32)


def gelu_pair(v):
    k0 = 0.7978845608028654
    k1 = 0.044715
    square = v * v
    t = jnp.tanh(k0 * v * (1.0 + k1 * square))
    half = 0.5 * (1.0 + t)
    return v * half, half + 0.5 * v * (1.0 - t * t) * k0 * (1.0 + 3.0 * k1 * square)


def cmul(a, b):
    return (a[0] * b[0] - a[1] * b[1], a[0] * b[1] + a[1] * b[0])


def cadd(a, b):
    return (a[0] + b[0], a[1] + b[1])


def discretized(step, decay, freq):
    return step[:, None] * (-decay), step[:, None] * freq


def coefficients(step, decay, freq, out_real, out_imag):
    a_real, a_imag = -decay, freq
    w_real, w_imag = discretized(step, decay, freq)
    growth = jnp.exp(w_real)
    minus_real = growth * jnp.cos(w_imag) - 1.0
    minus_imag = growth * jnp.sin(w_imag)
    modulus = a_real * a_real + a_imag * a_imag
    ratio_real = (minus_real * a_real + minus_imag * a_imag) / modulus
    ratio_imag = (minus_imag * a_real - minus_real * a_imag) / modulus
    return (
        out_real * ratio_real - out_imag * ratio_imag,
        out_real * ratio_imag + out_imag * ratio_real,
    )


def power(w, exponent):
    envelope = jnp.exp(w[0] * exponent)
    return envelope * jnp.cos(w[1] * exponent), envelope * jnp.sin(w[1] * exponent)


GROUP = 8


def four(pair, axis=-1):
    return jnp.concatenate([pair[0], pair[1], -pair[1], pair[0]], axis=axis)


def turn(values):
    return pltpu.roll(values, values.shape[1] // 2, 1)


def row_of_chunk(shape, chunks):
    return lax.rem(lax.broadcasted_iota(jnp.int32, shape, 0), chunks)


def groups_of(block):
    size = min(GROUP, block)
    return [range(k, k + size) for k in range(0, block, size)]


def scan_rows(states, pars_ref, group, chunks, backward):
    rows = states[0].shape[0]
    place = row_of_chunk(states[0].shape, chunks)
    step, k = 1, 0
    while step < chunks:
        if backward:
            moved = [
                jnp.where(place < chunks - step, pltpu.roll(s, rows - step, 0), 0.0) for s in states
            ]
        else:
            moved = [jnp.where(place >= step, pltpu.roll(s, step, 0), 0.0) for s in states]
        turned = [turn(m) for m in moved]
        states = [
            s + m * pars_ref[i, 2 * k : 2 * k + 1, :] + t * pars_ref[i, 2 * k + 1 : 2 * k + 2, :]
            for i, s, m, t in zip(group, states, moved, turned)
        ]
        step, k = 2 * step, k + 1
    return states


def entered(terms, into, chunks, backward):
    rows, width = terms.shape
    wide = jnp.concatenate(
        [jnp.broadcast_to(into[b : b + 1], (chunks, width)) for b in range(rows // chunks)], axis=0
    )
    if chunks == 1:
        return wide
    place = row_of_chunk(terms.shape, chunks)
    if backward:
        return jnp.where(place == chunks - 1, wide, pltpu.roll(terms, rows - 1, 0))
    return jnp.where(place == 0, wide, pltpu.roll(terms, 1, 0))


def weighed(states, turned, pars_ref, i):
    last = pars_ref.shape[1]
    return (
        states * pars_ref[i, last - 2 : last - 1, :] + turned * pars_ref[i, last - 1 : last, :]
    ).astype(bf16)


def toeplitz(taps):
    size = taps.shape[-1]
    rolled = pltpu.roll(jnp.broadcast_to(taps, (size, size)), 0, 1, stride=1, stride_axis=0)
    rows = lax.broadcasted_iota(jnp.int32, (size, size), 0)
    lanes = lax.broadcasted_iota(jnp.int32, (size, size), 1)
    return jnp.where(lanes >= rows, rolled, 0.0).astype(bf16)


def reversal(size):
    rows = lax.broadcasted_iota(jnp.int32, (size, size), 0)
    lanes = lax.broadcasted_iota(jnp.int32, (size, size), 1)
    return jnp.where(rows + lanes == size - 1, 1.0, 0.0).astype(bf16)


def circle(turns):
    x = (turns - jnp.floor(turns + 0.5)) * 3.14159265358979
    s = x * x
    sine = x * (
        1.0
        + s
        * (
            -1.0 / 6.0
            + s
            * (
                1.0 / 120.0
                + s * (-1.0 / 5040.0 + s * (1.0 / 362880.0 + s * (-1.0 / 39916800.0)))
            )
        )
    )
    cosine = 1.0 + s * (
        -0.5
        + s
        * (
            1.0 / 24.0
            + s
            * (
                -1.0 / 720.0
                + s * (1.0 / 40320.0 + s * (-1.0 / 3628800.0 + s * (1.0 / 479001600.0)))
            )
        )
    )
    return 1.0 - 2.0 * sine * sine, 2.0 * sine * cosine


def tables_kernel(
    chunk, steps, step_ref, decay_ref, freq_ref, real_ref, imag_ref,
    pars_ref, one_ref, two_ref, taps_ref, line_ref,
):
    block, modes = decay_ref.shape
    size = one_ref.shape[2]
    step = step_ref[...]
    a_real, a_imag = -decay_ref[...], freq_ref[...]
    w_real, turns = step * a_real, step * a_imag * 0.15915494309189535

    def z_power(exponent):
        envelope = jnp.exp(w_real * exponent)
        cosine, sine = circle(turns * exponent)
        return envelope * cosine, envelope * sine

    z = z_power(1.0)
    minus_real, minus_imag = z[0] - 1.0, z[1]
    modulus = 1.0 / (a_real * a_real + a_imag * a_imag)
    ratio = (
        (minus_real * a_real + minus_imag * a_imag) * modulus,
        (minus_imag * a_real - minus_real * a_imag) * modulus,
    )
    c = cmul((real_ref[...], imag_ref[...]), ratio)
    lines = []
    for k in range(steps):
        zk = z_power(float(chunk * 2**k))
        lines += [(zk[0], zk[0], zk[0], zk[0]), (zk[1], zk[1], -zk[1], -zk[1])]
    lines += [(c[0], -c[0], -c[0], c[0]), (c[1], -c[1], c[1], -c[1])]
    for k, line in enumerate(lines):
        pars_ref[:, k, :] = jnp.concatenate(line, axis=-1)
    line_ref[...] = jnp.zeros_like(line_ref)
    for k, line in enumerate((w_real, turns, c[0], c[1], z[0], z[1])):
        line_ref[:, k, 0:modes] = line
    places = lax.broadcasted_iota(jnp.int32, (modes, size), 1).astype(f32)
    flip = reversal(size)
    for i in range(block):
        cols = line_ref[i].T

        def col(k):
            return jnp.broadcast_to(cols[:modes, k : k + 1], (modes, size))

        envelope = jnp.exp(col(0) * places)
        cosine, sine = circle(col(1) * places)
        level = (envelope * cosine, envelope * sine)
        taps_ref[i : i + 1, :] = 2.0 * jnp.sum(
            col(2) * level[0] - col(3) * level[1], axis=0, keepdims=True
        )
        one_ref[i] = four(cmul(level, (col(4), col(5))), 0).astype(bf16)
        two_ref[i] = nn(four(level, 0).astype(bf16), flip).astype(bf16)


def states_kernel(chunks, x_ref, scale_ref, gain_ref, two_ref, pars_ref, u_ref, q_ref, end_ref):
    rows = x_ref.shape[1]
    for group in groups_of(x_ref.shape[0]):
        us = [
            (x_ref[i].astype(f32) * scale_ref[...] * gain_ref[i : i + 1, :]).astype(bf16)
            for i in group
        ]
        qs = [nt(u, two_ref[i]) for i, u in zip(group, us)]
        wholes = scan_rows(qs, pars_ref, group, chunks, False)
        for i, u, q, whole in zip(group, us, qs, wholes):
            u_ref[i] = u
            q_ref[i] = q
            for b in range(rows // chunks):
                last = b * chunks + chunks - 1
                end_ref[i, b : b + 1, :] = whole[last : last + 1, :]


def mix_kernel(
    chunks, u_ref, q_ref, into_ref, one_ref, taps_ref, skip_ref, pars_ref,
    mixed_ref, state_ref, lifted_ref, flat_ref,
):
    block, rows, size = u_ref.shape
    for group in groups_of(block):
        states = [entered(q_ref[i], into_ref[i], chunks, False) for i in group]
        states = scan_rows(states, pars_ref, group, chunks, False)
        for i, s in zip(group, states):
            state_ref[i] = s
        outs = [weighed(s, turn(s), pars_ref, i) for i, s in zip(group, states)]
        near = [nn(u_ref[i], toeplitz(taps_ref[i : i + 1, :])) for i in group]
        ys = [y + nn(o, one_ref[i]) for i, y, o in zip(group, near, outs)]
        mixes = [
            (y + skip_ref[i : i + 1, :] * u_ref[i].astype(f32)).astype(bf16)
            for i, y in zip(group, ys)
        ]
        for i, mixed in zip(group, mixes):
            mixed_ref[i] = mixed
            flat_ref[i * rows : (i + 1) * rows, :] = gelu_pair(mixed.astype(f32))[0]
    for r in range(rows):
        b, j = r // chunks, r % chunks
        lifted_ref[b, :, j * size : (j + 1) * size] = flat_ref[
            pl.ds(r, block, stride=rows), :
        ].astype(bf16)


def ends_kernel(chunks, gl_ref, mixed_ref, one_ref, pars_ref, g_ref, p_ref, end_ref, flat_ref):
    block, rows, size = mixed_ref.shape
    for r in range(rows):
        b, j = r // chunks, r % chunks
        flat_ref[pl.ds(r, block, stride=rows), :] = gl_ref[
            b, :, j * size : (j + 1) * size
        ].astype(f32)
    for group in groups_of(block):
        gs = [
            (
                flat_ref[i * rows : (i + 1) * rows, :] * gelu_pair(mixed_ref[i].astype(f32))[1]
            ).astype(bf16)
            for i in group
        ]
        ps = [nt(g, one_ref[i]) for i, g in zip(group, gs)]
        wholes = scan_rows(ps, pars_ref, group, chunks, True)
        for i, g, p, whole in zip(group, gs, ps, wholes):
            g_ref[i] = g
            p_ref[i] = p
            for b in range(rows // chunks):
                end_ref[i, b : b + 1, :] = whole[b * chunks : b * chunks + 1, :]


def summed(values):
    return jnp.sum(values, axis=0, keepdims=True)


def sums_kernel(g_ref, u_ref, state_ref, p_ref, one_ref, sum_ref):
    block, rows, size = g_ref.shape
    lanes = lax.broadcasted_iota(jnp.int32, (rows, size), 1).astype(f32)
    row_id = lax.broadcasted_iota(jnp.int32, (size, size), 0)
    lane_id = lax.broadcasted_iota(jnp.int32, (size, size), 1)
    places = lane_id[0:1].astype(f32)
    keep = lane_id <= row_id
    flip = reversal(size)
    for group in groups_of(block):
        flipped = [nt(flip, u_ref[i]).astype(bf16) for i in group]
        pas = [nt((g_ref[i].astype(f32) * lanes).astype(bf16), one_ref[i]) for i in group]
        outers = [nn(f, g_ref[i]) for i, f in zip(group, flipped)]
        lags = [
            summed(jnp.where(keep, pltpu.roll(o, 1, 1, stride=1, stride_axis=0), 0.0))
            for o in outers
        ]
        stacked = []
        for lag in lags:
            parts = []
            for v in (lag, lag * places):
                high = v.astype(bf16).astype(f32)
                parts += [high, v - high]
            stacked += [
                jnp.concatenate(parts + [jnp.zeros((4, size), f32)], axis=0).astype(bf16)
            ]
        withins = [nt(s, one_ref[i]) for i, s in zip(group, stacked)]
        for i, pa, within in zip(group, pas, withins):
            states = state_ref[i]
            p = p_ref[i]
            sum_ref[i, 0:1, :] = summed(states * p)
            sum_ref[i, 1:2, :] = summed(states * turn(p))
            sum_ref[i, 2:3, :] = summed(states * pa)
            sum_ref[i, 3:4, :] = summed(states * turn(pa))
            sum_ref[i, 4:5, :] = within[0:1] + within[1:2]
            sum_ref[i, 5:6, :] = within[2:3] + within[3:4]
            sum_ref[i, 6:7, :] = summed(g_ref[i].astype(f32) * u_ref[i].astype(f32))
            sum_ref[i, 7:8, :] = jnp.zeros((1, size), f32)


def back_kernel(
    chunks, g_ref, p_ref, into_ref, u_ref, state_ref, two_ref, taps_ref, skip_ref, pars_ref,
    out_ref, sum_ref, flat_ref,
):
    block, rows, size = g_ref.shape
    lanes = lax.broadcasted_iota(jnp.int32, (rows, size), 1).astype(f32)
    for group in groups_of(block):
        qps = [nt((u_ref[i].astype(f32) * lanes).astype(bf16), two_ref[i]) for i in group]
        near = [nt(g_ref[i], toeplitz(taps_ref[i : i + 1, :])) for i in group]
        adjoints = [entered(p_ref[i], into_ref[i], chunks, True) for i in group]
        adjoints = scan_rows(adjoints, pars_ref, group, chunks, True)
        turned = [turn(a) for a in adjoints]
        outs = [weighed(a, t, pars_ref, i) for i, a, t in zip(group, adjoints, turned)]
        ys = [y + nn(o, two_ref[i]) for i, y, o in zip(group, near, outs)]
        for i, y, qp, adjoint, t in zip(group, ys, qps, adjoints, turned):
            flat_ref[i * rows : (i + 1) * rows, :] = y + skip_ref[i : i + 1, :] * g_ref[i].astype(
                f32
            )
            states = state_ref[i]
            here = p_ref[i] + adjoint * pars_ref[i, 0:1, :] + t * pars_ref[i, 1:2, :]
            sum_ref[i, 0:1, :] = summed(states * here)
            sum_ref[i, 1:2, :] = summed(states * turn(here))
            sum_ref[i, 2:3, :] = summed(adjoint * qp)
            sum_ref[i, 3:4, :] = summed(adjoint * turn(qp))
            sum_ref[i, 4:8, :] = jnp.zeros((4, size), f32)
    for r in range(rows):
        b, j = r // chunks, r % chunks
        out_ref[b, :, j * size : (j + 1) * size] = flat_ref[
            pl.ds(r, block, stride=rows), :
        ].astype(bf16)


def over_blocks(kernel, steps, args, outs, us, scratch=(), ties=(), vmem=40):
    count = len(args)

    def run(*refs):
        kernel(*refs[:count], *refs[count + len(ties) :])

    moved = sum(a.size * a.dtype.itemsize for a, _, _ in args + outs)
    return pl.pallas_call(
        run,
        grid=(steps,),
        in_specs=[pl.BlockSpec(b, m) for _, b, m in args]
        + [pl.BlockSpec(memory_space=pl.ANY) for _ in ties],
        out_specs=[pl.BlockSpec(b, m) for _, b, m in outs],
        out_shape=[o for o, _, _ in outs],
        scratch_shapes=list(scratch),
        compiler_params=pltpu.CompilerParams(vmem_limit_bytes=vmem * 1024 * 1024),
        cost_estimate=pl.CostEstimate(
            flops=int(us * 1e9), bytes_accessed=moved, transcendentals=0
        ),
    )(*[a for a, _, _ in args], *ties)


def along(array, dim, block):
    shape = array.shape
    if dim is None:
        return (array, tuple(shape), lambda i: (0,) * len(shape))
    sizes = tuple(block if d == dim else size for d, size in enumerate(shape))
    return (array, sizes, lambda i: tuple(i if d == dim else 0 for d in range(len(shape))))


def by_channel(kernel, block, channels, args, outs, us, scratch=(), ties=()):
    return over_blocks(
        kernel,
        channels // block,
        [along(a, d, block) for a, d in args],
        [along(o, d, block) for o, d in outs],
        us,
        scratch,
        ties,
    )


def lane_sums(values):
    width = min(128, values.shape[1])
    total = values[:, :width]
    for k in range(1, values.shape[1] // width):
        total = total + values[:, k * width : (k + 1) * width]
    return total


def gated_kernel(
    x_ref, residual_ref, value_w_ref, gate_w_ref, value_b_ref, gate_b_ref, gain_ref,
    hidden_ref, normed_ref, value_ref, opening_ref, line_ref,
):
    x = x_ref[...]
    value = nn(value_w_ref[...], x) + value_b_ref[:, 0:1]
    gate = nn(gate_w_ref[...], x) + gate_b_ref[:, 0:1]
    opening = 1.0 / (1.0 + jnp.exp(-gate))
    branch = value * opening
    residual = residual_ref[...].astype(f32)
    hidden = residual + branch
    features = hidden.shape[0]
    scale = lax.rsqrt(summed(hidden * hidden) / features + epsilon)
    hidden_ref[...] = hidden
    value_ref[...] = value
    opening_ref[...] = opening
    normed_ref[...] = (hidden * scale * gain_ref[:, 0:1]).astype(bf16)
    line_ref[0:1, :] = scale
    line_ref[1:2, :] = summed(residual * residual)
    line_ref[2:3, :] = summed(branch * branch)
    line_ref[3:8, :] = jnp.zeros((5, hidden.shape[1]), f32)


def hidden_kernel(
    blocks, first, normed_ref, upstream_ref, up_a_ref, up_b_ref, down_a_ref, down_b_ref, bias_ref,
    *refs,
):
    if first:
        feed_out, grad_out, shrink_ref, expand_ref, line_ref, up_ref, down_ref = refs
    else:
        feed_in, grad_in, feed_out, grad_out, shrink_ref, expand_ref, line_ref, up_ref, down_ref = (
            refs
        )
    step = pl.program_id(0)

    @pl.when(step < blocks)
    def _():
        up_ref[...] = up_a_ref[...]
        down_ref[...] = down_a_ref[...]

    @pl.when(step >= blocks)
    def _():
        up_ref[...] = up_b_ref[...]
        down_ref[...] = down_b_ref[...]

    @pl.when(step == 0)
    def _():
        if first:
            feed_out[...] = jnp.zeros_like(feed_out)
            grad_out[...] = jnp.zeros_like(grad_out)
        else:
            feed_out[...] = feed_in[...]
            grad_out[...] = grad_in[...]

    expanded = nn(up_ref[...], normed_ref[...]) + bias_ref[:, 0:1]
    lifted, slope = gelu_pair(expanded)
    lifted = lifted.astype(bf16)
    grad = (nn(down_ref[...], upstream_ref[...]) * slope).astype(bf16)
    shrink_ref[...] = nt(lifted, upstream_ref[...]).astype(bf16)
    expand_ref[...] = nt(grad, normed_ref[...]).astype(bf16)
    line_ref[...] = lane_sums(grad.astype(f32))
    feed_out[...] += tn(down_ref[...], lifted)
    grad_out[...] += tn(up_ref[...], grad)


def gated_back_kernel(
    grad_ref, hidden_ref, value_ref, opening_ref, upstream_ref, feed_ref, x_ref, line_ref,
    value_w_ref, gate_w_ref, gain_ref, shrink_b_ref,
    result_ref, lifted_ref, grad_hidden_ref, value_g_ref, gate_g_ref, sums_ref, feed_line_ref,
    value_t, gate_t,
):
    step = pl.program_id(0)

    @pl.when(step == 0)
    def _():
        value_t[...] = jnp.zeros_like(value_t)
        gate_t[...] = jnp.zeros_like(gate_t)
        sums_ref[...] = jnp.zeros_like(sums_ref)

    hidden = hidden_ref[...]
    features = hidden.shape[0]
    scale = line_ref[0:1, :]
    feed = feed_ref[...] + shrink_b_ref[:, 0:1]
    result_ref[...] = (hidden + feed).astype(bf16)
    feed_line_ref[0:1, :] = summed(feed * feed)
    feed_line_ref[1:8, :] = jnp.zeros((7, hidden.shape[1]), f32)
    grad = grad_ref[...]
    inner = grad * gain_ref[:, 0:1]
    dot = summed(inner * hidden) / features
    upstream = upstream_ref[...].astype(f32)
    grad_hidden = scale * inner - hidden * (scale * scale * scale) * dot + upstream
    grad_hidden_ref[...] = grad_hidden.astype(bf16)
    opening = opening_ref[...]
    grad_value = (grad_hidden * opening).astype(bf16)
    grad_gate = (grad_hidden * value_ref[...] * opening * (1.0 - opening)).astype(bf16)
    sums_ref[0] += lane_sums(grad_value.astype(f32))
    sums_ref[1] += lane_sums(grad_gate.astype(f32))
    sums_ref[2] += lane_sums(grad * hidden * scale)
    sums_ref[3] += lane_sums(upstream)
    lifted_ref[...] = (tn(value_w_ref[...], grad_value) + tn(gate_w_ref[...], grad_gate)).astype(
        bf16
    )
    x = x_ref[...]
    value_t[...] += nt(grad_value, x)
    gate_t[...] += nt(grad_gate, x)

    @pl.when(step == pl.num_programs(0) - 1)
    def _():
        value_g_ref[...] = value_t[...].astype(bf16)
        gate_g_ref[...] = gate_t[...].astype(bf16)


def swap(values, axis, bit):
    size = lax.axis_size(axis)
    return lax.ppermute(values, axis, [(i, i ^ bit) for i in range(size)])


def added(a, b):
    return (a.astype(f32) + b.astype(f32)).astype(bf16)


def axis_total(values, axis):
    bit = 1
    while bit < lax.axis_size(axis):
        values = values + swap(values, axis, bit)
        bit *= 2
    return values


def bits_of(axis):
    return [1 << k for k in range(lax.axis_size(axis).bit_length() - 1)]


def down_step(terms, bit):
    if bit == 0:
        return added(terms[:1], swap(terms[1:], "mp", 2))
    me = lax.axis_index("seq")
    half = terms.shape[1] // 2
    mine = (me // bit) % 2
    kept = lax.dynamic_slice_in_dim(terms, mine * half, half, 1)
    sent = lax.dynamic_slice_in_dim(terms, (1 - mine) * half, half, 1)
    return added(kept, swap(sent, "seq", bit))


def up_step(terms, bit):
    me = lax.axis_index("seq")
    there = swap(terms, "seq", bit)
    first = (me // bit) % 2 == 0
    return jnp.concatenate(
        [jnp.where(first, terms, there), jnp.where(first, there, terms)], axis=1
    )


def shards(
    inputs,
    valid,
    cotangent,
    first_gain,
    step_size,
    decay_rate,
    frequency,
    readout_real,
    readout_imag,
    skip_weight,
    gated_weight,
    gated_bias,
    second_gain,
    expand_weight,
    expand_bias,
    shrink_weight,
    shrink_bias,
):
    mp = lax.axis_size("mp")
    seq = lax.axis_size("seq")
    mp_me = lax.axis_index("mp")
    seq_me = lax.axis_index("seq")
    features, contexts, local = inputs.shape
    chunk = min(CHUNK, local)
    chunks = local // chunk
    rows = contexts * chunks
    modes = decay_rate.shape[1]
    own_contexts = contexts // mp
    tokens = own_contexts * local
    hidden_own = expand_weight.shape[1]
    group = features // seq

    def exchanged(values):
        moved = lax.all_to_all(values, "mp", 0, 0, tiled=True)
        moved = moved.reshape(mp, own_contexts, features, local).swapaxes(1, 2)
        return moved.reshape(mp * features, tokens)

    def returned(values):
        moved = values.reshape(mp, features, own_contexts, local).swapaxes(1, 2)
        moved = moved.reshape(mp * own_contexts, features, local)
        return lax.all_to_all(moved, "mp", 0, 0, tiled=True)

    def all_places(own, upper):
        return own, upper, swap(own, "mp", 1), swap(upper, "mp", 1)

    gated_own = gated_weight.transpose(1, 2, 0)
    gated_places = all_places(gated_own, swap(gated_own, "mp", 2))
    small = jnp.concatenate([gated_bias.reshape(-1), second_gain, expand_bias, shrink_bias])
    small_near = jnp.stack([small, swap(small, "mp", 2)])
    small_places = jnp.concatenate([small_near, swap(small_near, "mp", 1)])
    expand_own = expand_weight.T
    part = hidden_own // seq
    slices = jnp.stack(
        [
            lax.dynamic_slice_in_dim(expand_own, seq_me * part, part, 0),
            lax.dynamic_slice_in_dim(shrink_weight, seq_me * part, part, 0),
        ]
    )
    slices = swap(slices, "mp", 2)
    expand_places = all_places(expand_own, lax.all_gather(slices[0], "seq", axis=0, tiled=True))
    shrink_places = all_places(shrink_weight, lax.all_gather(slices[1], "seq", axis=0, tiled=True))

    index = jnp.arange(mp, dtype=jnp.int32)
    device_of = jnp.bitwise_xor(mp_me, (index // 2) + 2 * (index % 2))
    place_of = jnp.bitwise_xor(mp_me, index)
    place_of = (place_of // 2) + 2 * (place_of % 2)

    def in_order(blocks):
        return jnp.concatenate(
            [lax.dynamic_slice_in_dim(blocks, place_of[k], 1, 0) for k in range(mp)]
        )

    def by_place(blocks):
        near = jnp.concatenate(
            [lax.dynamic_slice_in_dim(blocks, device_of[k], 1, 0) for k in range(2)]
        )
        far = jnp.concatenate(
            [lax.dynamic_slice_in_dim(blocks, device_of[k], 1, 0) for k in range(2, mp)]
        )
        return near, far

    gated_flat = in_order(jnp.stack(gated_places)).swapaxes(0, 1).reshape(2, D, D)
    cut = [0, 2 * features]
    cut += [cut[-1] + features]
    cut += [cut[-1] + hidden_own]
    cut += [cut[-1] + features]
    ordered = in_order(small_places)

    def wide(values):
        return jnp.broadcast_to(values[..., None], values.shape + (128,))

    whole_gated_bias = ordered[:, : cut[1]].reshape(mp, 2, features).swapaxes(0, 1).reshape(2, D)
    value_bias, gate_bias = wide(whole_gated_bias[0]), wide(whole_gated_bias[1])
    whole_gain_two = wide(ordered[:, cut[1] : cut[2]].reshape(D))
    whole_shrink_bias = wide(ordered[:, cut[3] :].reshape(D))
    whole_expand_bias = small_places[:, cut[2] : cut[3]]
    near_bias = wide(whole_expand_bias[:2].reshape(-1))
    far_bias = wide(whole_expand_bias[2:].reshape(-1))

    by_context = inputs.swapaxes(0, 1)
    square_one = axis_total(jnp.sum(jnp.square(by_context.astype(f32)), axis=1), "mp")
    scale_one = lax.rsqrt(square_one / D + epsilon)
    scale_rows = scale_one.reshape(rows, chunk)
    x_rows = inputs.reshape(features, rows, chunk)

    w = discretized(step_size, decay_rate, frequency)
    coeff = coefficients(step_size, decay_rate, frequency, readout_real, readout_imag)
    z_device = power(
        tuple(lax.dynamic_slice_in_dim(v, seq_me * group, group, 0) for v in w), float(local)
    )
    z_device = (z_device[0][:, None], z_device[1][:, None])

    def handed(ends, backward):
        sent = ends[..., : 2 * modes].reshape(features, contexts * 2 * modes)
        terms = lax.all_to_all(sent, "seq", 0, 0, tiled=True)
        terms = terms.reshape(seq, group, contexts, 2 * modes)
        state = (jnp.zeros((group, contexts, modes), f32),) * 2
        states = [None] * seq
        for k in range(seq - 1, -1, -1) if backward else range(seq):
            states[k] = jnp.concatenate(state, axis=-1)
            state = cadd(cmul(z_device, state), (terms[k, ..., :modes], terms[k, ..., modes:]))
        states = jnp.stack(states).reshape(features, contexts * 2 * modes)
        states = lax.all_to_all(states, "seq", 0, 0, tiled=True)
        states = states.reshape(features, contexts, 2 * modes)
        return four((states[..., :modes], states[..., modes:]))

    def out(shape, dtype):
        return jax.ShapeDtypeStruct(shape, dtype)

    block = min(16, features)
    state_shape = out((features, rows, 4 * modes), f32)
    end_shape = out((features, contexts, 4 * modes), f32)
    row_shape = out((features, rows, chunk), bf16)
    context_shape = out((contexts, features, local), bf16)
    table_shape = out((features, 4 * modes, chunk), bf16)
    sum_shape = out((features, 8, 4 * modes), f32)
    line_shape = out((features, chunk), f32)
    flat = [pltpu.VMEM((block * rows, chunk), f32)]
    skip_wide = jnp.broadcast_to(skip_weight[:, None], (features, chunk))
    gain_wide = jnp.broadcast_to(first_gain[:, None], (features, chunk))
    scan_steps = max(1, (chunks - 1).bit_length())
    pars, one, two, taps = by_channel(
        functools.partial(tables_kernel, chunk, scan_steps),
        block,
        features,
        [
            (step_size[:, None], 0),
            (decay_rate, 0),
            (frequency, 0),
            (readout_real, 0),
            (readout_imag, 0),
        ],
        [
            (out((features, 2 * scan_steps + 2, 4 * modes), f32), 0),
            (table_shape, 0),
            (table_shape, 0),
            (line_shape, 0),
        ],
        10,
        [pltpu.VMEM((block, 8, 4 * modes), f32)],
    )
    normed_one, terms, ends = by_channel(
        functools.partial(states_kernel, chunks),
        block,
        features,
        [(x_rows, 0), (scale_rows, None), (gain_wide, 0), (two, 0), (pars, 0)],
        [(row_shape, 0), (state_shape, 0), (end_shape, 0)],
        8,
    )
    mixed, states, lifted_one = by_channel(
        functools.partial(mix_kernel, chunks),
        block,
        features,
        [
            (normed_one, 0),
            (terms, 0),
            (handed(ends, False), 0),
            (one, 0),
            (taps, 0),
            (skip_wide, 0),
            (pars, 0),
        ],
        [(row_shape, 0), (state_shape, 0), (context_shape, 1)],
        14,
        flat,
    )

    whole_residual = exchanged(by_context)
    own_valid = lax.dynamic_slice_in_dim(valid, mp_me * own_contexts, own_contexts, 0)
    own_valid = own_valid.reshape(tokens).astype(f32)
    upstream = exchanged(cotangent.swapaxes(0, 1)) * own_valid.astype(bf16)
    whole_one = exchanged(lifted_one)

    token_block = min(256, tokens)
    token_steps = tokens // token_block
    wide_f = out((D, tokens), f32)
    wide_b = out((D, tokens), bf16)
    line_out = out((8, tokens), f32)

    def by_tokens(kernel, args, outs, us, scratch=(), ties=()):
        return over_blocks(
            kernel,
            token_steps,
            [along(a, d, token_block) for a, d in args],
            [along(o, d, token_block) for o, d in outs],
            us,
            scratch,
            ties,
            56,
        )

    hidden, normed_two, value_part, opening, lines = by_tokens(
        gated_kernel,
        [
            (whole_one, 1),
            (whole_residual, 1),
            (gated_flat[0], None),
            (gated_flat[1], None),
            (value_bias, None),
            (gate_bias, None),
            (whole_gain_two, None),
        ],
        [(wide_f, 1), (wide_b, 1), (wide_f, 1), (wide_f, 1), (line_out, 1)],
        12,
    )

    hidden_block = min(256, hidden_own)
    blocks = hidden_own // hidden_block
    near_rows = 2 * hidden_own

    def by_hidden(up, down, bias, carried, ties=()):
        first = carried is None
        low = ((hidden_block, D), lambda i: (jnp.minimum(i, blocks - 1), 0))
        high = ((hidden_block, D), lambda i: (jnp.maximum(i - blocks, 0), 0))
        args = [
            along(normed_two, None, 0),
            along(upstream, None, 0),
            (up[0], *low),
            (up[1], *high),
            (down[0], *low),
            (down[1], *high),
            along(bias, 0, hidden_block),
        ]
        if not first:
            args += [along(c, None, 0) for c in carried]
        grad_shape = out((near_rows, D), bf16)
        return over_blocks(
            functools.partial(hidden_kernel, blocks, first),
            2 * blocks,
            args,
            [
                along(wide_f, None, 0),
                along(wide_f, None, 0),
                along(grad_shape, 0, hidden_block),
                along(grad_shape, 0, hidden_block),
                along(out((near_rows, min(128, tokens)), f32), 0, hidden_block),
            ],
            35,
            [pltpu.VMEM((hidden_block, D), bf16)] * 2,
            ties,
            60,
        )

    feed, grad_normed_two, shrink_far, expand_far, far_lines = by_hidden(
        expand_places[2:], shrink_places[2:], far_bias, None
    )
    feed, grad_normed_two, shrink_near, expand_near, near_lines = by_hidden(
        expand_places[:2], shrink_places[:2], near_bias, (feed, grad_normed_two)
    )

    sums_out = out((4, D, min(128, token_block)), f32)
    gated_g = out((D, D), bf16)
    result, grad_lifted_one, grad_hidden, value_g, gate_g, sums, feed_lines = by_tokens(
        gated_back_kernel,
        [
            (grad_normed_two, 1),
            (hidden, 1),
            (value_part, 1),
            (opening, 1),
            (upstream, 1),
            (feed, 1),
            (whole_one, 1),
            (lines, 1),
            (gated_flat[0], None),
            (gated_flat[1], None),
            (whole_gain_two, None),
            (whole_shrink_bias, None),
        ],
        [
            (wide_b, 1),
            (wide_b, 1),
            (wide_b, 1),
            (gated_g, None),
            (gated_g, None),
            (sums_out, None),
            (line_out, 1),
        ],
        20,
        [pltpu.VMEM((D, D), f32)] * 2,
    )
    own_lifted_one = returned(grad_lifted_one)
    own_hidden = returned(grad_hidden).astype(f32)
    result = returned(result).swapaxes(0, 1)

    bits = bits_of("seq")

    def weight_total(near, far, order):
        near, far = near.reshape(2, -1, D), far.reshape(2, -1, D)
        terms = added(near, swap(far, "mp", 1))
        for bit in order:
            terms = down_step(terms, bit)
        for bit in [bit for bit in order if bit > 0][::-1]:
            terms = up_step(terms, bit)
        return terms[0].astype(f32)

    rotated = bits[1:] + bits[:1] if len(bits) > 1 else bits
    grad_shrink = weight_total(shrink_near, shrink_far, bits + [0])
    grad_expand = weight_total(expand_near, expand_far, [0] + bits).T
    gated_terms = jnp.stack([value_g.reshape(mp, features, D), gate_g.reshape(mp, features, D)], 1)
    grad_gated = weight_total(
        *by_place(gated_terms.reshape(mp, 2 * features, D)), rotated[:1] + [0] + rotated[1:]
    )
    grad_gated = grad_gated.reshape(2, features, D).transpose(2, 0, 1)

    grad_mixed, adj_terms, adj_ends = by_channel(
        functools.partial(ends_kernel, chunks),
        block,
        features,
        [(own_lifted_one, 1), (mixed, 0), (one, 0), (pars, 0)],
        [(row_shape, 0), (state_shape, 0), (end_shape, 0)],
        10,
        flat,
    )
    (sums_one,) = by_channel(
        sums_kernel,
        block,
        features,
        [(grad_mixed, 0), (normed_one, 0), (states, 0), (adj_terms, 0), (one, 0)],
        [(sum_shape, 0)],
        20,
    )
    grad_normed_one, sums_two = by_channel(
        functools.partial(back_kernel, chunks),
        block,
        features,
        [
            (grad_mixed, 0),
            (adj_terms, 0),
            (handed(adj_ends, True), 0),
            (normed_one, 0),
            (states, 0),
            (two, 0),
            (taps, 0),
            (skip_wide, 0),
            (pars, 0),
        ],
        [(context_shape, 1), (sum_shape, 0)],
        14,
        flat,
    )

    residual = by_context.astype(f32)
    grad_normed_one = grad_normed_one.astype(f32)
    inner_one = grad_normed_one * first_gain[:, None]
    wide_scale = scale_one[:, None, :]
    grad_first_gain = jnp.sum(grad_normed_one * residual * wide_scale, axis=(0, 2))
    dot_one = axis_total(jnp.sum(inner_one * residual, axis=1), "mp")[:, None, :]
    grad_inputs = (
        wide_scale * inner_one
        - residual * (wide_scale * wide_scale * wide_scale) * dot_one / D
        + own_hidden
    ).swapaxes(0, 1)

    stats = jnp.stack(
        [
            jnp.sum(own_valid * lines[1]),
            jnp.sum(own_valid * lines[2]),
            jnp.sum(own_valid * feed_lines[0]),
            jnp.sum(own_valid),
        ]
    )
    sums = jnp.sum(sums, axis=2)
    ordered_terms = jnp.concatenate(
        [
            sums[:2].reshape(2, mp, features).swapaxes(0, 1).reshape(mp, -1),
            sums[2].reshape(mp, -1),
            sums[3].reshape(mp, -1),
            jnp.broadcast_to(stats, (mp, 4)),
        ],
        axis=1,
    )
    near, far = by_place(ordered_terms)
    near = jnp.concatenate([near, jnp.sum(near_lines, axis=1).reshape(2, hidden_own)], axis=1)
    far = jnp.concatenate([far, jnp.sum(far_lines, axis=1).reshape(2, hidden_own)], axis=1)
    near = near + swap(far, "mp", 1)
    bias_own = axis_total((near[:1] + swap(near[1:], "mp", 2))[0], "seq")

    def quarter(values, k):
        return values[:, k * modes : (k + 1) * modes]

    def product_sums(lines, k):
        plain, turned = lines[:, k], lines[:, k + 1]
        return (
            quarter(plain, 0) - quarter(plain, 1),
            quarter(turned, 1) + quarter(turned, 3),
        )

    inverse = power(w, -1.0)
    within = [
        cmul(inverse, (quarter(sums_one[:, k], 0), quarter(sums_one[:, k], 1))) for k in (4, 5)
    ]
    sum_a = cadd(product_sums(sums_one, 0), within[0])
    crossing = product_sums(sums_two, 0)
    part_a = product_sums(sums_one, 2)
    part_p = product_sums(sums_two, 2)
    sum_b = [
        float(chunk) * crossing[k] + part_a[k] - part_p[k] + within[1][k] for k in range(2)
    ]
    late = jnp.concatenate(
        [
            *sum_a,
            *sum_b,
            jnp.sum(sums_one[:, 6], axis=1, keepdims=True),
            grad_first_gain[:, None],
        ],
        axis=1,
    )
    late = axis_total(late, "seq")
    sum_a = (quarter(late, 0), quarter(late, 1))
    sum_b = (quarter(late, 2), quarter(late, 3))
    grad_skip = late[:, 4 * modes]
    grad_first_gain = late[:, 4 * modes + 1]

    def form(step, decay, freq, out_real, out_imag):
        c = coefficients(step, decay, freq, out_real, out_imag)
        moved = cmul(coeff, discretized(step, decay, freq))
        return 2.0 * jnp.sum(
            c[0] * sum_a[0] - c[1] * sum_a[1] + moved[0] * sum_b[0] - moved[1] * sum_b[1]
        )

    kernel_grads = jax.grad(form, argnums=(0, 1, 2, 3, 4))(
        step_size, decay_rate, frequency, readout_real, readout_imag
    )
    ends_at = [0, 2 * features, 3 * features, 4 * features, 4 * features + 4]
    totals = bias_own[ends_at[3] : ends_at[4]]
    count = totals[3]
    rms = jnp.sqrt(totals[:3] / (count * D))
    return (
        result,
        grad_inputs,
        grad_first_gain,
        *kernel_grads,
        grad_skip,
        grad_gated,
        bias_own[: ends_at[1]].reshape(2, features),
        bias_own[ends_at[1] : ends_at[2]],
        grad_expand,
        bias_own[ends_at[4] :],
        grad_shrink,
        bias_own[ends_at[2] : ends_at[3]],
        rms[0],
        rms[1],
        rms[2],
    )


def solution(mesh):
    placed = (
        P("mp", None, "seq"),
        P(None, "seq"),
        P("mp", None, "seq"),
        P("mp"),
        P("mp"),
        P("mp", None),
        P("mp", None),
        P("mp", None),
        P("mp", None),
        P("mp"),
        P(None, None, "mp"),
        P(None, "mp"),
        P("mp"),
        P(None, "mp"),
        P("mp"),
        P("mp", None),
        P("mp"),
    )
    return jax.shard_map(
        shards,
        mesh=mesh,
        in_specs=placed,
        out_specs=(
            P("mp", None, "seq"),
            P("mp", None, "seq"),
            P("mp"),
            P("mp"),
            P("mp", None),
            P("mp", None),
            P("mp", None),
            P("mp", None),
            P("mp"),
            P(None, None, "mp"),
            P(None, "mp"),
            P("mp"),
            P(None, "mp"),
            P("mp"),
            P("mp", None),
            P("mp"),
            P(),
            P(),
            P(),
        ),
        check_vma=False,
    )
```

time: 1200 us -> 837 us (0.70)
  the two profiles are of different devices: /device:TPU:0 before, /device:TPU:4 now
where the time goes in v2:
time: 837 us; the launch traced here: 824 us
  waiting for transfers between devices  241 us (29%)
  Pallas kernels  223 us (27%)
  local copies, waits for them, and re-layouts  152 us (18%)
  other arithmetic  91.5 us (11%)
  starting transfers between devices  84.3 us (10%)
  between operations  32 us (4%)
    pallas_call x10, Pallas kernels, over_blocks(): pl.pallas_call(run, grid=(steps,), in_specs=[pl.BlockSpec(b, m) for _, b,...  223 us
    ppermute x46, waiting for transfers between devices, swap(): return lax.ppermute(values, axis, [(i, i ^ bit) for i in range(size)])  185 us
    unnamed x181, local copies, waits for them, and re-layouts  78.7 us
    ppermute x46, starting transfers between devices, swap(): return lax.ppermute(values, axis, [(i, i ^ bit) for i in range(size)])  34.2 us
    all_to_all x2, waiting for transfers between devices, handed(): terms = lax.all_to_all(sent, 'seq', 0, 0, tiled=True)  23.4 us
    slice x2, local copies, waits for them, and re-layouts, shards(): gated_flat[1]  20.4 us
    convert_element_type x15, other arithmetic, added(): return (a.astype(f32) + b.astype(f32)).astype(bf16)  20.1 us
    all_to_all x3, starting transfers between devices, exchanged(): moved = lax.all_to_all(values, 'mp', 0, 0, tiled=True)  17.3 us
  transfers between devices with their start and end apart: 58, of which 28 were waited for; matrix products, arithmetic and copies ran while one was open for 23% of the time, Pallas kernels for 15%

profile of v2, /device:TPU:4, one launch (start us, length us, event | category | flops | bytes accessed | tf_op | source)
XLA Modules:
  0.0 824.3 jit_solution(14569273080277773707)
XLA Ops:
  12.3 4.0 copy.202
  23.3 16.8 %shard_map.312 = (f32[256,8,128]{2,1,0:T(8,128)S(1)}, bf16[256,128,128]{2,1,0:T(8,128)(2,1)S(1)}, bf16[256,128,128]{2,1,0:T(8,128)(2,1)}, f32[256,128]{1,0:T(8,128)S(1)}) custom-call(f32[256,1]{1,0:T(8,128)S(1)} %copy.190.refs_0_, f32[256,32]{1,0:T(8,128)S(1)} %copy.191.refs_1_, f32[256,32]{1,0:T(8,128)S(1)} %copy.192.refs_2_, f32[256,32]{1,0:T(8,128)S(1)} %copy.193.refs_3_, ...), custom_call_target="tpu_custom_call" | custom-call | flops 10000000000 | bytes 18088960 | tf_op jit(solution)/shard_map/pallas_call | solution.py:380
  40.1 3.3 copy-done.10
  45.7 2.7 reshape.196.refs_0_
  53.6 3.5 copy.271
  62.3 3.5 copy.270
  79.6 14.2 %shard_map.313 = (bf16[256,32,128]{2,1,0:T(8,128)(2,1)S(1)}, f32[256,32,128]{2,1,0:T(8,128)S(1)}, f32[256,4,128]{2,1,0:T(4,128)S(1)}) custom-call(bf16[256,32,128]{2,1,0:T(8,128)(2,1)S(1)} %reshape.196.refs_0_, f32[32,128]{1,0:T(8,128)S(1)} %reshape.197.refs_1_, f32[256,128]{1,0:T(8,128)S(1)} %broadcast_in_dim.42.refs_2_, ...), custom_call_target="tpu_custom_call" | custom-call | flops 8000000000 | bytes 18497536 | tf_op jit(solution)/shard_map/pallas_call | solution.py:380
  98.2 6.1 all-to-all-start
  104.3 16.5 %all-to-all-done = f32[8,32,256]{2,1,0:T(8,128)S(1)} async-done(((f32[8,32,256]{2,1,0:T(8,128)}), f32[8,32,256]{2,1,0:T(8,128)S(1)}, u32[]{:S(2)}, u32[]{:S(2)}) %all-to-all-start) | async-done | bytes 262176 | tf_op jit(solution)/shard_map/all_to_all | solution.py:691
  127.1 3.6 all-to-all-start.1
  131.4 8.1 all-to-all-done.1
  139.5 5.4 all-to-all-start.4
  147.0 18.4 %shard_map.314 = (bf16[256,32,128]{2,1,0:T(8,128)(2,1)S(1)}, f32[256,32,128]{2,1,0:T(8,128)S(1)}, bf16[4,256,1024]{2,1,0:T(8,128)(2,1)}) custom-call(bf16[256,32,128]{2,1,0:T(8,128)(2,1)S(1)} %copy-done.16, f32[256,32,128]{2,1,0:T(8,128)} %copy-done.11, f32[256,4,128]{2,1,0:T(4,128)S(1)} %pad_maximum_fusion.6.refs_2_, bf16[256,128,128]{2,1,0:T(8,128)(2,1)} %copy-done.10, ...), custom_call_target="tpu_custom_call" | custom-call | flops 14000000000 | bytes 24903680 | tf_op jit(solution)/shard_map/pallas_call | solution.py:380
  169.5 5.8 all-to-all-start.3
  176.9 8.8 %pad_maximum_fusion = bf16[4,2,256,1024]{2,1,3,0:T(2,128)(2,1)S(1)} fusion(bf16[1,2,256,1024]{2,1,3,0:T(2,128)(2,1)S(1)} %bitcast.301, bf16[1,2,256,1024]{2,1,3,0:T(2,128)(2,1)} %bitcast.21, bf16[1,2,256,1024]{2,1,3,0:T(2,128)(2,1)} %bitcast.20, bf16[1,2,256,1024]{2,1,3,0:T(2,128)(2,1)S(1)} %bitcast.300), kind=kLoop, calls=%fused_computation.19 | loop fusion | flops 6291456 | bytes 8388608 | tf_op jit(solution)/shard_map/stack | solution.py:658
  185.6 3.7 constant_dynamic-slice_fusion.25
  189.4 10.0 %all-to-all-done.3 = bf16[4,256,1024]{2,1,0:T(8,128)(2,1)} async-done(((bf16[4,256,1024]{2,1,0:T(8,128)(2,1)}), bf16[4,256,1024]{2,1,0:T(8,128)(2,1)}, u32[]{:S(2)}, u32[]{:S(2)}) %all-to-all-start.3) | async-done | bytes 2097184 | tf_op jit(solution)/shard_map/all_to_all | solution.py:610
  199.4 6.1 all-to-all-start.2
  205.5 9.6 %maximum_bitcast_fusion = bf16[2,4,256,1024]{2,0,3,1:T(2,128)(2,1)} fusion(bf16[1,2,256,1024]{2,1,3,0:T(2,128)(2,1)S(1)} %get-tuple-element.237, bf16[1,2,256,1024]{2,1,3,0:T(2,128)(2,1)S(1)} %get-tuple-element.238, bf16[1,2,256,1024]{2,1,3,0:T(2,128)(2,1)} %get-tuple-element.239, bf16[1,2,256,1024]{2,1,3,0:T(2,128)(2,1)S(1)} %get-tuple-element.236), kind=kLoop, calls=%fused_computation.20 | loop fusion | flops 6291456 | bytes 8388608 | tf_op jit(solution)/shard_map/transpose | solution.py:658
  215.6 9.8 %fusion.96 = (bf16[1,4,256,1024]{2,0,3,1:T(2,128)(2,1)}, bf16[1,4,256,1024]{2,0,3,1:T(2,128)(2,1)}) fusion(bf16[2,4,256,1024]{2,0,3,1:T(2,128)(2,1)} %maximum_bitcast_fusion), kind=kLoop, calls=%fused_computation.313 | loop fusion | bytes 8388608 | tf_op jit(solution)/shard_map/slice | solution.py:794
  225.4 10.6 %copy.199 = bf16[1,4,256,1024]{3,2,1,0:T(8,128)(2,1)} copy(bf16[1,4,256,1024]{2,0,3,1:T(2,128)(2,1)} %get-tuple-element.235) | data formatting | bytes 4194304 | tf_op jit(solution)/shard_map/slice | solution.py:793
  236.0 10.6 %copy.200 = bf16[1,4,256,1024]{3,2,1,0:T(8,128)(2,1)} copy(bf16[1,4,256,1024]{2,0,3,1:T(2,128)(2,1)} %get-tuple-element.234) | data formatting | bytes 4194304 | tf_op jit(solution)/shard_map/slice | solution.py:794
  249.6 11.9 %shard_map.315 = (f32[1024,1024]{1,0:T(8,128)}, bf16[1024,1024]{1,0:T(8,128)(2,1)}, f32[1024,1024]{1,0:T(8,128)}, f32[1024,1024]{1,0:T(8,128)}, f32[8,1024]{1,0:T(8,128)}) custom-call(bf16[1024,1024]{1,0:T(8,128)(2,1)} %bitcast.16.refs_0_.refs_6_, bf16[1024,1024]{1,0:T(8,128)(2,1)} %bitcast.17.refs_1_, bf16[1024,1024]{1,0:T(8,128)(2,1)} %bitcast.284, ...), custom_call_target="tpu_custom_call" | custom-call | flops 12000000000 | bytes 24674304 | tf_op jit(solution)/shard_map/pallas_call | solution.py:380
  263.2 36.4 %shard_map.316 = (f32[1024,1024]{1,0:T(8,128)}, f32[1024,1024]{1,0:T(8,128)}, bf16[2048,1024]{1,0:T(8,128)(2,1)}, bf16[2048,1024]{1,0:T(8,128)(2,1)}, f32[2048,128]{1,0:T(8,128)}) custom-call(bf16[1024,1024]{1,0:T(8,128)(2,1)} %get-tuple-element.64.refs_0_, bf16[1024,1024]{1,0:T(8,128)(2,1)} %bitcast_multiply_fusion.refs_1_.refs_4_, ...), custom_call_target="tpu_custom_call" | custom-call | flops 35000000512 | bytes 31457280 | tf_op jit(solution)/shard_map/pallas_call | solution.py:380
  300.9 39.6 %shard_map.317 = (f32[1024,1024]{1,0:T(8,128)}, f32[1024,1024]{1,0:T(8,128)}, bf16[2048,1024]{1,0:T(8,128)(2,1)}, bf16[2048,1024]{1,0:T(8,128)(2,1)}, f32[2048,128]{1,0:T(8,128)}) custom-call(bf16[1024,1024]{1,0:T(8,128)(2,1)} %get-tuple-element.64.refs_0_, bf16[1024,1024]{1,0:T(8,128)(2,1)} %bitcast_multiply_fusion.refs_1_.refs_4_, ...), custom_call_target="tpu_custom_call" | custom-call | flops 35000000512 | bytes 39845888 | tf_op jit(solution)/shard_map/pallas_call | solution.py:380
  341.5 25.1 %shard_map.318 = (bf16[1024,1024]{1,0:T(8,128)(2,1)}, bf16[1024,1024]{1,0:T(8,128)(2,1)}, bf16[1024,1024]{1,0:T(8,128)(2,1)}, bf16[1024,1024]{1,0:T(8,128)(2,1)}...) custom-call(f32[1024,1024]{1,0:T(8,128)} %get-tuple-element.67.refs_0_, ...), custom_call_target="tpu_custom_call" | custom-call | flops 20000000000 | bytes 43057152 | tf_op jit(solution)/shard_map/pallas_call | solution.py:380
  370.9 4.0 all-to-all-start.6
  379.7 19.4 %collective-permute-done.26 = f32[1,2052]{1,0:T(1,128)S(1)} collective-permute-done((f32[1,2052]{1,0:T(1,128)S(1)}, f32[1,2052]{1,0:T(1,128)S(1)}, u32[]{:S(2)}, u32[]{:S(2)}) %collective-permute-start.26) | collective-permute-done | bytes 8240 | tf_op jit(solution)/shard_map/ppermute | solution.py:537
  409.1 2.9 collective-permute-done.29
  417.3 15.3 %shard_map.319 = (bf16[256,32,128]{2,1,0:T(8,128)(2,1)S(1)}, f32[256,32,128]{2,1,0:T(8,128)S(1)}, f32[256,4,128]{2,1,0:T(4,128)S(1)}) custom-call(bf16[4,256,1024]{2,1,0:T(8,128)(2,1)S(1)} %all-to-all-done.6.refs_0_, bf16[256,32,128]{2,1,0:T(8,128)(2,1)S(1)} %copy-done.22, bf16[256,128,128]{2,1,0:T(8,128)(2,1)} %copy-done.10, f32[256,8,128]{2,1,0:T(8,128)S(1)} %copy-done.29), custom_call_target="tpu_custom_call" | custom-call | flops 10000000000 | bytes 20447232 | tf_op jit(solution)/shard_map/pallas_call | solution.py:380
  437.1 3.4 all-to-all-start.7
  441.7 7.0 all-to-all-done.7
  448.7 6.2 all-to-all-start.5
  464.9 14.1 %all-to-all-done.5 = bf16[4,256,1024]{2,1,0:T(8,128)(2,1)} async-done(((bf16[4,256,1024]{2,1,0:T(8,128)(2,1)}), bf16[4,256,1024]{2,1,0:T(8,128)(2,1)}, u32[]{:S(2)}, u32[]{:S(2)}) %all-to-all-start.5) | async-done | bytes 2097184 | tf_op jit(solution)/shard_map/all_to_all | solution.py:617
  479.0 3.4 all-to-all-start.8
  488.4 21.8 %shard_map.321 = f32[256,8,128]{2,1,0:T(8,128)S(1)} custom-call(bf16[256,32,128]{2,1,0:T(8,128)(2,1)S(1)} %copy-done.24, bf16[256,32,128]{2,1,0:T(8,128)(2,1)S(1)} %copy-done.17, f32[256,32,128]{2,1,0:T(8,128)S(1)} %copy-done.20, f32[256,32,128]{2,1,0:T(8,128)S(1)} %copy-done.13, bf16[256,128,128]{2,1,0:T(8,128)(2,1)} %copy-done.10), custom_call_target="tpu_custom_call" | custom-call | flops 20000000000 | bytes 22020096 | tf_op jit(solution)/shard_map/pallas_call | solution.py:380
  513.3 4.5 copy.240
  517.9 6.1 all-to-all-start.9
  529.9 23.1 %shard_map.320 = (bf16[4,256,1024]{2,1,0:T(8,128)(2,1)S(1)}, f32[256,8,128]{2,1,0:T(8,128)S(1)}) custom-call(bf16[256,32,128]{2,1,0:T(8,128)(2,1)S(1)} %copy-done.25, f32[256,32,128]{2,1,0:T(8,128)S(1)} %copy-done.14, f32[256,4,128]{2,1,0:T(4,128)S(1)} %pad_maximum_fusion.8.refs_2_, bf16[256,32,128]{2,1,0:T(8,128)(2,1)S(1)} %copy-done.18, ...), custom_call_target="tpu_custom_call" | custom-call | flops 14000000000 | bytes 25952256 | tf_op jit(solution)/shard_map/pallas_call | solution.py:380
  567.4 3.0 add_convert_fusion.2
  570.7 3.5 collective-permute-done.14
  577.4 6.1 collective-permute-done.15
  583.6 2.7 collective-permute-start.16
  586.3 4.3 fusion.1
  595.1 4.3 fusion
  603.5 4.1 fusion.5
  607.6 4.7 copy.241
  617.7 31.4 %collective-permute-done.19 = bf16[1,256,1024]{2,1,0:T(8,128)(2,1)S(1)} collective-permute-done((bf16[1,256,1024]{2,1,0:T(8,128)(2,1)S(1)}, bf16[1,256,1024]{2,1,0:T(8,128)(2,1)S(1)}, u32[]{:S(2)}, u32[]{:S(2)}) %collective-permute-start.19) | collective-permute-done | bytes 524320 | tf_op jit(solution)/shard_map/ppermute | solution.py:537
  658.9 4.0 collective-permute-done.20
  663.7 11.8 %collective-permute-done.32 = bf16[1,512,1024]{2,1,0:T(8,128)(2,1)S(1)} collective-permute-done((bf16[1,512,1024]{2,1,0:T(8,128)(2,1)S(1)}, bf16[1,512,1024]{2,1,0:T(8,128)(2,1)S(1)}, u32[]{:S(2)}, u32[]{:S(2)}) %collective-permute-start.32) | collective-permute-done | bytes 1048608 | tf_op jit(solution)/shard_map/ppermute | solution.py:537
  679.1 10.3 %collective-permute-done.40 = bf16[2,256,1024]{2,1,0:T(8,128)(2,1)S(1)} collective-permute-done((bf16[2,256,1024]{2,1,0:T(8,128)(2,1)S(1)}, bf16[2,256,1024]{2,1,0:T(8,128)(2,1)S(1)}, u32[]{:S(2)}, u32[]{:S(2)}) %collective-permute-start.40) | collective-permute-done | bytes 1048608 | tf_op jit(solution)/shard_map/ppermute | solution.py:537
  689.8 11.0 %collective-permute-done.33 = bf16[1,256,1024]{2,1,0:T(8,128)(2,1)S(1)} collective-permute-done((bf16[1,256,1024]{2,1,0:T(8,128)(2,1)S(1)}, bf16[1,256,1024]{2,1,0:T(8,128)(2,1)S(1)}, u32[]{:S(2)}, u32[]{:S(2)}) %collective-permute-start.33) | collective-permute-done | bytes 524320 | tf_op jit(solution)/shard_map/ppermute | solution.py:537
  702.2 14.0 %collective-permute-done.41 = bf16[2,128,1024]{2,1,0:T(8,128)(2,1)S(1)} collective-permute-done((bf16[2,128,1024]{2,1,0:T(8,128)(2,1)S(1)}, bf16[2,128,1024]{2,1,0:T(8,128)(2,1)S(1)}, u32[]{:S(2)}, u32[]{:S(2)}) %collective-permute-start.41) | collective-permute-done | bytes 524320 | tf_op jit(solution)/shard_map/ppermute | solution.py:537
  719.0 17.4 %collective-permute-done.34 = bf16[1,128,1024]{2,1,0:T(8,128)(2,1)S(1)} collective-permute-done((bf16[1,128,1024]{2,1,0:T(8,128)(2,1)S(1)}, bf16[1,128,1024]{2,1,0:T(8,128)(2,1)S(1)}, u32[]{:S(2)}, u32[]{:S(2)}) %collective-permute-start.34) | collective-permute-done | bytes 262176 | tf_op jit(solution)/shard_map/ppermute | solution.py:537
  736.6 3.0 collective-permute-start.23
  739.7 7.1 collective-permute-done.35
  747.0 3.0 collective-permute-done.23
  750.1 3.1 collective-permute-done.43
  756.2 8.2 collective-permute-done.36
  765.7 9.5 %collective-permute-done.44 = bf16[1,256,1024]{2,1,0:T(8,128)(2,1)S(1)} collective-permute-done((bf16[1,256,1024]{2,1,0:T(8,128)(2,1)S(1)}, bf16[1,256,1024]{2,1,0:T(8,128)(2,1)S(1)}, u32[]{:S(2)}, u32[]{:S(2)}) %collective-permute-start.44) | collective-permute-done | bytes 524320 | tf_op jit(solution)/shard_map/ppermute | solution.py:537
  783.4 3.0 collective-permute-done.24
  788.9 3.2 collective-permute-done.37
  796.3 5.3 copy.246
  801.7 11.4 %collective-permute-done.45 = bf16[1,512,1024]{2,1,0:T(8,128)(2,1)} collective-permute-done((bf16[1,512,1024]{2,1,0:T(8,128)(2,1)}, bf16[1,512,1024]{2,1,0:T(8,128)(2,1)}, u32[]{:S(2)}, u32[]{:S(2)}) %collective-permute-start.45) | collective-permute-done | bytes 1048608 | tf_op jit(solution)/shard_map/ppermute | solution.py:537
  (427 shorter events, 177.3 us)
Async XLA Ops:
  7.2 207.9 %all-gather.7.cloned.1.call-start = ((), (), s32[]{:S(2)}) async-start(), calls=%async_computation.11 | async-start | bytes 2359296 | tf_op jit(solution)/shard_map/all_gather | solution.py:637
  7.2 138.9 %collective-permute-start.2 = (bf16[2,256,1024]{1,0,2:T(2,128)(2,1)}, bf16[2,256,1024]{1,0,2:T(2,128)(2,1)}, u32[]{:S(2)}, u32[]{:S(2)}) collective-permute-start(bf16[2,256,1024]{1,0,2:T(2,128)(2,1)} %bitcast.298), channel_id=1, source_target_pairs={{0,2},{1,3},{2,0},{3,1},{4,6},{5,7},{6,4},{7,5},{8,10},{9,11},{10,... | collective-permute-start | bytes 3145736 | tf_op jit(solution)/shard_map/ppermute | solution.py:537
  7.3 169.6 %collective-permute-start.3 = (bf16[2,256,1024]{1,0,2:T(2,128)(2,1)}, bf16[2,256,1024]{1,0,2:T(2,128)(2,1)}, u32[]{:S(2)}, u32[]{:S(2)}) collective-permute-start(bf16[2,256,1024]{1,0,2:T(2,128)(2,1)} %bitcast.299), channel_id=1, source_target_pairs={{0,1},{1,0},{2,3},{3,2},{4,5},{5,4},{6,7},{7,6},{8,9},{9,8},{10,11... | collective-permute-start | bytes 3145736 | tf_op jit(solution)/shard_map/ppermute | solution.py:537
  10.2 61.6 %collective-permute-start.5 = (f32[2048]{0:T(1024)S(1)}, f32[2048]{0:T(1024)S(1)}, u32[]{:S(2)}, u32[]{:S(2)}) collective-permute-start(f32[2048]{0:T(1024)S(1)} %constant_dynamic-update-slice_fusion.17), channel_id=1, source_target_pairs={{0,2},{1,3},{2,0},{3,1},{4,6},{5,7},{6,4},{7,5},{8,10},{9,11},{10,... | collective-permute-start | bytes 24584 | tf_op jit(solution)/shard_map/ppermute | solution.py:537
  12.1 249.4 %collective-permute-start.10 = (bf16[1024,1024]{1,0:T(8,128)(2,1)}, bf16[1024,1024]{1,0:T(8,128)(2,1)}, u32[]{:S(2)}, u32[]{:S(2)}) collective-permute-start(bf16[1024,1024]{1,0:T(8,128)(2,1)} %refs_4_.2), channel_id=1, source_target_pairs={{0,1},{1,0},{2,3},{3,2},{4,5},{5,4},{6,7},{7,6},{8,9},{9,8},{10,11... | collective-permute-start | bytes 6291464 | tf_op jit(solution)/shard_map/ppermute | solution.py:537
  19.3 54.0 %collective-permute-start.7 = (bf16[2,128,1024]{2,1,0:T(8,128)(2,1)}, bf16[2,128,1024]{2,1,0:T(8,128)(2,1)S(1)}, u32[]{:S(2)}, u32[]{:S(2)}) collective-permute-start(bf16[2,128,1024]{2,1,0:T(8,128)(2,1)} %pad_maximum_fusion.7), channel_id=1, source_target_pairs={{0,2},{1,3},{2,0},{3,1},{4,6},{5,7},{6,4},{7,5},{8,10},{9,11},{10,... | collective-permute-start | bytes 1572872 | tf_op jit(solution)/shard_map/ppermute | solution.py:537
  22.7 98.3 %copy-start.55 = (f32[32,32]{1,0:T(8,128)}, f32[32,32]{1,0:T(8,128)S(1)}, u32[]{:S(2)}) copy-start(f32[32,32]{1,0:T(8,128)S(1)} %get-tuple-element.227) | copy-start | bytes 12292
  22.7 98.7 %copy-start.48 = (f32[32,32]{1,0:T(8,128)}, f32[32,32]{1,0:T(8,128)S(1)}, u32[]{:S(2)}) copy-start(f32[32,32]{1,0:T(8,128)S(1)} %get-tuple-element.228) | copy-start | bytes 12292
  22.7 98.7 %copy-start.50 = (f32[32,32]{1,0:T(8,128)}, f32[32,32]{1,0:T(8,128)S(1)}, u32[]{:S(2)}) copy-start(f32[32,32]{1,0:T(8,128)S(1)} %get-tuple-element.229) | copy-start | bytes 12292
  23.3 97.8 %copy-start.57 = (f32[32,32]{1,0:T(8,128)}, f32[32,32]{1,0:T(8,128)S(1)}, u32[]{:S(2)}) copy-start(f32[32,32]{1,0:T(8,128)S(1)} %multiply_add_fusion.13) | copy-start | bytes 12292
  71.8 1.2 collective-permute-start
  73.1 188.4 %collective-permute-start.8 = (bf16[1024,1024]{1,0:T(8,128)(2,1)}, bf16[1024,1024]{1,0:T(8,128)(2,1)}, u32[]{:S(2)}, u32[]{:S(2)}) collective-permute-start(bf16[1024,1024]{1,0:T(8,128)(2,1)} %bitcast.282), channel_id=1, source_target_pairs={{0,1},{1,0},{2,3},{3,2},{4,5},{5,4},{6,7},{7,6},{8,9},{9,8},{10,11... | collective-permute-start | bytes 6291464 | tf_op jit(solution)/shard_map/ppermute | solution.py:537
  73.2 3.8 collective-permute-start.1
  77.1 27.2 %collective-permute-start.6 = (f32[2,2048]{1,0:T(2,128)S(1)}, f32[2,2048]{1,0:T(2,128)S(1)}, u32[]{:S(2)}, u32[]{:S(2)}) collective-permute-start(f32[2,2048]{1,0:T(2,128)S(1)} %pad_maximum_fusion.29), channel_id=1, source_target_pairs={{0,1},{1,0},{2,3},{3,2},{4,5},{5,4},{6,7},{7,6},{8,9},{9,8},{10,11... | collective-permute-start | bytes 49160 | tf_op jit(solution)/shard_map/ppermute | solution.py:537
  98.2 22.6 %all-to-all-start = ((f32[8,32,256]{2,1,0:T(8,128)}), f32[8,32,256]{2,1,0:T(8,128)S(1)}, u32[]{:S(2)}, u32[]{:S(2)}) async-start(f32[8,32,256]{2,1,0:T(8,128)} %all_to_all.38), calls=%async_computation | async-start | bytes 524288 | tf_op jit(solution)/shard_map/all_to_all | solution.py:691
  127.1 12.4 %all-to-all-start.1 = ((f32[8,32,256]{2,1,0:T(8,128)}), f32[8,32,256]{2,1,0:T(8,128)S(1)}, u32[]{:S(2)}, u32[]{:S(2)}) async-start(f32[8,32,256]{2,1,0:T(8,128)} %constant_dynamic-update-slice_fusion), calls=%async_computation.1 | async-start | bytes 524288 | tf_op jit(solution)/shard_map/all_to_all | solution.py:699
  130.7 84.6 %all-gather.5.cloned.1.call-start = ((), (), s32[]{:S(2)}) async-start(), calls=%async_computation.10 | async-start | bytes 2359296 | tf_op jit(solution)/shard_map/all_gather | solution.py:636
  139.5 29.9 %all-to-all-start.4 = ((bf16[4,256,1024]{2,1,0:T(8,128)(2,1)}), bf16[4,256,1024]{2,1,0:T(8,128)(2,1)S(1)}, u32[]{:S(2)}, u32[]{:S(2)}) async-start(bf16[4,256,1024]{2,1,0:T(8,128)(2,1)} %bitcast.268), calls=%async_computation.4 | async-start | bytes 4194304 | tf_op jit(solution)/shard_map/all_to_all | solution.py:610
  146.2 30.7 %collective-permute-start.4 = (bf16[2,256,1024]{1,0,2:T(2,128)(2,1)}, bf16[2,256,1024]{1,0,2:T(2,128)(2,1)S(1)}, u32[]{:S(2)}, u32[]{:S(2)}) collective-permute-start(bf16[2,256,1024]{1,0,2:T(2,128)(2,1)} %collective-permute-done.2), channel_id=1, source_target_pairs={{0,1},{1,0},{2,3},{3,2},{4,5},{5,4},{6,7},{7,6},{8,9},{9,8},{10,11... | collective-permute-start | bytes 3145736 | tf_op jit(solution)/shard_map/ppermute | solution.py:537
  169.5 29.9 %all-to-all-start.3 = ((bf16[4,256,1024]{2,1,0:T(8,128)(2,1)}), bf16[4,256,1024]{2,1,0:T(8,128)(2,1)}, u32[]{:S(2)}, u32[]{:S(2)}) async-start(bf16[4,256,1024]{2,1,0:T(8,128)(2,1)} %bitcast.269), calls=%async_computation.3 | async-start | bytes 4194304 | tf_op jit(solution)/shard_map/all_to_all | solution.py:610
  199.4 47.2 %all-to-all-start.2 = ((bf16[4,256,1024]{2,1,0:T(8,128)(2,1)}), bf16[4,256,1024]{2,1,0:T(8,128)(2,1)}, u32[]{:S(2)}, u32[]{:S(2)}) async-start(bf16[4,256,1024]{2,1,0:T(8,128)(2,1)} %get-tuple-element.63), calls=%async_computation.2 | async-start | bytes 4194304 | tf_op jit(solution)/shard_map/all_to_all | solution.py:610
  215.1 46.4 %collective-permute-start.11 = (bf16[1024,1024]{1,0:T(8,128)(2,1)}, bf16[1024,1024]{1,0:T(8,128)(2,1)S(1)}, u32[]{:S(2)}, u32[]{:S(2)}) collective-permute-start(bf16[1024,1024]{1,0:T(8,128)(2,1)} %bitcast.323), channel_id=1, source_target_pairs={{0,1},{1,0},{2,3},{3,2},{4,5},{5,4},{6,7},{7,6},{8,9},{9,8},{10,11... | collective-permute-start | bytes 6291464 | tf_op jit(solution)/shard_map/ppermute | solution.py:537
  215.2 46.3 %collective-permute-start.9 = (bf16[1024,1024]{1,0:T(8,128)(2,1)}, bf16[1024,1024]{1,0:T(8,128)(2,1)}, u32[]{:S(2)}, u32[]{:S(2)}) collective-permute-start(bf16[1024,1024]{1,0:T(8,128)(2,1)} %bitcast.325), channel_id=1, source_target_pairs={{0,1},{1,0},{2,3},{3,2},{4,5},{5,4},{6,7},{7,6},{8,9},{9,8},{10,11... | collective-permute-start | bytes 6291464 | tf_op jit(solution)/shard_map/ppermute | solution.py:537
  370.9 43.6 %all-to-all-start.6 = ((bf16[4,256,1024]{2,1,0:T(8,128)(2,1)}), bf16[4,256,1024]{2,1,0:T(8,128)(2,1)S(1)}, u32[]{:S(2)}, u32[]{:S(2)}) async-start(bf16[4,256,1024]{2,1,0:T(8,128)(2,1)} %bitcast.290), calls=%async_computation.6 | async-start | bytes 4194304 | tf_op jit(solution)/shard_map/all_to_all | solution.py:617
  377.7 1.2 collective-permute-start.25
  379.0 20.1 %collective-permute-start.26 = (f32[1,2052]{1,0:T(1,128)S(1)}, f32[1,2052]{1,0:T(1,128)S(1)}, u32[]{:S(2)}, u32[]{:S(2)}) collective-permute-start(f32[1,2052]{1,0:T(1,128)S(1)} %slice.562), channel_id=1, source_target_pairs={{0,2},{1,3},{2,0},{3,1},{4,6},{5,7},{6,4},{7,5},{8,10},{9,11},{10,... | collective-permute-start | bytes 24632 | tf_op jit(solution)/shard_map/ppermute | solution.py:537
  379.2 214.9 %collective-permute-start.38 = (bf16[2,1024,1024]{2,1,0:T(8,128)(2,1)}, bf16[2,1024,1024]{2,1,0:T(8,128)(2,1)}, u32[]{:S(2)}, u32[]{:S(2)}) collective-permute-start(bf16[2,1024,1024]{2,1,0:T(8,128)(2,1)} %bitcast.321), channel_id=1, source_target_pairs={{0,1},{1,0},{2,3},{3,2},{4,5},{5,4},{6,7},{7,6},{8,9},{9,8},{10,11... | collective-permute-start | bytes 12582920 | tf_op jit(solution)/shard_map/ppermute | solution.py:537
  379.4 207.0 %collective-permute-start.30 = (bf16[2,1024,1024]{2,1,0:T(8,128)(2,1)}, bf16[2,1024,1024]{2,1,0:T(8,128)(2,1)}, u32[]{:S(2)}, u32[]{:S(2)}) collective-permute-start(bf16[2,1024,1024]{2,1,0:T(8,128)(2,1)} %bitcast.322), channel_id=1, source_target_pairs={{0,1},{1,0},{2,3},{3,2},{4,5},{5,4},{6,7},{7,6},{8,9},{9,8},{10,11... | collective-permute-start | bytes 12582920 | tf_op jit(solution)/shard_map/ppermute | solution.py:537
  399.1 4.5 collective-permute-start.27
  403.6 3.8 collective-permute-start.28
  407.4 4.6 collective-permute-start.29
  409.1 158.3 %collective-permute-start.17 = (bf16[2,512,1024]{2,1,0:T(8,128)(2,1)}, bf16[2,512,1024]{2,1,0:T(8,128)(2,1)}, u32[]{:S(2)}, u32[]{:S(2)}) collective-permute-start(bf16[2,512,1024]{2,1,0:T(8,128)(2,1)} %pad_maximum_fusion.2), channel_id=1, source_target_pairs={{0,1},{1,0},{2,3},{3,2},{4,5},{5,4},{6,7},{7,6},{8,9},{9,8},{10,11... | collective-permute-start | bytes 6291464 | tf_op jit(solution)/shard_map/ppermute | solution.py:537
  437.1 11.6 %all-to-all-start.7 = ((f32[8,32,256]{2,1,0:T(8,128)}), f32[8,32,256]{2,1,0:T(8,128)S(1)}, u32[]{:S(2)}, u32[]{:S(2)}) async-start(f32[8,32,256]{2,1,0:T(8,128)} %all_to_all.46), calls=%async_computation.7 | async-start | bytes 524288 | tf_op jit(solution)/shard_map/all_to_all | solution.py:691
  448.7 30.4 %all-to-all-start.5 = ((bf16[4,256,1024]{2,1,0:T(8,128)(2,1)}), bf16[4,256,1024]{2,1,0:T(8,128)(2,1)}, u32[]{:S(2)}, u32[]{:S(2)}) async-start(bf16[4,256,1024]{2,1,0:T(8,128)(2,1)} %bitcast.289), calls=%async_computation.5 | async-start | bytes 4194304 | tf_op jit(solution)/shard_map/all_to_all | solution.py:617
  455.5 27.0 %copy-start.17 = (bf16[256,32,128]{2,1,0:T(8,128)(2,1)S(1)}, bf16[256,32,128]{2,1,0:T(8,128)(2,1)}, u32[]{:S(2)}) copy-start(bf16[256,32,128]{2,1,0:T(8,128)(2,1)} %copy-done.15) | copy-start | bytes 6291460
  479.0 38.8 %all-to-all-start.8 = ((f32[8,32,256]{2,1,0:T(8,128)}), f32[8,32,256]{2,1,0:T(8,128)S(1)}, u32[]{:S(2)}, u32[]{:S(2)}) async-start(f32[8,32,256]{2,1,0:T(8,128)} %constant_dynamic-update-slice_fusion.9), calls=%async_computation.8 | async-start | bytes 524288 | tf_op jit(solution)/shard_map/all_to_all | solution.py:699
  517.9 85.6 %all-to-all-start.9 = ((bf16[4,256,1024]{2,1,0:T(8,128)(2,1)}), bf16[4,256,1024]{2,1,0:T(8,128)(2,1)}, u32[]{:S(2)}, u32[]{:S(2)}) async-start(bf16[4,256,1024]{2,1,0:T(8,128)(2,1)} %bitcast.60), calls=%async_computation.9 | async-start | bytes 4194304 | tf_op jit(solution)/shard_map/all_to_all | solution.py:617
  565.5 8.7 %collective-permute-start.14 = (f32[256,130]{1,0:T(8,128)}, f32[256,130]{1,0:T(8,128)S(1)}, u32[]{:S(2)}, u32[]{:S(2)}) collective-permute-start(f32[256,130]{1,0:T(8,128)} %concatenate.135), channel_id=1, source_target_pairs={{0,4},{4,0},{8,12},{12,8},{16,20},{20,16},{24,28},{28,24},{1,5},{5... | collective-permute-start | bytes 399368 | tf_op jit(solution)/shard_map/ppermute | solution.py:537
  567.4 3.1 collective-permute-start.12
  570.5 6.9 collective-permute-start.13
  574.2 9.3 %collective-permute-start.15 = (f32[256,130]{1,0:T(8,128)S(1)}, f32[256,130]{1,0:T(8,128)S(1)}, u32[]{:S(2)}, u32[]{:S(2)}) collective-permute-start(f32[256,130]{1,0:T(8,128)S(1)} %add.455), channel_id=1, source_target_pairs={{0,8},{4,12},{8,0},{12,4},{16,24},{20,28},{24,16},{28,20},{1,9},{5... | collective-permute-start | bytes 399368 | tf_op jit(solution)/shard_map/ppermute | solution.py:537
  577.1 36.0 %collective-permute-start.18 = (bf16[2,256,1024]{2,1,0:T(8,128)(2,1)}, bf16[2,256,1024]{2,1,0:T(8,128)(2,1)}, u32[]{:S(2)}, u32[]{:S(2)}) collective-permute-start(bf16[2,256,1024]{2,1,0:T(8,128)(2,1)} %constant_dynamic-slice_fusion.12), channel_id=1, source_target_pairs={{0,8},{4,12},{8,0},{12,4},{16,24},{20,28},{24,16},{28,20},{1,9},{5... | collective-permute-start | bytes 3145736 | tf_op jit(solution)/shard_map/ppermute | solution.py:537
  583.6 28.7 %collective-permute-start.16 = (f32[256,130]{1,0:T(8,128)S(1)}, f32[256,130]{1,0:T(8,128)S(1)}, u32[]{:S(2)}, u32[]{:S(2)}) collective-permute-start(f32[256,130]{1,0:T(8,128)S(1)} %add.456), channel_id=1, source_target_pairs={{0,16},{4,20},{8,24},{12,28},{16,0},{20,4},{24,8},{28,12},{1,17},{... | collective-permute-start | bytes 399368 | tf_op jit(solution)/shard_map/ppermute | solution.py:537
  593.8 55.6 %collective-permute-start.31 = (bf16[1,1024,1024]{2,1,0:T(8,128)(2,1)}, bf16[1,1024,1024]{2,1,0:T(8,128)(2,1)}, u32[]{:S(2)}, u32[]{:S(2)}) collective-permute-start(bf16[1,1024,1024]{2,1,0:T(8,128)(2,1)} %slice.566), channel_id=1, source_target_pairs={{0,2},{1,3},{2,0},{3,1},{4,6},{5,7},{6,4},{7,5},{8,10},{9,11},{10,... | collective-permute-start | bytes 6291464 | tf_op jit(solution)/shard_map/ppermute | solution.py:537
  602.0 52.4 %collective-permute-start.39 = (bf16[2,512,1024]{2,1,0:T(8,128)(2,1)}, bf16[2,512,1024]{2,1,0:T(8,128)(2,1)}, u32[]{:S(2)}, u32[]{:S(2)}) collective-permute-start(bf16[2,512,1024]{2,1,0:T(8,128)(2,1)} %constant_dynamic-slice_fusion.2), channel_id=1, source_target_pairs={{0,4},{4,0},{8,12},{12,8},{16,20},{20,16},{24,28},{28,24},{1,5},{5... | collective-permute-start | bytes 6291464 | tf_op jit(solution)/shard_map/ppermute | solution.py:537
  614.9 34.2 %collective-permute-start.19 = (bf16[1,256,1024]{2,1,0:T(8,128)(2,1)S(1)}, bf16[1,256,1024]{2,1,0:T(8,128)(2,1)S(1)}, u32[]{:S(2)}, u32[]{:S(2)}) collective-permute-start(bf16[1,256,1024]{2,1,0:T(8,128)(2,1)S(1)} %slice.557), channel_id=1, source_target_pairs={{0,2},{1,3},{2,0},{3,1},{4,6},{5,7},{6,4},{7,5},{8,10},{9,11},{10,... | collective-permute-start | bytes 1572872 | tf_op jit(solution)/shard_map/ppermute | solution.py:537
  615.7 33.6 %copy-start.36 = (bf16[2,1024,1024]{2,1,0:T(8,128)(2,1)S(1)}, bf16[2,1024,1024]{2,1,0:T(8,128)(2,1)}, u32[]{:S(2)}) copy-start(bf16[2,1024,1024]{2,1,0:T(8,128)(2,1)} %copy-done.35) | copy-start | bytes 12582916
  652.2 23.3 %collective-permute-start.32 = (bf16[1,512,1024]{2,1,0:T(8,128)(2,1)S(1)}, bf16[1,512,1024]{2,1,0:T(8,128)(2,1)S(1)}, u32[]{:S(2)}, u32[]{:S(2)}) collective-permute-start(bf16[1,512,1024]{2,1,0:T(8,128)(2,1)S(1)} %constant_dynamic-slice_fusion.5), channel_id=1, source_target_pairs={{0,4},{4,0},{8,12},{12,8},{16,20},{20,16},{24,28},{28,24},{1,5},{5... | collective-permute-start | bytes 3145736 | tf_op jit(solution)/shard_map/ppermute | solution.py:537
  653.7 9.2 %collective-permute-start.20 = (bf16[1,128,1024]{2,1,0:T(8,128)(2,1)S(1)}, bf16[1,128,1024]{2,1,0:T(8,128)(2,1)S(1)}, u32[]{:S(2)}, u32[]{:S(2)}) collective-permute-start(bf16[1,128,1024]{2,1,0:T(8,128)(2,1)S(1)} %constant_dynamic-slice_fusion.11), channel_id=1, source_target_pairs={{0,16},{4,20},{8,24},{12,28},{16,0},{20,4},{24,8},{28,12},{1,17},{... | collective-permute-start | bytes 786440 | tf_op jit(solution)/shard_map/ppermute | solution.py:537
  657.0 32.3 %collective-permute-start.40 = (bf16[2,256,1024]{2,1,0:T(8,128)(2,1)S(1)}, bf16[2,256,1024]{2,1,0:T(8,128)(2,1)S(1)}, u32[]{:S(2)}, u32[]{:S(2)}) collective-permute-start(bf16[2,256,1024]{2,1,0:T(8,128)(2,1)S(1)} %constant_dynamic-slice_fusion.1), channel_id=1, source_target_pairs={{0,8},{4,12},{8,0},{12,4},{16,24},{20,28},{24,16},{28,20},{1,9},{5... | collective-permute-start | bytes 3145736 | tf_op jit(solution)/shard_map/ppermute | solution.py:537
  663.0 14.5 %collective-permute-start.21 = (bf16[1,64,1024]{2,1,0:T(8,128)(2,1)S(1)}, bf16[1,64,1024]{2,1,0:T(8,128)(2,1)S(1)}, u32[]{:S(2)}, u32[]{:S(2)}) collective-permute-start(bf16[1,64,1024]{2,1,0:T(8,128)(2,1)S(1)} %constant_dynamic-slice_fusion.10), channel_id=1, source_target_pairs={{0,4},{4,0},{8,12},{12,8},{16,20},{20,16},{24,28},{28,24},{1,5},{5... | collective-permute-start | bytes 393224 | tf_op jit(solution)/shard_map/ppermute | solution.py:537
  676.0 24.9 %collective-permute-start.33 = (bf16[1,256,1024]{2,1,0:T(8,128)(2,1)S(1)}, bf16[1,256,1024]{2,1,0:T(8,128)(2,1)S(1)}, u32[]{:S(2)}, u32[]{:S(2)}) collective-permute-start(bf16[1,256,1024]{2,1,0:T(8,128)(2,1)S(1)} %constant_dynamic-slice_fusion.4), channel_id=1, source_target_pairs={{0,8},{4,12},{8,0},{12,4},{16,24},{20,28},{24,16},{28,20},{1,9},{5... | collective-permute-start | bytes 1572872 | tf_op jit(solution)/shard_map/ppermute | solution.py:537
  677.5 24.6 %collective-permute-start.22 = (bf16[1,64,1024]{2,1,0:T(8,128)(2,1)S(1)}, bf16[1,64,1024]{2,1,0:T(8,128)(2,1)S(1)}, u32[]{:S(2)}, u32[]{:S(2)}) collective-permute-start(bf16[1,64,1024]{2,1,0:T(8,128)(2,1)S(1)} %add_convert_fusion.12), channel_id=1, source_target_pairs={{0,4},{4,0},{8,12},{12,8},{16,20},{20,16},{24,28},{28,24},{1,5},{5... | collective-permute-start | bytes 393224 | tf_op jit(solution)/shard_map/ppermute | solution.py:537
  689.8 26.4 %collective-permute-start.41 = (bf16[2,128,1024]{2,1,0:T(8,128)(2,1)S(1)}, bf16[2,128,1024]{2,1,0:T(8,128)(2,1)S(1)}, u32[]{:S(2)}, u32[]{:S(2)}) collective-permute-start(bf16[2,128,1024]{2,1,0:T(8,128)(2,1)S(1)} %constant_dynamic-slice_fusion), channel_id=1, source_target_pairs={{0,16},{4,20},{8,24},{12,28},{16,0},{20,4},{24,8},{28,12},{1,17},{... | collective-permute-start | bytes 1572872 | tf_op jit(solution)/shard_map/ppermute | solution.py:537
  701.1 35.3 %collective-permute-start.34 = (bf16[1,128,1024]{2,1,0:T(8,128)(2,1)S(1)}, bf16[1,128,1024]{2,1,0:T(8,128)(2,1)S(1)}, u32[]{:S(2)}, u32[]{:S(2)}) collective-permute-start(bf16[1,128,1024]{2,1,0:T(8,128)(2,1)S(1)} %constant_dynamic-slice_fusion.3), channel_id=1, source_target_pairs={{0,16},{4,20},{8,24},{12,28},{16,0},{20,4},{24,8},{28,12},{1,17},{... | collective-permute-start | bytes 786440 | tf_op jit(solution)/shard_map/ppermute | solution.py:537
  716.4 23.2 %collective-permute-start.42 = (bf16[1,128,1024]{2,1,0:T(8,128)(2,1)S(1)}, bf16[1,128,1024]{2,1,0:T(8,128)(2,1)S(1)}, u32[]{:S(2)}, u32[]{:S(2)}) collective-permute-start(bf16[1,128,1024]{2,1,0:T(8,128)(2,1)S(1)} %slice.569), channel_id=1, source_target_pairs={{0,2},{1,3},{2,0},{3,1},{4,6},{5,7},{6,4},{7,5},{8,10},{9,11},{10,... | collective-permute-start | bytes 786440 | tf_op jit(solution)/shard_map/ppermute | solution.py:537
  736.5 10.3 %collective-permute-start.35 = (bf16[1,128,1024]{2,1,0:T(8,128)(2,1)S(1)}, bf16[1,128,1024]{2,1,0:T(8,128)(2,1)S(1)}, u32[]{:S(2)}, u32[]{:S(2)}) collective-permute-start(bf16[1,128,1024]{2,1,0:T(8,128)(2,1)S(1)} %add_convert_fusion.10), channel_id=1, source_target_pairs={{0,16},{4,20},{8,24},{12,28},{16,0},{20,4},{24,8},{28,12},{1,17},{... | collective-permute-start | bytes 786440 | tf_op jit(solution)/shard_map/ppermute | solution.py:537
  736.6 13.4 %collective-permute-start.23 = (bf16[1,128,1024]{2,1,0:T(8,128)(2,1)S(1)}, bf16[1,128,1024]{2,1,0:T(8,128)(2,1)S(1)}, u32[]{:S(2)}, u32[]{:S(2)}) collective-permute-start(bf16[1,128,1024]{2,1,0:T(8,128)(2,1)S(1)} %pad_maximum_fusion.12), channel_id=1, source_target_pairs={{0,16},{4,20},{8,24},{12,28},{16,0},{20,4},{24,8},{28,12},{1,17},{... | collective-permute-start | bytes 786440 | tf_op jit(solution)/shard_map/ppermute | solution.py:537
  739.6 13.5 %collective-permute-start.43 = (bf16[1,128,1024]{2,1,0:T(8,128)(2,1)S(1)}, bf16[1,128,1024]{2,1,0:T(8,128)(2,1)S(1)}, u32[]{:S(2)}, u32[]{:S(2)}) collective-permute-start(bf16[1,128,1024]{2,1,0:T(8,128)(2,1)S(1)} %add_convert_fusion.9), channel_id=1, source_target_pairs={{0,16},{4,20},{8,24},{12,28},{16,0},{20,4},{24,8},{28,12},{1,17},{... | collective-permute-start | bytes 786440 | tf_op jit(solution)/shard_map/ppermute | solution.py:537
  746.9 17.5 %collective-permute-start.36 = (bf16[1,256,1024]{2,1,0:T(8,128)(2,1)S(1)}, bf16[1,256,1024]{2,1,0:T(8,128)(2,1)S(1)}, u32[]{:S(2)}, u32[]{:S(2)}) collective-permute-start(bf16[1,256,1024]{2,1,0:T(8,128)(2,1)S(1)} %pad_maximum_fusion.10), channel_id=1, source_target_pairs={{0,8},{4,12},{8,0},{12,4},{16,24},{20,28},{24,16},{28,20},{1,9},{5... | collective-permute-start | bytes 1572872 | tf_op jit(solution)/shard_map/ppermute | solution.py:537
  753.3 22.0 %collective-permute-start.44 = (bf16[1,256,1024]{2,1,0:T(8,128)(2,1)S(1)}, bf16[1,256,1024]{2,1,0:T(8,128)(2,1)S(1)}, u32[]{:S(2)}, u32[]{:S(2)}) collective-permute-start(bf16[1,256,1024]{2,1,0:T(8,128)(2,1)S(1)} %pad_maximum_fusion.11), channel_id=1, source_target_pairs={{0,8},{4,12},{8,0},{12,4},{16,24},{20,28},{24,16},{28,20},{1,9},{5... | collective-permute-start | bytes 1572872 | tf_op jit(solution)/shard_map/ppermute | solution.py:537
  754.2 32.2 %collective-permute-start.24 = (bf16[1,256,1024]{2,1,0:T(8,128)(2,1)}, bf16[1,256,1024]{2,1,0:T(8,128)(2,1)S(1)}, u32[]{:S(2)}, u32[]{:S(2)}) collective-permute-start(bf16[1,256,1024]{2,1,0:T(8,128)(2,1)} %pad_maximum_fusion.9), channel_id=1, source_target_pairs={{0,8},{4,12},{8,0},{12,4},{16,24},{20,28},{24,16},{28,20},{1,9},{5... | collective-permute-start | bytes 1572872 | tf_op jit(solution)/shard_map/ppermute | solution.py:537
  765.7 26.4 %collective-permute-start.37 = (bf16[1,512,1024]{2,1,0:T(8,128)(2,1)}, bf16[1,512,1024]{2,1,0:T(8,128)(2,1)}, u32[]{:S(2)}, u32[]{:S(2)}) collective-permute-start(bf16[1,512,1024]{2,1,0:T(8,128)(2,1)} %pad_maximum_fusion.4), channel_id=1, source_target_pairs={{0,4},{4,0},{8,12},{12,8},{16,20},{20,16},{24,28},{28,24},{1,5},{5... | collective-permute-start | bytes 3145736 | tf_op jit(solution)/shard_map/ppermute | solution.py:537
  776.6 36.5 %collective-permute-start.45 = (bf16[1,512,1024]{2,1,0:T(8,128)(2,1)}, bf16[1,512,1024]{2,1,0:T(8,128)(2,1)}, u32[]{:S(2)}, u32[]{:S(2)}) collective-permute-start(bf16[1,512,1024]{2,1,0:T(8,128)(2,1)} %pad_maximum_fusion.5), channel_id=1, source_target_pairs={{0,4},{4,0},{8,12},{12,8},{16,20},{20,16},{24,28},{28,24},{1,5},{5... | collective-permute-start | bytes 3145736 | tf_op jit(solution)/shard_map/ppermute | solution.py:537
  (66 other events, 343.4 us)
Sparse Core Ops, SparseCore 0:
  76.1 53.6 all-gather.6
  133.6 51.2 all-gather.4

commit v3 on v2

v3 whole, which is shorter than its diff:
```python
import functools

import jax
import jax.numpy as jnp
from jax import lax
from jax.experimental import pallas as pl
from jax.experimental.pallas import tpu as pltpu
from jax.sharding import PartitionSpec as P

D = 1024
epsilon = 1e-05
CHUNK = 128
f32 = jnp.float32
bf16 = jnp.bfloat16


def contract(left, right, left_dim, right_dim):
    return lax.dot_general(
        left, right, (((left_dim,), (right_dim,)), ((), ())), preferred_element_type=f32
    )


def nt(left, right):
    return lax.dot_general(left, right, (((1,), (1,)), ((), ())), preferred_element_type=f32)


def nn(left, right):
    return lax.dot_general(left, right, (((1,), (0,)), ((), ())), preferred_element_type=f32)


def tn(left, right):
    return lax.dot_general(left, right, (((0,), (0,)), ((), ())), preferred_element_type=f32)


def gelu_pair(v):
    k0 = 0.7978845608028654
    k1 = 0.044715
    square = v * v
    t = jnp.tanh(k0 * v * (1.0 + k1 * square))
    half = 0.5 * (1.0 + t)
    return v * half, half + 0.5 * v * (1.0 - t * t) * k0 * (1.0 + 3.0 * k1 * square)


def cmul(a, b):
    return (a[0] * b[0] - a[1] * b[1], a[0] * b[1] + a[1] * b[0])


def cadd(a, b):
    return (a[0] + b[0], a[1] + b[1])


def discretized(step, decay, freq):
    return step[:, None] * (-decay), step[:, None] * freq


def coefficients(step, decay, freq, out_real, out_imag):
    a_real, a_imag = -decay, freq
    w_real, w_imag = discretized(step, decay, freq)
    growth = jnp.exp(w_real)
    minus_real = growth * jnp.cos(w_imag) - 1.0
    minus_imag = growth * jnp.sin(w_imag)
    modulus = a_real * a_real + a_imag * a_imag
    ratio_real = (minus_real * a_real + minus_imag * a_imag) / modulus
    ratio_imag = (minus_imag * a_real - minus_real * a_imag) / modulus
    return (
        out_real * ratio_real - out_imag * ratio_imag,
        out_real * ratio_imag + out_imag * ratio_real,
    )


def power(w, exponent):
    envelope = jnp.exp(w[0] * exponent)
    return envelope * jnp.cos(w[1] * exponent), envelope * jnp.sin(w[1] * exponent)


GROUP = 8


def four(pair, axis=-1):
    return jnp.concatenate([pair[0], pair[1], -pair[1], pair[0]], axis=axis)


def turn(values):
    return pltpu.roll(values, values.shape[1] // 2, 1)


def row_of_chunk(shape, chunks):
    return lax.rem(lax.broadcasted_iota(jnp.int32, shape, 0), chunks)


def groups_of(block):
    size = min(GROUP, block)
    return [range(k, k + size) for k in range(0, block, size)]


def moved_rows(values, step, chunks, backward):
    rows, width = values.shape
    if chunks == 8:
        cube = values.reshape(rows // 8, 8, width)
        place = lax.broadcasted_iota(jnp.int32, cube.shape, 1)
        if backward:
            cube = jnp.where(place < 8 - step, pltpu.roll(cube, 8 - step, 1), 0.0)
        else:
            cube = jnp.where(place >= step, pltpu.roll(cube, step, 1), 0.0)
        return cube.reshape(rows, width)
    place = row_of_chunk(values.shape, chunks)
    if backward:
        return jnp.where(place < chunks - step, pltpu.roll(values, rows - step, 0), 0.0)
    return jnp.where(place >= step, pltpu.roll(values, step, 0), 0.0)


def scan_rows(states, pars_ref, group, chunks, backward):
    step, k = 1, 0
    while step < chunks:
        moved = [moved_rows(s, step, chunks, backward) for s in states]
        turned = [turn(m) for m in moved]
        states = [
            s + m * pars_ref[i, 2 * k : 2 * k + 1, :] + t * pars_ref[i, 2 * k + 1 : 2 * k + 2, :]
            for i, s, m, t in zip(group, states, moved, turned)
        ]
        step, k = 2 * step, k + 1
    return states


def entered(terms, into, chunks, backward):
    rows, width = terms.shape
    wide = jnp.concatenate(
        [jnp.broadcast_to(into[b : b + 1], (chunks, width)) for b in range(rows // chunks)], axis=0
    )
    if chunks == 1:
        return wide
    place = row_of_chunk(terms.shape, chunks)
    edge = chunks - 1 if backward else 0
    return jnp.where(place == edge, wide, moved_rows(terms, 1, chunks, backward))


def weighed(states, turned, pars_ref, i):
    last = pars_ref.shape[1]
    return (
        states * pars_ref[i, last - 2 : last - 1, :] + turned * pars_ref[i, last - 1 : last, :]
    ).astype(bf16)


def toeplitz(taps):
    size = taps.shape[-1]
    rolled = pltpu.roll(jnp.broadcast_to(taps, (size, size)), 0, 1, stride=1, stride_axis=0)
    rows = lax.broadcasted_iota(jnp.int32, (size, size), 0)
    lanes = lax.broadcasted_iota(jnp.int32, (size, size), 1)
    return jnp.where(lanes >= rows, rolled, 0.0).astype(bf16)


def reversal(size):
    rows = lax.broadcasted_iota(jnp.int32, (size, size), 0)
    lanes = lax.broadcasted_iota(jnp.int32, (size, size), 1)
    return jnp.where(rows + lanes == size - 1, 1.0, 0.0).astype(bf16)


def circle(turns):
    x = (turns - jnp.floor(turns + 0.5)) * 3.14159265358979
    s = x * x
    sine = x * (
        1.0
        + s
        * (
            -1.0 / 6.0
            + s
            * (
                1.0 / 120.0
                + s * (-1.0 / 5040.0 + s * (1.0 / 362880.0 + s * (-1.0 / 39916800.0)))
            )
        )
    )
    cosine = 1.0 + s * (
        -0.5
        + s
        * (
            1.0 / 24.0
            + s
            * (
                -1.0 / 720.0
                + s * (1.0 / 40320.0 + s * (-1.0 / 3628800.0 + s * (1.0 / 479001600.0)))
            )
        )
    )
    return 1.0 - 2.0 * sine * sine, 2.0 * sine * cosine


def tables_kernel(
    chunk, steps, local, step_ref, decay_ref, freq_ref, real_ref, imag_ref,
    pars_ref, whole_ref, one_ref, two_ref, taps_ref, line_ref,
):
    block, modes = decay_ref.shape
    size = one_ref.shape[2]
    step = step_ref[...]
    a_real, a_imag = -decay_ref[...], freq_ref[...]
    w_real, turns = step * a_real, step * a_imag * 0.15915494309189535

    def z_power(exponent):
        envelope = jnp.exp(w_real * exponent)
        cosine, sine = circle(turns * exponent)
        return envelope * cosine, envelope * sine

    z = z_power(1.0)
    minus_real, minus_imag = z[0] - 1.0, z[1]
    modulus = 1.0 / (a_real * a_real + a_imag * a_imag)
    ratio = (
        (minus_real * a_real + minus_imag * a_imag) * modulus,
        (minus_imag * a_real - minus_real * a_imag) * modulus,
    )
    c = cmul((real_ref[...], imag_ref[...]), ratio)
    zk = z_power(float(local))
    whole = [(zk[0], zk[0], zk[0], zk[0]), (zk[1], zk[1], -zk[1], -zk[1])]
    lines = []
    for k in range(steps):
        zk = z_power(float(chunk * 2**k))
        lines += [(zk[0], zk[0], zk[0], zk[0]), (zk[1], zk[1], -zk[1], -zk[1])]
    lines += [(c[0], -c[0], -c[0], c[0]), (c[1], -c[1], c[1], -c[1])]
    for k, line in enumerate(whole):
        whole_ref[:, k, :] = jnp.concatenate(line, axis=-1)
    for k, line in enumerate(lines):
        pars_ref[:, k, :] = jnp.concatenate(line, axis=-1)
    line_ref[...] = jnp.zeros_like(line_ref)
    for k, line in enumerate((w_real, turns, c[0], c[1], z[0], z[1])):
        line_ref[:, k, 0:modes] = line
    places = lax.broadcasted_iota(jnp.int32, (modes, size), 1).astype(f32)
    flip = reversal(size)
    for i in range(block):
        cols = line_ref[i].T

        def col(k):
            return jnp.broadcast_to(cols[:modes, k : k + 1], (modes, size))

        envelope = jnp.exp(col(0) * places)
        cosine, sine = circle(col(1) * places)
        level = (envelope * cosine, envelope * sine)
        taps_ref[i : i + 1, :] = 2.0 * jnp.sum(
            col(2) * level[0] - col(3) * level[1], axis=0, keepdims=True
        )
        one_ref[i] = four(cmul(level, (col(4), col(5))), 0).astype(bf16)
        two_ref[i] = nn(four(level, 0).astype(bf16), flip).astype(bf16)


def states_kernel(
    chunks, x_ref, scale_ref, gain_ref, two_ref, pars_ref, u_ref, q_ref, end_ref, flat_ref
):
    block, rows, size = u_ref.shape
    for r in range(rows):
        b, j = r // chunks, r % chunks
        flat_ref[pl.ds(r, block, stride=rows), :] = x_ref[b, :, j * size : (j + 1) * size].astype(
            f32
        )
    for group in groups_of(block):
        us = [
            (
                flat_ref[i * rows : (i + 1) * rows, :] * scale_ref[...] * gain_ref[i : i + 1, :]
            ).astype(bf16)
            for i in group
        ]
        qs = [nt(u, two_ref[i]) for i, u in zip(group, us)]
        wholes = scan_rows(qs, pars_ref, group, chunks, False)
        for i, u, q, whole in zip(group, us, qs, wholes):
            u_ref[i] = u
            q_ref[i] = q
            for b in range(rows // chunks):
                last = b * chunks + chunks - 1
                end_ref[i, b : b + 1, :] = whole[last : last + 1, :].astype(bf16)


def hand_kernel(seq, backward, terms_ref, pars_ref, out_ref):
    group = terms_ref.shape[0] // seq
    state = jnp.zeros((group,) + terms_ref.shape[1:], f32)
    half = terms_ref.shape[2] // 2
    for k in range(seq - 1, -1, -1) if backward else range(seq):
        out_ref[k * group : (k + 1) * group] = state.astype(bf16)
        state = (
            state * pars_ref[:, 0:1, :]
            + pltpu.roll(state, half, 2) * pars_ref[:, 1:2, :]
            + terms_ref[k * group : (k + 1) * group].astype(f32)
        )


def mix_kernel(
    chunks, u_ref, q_ref, into_ref, one_ref, taps_ref, skip_ref, pars_ref,
    mixed_ref, state_ref, lifted_ref, flat_ref,
):
    block, rows, size = u_ref.shape
    for group in groups_of(block):
        states = [entered(q_ref[i], into_ref[i].astype(f32), chunks, False) for i in group]
        states = scan_rows(states, pars_ref, group, chunks, False)
        for i, s in zip(group, states):
            state_ref[i] = s
        outs = [weighed(s, turn(s), pars_ref, i) for i, s in zip(group, states)]
        near = [nn(u_ref[i], toeplitz(taps_ref[i : i + 1, :])) for i in group]
        ys = [y + nn(o, one_ref[i]) for i, y, o in zip(group, near, outs)]
        mixes = [
            (y + skip_ref[i : i + 1, :] * u_ref[i].astype(f32)).astype(bf16)
            for i, y in zip(group, ys)
        ]
        for i, mixed in zip(group, mixes):
            mixed_ref[i] = mixed
            flat_ref[i * rows : (i + 1) * rows, :] = gelu_pair(mixed.astype(f32))[0]
    for r in range(rows):
        b, j = r // chunks, r % chunks
        lifted_ref[b, :, j * size : (j + 1) * size] = flat_ref[
            pl.ds(r, block, stride=rows), :
        ].astype(bf16)


def ends_kernel(chunks, gl_ref, mixed_ref, one_ref, pars_ref, g_ref, p_ref, end_ref, flat_ref):
    block, rows, size = mixed_ref.shape
    for r in range(rows):
        b, j = r // chunks, r % chunks
        flat_ref[pl.ds(r, block, stride=rows), :] = gl_ref[
            b, :, j * size : (j + 1) * size
        ].astype(f32)
    for group in groups_of(block):
        gs = [
            (
                flat_ref[i * rows : (i + 1) * rows, :] * gelu_pair(mixed_ref[i].astype(f32))[1]
            ).astype(bf16)
            for i in group
        ]
        ps = [nt(g, one_ref[i]) for i, g in zip(group, gs)]
        wholes = scan_rows(ps, pars_ref, group, chunks, True)
        for i, g, p, whole in zip(group, gs, ps, wholes):
            g_ref[i] = g
            p_ref[i] = p
            for b in range(rows // chunks):
                end_ref[i, b : b + 1, :] = whole[b * chunks : b * chunks + 1, :].astype(bf16)


def summed(values):
    return jnp.sum(values, axis=0, keepdims=True)


def sums_kernel(g_ref, u_ref, state_ref, p_ref, one_ref, sum_ref):
    block, rows, size = g_ref.shape
    lanes = lax.broadcasted_iota(jnp.int32, (rows, size), 1).astype(f32)
    row_id = lax.broadcasted_iota(jnp.int32, (size, size), 0)
    lane_id = lax.broadcasted_iota(jnp.int32, (size, size), 1)
    places = lane_id[0:1].astype(f32)
    keep = lane_id <= row_id
    flip = reversal(size)
    for group in groups_of(block):
        flipped = [nt(flip, u_ref[i]).astype(bf16) for i in group]
        pas = [nt((g_ref[i].astype(f32) * lanes).astype(bf16), one_ref[i]) for i in group]
        outers = [nn(f, g_ref[i]) for i, f in zip(group, flipped)]
        lags = [
            summed(jnp.where(keep, pltpu.roll(o, 1, 1, stride=1, stride_axis=0), 0.0))
            for o in outers
        ]
        stacked = []
        for lag in lags:
            parts = []
            for v in (lag, lag * places):
                high = v.astype(bf16).astype(f32)
                parts += [high, v - high]
            stacked += [
                jnp.concatenate(parts + [jnp.zeros((4, size), f32)], axis=0).astype(bf16)
            ]
        withins = [nt(s, one_ref[i]) for i, s in zip(group, stacked)]
        for i, pa, within in zip(group, pas, withins):
            states = state_ref[i]
            p = p_ref[i]
            sum_ref[i, 0:1, :] = summed(states * p)
            sum_ref[i, 1:2, :] = summed(states * turn(p))
            sum_ref[i, 2:3, :] = summed(states * pa)
            sum_ref[i, 3:4, :] = summed(states * turn(pa))
            sum_ref[i, 4:5, :] = within[0:1] + within[1:2]
            sum_ref[i, 5:6, :] = within[2:3] + within[3:4]
            skip = summed(g_ref[i].astype(f32) * u_ref[i].astype(f32))
            sum_ref[i, 6:7, :] = jnp.broadcast_to(jnp.sum(skip, axis=1, keepdims=True), (1, size))
            sum_ref[i, 7:8, :] = jnp.zeros((1, size), f32)


def back_kernel(
    chunks, g_ref, p_ref, into_ref, u_ref, state_ref, two_ref, taps_ref, skip_ref, pars_ref,
    x_ref, scale_ref, gain_ref, out_ref, sum_ref, dot_ref, first_ref, flat_ref,
):
    block, rows, size = g_ref.shape

    @pl.when(pl.program_id(0) == 0)
    def _():
        dot_ref[...] = jnp.zeros_like(dot_ref)

    lanes = lax.broadcasted_iota(jnp.int32, (rows, size), 1).astype(f32)
    for group in groups_of(block):
        qps = [nt((u_ref[i].astype(f32) * lanes).astype(bf16), two_ref[i]) for i in group]
        near = [nt(g_ref[i], toeplitz(taps_ref[i : i + 1, :])) for i in group]
        adjoints = [entered(p_ref[i], into_ref[i].astype(f32), chunks, True) for i in group]
        adjoints = scan_rows(adjoints, pars_ref, group, chunks, True)
        turned = [turn(a) for a in adjoints]
        outs = [weighed(a, t, pars_ref, i) for i, a, t in zip(group, adjoints, turned)]
        ys = [y + nn(o, two_ref[i]) for i, y, o in zip(group, near, outs)]
        for i, y, qp, adjoint, t in zip(group, ys, qps, adjoints, turned):
            flat_ref[i * rows : (i + 1) * rows, :] = y + skip_ref[i : i + 1, :] * g_ref[i].astype(
                f32
            )
            states = state_ref[i]
            here = p_ref[i] + adjoint * pars_ref[i, 0:1, :] + t * pars_ref[i, 1:2, :]
            sum_ref[i, 0:1, :] = summed(states * here)
            sum_ref[i, 1:2, :] = summed(states * turn(here))
            sum_ref[i, 2:3, :] = summed(adjoint * qp)
            sum_ref[i, 3:4, :] = summed(adjoint * turn(qp))
            sum_ref[i, 4:8, :] = jnp.zeros((4, size), f32)
    gain = gain_ref[...]
    first = jnp.zeros((block, size), f32)
    for r in range(rows):
        b, j = r // chunks, r % chunks
        lanes_r = slice(j * size, (j + 1) * size)
        grad = flat_ref[pl.ds(r, block, stride=rows), :].astype(bf16)
        out_ref[b, :, lanes_r] = grad
        product = grad.astype(f32) * x_ref[b, :, lanes_r].astype(f32)
        dot_ref[r : r + 1, :] += summed(product * gain)
        first += product * scale_ref[r : r + 1, :]
    first_ref[...] = first


def last_kernel(
    half, x_ref, low_ref, high_ref, hidden_ref, result_ref, scale_ref, cubic_ref, gain_ref,
    out_ref, copy_ref,
):
    gain = gain_ref[:, 0:1]

    def run(grad_ref):
        for b in range(x_ref.shape[0]):
            out_ref[:, b, :] = (
                scale_ref[b : b + 1, :] * gain * grad_ref[b].astype(f32)
                - cubic_ref[b : b + 1, :] * x_ref[b].astype(f32)
                + hidden_ref[b].astype(f32)
            )
            copy_ref[:, b, :] = result_ref[b]

    @pl.when(pl.program_id(0) < half)
    def _():
        run(low_ref)

    @pl.when(pl.program_id(0) >= half)
    def _():
        run(high_ref)


def over_blocks(kernel, steps, args, outs, us, scratch=(), ties=(), vmem=60):
    count = len(args)

    def run(*refs):
        kernel(*refs[:count], *refs[count + len(ties) :])

    moved = sum(a.size * a.dtype.itemsize for a, _, _ in args + outs)
    return pl.pallas_call(
        run,
        grid=(steps,),
        in_specs=[
            pl.BlockSpec(memory_space=pltpu.SMEM) if b is None else pl.BlockSpec(b, m)
            for _, b, m in args
        ]
        + [pl.BlockSpec(memory_space=pl.ANY) for _ in ties],
        out_specs=[pl.BlockSpec(b, m) for _, b, m in outs],
        out_shape=[o for o, _, _ in outs],
        scratch_shapes=list(scratch),
        compiler_params=pltpu.CompilerParams(vmem_limit_bytes=vmem * 1024 * 1024),
        cost_estimate=pl.CostEstimate(
            flops=int(us * 1e9), bytes_accessed=moved, transcendentals=0
        ),
    )(*[a for a, _, _ in args], *ties)


def along(array, dim, block, first=0):
    shape = array.shape
    if dim is None:
        return (array, tuple(shape), lambda i: (0,) * len(shape))
    sizes = tuple(block if d == dim else size for d, size in enumerate(shape))
    return (
        array,
        sizes,
        lambda i: tuple(i + first if d == dim else 0 for d in range(len(shape))),
    )


def by_channel(kernel, block, channels, args, outs, us, scratch=(), ties=(), first=0):
    return over_blocks(
        kernel,
        channels // block,
        [along(a, d, block, first) if d != "smem" else (a, None, None) for a, d in args],
        [along(o, d, block) for o, d in outs],
        us,
        scratch,
        ties,
    )


def lane_sums(values):
    width = min(128, values.shape[1])
    total = values[:, :width]
    for k in range(1, values.shape[1] // width):
        total = total + values[:, k * width : (k + 1) * width]
    return total


def gated_kernel(mp, at_ref, valid_ref, x_ref, residual_ref, *refs):
    up_refs, w_refs, refs = refs[:mp], refs[mp : 2 * mp], refs[2 * mp :]
    bias_ref, gain_ref, upstream_ref, hidden_ref, normed_ref, *refs = refs
    value_ref, opening_ref, line_ref = refs
    features = w_refs[0].shape[0] // 2

    def rows(k):
        return pl.ds(pl.multiple_of(at_ref[k] * features, features), features)

    for k in range(mp):
        upstream_ref[rows(k), :] = (up_refs[k][...].astype(f32) * valid_ref[...]).astype(bf16)
    x = x_ref[...]
    squares = branches = inner = 0.0
    for k in range(mp):
        own = slice(k * features, (k + 1) * features)
        value = nn(w_refs[k][:features], x) + bias_ref[0, own, 0:1]
        gate = nn(w_refs[k][features:], x) + bias_ref[1, own, 0:1]
        opening = 1.0 / (1.0 + jnp.exp(-gate))
        branch = value * opening
        residual = residual_ref[rows(k), :].astype(f32)
        hidden = residual + branch
        hidden_ref[own, :] = hidden
        value_ref[own, :] = value
        opening_ref[own, :] = opening
        squares += summed(residual * residual)
        branches += summed(branch * branch)
        inner += summed(hidden * hidden)
    scale = lax.rsqrt(inner / (mp * features) + epsilon)
    for k in range(mp):
        own = slice(k * features, (k + 1) * features)
        normed_ref[rows(k), :] = (hidden_ref[own, :] * scale * gain_ref[own, 0:1]).astype(bf16)
    line_ref[0:1, :] = scale
    line_ref[1:2, :] = squares
    line_ref[2:3, :] = branches
    line_ref[3:8, :] = jnp.zeros((5, scale.shape[1]), f32)


def hidden_kernel(
    blocks, first, normed_ref, upstream_ref, up_a_ref, up_b_ref, down_a_ref, down_b_ref, bias_ref,
    *refs,
):
    if first:
        feed_out, grad_out, shrink_ref, expand_ref, line_ref, up_ref, down_ref = refs
    else:
        feed_in, grad_in, feed_out, grad_out, shrink_ref, expand_ref, line_ref, up_ref, down_ref = (
            refs
        )
    step = pl.program_id(0)

    @pl.when(step < blocks)
    def _():
        up_ref[...] = up_a_ref[...]
        down_ref[...] = down_a_ref[...]

    @pl.when(step >= blocks)
    def _():
        up_ref[...] = up_b_ref[...].reshape(up_ref.shape)
        down_ref[...] = down_b_ref[...].reshape(up_ref.shape)

    @pl.when(step == 0)
    def _():
        if first:
            feed_out[...] = jnp.zeros_like(feed_out)
            grad_out[...] = jnp.zeros_like(grad_out)
        else:
            feed_out[...] = feed_in[...]
            grad_out[...] = grad_in[...]

    expanded = nn(up_ref[...], normed_ref[...]) + bias_ref[:, 0:1]
    lifted, slope = gelu_pair(expanded)
    lifted = lifted.astype(bf16)
    grad = (nn(down_ref[...], upstream_ref[...]) * slope).astype(bf16)
    shrink_ref[...] = nt(lifted, upstream_ref[...]).astype(bf16)
    expand_ref[0] = nt(normed_ref[...], grad).astype(bf16)
    line_ref[...] = lane_sums(grad.astype(f32))
    feed_out[...] += tn(down_ref[...], lifted)
    grad_out[...] += tn(up_ref[...], grad)


def gated_back_kernel(
    mp, at_ref, grad_ref, hidden_ref, value_ref, opening_ref, upstream_ref, line_ref, *refs
):
    w_refs, refs = refs[:mp], refs[mp:]
    gain_ref, lifted_ref, grad_hidden_ref, both_ref, sums_ref = refs

    @pl.when(pl.program_id(0) == 0)
    def _():
        sums_ref[...] = jnp.zeros_like(sums_ref)

    features = w_refs[0].shape[0] // 2

    def rows(k):
        return pl.ds(pl.multiple_of(at_ref[k] * features, features), features)

    scale = line_ref[0:1, :]
    dot = 0.0
    for k in range(mp):
        own = slice(k * features, (k + 1) * features)
        dot += summed(grad_ref[rows(k), :] * gain_ref[own, 0:1] * hidden_ref[own, :])
    cubic = scale * scale * scale * dot / (mp * features)
    lifted = 0.0
    for k in range(mp):
        own = slice(k * features, (k + 1) * features)
        hidden = hidden_ref[own, :]
        grad = grad_ref[rows(k), :]
        upstream = upstream_ref[rows(k), :].astype(f32)
        grad_hidden = scale * grad * gain_ref[own, 0:1] - hidden * cubic + upstream
        grad_hidden_ref[rows(k), :] = grad_hidden.astype(bf16)
        opening = opening_ref[own, :]
        grad_value = grad_hidden * opening
        grad_gate = (grad_value * value_ref[own, :] * (1.0 - opening)).astype(bf16)
        grad_value = grad_value.astype(bf16)
        sums_ref[k, 0] += lane_sums(grad_value.astype(f32))
        sums_ref[k, 1] += lane_sums(grad_gate.astype(f32))
        sums_ref[k, 2] += lane_sums(grad * hidden * scale)
        sums_ref[k, 3] += lane_sums(upstream)
        both = jnp.concatenate([grad_value, grad_gate], axis=0)
        both_ref[2 * k * features : 2 * (k + 1) * features, :] = both
        lifted += tn(w_refs[k][...], both)
    lifted_ref[...] = lifted.astype(bf16)


def gated_terms_kernel(
    features, at_ref, both_ref, x_ref, hidden_ref, feed_ref, bias_ref,
    near_ref, far_ref, result_ref, line_ref,
):
    step = pl.program_id(0)
    terms = nt(x_ref[...], both_ref[...]).astype(bf16)
    rows = pl.ds(pl.multiple_of(at_ref[step] * features, features), features)
    feed = feed_ref[rows, :] + bias_ref[:, 0:1]
    result_ref[rows, :] = (hidden_ref[...] + feed).astype(bf16)

    @pl.when(step == 0)
    def _():
        line_ref[...] = jnp.zeros_like(line_ref)

    line_ref[0:1, :] += summed(feed * feed)

    @pl.when(step < 2)
    def _():
        near_ref[0] = terms

    @pl.when(step >= 2)
    def _():
        far_ref[0] = terms


def swap(values, axis, bit):
    size = lax.axis_size(axis)
    return lax.ppermute(values, axis, [(i, i ^ bit) for i in range(size)])


def added(a, b):
    return (a.astype(f32) + b.astype(f32)).astype(bf16)


def axis_total(values, axis):
    bit = 1
    while bit < lax.axis_size(axis):
        values = values + swap(values, axis, bit)
        bit *= 2
    return values


def bits_of(axis):
    return [1 << k for k in range(lax.axis_size(axis).bit_length() - 1)]


def axis_of(bit):
    return 0 if bit == 0 else 1 + len(bits_of("seq")) - bit.bit_length()


def sent_down(terms, bit):
    if bit == 0:
        return terms[:1], terms[1:], swap(terms[1:], "mp", 2)
    mine = (lax.axis_index("seq") // bit) % 2
    kept = lax.dynamic_slice_in_dim(terms, mine, 1, axis_of(bit))
    sent = lax.dynamic_slice_in_dim(terms, 1 - mine, 1, axis_of(bit))
    return kept, sent, swap(sent, "seq", bit)


def up_step(terms, bit):
    there = swap(terms, "seq", bit)
    first = (lax.axis_index("seq") // bit) % 2 == 0
    return jnp.concatenate(
        [jnp.where(first, terms, there), jnp.where(first, there, terms)], axis=axis_of(bit)
    )


def shards(
    inputs,
    valid,
    cotangent,
    first_gain,
    step_size,
    decay_rate,
    frequency,
    readout_real,
    readout_imag,
    skip_weight,
    gated_weight,
    gated_bias,
    second_gain,
    expand_weight,
    expand_bias,
    shrink_weight,
    shrink_bias,
):
    mp = lax.axis_size("mp")
    seq = lax.axis_size("seq")
    mp_me = lax.axis_index("mp")
    seq_me = lax.axis_index("seq")
    features, contexts, local = inputs.shape
    chunk = min(CHUNK, local)
    chunks = local // chunk
    rows = contexts * chunks
    modes = decay_rate.shape[1]
    tokens = local
    hidden_own = expand_weight.shape[1]
    group = features // seq

    bits_at = [(k // 2) + 2 * (k % 2) for k in range(mp)]
    device_at = [jnp.bitwise_xor(mp_me, bit) for bit in bits_at]
    at = jnp.stack(device_at).astype(jnp.int32)

    def exchanged(values):
        sent = [lax.dynamic_index_in_dim(values, device_at[k], 0, keepdims=False) for k in range(mp)]
        return [sent[0]] + [swap(sent[k], "mp", bits_at[k]) for k in range(1, mp)]

    def returned(values):
        return lax.all_to_all(values.reshape(mp, features, local), "mp", 0, 0, tiled=True)

    def after(value, earlier):
        return lax.optimization_barrier((value, earlier))[0]

    def all_places(own, upper):
        return own, upper, swap(own, "mp", 1), swap(upper, "mp", 1)

    gated_own = gated_weight.transpose(1, 2, 0).reshape(2 * features, D)
    small = jnp.concatenate([gated_bias.reshape(-1), second_gain, expand_bias, shrink_bias])
    by_context = inputs.swapaxes(0, 1)
    squares = jnp.sum(jnp.square(by_context.astype(f32)), axis=1)
    sent = jnp.concatenate([squares.reshape(-1), small])
    flats = [sent] + [swap(sent, "mp", bits_at[k]) for k in range(1, mp)]
    small_places = jnp.stack([v[contexts * local :] for v in flats])
    square_one = sum(v[: contexts * local] for v in flats).reshape(contexts, local)

    expand_own = expand_weight.T
    part = hidden_own // seq

    slices_sent = jnp.stack(
        [
            lax.dynamic_slice_in_dim(expand_own, seq_me * part, part, 0),
            lax.dynamic_slice_in_dim(shrink_weight, seq_me * part, part, 0),
        ]
    )
    slices = swap(slices_sent, "mp", 2)
    residual = lax.all_to_all(by_context, "mp", 0, 0, tiled=True)
    expand_far = swap(expand_own, "mp", 1)

    cut = [0, 2 * features]
    cut += [cut[-1] + features]
    cut += [cut[-1] + hidden_own]
    cut += [cut[-1] + features]

    def wide(values):
        return jnp.broadcast_to(values[..., None], values.shape + (128,))

    gated_bias_wide = wide(
        small_places[:, : cut[1]].reshape(mp, 2, features).swapaxes(0, 1).reshape(2, D)
    )
    gain_two_wide = wide(small_places[:, cut[1] : cut[2]].reshape(D))
    shrink_bias_wide = wide(small_places[:, cut[3] :].reshape(D))
    near_bias = wide(small_places[:2, cut[2] : cut[3]].reshape(-1))
    far_bias = wide(small_places[2:, cut[2] : cut[3]].reshape(-1))

    scale_one = lax.rsqrt(square_one / D + epsilon)
    scale_rows = scale_one.reshape(rows, chunk)

    w = discretized(step_size, decay_rate, frequency)
    coeff = coefficients(step_size, decay_rate, frequency, readout_real, readout_imag)

    def handed(ends, backward, ties=()):
        terms = lax.all_to_all(ends, "seq", 0, 0, tiled=True)
        (states,) = over_blocks(
            functools.partial(hand_kernel, seq, backward),
            1,
            [along(terms, None, 0), along(z_device, None, 0)],
            [along(out(terms.shape, bf16), None, 0)],
            3,
            (),
            ties,
        )
        return lax.all_to_all(states, "seq", 0, 0, tiled=True)

    def out(shape, dtype):
        return jax.ShapeDtypeStruct(shape, dtype)

    block = min(16, features)
    state_shape = out((features, rows, 4 * modes), f32)
    end_shape = out((features, contexts, 4 * modes), bf16)
    row_shape = out((features, rows, chunk), bf16)
    context_shape = out((contexts, features, local), bf16)
    table_shape = out((features, 4 * modes, chunk), bf16)
    sum_shape = out((features, 8, 4 * modes), f32)
    line_shape = out((features, chunk), f32)
    flat = [pltpu.VMEM((block * rows, chunk), f32)]
    skip_wide = jnp.broadcast_to(skip_weight[:, None], (features, chunk))
    gain_wide = jnp.broadcast_to(first_gain[:, None], (features, chunk))
    scan_steps = max(1, (chunks - 1).bit_length())
    pars, whole_pars, one, two, taps = by_channel(
        functools.partial(tables_kernel, chunk, scan_steps, local),
        block,
        features,
        [
            (step_size[:, None], 0),
            (decay_rate, 0),
            (frequency, 0),
            (readout_real, 0),
            (readout_imag, 0),
        ],
        [
            (out((features, 2 * scan_steps + 2, 4 * modes), f32), 0),
            (out((features, 2, 4 * modes), f32), 0),
            (table_shape, 0),
            (table_shape, 0),
            (line_shape, 0),
        ],
        10,
        [pltpu.VMEM((block, 8, 4 * modes), f32)],
        (sent, slices_sent, by_context),
    )
    gated_upper = swap(gated_own, "mp", 2)
    shrink_far = swap(shrink_weight, "mp", 1)
    z_device = lax.dynamic_slice_in_dim(whole_pars, seq_me * group, group, 0)
    cotangent_by_context = after(cotangent.swapaxes(0, 1), taps)
    upstream_parts = exchanged(cotangent_by_context)
    normed_one, terms, ends = by_channel(
        functools.partial(states_kernel, chunks),
        block,
        features,
        [(by_context, 1), (scale_rows, None), (gain_wide, 0), (two, 0), (pars, 0)],
        [(row_shape, 0), (state_shape, 0), (end_shape, 0)],
        8,
        flat,
        (slices, residual, expand_far, cotangent_by_context),
    )
    upper = lax.all_gather(after(slices, normed_one), "seq", axis=0)
    gated_places = (
        gated_own,
        gated_upper,
        swap(after(gated_own, normed_one), "mp", 1),
        swap(gated_upper, "mp", 1),
    )
    states_in = handed(ends, False, (shrink_far,))
    mixed, states, lifted_one = by_channel(
        functools.partial(mix_kernel, chunks),
        block,
        features,
        [
            (normed_one, 0),
            (terms, 0),
            (states_in, 0),
            (one, 0),
            (taps, 0),
            (skip_wide, 0),
            (pars, 0),
        ],
        [(row_shape, 0), (state_shape, 0), (context_shape, 1)],
        14,
        flat,
        (gated_upper,),
    )


    lifted_sent = after(lifted_one, (*upstream_parts, *gated_places))
    whole_one = lax.all_to_all(lifted_sent, "mp", 0, 0, tiled=True).reshape(D, tokens)
    upper_far = swap(after(upper, whole_one), "mp", 1)
    own_valid = lax.dynamic_slice_in_dim(valid, mp_me, 1, 0).astype(f32)

    token_block = min(256, tokens)
    token_steps = tokens // token_block
    wide_f = out((D, tokens), f32)
    wide_b = out((D, tokens), bf16)
    line_out = out((8, tokens), f32)

    def by_tokens(kernel, args, outs, us, scratch=(), ties=()):
        return over_blocks(
            kernel,
            token_steps,
            [along(a, d, token_block) if d != "smem" else (a, None, None) for a, d in args],
            [along(o, d, token_block) for o, d in outs],
            us,
            scratch,
            ties,
            60,
        )

    upstream, hidden, normed_two, value_part, opening, lines = by_tokens(
        functools.partial(gated_kernel, mp),
        [
            (at, "smem"),
            (own_valid, 1),
            (whole_one, 1),
            (residual.reshape(D, tokens), 1),
            *[(part_k, 1) for part_k in upstream_parts],
            *[(w_place, None) for w_place in gated_places],
            (gated_bias_wide, None),
            (gain_two_wide, None),
        ],
        [
            (wide_b, 1),
            (wide_f, 1),
            (wide_b, 1),
            (wide_f, 1),
            (wide_f, 1),
            (line_out, 1),
        ],
        12,
    )

    hidden_block = min(256, hidden_own)
    blocks = hidden_own // hidden_block
    near_rows = 2 * hidden_own

    parts = hidden_block // part
    low = ((hidden_block, D), lambda i: (jnp.minimum(i, blocks - 1), 0))
    grad_shape = out((near_rows, D), bf16)

    def half(which):
        return ((parts, 1, part, D), lambda i: (jnp.maximum(i - blocks, 0), which, 0, 0))

    def by_hidden(up, down, both, bias, carried, ties=()):
        first = carried is None
        args = [
            along(normed_two, None, 0),
            along(upstream, None, 0),
            (up, *low),
            (both, *half(0)),
            (down, *low),
            (both, *half(1)),
            along(bias, 0, hidden_block),
        ]
        if not first:
            args += [along(c, None, 0) for c in carried]
        return over_blocks(
            functools.partial(hidden_kernel, blocks, first),
            2 * blocks,
            args,
            [
                along(wide_f, None, 0),
                along(wide_f, None, 0),
                along(grad_shape, 0, hidden_block),
                (
                    out((2, D, hidden_own), bf16),
                    (1, D, hidden_block),
                    lambda i: (i // blocks, 0, i % blocks),
                ),
                along(out((near_rows, min(128, tokens)), f32), 0, hidden_block),
            ],
            38,
            [pltpu.VMEM((hidden_block, D), bf16)] * 2,
            ties,
        )

    feed, grad_normed_two, shrink_far_g, expand_far_g, far_lines = by_hidden(
        expand_far, shrink_far, upper_far, far_bias, None
    )
    core_shrink, core_expand = swap(shrink_far_g, "mp", 1), swap(expand_far_g, "mp", 1)
    feed, grad_normed_two, shrink_near_g, expand_near_g, near_lines = by_hidden(
        expand_own, shrink_weight, upper, near_bias, (feed, grad_normed_two)
    )
    bits = bits_of("seq")
    split = (2,) * (1 + len(bits))
    cubes = split + (-1, D)
    first, second, third, rest = bits[0], bits[1], bits[2], bits[3:]
    upper_bit = 0
    s_kept, s_sent, s_there = sent_down(added(shrink_near_g, core_shrink).reshape(cubes), first)
    e_kept, e_sent, e_there = sent_down(added(expand_near_g, core_expand).reshape(split + (-1, hidden_own)), second)

    def onwards(kept, there, bit):
        return sent_down(added(kept, there), bit)

    sums_out = out((mp, 4, features, min(128, token_block)), f32)
    grad_lifted_one, grad_hidden, both_g, sums = by_tokens(
        functools.partial(gated_back_kernel, mp),
        [
            (at, "smem"),
            (grad_normed_two, 1),
            (hidden, 1),
            (value_part, 1),
            (opening, 1),
            (upstream, 1),
            (lines, 1),
            *[(w_place, None) for w_place in gated_places],
            (gain_two_wide, None),
        ],
        [(wide_b, 1), (wide_b, 1), (out((2 * D, tokens), bf16), 1), (sums_out, None)],
        14,
        (),
        (s_sent, e_sent),
    )
    own_lifted_one = returned(grad_lifted_one)
    gated_near, gated_far, result, feed_lines = over_blocks(
        functools.partial(gated_terms_kernel, features),
        mp,
        [
            (at, None, None),
            along(both_g, 0, 2 * features),
            along(whole_one, None, 0),
            along(hidden, 0, features),
            along(feed, None, 0),
            along(shrink_bias_wide, 0, features),
        ],
        [
            (
                out((2, D, 2 * features), bf16),
                (1, D, 2 * features),
                lambda i: (jnp.minimum(i, 1), 0, 0),
            ),
            (
                out((2, D, 2 * features), bf16),
                (1, D, 2 * features),
                lambda i: (jnp.maximum(i - 2, 0), 0, 0),
            ),
            along(wide_b, None, 0),
            along(line_out, None, 0),
        ],
        10,
    )
    core_gated = swap(gated_far, "mp", 1)

    grad_mixed, adj_terms, adj_ends = by_channel(
        functools.partial(ends_kernel, chunks),
        block,
        features,
        [(own_lifted_one, 1), (mixed, 0), (one, 0), (pars, 0)],
        [(row_shape, 0), (state_shape, 0), (end_shape, 0)],
        10,
        flat,
        (s_there, e_there, core_gated),
    )
    s_kept, s_sent, s_there = onwards(s_kept, s_there, second)
    e_kept, e_sent, e_there = onwards(e_kept, e_there, first)
    g_kept, g_sent, g_there = sent_down(added(gated_near, core_gated).reshape(split + (-1, 2 * features)), first)
    adjoint_in = handed(adj_ends, True, (s_sent, e_sent, g_sent))
    s_kept, s_sent, s_there = onwards(s_kept, s_there, third)
    e_kept, e_sent, e_there = onwards(e_kept, e_there, upper_bit)
    (sums_one,) = by_channel(
        sums_kernel,
        block,
        features,
        [(grad_mixed, 0), (normed_one, 0), (states, 0), (adj_terms, 0), (one, 0)],
        [(sum_shape, 0)],
        20,
        (),
        (s_sent, e_sent, adjoint_in),
    )
    own_hidden = returned(after(grad_hidden, adjoint_in))
    s_there, e_there, g_there = after((s_there, e_there, g_there), sums_one)
    g_kept, g_sent, g_there = onwards(g_kept, g_there, upper_bit)
    s_kept, s_sent, s_there = onwards(s_kept, s_there, upper_bit)
    e_kept, e_sent, e_there = onwards(e_kept, e_there, third)
    half = features // 2 // block
    back_args = [
        (grad_mixed, 0),
        (adj_terms, 0),
        (adjoint_in, 0),
        (normed_one, 0),
        (states, 0),
        (two, 0),
        (taps, 0),
        (skip_wide, 0),
        (pars, 0),
        (by_context, 1),
        (scale_rows, None),
        (gain_wide, 0),
    ]

    def back(first_block, ties):
        return by_channel(
            functools.partial(back_kernel, chunks),
            block,
            features // 2,
            back_args,
            [
                (out((contexts, features // 2, local), bf16), 1),
                (out((features // 2, 8, 4 * modes), f32), 0),
                (out((rows, chunk), f32), None),
                (out((features // 2, chunk), f32), 0),
            ],
            12,
            flat,
            ties,
            first_block,
        )

    def up(values, bit):
        return up_step(values, bit)

    def exchange(values, bit):
        return added(values, swap(values, "seq", bit))

    low = back(0, (s_sent, e_sent, g_sent, sums_one, own_hidden))
    result = returned(after(result, own_hidden))
    s_there, e_there, g_there = after((s_there, e_there, g_there), low[2])
    s_all, e_all, g_all = added(s_kept, s_there), added(e_kept, e_there), added(g_kept, g_there)
    for bit in rest:
        s_all, e_all = (added(*sent_down(v, bit)[::2]) for v in (s_all, e_all))
        g_all = exchange(g_all, bit)
    high = back(half, (s_all, e_all, g_all, low[2], result))
    for bit in rest[::-1]:
        s_all, e_all = up(s_all, bit), up(e_all, bit)
    s_all, e_all, g_all = up(s_all, third), up(e_all, first), exchange(g_all, second)
    s_all, e_all, g_all = after((s_all, e_all, g_all), high[2])
    grad_first_gain = jnp.sum(jnp.concatenate([low[3], high[3]]), axis=1)

    dot_one = axis_total(low[2] + high[2], "mp").reshape(contexts, local)
    cubic = scale_one * scale_one * scale_one * dot_one / D
    grad_inputs, result = over_blocks(
        functools.partial(last_kernel, half),
        features // block,
        [
            along(by_context, 1, block),
            (low[0], (contexts, block, local), lambda i: (0, jnp.minimum(i, half - 1), 0)),
            (high[0], (contexts, block, local), lambda i: (0, jnp.maximum(i - half, 0), 0)),
            along(own_hidden, 1, block),
            along(result, 1, block),
            along(scale_one, None, 0),
            along(cubic, None, 0),
            along(gain_wide, 0, block),
        ],
        [along(out(inputs.shape, f32), 0, block), along(out(inputs.shape, bf16), 0, block)],
        8,
    )
    s_all, e_all, g_all = up(s_all, second), up(e_all, third), exchange(g_all, third)
    s_all, e_all, g_all = after((s_all, e_all, g_all), grad_inputs)

    stats = jnp.stack(
        [
            jnp.sum(own_valid[0] * lines[1]),
            jnp.sum(own_valid[0] * lines[2]),
            jnp.sum(own_valid[0] * feed_lines[0]),
            jnp.sum(own_valid[0]),
        ]
    )
    sums = jnp.sum(sums, axis=3).reshape(mp, 4 * features)
    sums = jnp.concatenate([sums, jnp.broadcast_to(stats, (mp, 4))], axis=1)
    near = jnp.concatenate([sums[:2], jnp.sum(near_lines, axis=1).reshape(2, hidden_own)], axis=1)
    far = jnp.concatenate([sums[2:], jnp.sum(far_lines, axis=1).reshape(2, hidden_own)], axis=1)
    near = near + swap(far, "mp", 1)
    bias_size = near.shape[1]

    def quarter(values, k):
        return values[:, k * modes : (k + 1) * modes]

    def product_sums(lines, k):
        plain, turned = lines[:, k], lines[:, k + 1]
        return (
            quarter(plain, 0) - quarter(plain, 1),
            quarter(turned, 1) + quarter(turned, 3),
        )

    inverse = power(w, -1.0)
    within = [
        cmul(inverse, (quarter(sums_one[:, k], 0), quarter(sums_one[:, k], 1))) for k in (4, 5)
    ]
    sum_a = cadd(product_sums(sums_one, 0), within[0])
    def both_halves(k):
        pairs = [product_sums(part_k[1], k) for part_k in (low, high)]
        return tuple(jnp.concatenate(v) for v in zip(*pairs))

    crossing = both_halves(0)
    part_a = product_sums(sums_one, 2)
    part_p = both_halves(2)
    sum_b = [
        float(chunk) * crossing[k] + part_a[k] - part_p[k] + within[1][k] for k in range(2)
    ]
    lines_late = jnp.concatenate(
        [sums_one[:, 6, 0], grad_first_gain, near.reshape(-1)]
    )
    width = 4 * modes
    pad = -lines_late.shape[0] % width
    late = jnp.concatenate(
        [
            jnp.concatenate([*sum_a, *sum_b], axis=1),
            jnp.pad(lines_late, (0, pad)).reshape(-1, width),
        ],
        axis=0,
    )
    s_all, e_all, g_all = up(s_all, first), up(e_all, second), up(g_all, first)
    late = axis_total(late, "seq")
    grad_shrink = s_all.reshape(-1, D).astype(f32)
    grad_expand = e_all.reshape(D, hidden_own).astype(f32)
    grad_gated = g_all.reshape(D, 2, features).astype(f32)
    lines_late = late[features:].reshape(-1)
    late = late[:features]
    sum_a = (quarter(late, 0), quarter(late, 1))
    sum_b = (quarter(late, 2), quarter(late, 3))
    grad_skip = lines_late[:features]
    grad_first_gain = lines_late[features : 2 * features]
    bias_own = lines_late[2 * features : 2 * features + 2 * bias_size].reshape(2, bias_size)
    bias_own = bias_own[0] + swap(bias_own[1], "mp", 2)

    def form(step, decay, freq, out_real, out_imag):
        c = coefficients(step, decay, freq, out_real, out_imag)
        moved = cmul(coeff, discretized(step, decay, freq))
        return 2.0 * jnp.sum(
            c[0] * sum_a[0] - c[1] * sum_a[1] + moved[0] * sum_b[0] - moved[1] * sum_b[1]
        )

    kernel_grads = jax.grad(form, argnums=(0, 1, 2, 3, 4))(
        step_size, decay_rate, frequency, readout_real, readout_imag
    )
    ends_at = [0, 2 * features, 3 * features, 4 * features, 4 * features + 4]
    totals = bias_own[ends_at[3] : ends_at[4]]
    count = totals[3]
    rms = jnp.sqrt(totals[:3] / (count * D))
    return (
        result,
        grad_inputs,
        grad_first_gain,
        *kernel_grads,
        grad_skip,
        grad_gated,
        bias_own[: ends_at[1]].reshape(2, features),
        bias_own[ends_at[1] : ends_at[2]],
        grad_expand,
        bias_own[ends_at[4] :],
        grad_shrink,
        bias_own[ends_at[2] : ends_at[3]],
        rms[0],
        rms[1],
        rms[2],
    )


def solution(mesh):
    placed = (
        P("mp", None, "seq"),
        P(None, "seq"),
        P("mp", None, "seq"),
        P("mp"),
        P("mp"),
        P("mp", None),
        P("mp", None),
        P("mp", None),
        P("mp", None),
        P("mp"),
        P(None, None, "mp"),
        P(None, "mp"),
        P("mp"),
        P(None, "mp"),
        P("mp"),
        P("mp", None),
        P("mp"),
    )
    return jax.shard_map(
        shards,
        mesh=mesh,
        in_specs=placed,
        out_specs=(
            P("mp", None, "seq"),
            P("mp", None, "seq"),
            P("mp"),
            P("mp"),
            P("mp", None),
            P("mp", None),
            P("mp", None),
            P("mp", None),
            P("mp"),
            P(None, None, "mp"),
            P(None, "mp"),
            P("mp"),
            P(None, "mp"),
            P("mp"),
            P("mp", None),
            P("mp"),
            P(),
            P(),
            P(),
        ),
        check_vma=False,
    )
```

time: 837 us -> 633 us (0.76)
  the two profiles are of different devices: /device:TPU:4 before, /device:TPU:0 now
where the time goes in v3:
time: 633 us; the launch traced here: 622 us
  Pallas kernels  254 us (40%)
  waiting for transfers between devices  115 us (18%)
  starting transfers between devices  78.5 us (12%)
  local copies, waits for them, and re-layouts  65.5 us (10%)
  other arithmetic  62.1 us (10%)
  blocking collectives  30.7 us (5%)
  between operations  16.6 us (3%)
    pallas_call x15, Pallas kernels, over_blocks(): pl.pallas_call(run, grid=(steps,), in_specs=[pl.BlockSpec(memory_space=pl...  254 us
    ppermute x42, waiting for transfers between devices, swap(): return lax.ppermute(values, axis, [(i, i ^ bit) for i in range(size)])  80.5 us
    ppermute x42, starting transfers between devices, swap(): return lax.ppermute(values, axis, [(i, i ^ bit) for i in range(size)])  41 us
    all_to_all x1, blocking collectives, shards(): lax.all_to_all(lifted_sent, 'mp', 0, 0, tiled=True).reshape(D, tokens)  30.7 us
    convert_element_type x15, other arithmetic, added(): return (a.astype(f32) + b.astype(f32)).astype(bf16)  29.1 us
    unnamed x166, local copies, waits for them, and re-layouts  23 us
    all_to_all x2, waiting for transfers between devices, handed(): terms = lax.all_to_all(ends, 'seq', 0, 0, tiled=True)  14.7 us
    all_to_all x3, starting transfers between devices, returned(): lax.all_to_all(values.reshape(mp, features, local), 'mp', 0, 0, tiled=True)  14 us
  transfers between devices with their start and end apart: 51, of which 17 were waited for; matrix products, arithmetic and copies ran while one was open for 17% of the time, Pallas kernels for 32%

profile of v3, /device:TPU:0, one launch (start us, length us, event | category | flops | bytes accessed | tf_op | source)
XLA Modules:
  0.0 622.4 jit_solution(9763383717744609027)
XLA Ops:
  7.2 3.5 copy.299
  10.7 4.5 all-to-all-start
  15.3 4.1 copy.232
  20.7 2.6 collective-permute-start
  25.6 2.0 collective-permute-start.3
  31.3 18.5 %shard_map.312 = (f32[256,8,128]{2,1,0:T(8,128)}, f32[256,2,128]{2,1,0:T(2,128)}, bf16[256,128,128]{2,1,0:T(8,128)(2,1)}, bf16[256,128,128]{2,1,0:T(8,128)(2,1)}, f32[256,128]{1,0:T(8,128)}) custom-call(f32[256,1]{1,0:T(8,128)} %copy.233.refs_0_, f32[256,32]{1,0:T(8,128)} %copy.234.refs_1_, f32[256,32]{1,0:T(8,128)} %copy.235.refs_2_, ...), custom_call_target="tpu_custom_call" | custom-call | flops 10000000000 | bytes 18351104 | tf_op jit(solution)/shard_map/pallas_call | solution.py:450
  49.9 1.9 copy.298
  54.6 16.3 %shard_map.313 = (bf16[256,32,128]{2,1,0:T(8,128)(2,1)}, f32[256,32,128]{2,1,0:T(8,128)}, bf16[256,4,128]{2,1,0:T(4,128)(2,1)}) custom-call(bf16[4,256,1024]{2,1,0:T(8,128)(2,1)} %bitcast.123.refs_7_.refs_0_.refs_9_, f32[32,128]{1,0:T(8,128)} %reshape.169.refs_1_.refs_10_, f32[256,128]{1,0:T(8,128)} %broadcast_in_dim.34.refs_2_.refs_11_.refs_7_, ...), custom_call_target="tpu_custom_call" | custom-call | flops 8000000000 | bytes 18235392 | tf_op jit(solution)/shard_map/pallas_call | solution.py:450
  71.0 6.6 %all-to-all-start.1 = ((bf16[256,4,128]{2,1,0:T(4,128)(2,1)}), bf16[256,4,128]{2,1,0:T(4,128)(2,1)S(1)}, u32[]{:S(2)}, u32[]{:S(2)}) async-start(bf16[256,4,128]{2,1,0:T(4,128)(2,1)} %get-tuple-element.92), calls=%async_computation.1 | async-start | bytes 524288 | tf_op jit(solution)/shard_map/all_to_all | solution.py:783
  81.0 9.7 %all-to-all-done.1.refs_0_ = bf16[256,4,128]{2,1,0:T(4,128)(2,1)S(1)} async-done(((bf16[256,4,128]{2,1,0:T(4,128)(2,1)}), bf16[256,4,128]{2,1,0:T(4,128)(2,1)S(1)}, u32[]{:S(2)}, u32[]{:S(2)}) %all-to-all-start.1) | async-done | bytes 262176 | tf_op jit(solution)/shard_map/all_to_all | solution.py:783
  91.3 2.2 shard_map.314
  93.5 5.5 all-to-all-start.2
  100.4 2.1 collective-permute-start.9
  102.6 2.7 collective-permute-done.6.refs_7_.refs_9_.refs_8_
  105.8 3.8 all-to-all-done.2.refs_2_
  110.4 18.7 %shard_map.315 = (bf16[256,32,128]{2,1,0:T(8,128)(2,1)}, f32[256,32,128]{2,1,0:T(8,128)}, bf16[4,256,1024]{2,1,0:T(8,128)(2,1)}) custom-call(bf16[256,32,128]{2,1,0:T(8,128)(2,1)} %get-tuple-element.90.refs_0_.refs_1_.refs_3_, f32[256,32,128]{2,1,0:T(8,128)} %get-tuple-element.91.refs_1_, bf16[256,4,128]{2,1,0:T(4,128)(2,1)} %copy-done.41, ...), custom_call_target="tpu_custom_call" | custom-call | flops 14000000000 | bytes 24641536 | tf_op jit(solution)/shard_map/pallas_call | solution.py:450
  129.2 30.7 %all_to_all.45 = bf16[4,256,1024]{2,1,0:T(8,128)(2,1)} all-to-all(bf16[4,256,1024]{2,1,0:T(8,128)(2,1)} %get-tuple-element.97), channel_id=1, replica_groups=mesh['seq'=8,'mp'=4] {'mp'}, dimensions={0} | all-to-all | bytes 4194304 | tf_op jit(solution)/shard_map/all_to_all | solution.py:876
  163.7 12.9 %shard_map.316 = (bf16[1024,1024]{1,0:T(8,128)(2,1)}, f32[1024,1024]{1,0:T(8,128)}, bf16[1024,1024]{1,0:T(8,128)(2,1)}, f32[1024,1024]{1,0:T(8,128)}, f32[1024,1024]{1,0:T(8,128)}, /*index=5*/f32[8,1024]{1,0:T(8,128)}) custom-call(s32[4]{0:T(128)} %pad_add_fusion.refs_0_, f32[1,1024]{1,0:T(1,128)} %fusion.17.refs_1_, bf16[1024,1024]{1,0:T(8,128)(2,1)} %bitcast.139, ...), custom_call_target="tpu_custom_call" | custom-call | flops 12000000000 | bytes 28872720 | tf_op jit(solution)/shard_map/pallas_call | solution.py:450
  177.9 36.3 %shard_map.317 = (f32[1024,1024]{1,0:T(8,128)}, f32[1024,1024]{1,0:T(8,128)}, bf16[2048,1024]{1,0:T(8,128)(2,1)}, bf16[2,1024,1024]{2,1,0:T(8,128)(2,1)}, f32[2048,128]{1,0:T(8,128)}) custom-call(bf16[1024,1024]{1,0:T(8,128)(2,1)} %get-tuple-element.98.refs_0_, bf16[1024,1024]{1,0:T(8,128)(2,1)} %get-tuple-element.99.refs_1_.refs_5_, ...), custom_call_target="tpu_custom_call" | custom-call | flops 38000001024 | bytes 35651584 | tf_op jit(solution)/shard_map/pallas_call | solution.py:450
  217.9 38.9 %shard_map.318 = (f32[1024,1024]{1,0:T(8,128)}, f32[1024,1024]{1,0:T(8,128)}, bf16[2048,1024]{1,0:T(8,128)(2,1)}, bf16[2,1024,1024]{2,1,0:T(8,128)(2,1)}, f32[2048,128]{1,0:T(8,128)}) custom-call(bf16[1024,1024]{1,0:T(8,128)(2,1)} %get-tuple-element.98.refs_0_, bf16[1024,1024]{1,0:T(8,128)(2,1)} %get-tuple-element.99.refs_1_.refs_5_, ...), custom_call_target="tpu_custom_call" | custom-call | flops 38000001024 | bytes 44040192 | tf_op jit(solution)/shard_map/pallas_call | solution.py:450
  258.4 5.6 add_convert_fusion
  268.4 4.3 add_convert_fusion.1
  272.7 1.7 constant_dynamic-slice_fusion.6.refs_12_
  276.8 15.2 %shard_map.319 = (bf16[1024,1024]{1,0:T(8,128)(2,1)}, bf16[1024,1024]{1,0:T(8,128)(2,1)}, bf16[2048,1024]{1,0:T(8,128)(2,1)}, f32[4,4,256,128]{3,2,1,0:T(8,128)}) custom-call(s32[4]{0:T(128)} %pad_add_fusion.refs_0_, f32[1024,1024]{1,0:T(8,128)} %get-tuple-element.104.refs_1_, f32[1024,1024]{1,0:T(8,128)} %get-tuple-element.105.refs_2_.refs_3_, ...), custom_call_target="tpu_custom_call" | custom-call | flops 14000000000 | bytes 34111504 | tf_op jit(solution)/shard_map/pallas_call | solution.py:450
  293.1 12.4 %shard_map.320 = (bf16[2,1024,512]{2,1,0:T(8,128)(2,1)}, bf16[2,1024,512]{2,1,0:T(8,128)(2,1)}, bf16[1024,1024]{1,0:T(8,128)(2,1)}, f32[8,1024]{1,0:T(8,128)}) custom-call(s32[4]{0:T(128)} %pad_add_fusion.refs_0_, bf16[2048,1024]{1,0:T(8,128)(2,1)} %get-tuple-element.115.refs_1_, bf16[1024,1024]{1,0:T(8,128)(2,1)} %bitcast.140, ...), custom_call_target="tpu_custom_call" | custom-call | flops 10000000000 | bytes 21528592 | tf_op jit(solution)/shard_map/pallas_call | solution.py:450
  305.7 4.7 all-to-all-start.4
  310.4 2.2 reduce_sum.118
  314.1 2.7 pad_maximum_fusion.10
  317.4 3.4 add_convert_fusion.3
  323.6 2.6 add_convert_fusion.4
  330.3 5.9 all-to-all-done.4.refs_0_
  336.1 16.9 %shard_map.321 = (bf16[256,32,128]{2,1,0:T(8,128)(2,1)}, f32[256,32,128]{2,1,0:T(8,128)}, bf16[256,4,128]{2,1,0:T(4,128)(2,1)}) custom-call(bf16[4,256,1024]{2,1,0:T(8,128)(2,1)} %all-to-all-done.4.refs_0_, bf16[256,32,128]{2,1,0:T(8,128)(2,1)} %get-tuple-element.114.refs_1_, bf16[256,128,128]{2,1,0:T(8,128)(2,1)} %get-tuple-element.94.refs_3_.refs_2_.refs_4_, ...), custom_call_target="tpu_custom_call" | custom-call | flops 10000000000 | bytes 20185088 | tf_op jit(solution)/shard_map/pallas_call | solution.py:450
  353.0 3.4 all-to-all-start.5
  356.5 2.8 add_convert_fusion.2
  360.4 5.0 all-to-all-done.5.refs_0_
  366.1 2.2 shard_map.322
  368.3 3.6 all-to-all-start.6
  372.6 2.0 collective-permute-start.22
  374.6 5.9 all-to-all-done.6.refs_7_.refs_2_
  381.3 4.4 all-to-all-start.7
  385.7 2.1 add_convert_fusion.6
  388.7 2.0 collective-permute-start.21
  394.2 23.0 %shard_map.323.refs_15_ = f32[256,8,128]{2,1,0:T(8,128)} custom-call(bf16[256,32,128]{2,1,0:T(8,128)(2,1)} %get-tuple-element.118.refs_0_, bf16[256,32,128]{2,1,0:T(8,128)(2,1)} %get-tuple-element.90.refs_0_.refs_1_.refs_3_, f32[256,32,128]{2,1,0:T(8,128)} %get-tuple-element.122.refs_2_.refs_4_, f32[256,32,128]{2,1,0:T(8,128)} %get-tuple-element.119.refs_3_.refs_1_, ...), custom_call_target="tpu_custom_call" | custom-call | flops 20000000000 | bytes 22020096 | tf_op jit(solution)/shard_map/pallas_call | solution.py:450
  417.3 5.1 fusion.26
  422.4 2.8 slice_reduce_fusion
  432.2 1.9 collective-permute-start.24
  434.1 2.0 collective-permute-start.23
  436.1 13.8 %shard_map.324 = (bf16[4,128,1024]{2,1,0:T(8,128)(2,1)}, f32[128,8,128]{2,1,0:T(8,128)}, f32[32,128]{1,0:T(8,128)}, f32[128,128]{1,0:T(8,128)}) custom-call(bf16[256,32,128]{2,1,0:T(8,128)(2,1)} %get-tuple-element.118.refs_0_, f32[256,32,128]{2,1,0:T(8,128)} %get-tuple-element.119.refs_3_.refs_1_, bf16[256,4,128]{2,1,0:T(4,128)(2,1)} %copy-done.40, ...), custom_call_target="tpu_custom_call" | custom-call | flops 12000000000 | bytes 26443776 | tf_op jit(solution)/shard_map/pallas_call | solution.py:450
  451.1 4.8 all-to-all-start.8
  460.8 2.0 collective-permute-start.32
  464.3 4.5 collective-permute-done.33
  468.9 8.9 %collective-permute-done.32 = bf16[1,1,1,1,128,1024]{5,4,3,2,1,0:T(8,128)(2,1)S(1)} collective-permute-done((bf16[1,1,1,1,128,1024]{5,4,3,2,1,0:T(8,128)(2,1)S(1)}, bf16[1,1,1,1,128,1024]{5,4,3,2,1,0:T(8,128)(2,1)S(1)}, u32[]{:S(2)}, u32[]{:S(2)}) %collective-permute-start.32) | collective-permute-done | bytes 262176 | tf_op jit(solution)/shard_map/ppermute | solution.py:649
  477.9 3.8 all-to-all-done.8.refs_16_.refs_4_
  481.7 13.9 %shard_map.325 = (bf16[4,128,1024]{2,1,0:T(8,128)(2,1)}, f32[128,8,128]{2,1,0:T(8,128)}, f32[32,128]{1,0:T(8,128)}, f32[128,128]{1,0:T(8,128)}) custom-call(bf16[256,32,128]{2,1,0:T(8,128)(2,1)} %get-tuple-element.118.refs_0_, f32[256,32,128]{2,1,0:T(8,128)} %get-tuple-element.119.refs_3_.refs_1_, bf16[256,4,128]{2,1,0:T(4,128)(2,1)} %copy-done.40, ...), custom_call_target="tpu_custom_call" | custom-call | flops 12000000000 | bytes 26443776 | tf_op jit(solution)/shard_map/pallas_call | solution.py:450
  503.2 2.7 collective-permute-start.36
  506.3 1.7 collective-permute-start.30
  508.7 31.6 %collective-permute-done.30 = f32[293,128]{1,0:T(8,128)S(1)} collective-permute-done((f32[293,128]{1,0:T(8,128)S(1)}, f32[293,128]{1,0:T(8,128)S(1)}, u32[]{:S(2)}, u32[]{:S(2)}) %collective-permute-start.30) | collective-permute-done | bytes 150048 | tf_op jit(solution)/shard_map/ppermute | solution.py:649
  540.3 3.2 collective-permute-start.31
  543.6 13.0 %shard_map.326 = (f32[256,4,1024]{2,1,0:T(4,128)}, bf16[256,4,1024]{2,1,0:T(4,128)(2,1)}) custom-call(bf16[4,256,1024]{2,1,0:T(8,128)(2,1)} %bitcast.123.refs_7_.refs_0_.refs_9_, bf16[4,128,1024]{2,1,0:T(8,128)(2,1)} %get-tuple-element.128.refs_1_, bf16[4,128,1024]{2,1,0:T(8,128)(2,1)} %get-tuple-element.135.refs_2_, ...), custom_call_target="tpu_custom_call" | custom-call | flops 8000000000 | bytes 14843904 | tf_op jit(solution)/shard_map/pallas_call | solution.py:450
  575.5 11.6 %collective-permute-done.38 = bf16[1,2,2,1,128,512]{5,4,3,2,1,0:T(8,128)(2,1)S(1)} collective-permute-done((bf16[1,2,2,1,128,512]{5,4,3,2,1,0:T(8,128)(2,1)S(1)}, bf16[1,2,2,1,128,512]{5,4,3,2,1,0:T(8,128)(2,1)S(1)}, u32[]{:S(2)}, u32[]{:S(2)}) %collective-permute-start.38) | collective-permute-done | bytes 524320 | tf_op jit(solution)/shard_map/ppermute | solution.py:649
  587.4 2.4 reshape.188
  589.7 4.9 collective-permute-done.40
  596.2 12.2 %collective-permute-done.41 = bf16[1,2,2,1,128,1024]{5,4,3,2,1,0:T(8,128)(2,1)} collective-permute-done((bf16[1,2,2,1,128,1024]{5,4,3,2,1,0:T(8,128)(2,1)}, bf16[1,2,2,1,128,1024]{5,4,3,2,1,0:T(8,128)(2,1)}, u32[]{:S(2)}, u32[]{:S(2)}) %collective-permute-start.41) | collective-permute-done | bytes 1048608 | tf_op jit(solution)/shard_map/ppermute | solution.py:649
  610.4 4.7 bitcast_convert_fusion
  (349 shorter events, 96.6 us)
Async XLA Ops:
  10.7 43.0 %all-to-all-start = ((bf16[4,256,1024]{2,1,0:T(8,128)(2,1)}), bf16[4,256,1024]{2,1,0:T(8,128)(2,1)}, u32[]{:S(2)}, u32[]{:S(2)}) async-start(bf16[4,256,1024]{2,1,0:T(8,128)(2,1)} %bitcast.123.refs_7_.refs_0_.refs_9_), calls=%async_computation | async-start | bytes 4194304 | tf_op jit(solution)/shard_map/all_to_all | solution.py:757
  15.2 144.8 %all-gather.3.cloned.1.call-start = ((), (), s32[]{:S(2)}) async-start(), calls=%async_computation.9 | async-start | bytes 4718592 | tf_op jit(solution)/shard_map/all_gather | solution.py:847
  19.4 34.4 %collective-permute-start.4 = (bf16[1024,1024]{1,0:T(8,128)(2,1)}, bf16[1024,1024]{1,0:T(8,128)(2,1)}, u32[]{:S(2)}, u32[]{:S(2)}) collective-permute-start(bf16[1024,1024]{1,0:T(8,128)(2,1)} %bitcast.136), channel_id=1, source_target_pairs={{0,1},{1,0},{2,3},{3,2},{4,5},{5,4},{6,7},{7,6},{8,9},{9,8},{10,11... | collective-permute-start | bytes 6291464 | tf_op jit(solution)/shard_map/ppermute | solution.py:649
  20.7 31.1 %collective-permute-start = (f32[6144]{0:T(1024)S(1)}, f32[6144]{0:T(1024)S(1)}, u32[]{:S(2)}, u32[]{:S(2)}) collective-permute-start(f32[6144]{0:T(1024)S(1)} %constant_dynamic-update-slice_fusion.refs_5_), channel_id=1, source_target_pairs={{0,2},{1,3},{2,0},{3,1},{4,6},{5,7},{6,4},{7,5},{8,10},{9,11},{10,... | collective-permute-start | bytes 73736 | tf_op jit(solution)/shard_map/ppermute | solution.py:649
  23.3 28.5 %collective-permute-start.1 = (f32[6144]{0:T(1024)S(1)}, f32[6144]{0:T(1024)S(1)}, u32[]{:S(2)}, u32[]{:S(2)}) collective-permute-start(f32[6144]{0:T(1024)S(1)} %constant_dynamic-update-slice_fusion.refs_5_), channel_id=1, source_target_pairs={{0,1},{1,0},{2,3},{3,2},{4,5},{5,4},{6,7},{7,6},{8,9},{9,8},{10,11... | collective-permute-start | bytes 73736 | tf_op jit(solution)/shard_map/ppermute | solution.py:649
  23.5 28.4 %collective-permute-start.2 = (f32[6144]{0:T(1024)S(1)}, f32[6144]{0:T(1024)S(1)}, u32[]{:S(2)}, u32[]{:S(2)}) collective-permute-start(f32[6144]{0:T(1024)S(1)} %constant_dynamic-update-slice_fusion.refs_5_), channel_id=1, source_target_pairs={{0,3},{1,2},{2,1},{3,0},{4,7},{5,6},{6,5},{7,4},{8,11},{9,10},{10,... | collective-permute-start | bytes 73736 | tf_op jit(solution)/shard_map/ppermute | solution.py:649
  25.6 28.2 %collective-permute-start.3 = (bf16[2,128,1024]{2,1,0:T(8,128)(2,1)S(1)}, bf16[2,128,1024]{2,1,0:T(8,128)(2,1)S(1)}, u32[]{:S(2)}, u32[]{:S(2)}) collective-permute-start(bf16[2,128,1024]{2,1,0:T(8,128)(2,1)S(1)} %pad_maximum_fusion.4.refs_6_), channel_id=1, source_target_pairs={{0,2},{1,3},{2,0},{3,1},{4,6},{5,7},{6,4},{7,5},{8,10},{9,11},{10,... | collective-permute-start | bytes 1572872 | tf_op jit(solution)/shard_map/ppermute | solution.py:649
  31.3 18.5 %copy-start.20 = (bf16[256,4,1024]{2,1,0:T(4,128)(2,1)S(1)}, bf16[256,4,1024]{2,1,0:T(4,128)(2,1)}, u32[]{:S(2)}) copy-start(bf16[256,4,1024]{2,1,0:T(4,128)(2,1)} %param.19) | copy-start | bytes 6291460
  54.6 23.0 %copy-start.28 = (bf16[1024,2,256]{2,1,0:T(2,128)(2,1)S(1)}, bf16[1024,2,256]{2,1,0:T(2,128)(2,1)}, u32[]{:S(2)}) copy-start(bf16[1024,2,256]{2,1,0:T(2,128)(2,1)} %param.27) | copy-start | bytes 3145732
  70.9 10.0 %collective-permute-start.5 = (bf16[1024,1024]{1,0:T(8,128)(2,1)}, bf16[1024,1024]{1,0:T(8,128)(2,1)}, u32[]{:S(2)}, u32[]{:S(2)}) collective-permute-start(bf16[1024,1024]{1,0:T(8,128)(2,1)} %refs_4_.2), channel_id=1, source_target_pairs={{0,1},{1,0},{2,3},{3,2},{4,5},{5,4},{6,7},{7,6},{8,9},{9,8},{10,11... | collective-permute-start | bytes 6291464 | tf_op jit(solution)/shard_map/ppermute | solution.py:649
  71.0 19.6 %all-to-all-start.1 = ((bf16[256,4,128]{2,1,0:T(4,128)(2,1)}), bf16[256,4,128]{2,1,0:T(4,128)(2,1)S(1)}, u32[]{:S(2)}, u32[]{:S(2)}) async-start(bf16[256,4,128]{2,1,0:T(4,128)(2,1)} %get-tuple-element.92), calls=%async_computation.1 | async-start | bytes 524288 | tf_op jit(solution)/shard_map/all_to_all | solution.py:783
  79.1 26.2 %copy-start.29 = (bf16[2,256,1024]{2,1,0:T(8,128)(2,1)}, bf16[2,256,1024]{2,1,0:T(8,128)(2,1)S(1)}, u32[]{:S(2)}) copy-start(bf16[2,256,1024]{2,1,0:T(8,128)(2,1)S(1)} %copy.240) | copy-start | bytes 3145732
  79.1 26.2 %collective-permute-start.6 = (bf16[512,1024]{1,0:T(8,128)(2,1)S(1)}, bf16[512,1024]{1,0:T(8,128)(2,1)}, u32[]{:S(2)}, u32[]{:S(2)}) collective-permute-start(bf16[512,1024]{1,0:T(8,128)(2,1)S(1)} %bitcast.149), channel_id=1, source_target_pairs={{0,2},{1,3},{2,0},{3,1},{4,6},{5,7},{6,4},{7,5},{8,10},{9,11},{10,... | collective-permute-start | bytes 3145736 | tf_op jit(solution)/shard_map/ppermute | solution.py:649
  81.0 18.1 %copy-start.7 = (bf16[256,4,1024]{2,0,1:T(8,128)(2,1)S(1)}, bf16[256,4,1024]{2,0,1:T(8,128)(2,1)}, u32[]{:S(2)}) copy-start(bf16[256,4,1024]{2,0,1:T(8,128)(2,1)} %copy.298) | copy-start | bytes 6291460
  93.5 16.1 %all-to-all-start.2 = ((bf16[256,4,128]{2,1,0:T(4,128)(2,1)}), bf16[256,4,128]{2,1,0:T(4,128)(2,1)S(1)}, u32[]{:S(2)}, u32[]{:S(2)}) async-start(bf16[256,4,128]{2,1,0:T(4,128)(2,1)} %shard_map.314), calls=%async_computation.2 | async-start | bytes 524288 | tf_op jit(solution)/shard_map/all_to_all | solution.py:793
  100.4 28.7 %collective-permute-start.7 = (bf16[256,1024]{1,0:T(8,128)(2,1)}, bf16[256,1024]{1,0:T(8,128)(2,1)S(1)}, u32[]{:S(2)}, u32[]{:S(2)}) collective-permute-start(bf16[256,1024]{1,0:T(8,128)(2,1)} %get-tuple-element.276), channel_id=1, source_target_pairs={{0,2},{1,3},{2,0},{3,1},{4,6},{5,7},{6,4},{7,5},{8,10},{9,11},{10,... | collective-permute-start | bytes 1572872 | tf_op jit(solution)/shard_map/ppermute | solution.py:649
  100.4 28.7 %collective-permute-start.8 = (bf16[256,1024]{1,0:T(8,128)(2,1)}, bf16[256,1024]{1,0:T(8,128)(2,1)}, u32[]{:S(2)}, u32[]{:S(2)}) collective-permute-start(bf16[256,1024]{1,0:T(8,128)(2,1)} %get-tuple-element.275), channel_id=1, source_target_pairs={{0,1},{1,0},{2,3},{3,2},{4,5},{5,4},{6,7},{7,6},{8,9},{9,8},{10,11... | collective-permute-start | bytes 1572872 | tf_op jit(solution)/shard_map/ppermute | solution.py:649
  100.4 28.7 %collective-permute-start.9 = (bf16[256,1024]{1,0:T(8,128)(2,1)}, bf16[256,1024]{1,0:T(8,128)(2,1)}, u32[]{:S(2)}, u32[]{:S(2)}) collective-permute-start(bf16[256,1024]{1,0:T(8,128)(2,1)} %get-tuple-element.274), channel_id=1, source_target_pairs={{0,3},{1,2},{2,1},{3,0},{4,7},{5,6},{6,5},{7,4},{8,11},{9,10},{10,... | collective-permute-start | bytes 1572872 | tf_op jit(solution)/shard_map/ppermute | solution.py:649
  105.3 23.9 %collective-permute-start.11 = (bf16[512,1024]{1,0:T(8,128)(2,1)}, bf16[512,1024]{1,0:T(8,128)(2,1)S(1)}, u32[]{:S(2)}, u32[]{:S(2)}) collective-permute-start(bf16[512,1024]{1,0:T(8,128)(2,1)} %collective-permute-done.6.refs_7_.refs_9_.refs_8_), channel_id=1, source_target_pairs={{0,1},{1,0},{2,3},{3,2},{4,5},{5,4},{6,7},{7,6},{8,9},{9,8},{10,11... | collective-permute-start | bytes 3145736 | tf_op jit(solution)/shard_map/ppermute | solution.py:649
  105.3 23.9 %collective-permute-start.10 = (bf16[512,1024]{1,0:T(8,128)(2,1)S(1)}, bf16[512,1024]{1,0:T(8,128)(2,1)}, u32[]{:S(2)}, u32[]{:S(2)}) collective-permute-start(bf16[512,1024]{1,0:T(8,128)(2,1)S(1)} %bitcast.150), channel_id=1, source_target_pairs={{0,1},{1,0},{2,3},{3,2},{4,5},{5,4},{6,7},{7,6},{8,9},{9,8},{10,11... | collective-permute-start | bytes 3145736 | tf_op jit(solution)/shard_map/ppermute | solution.py:649
  129.1 30.8 %copy-start.71 = (bf16[256,1024]{1,0:T(8,128)(2,1)}, bf16[256,1024]{1,0:T(8,128)(2,1)S(1)}, u32[]{:S(2)}) copy-start(bf16[256,1024]{1,0:T(8,128)(2,1)S(1)} %collective-permute-done.7.refs_5_) | copy-start | bytes 1572868
  129.2 30.8 %copy-start.70 = (bf16[512,1024]{1,0:T(8,128)(2,1)}, bf16[512,1024]{1,0:T(8,128)(2,1)S(1)}, u32[]{:S(2)}) copy-start(bf16[512,1024]{1,0:T(8,128)(2,1)S(1)} %collective-permute-done.11.refs_11_.refs_10_) | copy-start | bytes 3145732
  129.2 31.4 %copy-start.64 = (s32[4,1024]{1,0:T(4,128)S(1)}, s32[4,1024]{1,0:T(4,128)}, u32[]{:S(2)}) copy-start(s32[4,1024]{1,0:T(4,128)} %param.18) | copy-start | bytes 49156
  160.0 16.6 %collective-permute-start.12 = (bf16[8,2,128,1024]{3,2,1,0:T(8,128)(2,1)}, bf16[8,2,128,1024]{3,2,1,0:T(8,128)(2,1)}, u32[]{:S(2)}, u32[]{:S(2)}) collective-permute-start(bf16[8,2,128,1024]{3,2,1,0:T(8,128)(2,1)} %bitcast.179), channel_id=1, source_target_pairs={{0,1},{1,0},{2,3},{3,2},{4,5},{5,4},{6,7},{7,6},{8,9},{9,8},{10,11... | collective-permute-start | bytes 12582920 | tf_op jit(solution)/shard_map/ppermute | solution.py:649
  214.2 44.2 %collective-permute-start.14 = (bf16[2,1024,1024]{2,1,0:T(8,128)(2,1)}, bf16[2,1024,1024]{2,1,0:T(8,128)(2,1)}, u32[]{:S(2)}, u32[]{:S(2)}) collective-permute-start(bf16[2,1024,1024]{2,1,0:T(8,128)(2,1)} %get-tuple-element.112), channel_id=1, source_target_pairs={{0,1},{1,0},{2,3},{3,2},{4,5},{5,4},{6,7},{7,6},{8,9},{9,8},{10,11... | collective-permute-start | bytes 12582920 | tf_op jit(solution)/shard_map/ppermute | solution.py:649
  214.8 53.5 %collective-permute-start.13 = (bf16[2048,1024]{1,0:T(8,128)(2,1)}, bf16[2048,1024]{1,0:T(8,128)(2,1)}, u32[]{:S(2)}, u32[]{:S(2)}) collective-permute-start(bf16[2048,1024]{1,0:T(8,128)(2,1)} %get-tuple-element.110), channel_id=1, source_target_pairs={{0,1},{1,0},{2,3},{3,2},{4,5},{5,4},{6,7},{7,6},{8,9},{9,8},{10,11... | collective-permute-start | bytes 12582920 | tf_op jit(solution)/shard_map/ppermute | solution.py:649
  267.1 50.2 %collective-permute-start.16 = (bf16[2,2,1,2,128,1024]{5,4,3,2,1,0:T(8,128)(2,1)}, bf16[2,2,1,2,128,1024]{5,4,3,2,1,0:T(8,128)(2,1)S(1)}, u32[]{:S(2)}, u32[]{:S(2)}) collective-permute-start(bf16[2,2,1,2,128,1024]{5,4,3,2,1,0:T(8,128)(2,1)} %constant_dynamic-slice_fusion.5.refs_13_), channel_id=1, source_target_pairs={{0,8},{4,12},{8,0},{12,4},{16,24},{20,28},{24,16},{28,20},{1,9},{5... | collective-permute-start | bytes 6291464 | tf_op jit(solution)/shard_map/ppermute | solution.py:649
  275.3 48.3 %collective-permute-start.15 = (bf16[2,2,2,1,128,1024]{5,4,3,2,1,0:T(8,128)(2,1)}, bf16[2,2,2,1,128,1024]{5,4,3,2,1,0:T(8,128)(2,1)}, u32[]{:S(2)}, u32[]{:S(2)}) collective-permute-start(bf16[2,2,2,1,128,1024]{5,4,3,2,1,0:T(8,128)(2,1)} %constant_dynamic-slice_fusion.6.refs_12_), channel_id=1, source_target_pairs={{0,4},{4,0},{8,12},{12,8},{16,20},{20,16},{24,28},{28,24},{1,5},{5... | collective-permute-start | bytes 6291464 | tf_op jit(solution)/shard_map/ppermute | solution.py:649
  305.5 30.6 %collective-permute-start.17 = (bf16[2,1024,512]{2,1,0:T(8,128)(2,1)}, bf16[2,1024,512]{2,1,0:T(8,128)(2,1)}, u32[]{:S(2)}, u32[]{:S(2)}) collective-permute-start(bf16[2,1024,512]{2,1,0:T(8,128)(2,1)} %get-tuple-element.117), channel_id=1, source_target_pairs={{0,1},{1,0},{2,3},{3,2},{4,5},{5,4},{6,7},{7,6},{8,9},{9,8},{10,11... | collective-permute-start | bytes 6291464 | tf_op jit(solution)/shard_map/ppermute | solution.py:649
  305.7 30.4 %all-to-all-start.4 = ((bf16[4,256,1024]{2,1,0:T(8,128)(2,1)}), bf16[4,256,1024]{2,1,0:T(8,128)(2,1)}, u32[]{:S(2)}, u32[]{:S(2)}) async-start(bf16[4,256,1024]{2,1,0:T(8,128)(2,1)} %bitcast.142), calls=%async_computation.4 | async-start | bytes 4194304 | tf_op jit(solution)/shard_map/all_to_all | solution.py:730
  316.9 55.0 %collective-permute-start.28 = (f32[2,2052]{1,0:T(2,128)S(1)}, f32[2,2052]{1,0:T(2,128)S(1)}, u32[]{:S(2)}, u32[]{:S(2)}) collective-permute-start(f32[2,2052]{1,0:T(2,128)S(1)} %pad_maximum_fusion.9), channel_id=1, source_target_pairs={{0,1},{1,0},{2,3},{3,2},{4,5},{5,4},{6,7},{7,6},{8,9},{9,8},{10,11... | collective-permute-start | bytes 49256 | tf_op jit(solution)/shard_map/ppermute | solution.py:649
  320.8 64.9 %collective-permute-start.20 = (bf16[2,2,1,1,128,1024]{5,4,3,2,1,0:T(8,128)(2,1)S(1)}, bf16[2,2,1,1,128,1024]{5,4,3,2,1,0:T(8,128)(2,1)}, u32[]{:S(2)}, u32[]{:S(2)}) collective-permute-start(bf16[2,2,1,1,128,1024]{5,4,3,2,1,0:T(8,128)(2,1)S(1)} %constant_dynamic-slice_fusion.3.refs_3_), channel_id=1, source_target_pairs={{0,4},{4,0},{8,12},{12,8},{16,20},{20,16},{24,28},{28,24},{1,5},{5... | collective-permute-start | bytes 3145736 | tf_op jit(solution)/shard_map/ppermute | solution.py:649
  328.6 62.1 %collective-permute-start.18 = (bf16[2,2,1,1,128,1024]{5,4,3,2,1,0:T(8,128)(2,1)}, bf16[2,2,1,1,128,1024]{5,4,3,2,1,0:T(8,128)(2,1)}, u32[]{:S(2)}, u32[]{:S(2)}) collective-permute-start(bf16[2,2,1,1,128,1024]{5,4,3,2,1,0:T(8,128)(2,1)} %constant_dynamic-slice_fusion.4.refs_2_), channel_id=1, source_target_pairs={{0,8},{4,12},{8,0},{12,4},{16,24},{20,28},{24,16},{28,20},{1,9},{5... | collective-permute-start | bytes 3145736 | tf_op jit(solution)/shard_map/ppermute | solution.py:649
  353.0 12.3 %all-to-all-start.5 = ((bf16[256,4,128]{2,1,0:T(4,128)(2,1)}), bf16[256,4,128]{2,1,0:T(4,128)(2,1)S(1)}, u32[]{:S(2)}, u32[]{:S(2)}) async-start(bf16[256,4,128]{2,1,0:T(4,128)(2,1)} %get-tuple-element.120), calls=%async_computation.5 | async-start | bytes 524288 | tf_op jit(solution)/shard_map/all_to_all | solution.py:783
  368.3 12.3 %all-to-all-start.6 = ((bf16[256,4,128]{2,1,0:T(4,128)(2,1)}), bf16[256,4,128]{2,1,0:T(4,128)(2,1)S(1)}, u32[]{:S(2)}, u32[]{:S(2)}) async-start(bf16[256,4,128]{2,1,0:T(4,128)(2,1)} %shard_map.322), calls=%async_computation.6 | async-start | bytes 524288 | tf_op jit(solution)/shard_map/all_to_all | solution.py:793
  372.6 54.7 %collective-permute-start.22 = (bf16[2,2,2,1,128,512]{5,4,3,2,1,0:T(8,128)(2,1)}, bf16[2,2,2,1,128,512]{5,4,3,2,1,0:T(8,128)(2,1)}, u32[]{:S(2)}, u32[]{:S(2)}) collective-permute-start(bf16[2,2,2,1,128,512]{5,4,3,2,1,0:T(8,128)(2,1)} %constant_dynamic-slice_fusion.2.refs_4_), channel_id=1, source_target_pairs={{0,4},{4,0},{8,12},{12,8},{16,20},{20,16},{24,28},{28,24},{1,5},{5... | collective-permute-start | bytes 3145736 | tf_op jit(solution)/shard_map/ppermute | solution.py:649
  381.3 54.8 %all-to-all-start.7 = ((bf16[4,256,1024]{2,1,0:T(8,128)(2,1)}), bf16[4,256,1024]{2,1,0:T(8,128)(2,1)}, u32[]{:S(2)}, u32[]{:S(2)}) async-start(bf16[4,256,1024]{2,1,0:T(8,128)(2,1)} %bitcast.141), calls=%async_computation.7 | async-start | bytes 4194304 | tf_op jit(solution)/shard_map/all_to_all | solution.py:730
  388.7 38.6 %collective-permute-start.21 = (bf16[1,2,1,1,128,1024]{5,4,3,2,1,0:T(8,128)(2,1)}, bf16[1,2,1,1,128,1024]{5,4,3,2,1,0:T(8,128)(2,1)S(1)}, u32[]{:S(2)}, u32[]{:S(2)}) collective-permute-start(bf16[1,2,1,1,128,1024]{5,4,3,2,1,0:T(8,128)(2,1)} %slice.401.refs_6_), channel_id=1, source_target_pairs={{0,2},{1,3},{2,0},{3,1},{4,6},{5,7},{6,4},{7,5},{8,10},{9,11},{10,... | collective-permute-start | bytes 1572872 | tf_op jit(solution)/shard_map/ppermute | solution.py:649
  393.2 34.1 %collective-permute-start.19 = (bf16[2,1,1,1,128,1024]{5,4,3,2,1,0:T(8,128)(2,1)}, bf16[2,1,1,1,128,1024]{5,4,3,2,1,0:T(8,128)(2,1)}, u32[]{:S(2)}, u32[]{:S(2)}) collective-permute-start(bf16[2,1,1,1,128,1024]{5,4,3,2,1,0:T(8,128)(2,1)} %constant_dynamic-slice_fusion.1.refs_5_), channel_id=1, source_target_pairs={{0,16},{4,20},{8,24},{12,28},{16,0},{20,4},{24,8},{28,12},{1,17},{... | collective-permute-start | bytes 1572872 | tf_op jit(solution)/shard_map/ppermute | solution.py:649
  394.2 30.9 %copy-start.8 = (f32[256,32]{1,0:T(8,128)S(1)}, f32[256,32]{1,0:T(8,128)}, u32[]{:S(2)}) copy-start(f32[256,32]{1,0:T(8,128)} %copy.234.refs_1_) | copy-start | bytes 98308
  394.2 30.9 %copy-start.9 = (f32[256,32]{1,0:T(8,128)S(1)}, f32[256,32]{1,0:T(8,128)}, u32[]{:S(2)}) copy-start(f32[256,32]{1,0:T(8,128)} %copy.235.refs_2_) | copy-start | bytes 98308
  394.2 30.9 %copy-start.54 = (f32[256]{0:T(256)S(1)}, f32[256]{0:T(256)}, u32[]{:S(2)}) copy-start(f32[256]{0:T(256)} %param.21) | copy-start | bytes 3076
  431.1 18.9 %copy-start.18 = (bf16[2,1,1,1,128,1024]{5,4,3,2,1,0:T(8,128)(2,1)}, bf16[2,1,1,1,128,1024]{5,4,3,2,1,0:T(8,128)(2,1)S(1)}, u32[]{:S(2)}) copy-start(bf16[2,1,1,1,128,1024]{5,4,3,2,1,0:T(8,128)(2,1)S(1)} %add_convert_fusion.12) | copy-start | bytes 1572868
  431.8 24.1 %collective-permute-start.25 = (bf16[1,2,2,1,128,512]{5,4,3,2,1,0:T(8,128)(2,1)}, bf16[1,2,2,1,128,512]{5,4,3,2,1,0:T(8,128)(2,1)S(1)}, u32[]{:S(2)}, u32[]{:S(2)}) collective-permute-start(bf16[1,2,2,1,128,512]{5,4,3,2,1,0:T(8,128)(2,1)} %slice.404.refs_14_), channel_id=1, source_target_pairs={{0,2},{1,3},{2,0},{3,1},{4,6},{5,7},{6,4},{7,5},{8,10},{9,11},{10,... | collective-permute-start | bytes 1572872 | tf_op jit(solution)/shard_map/ppermute | solution.py:649
  432.2 23.8 %collective-permute-start.24 = (bf16[1,1,1,1,128,1024]{5,4,3,2,1,0:T(8,128)(2,1)S(1)}, bf16[1,1,1,1,128,1024]{5,4,3,2,1,0:T(8,128)(2,1)}, u32[]{:S(2)}, u32[]{:S(2)}) collective-permute-start(bf16[1,1,1,1,128,1024]{5,4,3,2,1,0:T(8,128)(2,1)S(1)} %constant_dynamic-slice_fusion.refs_13_), channel_id=1, source_target_pairs={{0,16},{4,20},{8,24},{12,28},{16,0},{20,4},{24,8},{28,12},{1,17},{... | collective-permute-start | bytes 786440 | tf_op jit(solution)/shard_map/ppermute | solution.py:649
  434.1 21.9 %collective-permute-start.23 = (bf16[1,1,1,1,128,1024]{5,4,3,2,1,0:T(8,128)(2,1)}, bf16[1,1,1,1,128,1024]{5,4,3,2,1,0:T(8,128)(2,1)S(1)}, u32[]{:S(2)}, u32[]{:S(2)}) collective-permute-start(bf16[1,1,1,1,128,1024]{5,4,3,2,1,0:T(8,128)(2,1)} %slice.402.refs_12_), channel_id=1, source_target_pairs={{0,2},{1,3},{2,0},{3,1},{4,6},{5,7},{6,4},{7,5},{8,10},{9,11},{10,... | collective-permute-start | bytes 786440 | tf_op jit(solution)/shard_map/ppermute | solution.py:649
  451.1 30.6 %all-to-all-start.8 = ((bf16[4,256,1024]{2,1,0:T(8,128)(2,1)}), bf16[4,256,1024]{2,1,0:T(8,128)(2,1)}, u32[]{:S(2)}, u32[]{:S(2)}) async-start(bf16[4,256,1024]{2,1,0:T(8,128)(2,1)} %bitcast.138), calls=%async_computation.8 | async-start | bytes 4194304 | tf_op jit(solution)/shard_map/all_to_all | solution.py:730
  459.2 42.5 %collective-permute-start.34 = (bf16[1,2,2,1,128,512]{5,4,3,2,1,0:T(8,128)(2,1)S(1)}, bf16[1,2,2,1,128,512]{5,4,3,2,1,0:T(8,128)(2,1)}, u32[]{:S(2)}, u32[]{:S(2)}) collective-permute-start(bf16[1,2,2,1,128,512]{5,4,3,2,1,0:T(8,128)(2,1)S(1)} %add_convert_fusion.10.refs_14_), channel_id=1, source_target_pairs={{0,8},{4,12},{8,0},{12,4},{16,24},{20,28},{24,16},{28,20},{1,9},{5... | collective-permute-start | bytes 1572872 | tf_op jit(solution)/shard_map/ppermute | solution.py:649
  460.3 8.4 %collective-permute-start.33 = (bf16[1,1,1,1,128,1024]{5,4,3,2,1,0:T(8,128)(2,1)S(1)}, bf16[1,1,1,1,128,1024]{5,4,3,2,1,0:T(8,128)(2,1)S(1)}, u32[]{:S(2)}, u32[]{:S(2)}) collective-permute-start(bf16[1,1,1,1,128,1024]{5,4,3,2,1,0:T(8,128)(2,1)S(1)} %add_convert_fusion.13.refs_13_), channel_id=1, source_target_pairs={{0,4},{4,0},{8,12},{12,8},{16,20},{20,16},{24,28},{28,24},{1,5},{5... | collective-permute-start | bytes 786440 | tf_op jit(solution)/shard_map/ppermute | solution.py:649
  460.7 17.1 %copy-start.30 = (bf16[1,1,1,1,128,1024]{5,4,3,2,1,0:T(8,128)(2,1)}, bf16[1,1,1,1,128,1024]{5,4,3,2,1,0:T(8,128)(2,1)S(1)}, u32[]{:S(2)}) copy-start(bf16[1,1,1,1,128,1024]{5,4,3,2,1,0:T(8,128)(2,1)S(1)} %add_convert_fusion.14.refs_12_) | copy-start | bytes 786436
  460.8 17.0 %collective-permute-start.32 = (bf16[1,1,1,1,128,1024]{5,4,3,2,1,0:T(8,128)(2,1)S(1)}, bf16[1,1,1,1,128,1024]{5,4,3,2,1,0:T(8,128)(2,1)S(1)}, u32[]{:S(2)}, u32[]{:S(2)}) collective-permute-start(bf16[1,1,1,1,128,1024]{5,4,3,2,1,0:T(8,128)(2,1)S(1)} %add_convert_fusion.14.refs_12_), channel_id=1, source_target_pairs={{0,16},{4,20},{8,24},{12,28},{16,0},{20,4},{24,8},{28,12},{1,17},{... | collective-permute-start | bytes 786440 | tf_op jit(solution)/shard_map/ppermute | solution.py:649
  477.9 20.3 %copy-start.60 = (f32[32,128]{1,0:T(8,128)S(1)}, f32[32,128]{1,0:T(8,128)}, u32[]{:S(2)}) copy-start(f32[32,128]{1,0:T(8,128)} %get-tuple-element.129.refs_15_) | copy-start | bytes 49156
  499.0 2.3 collective-permute-start.26
  499.9 6.4 %collective-permute-start.29 = (f32[293,128]{1,0:T(8,128)S(1)}, f32[293,128]{1,0:T(8,128)S(1)}, u32[]{:S(2)}, u32[]{:S(2)}) collective-permute-start(f32[293,128]{1,0:T(8,128)S(1)} %pad_maximum_fusion.7), channel_id=1, source_target_pairs={{0,4},{4,0},{8,12},{12,8},{16,20},{20,16},{24,28},{28,24},{1,5},{5... | collective-permute-start | bytes 450056 | tf_op jit(solution)/shard_map/ppermute | solution.py:649
  501.3 4.6 collective-permute-start.27
  502.9 64.5 %collective-permute-start.37 = (bf16[1,2,2,1,128,512]{5,4,3,2,1,0:T(8,128)(2,1)S(1)}, bf16[1,2,2,1,128,512]{5,4,3,2,1,0:T(8,128)(2,1)S(1)}, u32[]{:S(2)}, u32[]{:S(2)}) collective-permute-start(bf16[1,2,2,1,128,512]{5,4,3,2,1,0:T(8,128)(2,1)S(1)} %add_convert_fusion.9), channel_id=1, source_target_pairs={{0,16},{4,20},{8,24},{12,28},{16,0},{20,4},{24,8},{28,12},{1,17},{... | collective-permute-start | bytes 1572872 | tf_op jit(solution)/shard_map/ppermute | solution.py:649
  503.2 63.0 %collective-permute-start.36 = (bf16[1,1,1,2,128,1024]{5,4,3,2,1,0:T(8,128)(2,1)S(1)}, bf16[1,1,1,2,128,1024]{5,4,3,2,1,0:T(8,128)(2,1)}, u32[]{:S(2)}, u32[]{:S(2)}) collective-permute-start(bf16[1,1,1,2,128,1024]{5,4,3,2,1,0:T(8,128)(2,1)S(1)} %pad_maximum_fusion.6), channel_id=1, source_target_pairs={{0,16},{4,20},{8,24},{12,28},{16,0},{20,4},{24,8},{28,12},{1,17},{... | collective-permute-start | bytes 1572872 | tf_op jit(solution)/shard_map/ppermute | solution.py:649
  505.9 61.7 %collective-permute-start.35 = (bf16[1,2,1,1,128,1024]{5,4,3,2,1,0:T(8,128)(2,1)S(1)}, bf16[1,2,1,1,128,1024]{5,4,3,2,1,0:T(8,128)(2,1)}, u32[]{:S(2)}, u32[]{:S(2)}) collective-permute-start(bf16[1,2,1,1,128,1024]{5,4,3,2,1,0:T(8,128)(2,1)S(1)} %pad_maximum_fusion.5), channel_id=1, source_target_pairs={{0,8},{4,12},{8,0},{12,4},{16,24},{20,28},{24,16},{28,20},{1,9},{5... | collective-permute-start | bytes 1572872 | tf_op jit(solution)/shard_map/ppermute | solution.py:649
  506.3 34.0 %collective-permute-start.30 = (f32[293,128]{1,0:T(8,128)S(1)}, f32[293,128]{1,0:T(8,128)S(1)}, u32[]{:S(2)}, u32[]{:S(2)}) collective-permute-start(f32[293,128]{1,0:T(8,128)S(1)} %add.268), channel_id=1, source_target_pairs={{0,8},{4,12},{8,0},{12,4},{16,24},{20,28},{24,16},{28,20},{1,9},{5... | collective-permute-start | bytes 450056 | tf_op jit(solution)/shard_map/ppermute | solution.py:649
  540.3 17.0 %collective-permute-start.31 = (f32[293,128]{1,0:T(8,128)S(1)}, f32[293,128]{1,0:T(8,128)S(1)}, u32[]{:S(2)}, u32[]{:S(2)}) collective-permute-start(f32[293,128]{1,0:T(8,128)S(1)} %add.269), channel_id=1, source_target_pairs={{0,16},{4,20},{8,24},{12,28},{16,0},{20,4},{24,8},{28,12},{1,17},{... | collective-permute-start | bytes 450056 | tf_op jit(solution)/shard_map/ppermute | solution.py:649
  558.1 11.7 %collective-permute-start.39 = (f32[2052]{0:T(1024)S(1)}, f32[2052]{0:T(1024)S(1)}, u32[]{:S(2)}, u32[]{:S(2)}) collective-permute-start(f32[2052]{0:T(1024)S(1)} %slice.459), channel_id=1, source_target_pairs={{0,2},{1,3},{2,0},{3,1},{4,6},{5,7},{6,4},{7,5},{8,10},{9,11},{10,... | collective-permute-start | bytes 24632 | tf_op jit(solution)/shard_map/ppermute | solution.py:649
  569.8 24.9 %collective-permute-start.40 = (bf16[1,2,1,2,128,1024]{5,4,3,2,1,0:T(8,128)(2,1)S(1)}, bf16[1,2,1,2,128,1024]{5,4,3,2,1,0:T(8,128)(2,1)}, u32[]{:S(2)}, u32[]{:S(2)}) collective-permute-start(bf16[1,2,1,2,128,1024]{5,4,3,2,1,0:T(8,128)(2,1)S(1)} %pad_maximum_fusion.3), channel_id=1, source_target_pairs={{0,8},{4,12},{8,0},{12,4},{16,24},{20,28},{24,16},{28,20},{1,9},{5... | collective-permute-start | bytes 3145736 | tf_op jit(solution)/shard_map/ppermute | solution.py:649
  572.3 14.9 %collective-permute-start.38 = (bf16[1,2,2,1,128,512]{5,4,3,2,1,0:T(8,128)(2,1)S(1)}, bf16[1,2,2,1,128,512]{5,4,3,2,1,0:T(8,128)(2,1)S(1)}, u32[]{:S(2)}, u32[]{:S(2)}) collective-permute-start(bf16[1,2,2,1,128,512]{5,4,3,2,1,0:T(8,128)(2,1)S(1)} %add_convert_fusion.8), channel_id=1, source_target_pairs={{0,4},{4,0},{8,12},{12,8},{16,20},{20,16},{24,28},{28,24},{1,5},{5... | collective-permute-start | bytes 1572872 | tf_op jit(solution)/shard_map/ppermute | solution.py:649
  574.1 34.4 %collective-permute-start.41 = (bf16[1,2,2,1,128,1024]{5,4,3,2,1,0:T(8,128)(2,1)}, bf16[1,2,2,1,128,1024]{5,4,3,2,1,0:T(8,128)(2,1)}, u32[]{:S(2)}, u32[]{:S(2)}) collective-permute-start(bf16[1,2,2,1,128,1024]{5,4,3,2,1,0:T(8,128)(2,1)} %pad_maximum_fusion.2), channel_id=1, source_target_pairs={{0,4},{4,0},{8,12},{12,8},{16,20},{20,16},{24,28},{28,24},{1,5},{5... | collective-permute-start | bytes 3145736 | tf_op jit(solution)/shard_map/ppermute | solution.py:649
  (59 other events, 285.0 us)
Sparse Core Ops, SparseCore 0:
  71.0 80.7 all-gather.2

commit v4 on v3

--- a/solution.py
+++ b/solution.py
@@ -362,15 +362,14 @@
         for i, pa, within in zip(group, pas, withins):
             states = state_ref[i]
             p = p_ref[i]
-            sum_ref[i, 0:1, :] = summed(states * p)
-            sum_ref[i, 1:2, :] = summed(states * turn(p))
-            sum_ref[i, 2:3, :] = summed(states * pa)
-            sum_ref[i, 3:4, :] = summed(states * turn(pa))
-            sum_ref[i, 4:5, :] = within[0:1] + within[1:2]
-            sum_ref[i, 5:6, :] = within[2:3] + within[3:4]
+            sum_ref[0, i : i + 1, :] = summed(states * p)
+            sum_ref[1, i : i + 1, :] = summed(states * turn(p))
+            sum_ref[2, i : i + 1, :] = summed(states * pa)
+            sum_ref[3, i : i + 1, :] = summed(states * turn(pa))
+            sum_ref[4, i : i + 1, :] = within[0:1] + within[1:2]
+            sum_ref[5, i : i + 1, :] = within[2:3] + within[3:4]
             skip = summed(g_ref[i].astype(f32) * u_ref[i].astype(f32))
-            sum_ref[i, 6:7, :] = jnp.broadcast_to(jnp.sum(skip, axis=1, keepdims=True), (1, size))
-            sum_ref[i, 7:8, :] = jnp.zeros((1, size), f32)
+            sum_ref[6, i : i + 1, :] = jnp.broadcast_to(jnp.sum(skip, axis=1, keepdims=True), (1, size))
 
 
 def back_kernel(
@@ -398,11 +397,10 @@
             )
             states = state_ref[i]
             here = p_ref[i] + adjoint * pars_ref[i, 0:1, :] + t * pars_ref[i, 1:2, :]
-            sum_ref[i, 0:1, :] = summed(states * here)
-            sum_ref[i, 1:2, :] = summed(states * turn(here))
-            sum_ref[i, 2:3, :] = summed(adjoint * qp)
-            sum_ref[i, 3:4, :] = summed(adjoint * turn(qp))
-            sum_ref[i, 4:8, :] = jnp.zeros((4, size), f32)
+            sum_ref[0, i : i + 1, :] = summed(states * here)
+            sum_ref[1, i : i + 1, :] = summed(states * turn(here))
+            sum_ref[2, i : i + 1, :] = summed(adjoint * qp)
+            sum_ref[3, i : i + 1, :] = summed(adjoint * turn(qp))
     gain = gain_ref[...]
     first = jnp.zeros((block, size), f32)
     for r in range(rows):
@@ -417,8 +415,7 @@
 
 
 def last_kernel(
-    half, x_ref, low_ref, high_ref, hidden_ref, result_ref, scale_ref, cubic_ref, gain_ref,
-    out_ref, copy_ref,
+    half, x_ref, low_ref, high_ref, hidden_ref, scale_ref, cubic_ref, gain_ref, out_ref
 ):
     gain = gain_ref[:, 0:1]
 
@@ -429,7 +426,6 @@
                 - cubic_ref[b : b + 1, :] * x_ref[b].astype(f32)
                 + hidden_ref[b].astype(f32)
             )
-            copy_ref[:, b, :] = result_ref[b]
 
     @pl.when(pl.program_id(0) < half)
     def _():
@@ -438,6 +434,11 @@
     @pl.when(pl.program_id(0) >= half)
     def _():
         run(high_ref)
+
+
+def turned_kernel(values_ref, out_ref):
+    for b in range(values_ref.shape[0]):
+        out_ref[:, b, :] = values_ref[b]
 
 
 def over_blocks(kernel, steps, args, outs, us, scratch=(), ties=(), vmem=60):
@@ -678,8 +679,8 @@
     return kept, sent, swap(sent, "seq", bit)
 
 
-def up_step(terms, bit):
-    there = swap(terms, "seq", bit)
+def up_step(terms, bit, gate):
+    there = lax.optimization_barrier((swap(terms, "seq", bit), gate))[0]
     first = (lax.axis_index("seq") // bit) % 2 == 0
     return jnp.concatenate(
         [jnp.where(first, terms, there), jnp.where(first, there, terms)], axis=axis_of(bit)
@@ -744,9 +745,9 @@
     small_places = jnp.stack([v[contexts * local :] for v in flats])
     square_one = sum(v[: contexts * local] for v in flats).reshape(contexts, local)
 
-    expand_own = expand_weight.T
     part = hidden_own // seq
 
+    expand_own = after(expand_weight, sent).T
     slices_sent = jnp.stack(
         [
             lax.dynamic_slice_in_dim(expand_own, seq_me * part, part, 0),
@@ -795,21 +796,22 @@
     def out(shape, dtype):
         return jax.ShapeDtypeStruct(shape, dtype)
 
-    block = min(16, features)
+    block, small_block = min(32, features), min(16, features)
     state_shape = out((features, rows, 4 * modes), f32)
     end_shape = out((features, contexts, 4 * modes), bf16)
     row_shape = out((features, rows, chunk), bf16)
     context_shape = out((contexts, features, local), bf16)
     table_shape = out((features, 4 * modes, chunk), bf16)
-    sum_shape = out((features, 8, 4 * modes), f32)
+    sum_shape = out((7, features, 4 * modes), f32)
     line_shape = out((features, chunk), f32)
     flat = [pltpu.VMEM((block * rows, chunk), f32)]
+    small_flat = [pltpu.VMEM((small_block * rows, chunk), f32)]
     skip_wide = jnp.broadcast_to(skip_weight[:, None], (features, chunk))
     gain_wide = jnp.broadcast_to(first_gain[:, None], (features, chunk))
     scan_steps = max(1, (chunks - 1).bit_length())
     pars, whole_pars, one, two, taps = by_channel(
         functools.partial(tables_kernel, chunk, scan_steps, local),
-        block,
+        small_block,
         features,
         [
             (step_size[:, None], 0),
@@ -826,14 +828,12 @@
             (line_shape, 0),
         ],
         10,
-        [pltpu.VMEM((block, 8, 4 * modes), f32)],
-        (sent, slices_sent, by_context),
+        [pltpu.VMEM((small_block, 8, 4 * modes), f32)],
+        (sent,),
     )
     gated_upper = swap(gated_own, "mp", 2)
     shrink_far = swap(shrink_weight, "mp", 1)
     z_device = lax.dynamic_slice_in_dim(whole_pars, seq_me * group, group, 0)
-    cotangent_by_context = after(cotangent.swapaxes(0, 1), taps)
-    upstream_parts = exchanged(cotangent_by_context)
     normed_one, terms, ends = by_channel(
         functools.partial(states_kernel, chunks),
         block,
@@ -842,9 +842,10 @@
         [(row_shape, 0), (state_shape, 0), (end_shape, 0)],
         8,
         flat,
-        (slices, residual, expand_far, cotangent_by_context),
+        (slices_sent, residual),
     )
     upper = lax.all_gather(after(slices, normed_one), "seq", axis=0)
+    upstream_parts = exchanged(after(cotangent, normed_one).swapaxes(0, 1))
     gated_places = (
         gated_own,
         gated_upper,
@@ -1047,10 +1048,10 @@
     e_kept, e_sent, e_there = onwards(e_kept, e_there, upper_bit)
     (sums_one,) = by_channel(
         sums_kernel,
-        block,
+        small_block,
         features,
         [(grad_mixed, 0), (normed_one, 0), (states, 0), (adj_terms, 0), (one, 0)],
-        [(sum_shape, 0)],
+        [(sum_shape, 1)],
         20,
         (),
         (s_sent, e_sent, adjoint_in),
@@ -1060,7 +1061,7 @@
     g_kept, g_sent, g_there = onwards(g_kept, g_there, upper_bit)
     s_kept, s_sent, s_there = onwards(s_kept, s_there, upper_bit)
     e_kept, e_sent, e_there = onwards(e_kept, e_there, third)
-    half = features // 2 // block
+    half = features // 2 // small_block
     back_args = [
         (grad_mixed, 0),
         (adj_terms, 0),
@@ -1079,61 +1080,54 @@
     def back(first_block, ties):
         return by_channel(
             functools.partial(back_kernel, chunks),
-            block,
+            small_block,
             features // 2,
             back_args,
             [
                 (out((contexts, features // 2, local), bf16), 1),
-                (out((features // 2, 8, 4 * modes), f32), 0),
+                (out((4, features // 2, 4 * modes), f32), 1),
                 (out((rows, chunk), f32), None),
                 (out((features // 2, chunk), f32), 0),
             ],
             12,
-            flat,
+            small_flat,
             ties,
             first_block,
         )
 
-    def up(values, bit):
-        return up_step(values, bit)
-
-    def exchange(values, bit):
-        return added(values, swap(values, "seq", bit))
+    def exchange(values, bit, gate):
+        return added(values, after(swap(values, "seq", bit), gate))
 
     low = back(0, (s_sent, e_sent, g_sent, sums_one, own_hidden))
-    result = returned(after(result, own_hidden))
     s_there, e_there, g_there = after((s_there, e_there, g_there), low[2])
     s_all, e_all, g_all = added(s_kept, s_there), added(e_kept, e_there), added(g_kept, g_there)
     for bit in rest:
         s_all, e_all = (added(*sent_down(v, bit)[::2]) for v in (s_all, e_all))
-        g_all = exchange(g_all, bit)
-    high = back(half, (s_all, e_all, g_all, low[2], result))
-    for bit in rest[::-1]:
-        s_all, e_all = up(s_all, bit), up(e_all, bit)
-    s_all, e_all, g_all = up(s_all, third), up(e_all, first), exchange(g_all, second)
-    s_all, e_all, g_all = after((s_all, e_all, g_all), high[2])
+        g_all = exchange(g_all, bit, low[2])
+    both_parts = jnp.stack([s_all.reshape(-1, D), e_all.reshape(-1, hidden_own)])
+    both_all = lax.all_gather(both_parts, "seq", axis=0)
+    high = back(half, (both_parts, g_all, low[2]))
+    g_all = exchange(g_all, third, high[2])
+    result = returned(after(result, (own_hidden, low[2])))
     grad_first_gain = jnp.sum(jnp.concatenate([low[3], high[3]]), axis=1)
 
     dot_one = axis_total(low[2] + high[2], "mp").reshape(contexts, local)
     cubic = scale_one * scale_one * scale_one * dot_one / D
-    grad_inputs, result = over_blocks(
+    (grad_inputs,) = over_blocks(
         functools.partial(last_kernel, half),
-        features // block,
+        features // small_block,
         [
-            along(by_context, 1, block),
-            (low[0], (contexts, block, local), lambda i: (0, jnp.minimum(i, half - 1), 0)),
-            (high[0], (contexts, block, local), lambda i: (0, jnp.maximum(i - half, 0), 0)),
-            along(own_hidden, 1, block),
-            along(result, 1, block),
+            along(by_context, 1, small_block),
+            (low[0], (contexts, small_block, local), lambda i: (0, jnp.minimum(i, half - 1), 0)),
+            (high[0], (contexts, small_block, local), lambda i: (0, jnp.maximum(i - half, 0), 0)),
+            along(own_hidden, 1, small_block),
             along(scale_one, None, 0),
             along(cubic, None, 0),
-            along(gain_wide, 0, block),
+            along(gain_wide, 0, small_block),
         ],
-        [along(out(inputs.shape, f32), 0, block), along(out(inputs.shape, bf16), 0, block)],
+        [along(out(inputs.shape, f32), 0, small_block)],
         8,
     )
-    s_all, e_all, g_all = up(s_all, second), up(e_all, third), exchange(g_all, third)
-    s_all, e_all, g_all = after((s_all, e_all, g_all), grad_inputs)
 
     stats = jnp.stack(
         [
@@ -1154,7 +1148,7 @@
         return values[:, k * modes : (k + 1) * modes]
 
     def product_sums(lines, k):
-        plain, turned = lines[:, k], lines[:, k + 1]
+        plain, turned = lines[k], lines[k + 1]
         return (
             quarter(plain, 0) - quarter(plain, 1),
             quarter(turned, 1) + quarter(turned, 3),
@@ -1162,7 +1156,7 @@
 
     inverse = power(w, -1.0)
     within = [
-        cmul(inverse, (quarter(sums_one[:, k], 0), quarter(sums_one[:, k], 1))) for k in (4, 5)
+        cmul(inverse, (quarter(sums_one[k], 0), quarter(sums_one[k], 1))) for k in (4, 5)
     ]
     sum_a = cadd(product_sums(sums_one, 0), within[0])
     def both_halves(k):
@@ -1176,7 +1170,7 @@
         float(chunk) * crossing[k] + part_a[k] - part_p[k] + within[1][k] for k in range(2)
     ]
     lines_late = jnp.concatenate(
-        [sums_one[:, 6, 0], grad_first_gain, near.reshape(-1)]
+        [sums_one[6, :, 0], grad_first_gain, near.reshape(-1)]
     )
     width = 4 * modes
     pad = -lines_late.shape[0] % width
@@ -1187,10 +1181,16 @@
         ],
         axis=0,
     )
-    s_all, e_all, g_all = up(s_all, first), up(e_all, second), up(g_all, first)
-    late = axis_total(late, "seq")
-    grad_shrink = s_all.reshape(-1, D).astype(f32)
-    grad_expand = e_all.reshape(D, hidden_own).astype(f32)
+    for bit in bits:
+        late = late + swap(late, "seq", bit)
+    g_all = exchange(g_all, second, grad_inputs)
+    g_all = up_step(g_all, first, late)
+    result = result.reshape(contexts, features, local)
+    (result,) = by_channel(
+        turned_kernel, 2 * block, features, [(result, 1)], [(out(inputs.shape, bf16), 0)], 5
+    )
+    grad_shrink = both_all[:, 0].reshape(-1, D).astype(f32)
+    grad_expand = both_all[:, 1].reshape(D, hidden_own).astype(f32)
     grad_gated = g_all.reshape(D, 2, features).astype(f32)
     lines_late = late[features:].reshape(-1)
     late = late[:features]

time: 633 us -> 588 us (0.929)
  waiting for transfers between devices: 115 us -> 98.1 us
  Pallas kernels: 254 us -> 246 us
  other arithmetic: 62.1 us -> 54.9 us
    ppermute x42 -> x36, waiting for transfers between devices: 80.5 us -> 63.6 us  [swap(): return lax.ppermute(values, axis, [(i, i ^ bit) for i in range(size)])]
    pallas_call x15 -> x16, Pallas kernels: 254 us -> 246 us  [over_blocks(): pl.pallas_call(run, grid=(steps,), in_specs=[pl.BlockSpec(memory_space=pl...]
    unnamed x166 -> x132, local copies, waits for them, and re-layouts: 23 us -> 16.1 us
    ppermute x42 -> x36, starting transfers between devices: 41 us -> 35.5 us  [swap(): return lax.ppermute(values, axis, [(i, i ^ bit) for i in range(size)])]
    convert_element_type x15 -> x13, other arithmetic: 29.1 us -> 27.6 us  [added(): return (a.astype(f32) + b.astype(f32)).astype(bf16)]
  transfers between devices with their start and end apart: 51 -> 46, of which waited for: 17 -> 13; matrix products, arithmetic and copies ran while one was open for 17% -> 16% of each run, Pallas kernels for 32% -> 36%
where the time goes in v4:
time: 588 us; the launch traced here: 578 us
  Pallas kernels  246 us (42%)
  waiting for transfers between devices  98.1 us (17%)
  starting transfers between devices  72.7 us (12%)
  local copies, waits for them, and re-layouts  59.3 us (10%)
  other arithmetic  54.9 us (9%)
  blocking collectives  30.8 us (5%)
  between operations  16.6 us (3%)
    pallas_call x16, Pallas kernels, over_blocks(): pl.pallas_call(run, grid=(steps,), in_specs=[pl.BlockSpec(memory_space=pl...  246 us
    ppermute x36, waiting for transfers between devices, swap(): return lax.ppermute(values, axis, [(i, i ^ bit) for i in range(size)])  63.6 us
    ppermute x36, starting transfers between devices, swap(): return lax.ppermute(values, axis, [(i, i ^ bit) for i in range(size)])  35.5 us
    all_to_all x1, blocking collectives, shards(): lax.all_to_all(lifted_sent, 'mp', 0, 0, tiled=True).reshape(D, tokens)  30.8 us
    convert_element_type x13, other arithmetic, added(): return (a.astype(f32) + b.astype(f32)).astype(bf16)  27.6 us
    all_to_all x2, waiting for transfers between devices, handed(): terms = lax.all_to_all(ends, 'seq', 0, 0, tiled=True)  19.1 us
    unnamed x132, local copies, waits for them, and re-layouts  16.1 us
    all_to_all x3, starting transfers between devices, returned(): lax.all_to_all(values.reshape(mp, features, local), 'mp', 0, 0, tiled=True)  14 us
  transfers between devices with their start and end apart: 46, of which 13 were waited for; matrix products, arithmetic and copies ran while one was open for 16% of the time, Pallas kernels for 36%

profile of v4, /device:TPU:0, one launch (start us, length us, event | category | flops | bytes accessed | tf_op | source)
XLA Modules:
  0.0 578.3 jit_solution(18443673241308557861)
XLA Ops:
  7.2 3.5 copy.247
  10.7 4.6 all-to-all-start
  16.2 3.0 collective-permute-start
  19.4 2.9 copy.201
  24.6 1.9 collective-permute-start.10
  30.4 18.4 %shard_map.312 = (f32[256,8,128]{2,1,0:T(8,128)}, f32[256,2,128]{2,1,0:T(2,128)}, bf16[256,128,128]{2,1,0:T(8,128)(2,1)}, bf16[256,128,128]{2,1,0:T(8,128)(2,1)}, f32[256,128]{1,0:T(8,128)}) custom-call(f32[256,1]{1,0:T(8,128)} %copy.196.refs_0_, f32[256,32]{1,0:T(8,128)} %copy.197.refs_1_, f32[256,32]{1,0:T(8,128)} %copy.198.refs_2_, ...), custom_call_target="tpu_custom_call" | custom-call | flops 10000000000 | bytes 18351104 | tf_op jit(solution)/shard_map/pallas_call | solution.py:451
  50.3 11.8 %shard_map.313 = (bf16[256,32,128]{2,1,0:T(8,128)(2,1)}, f32[256,32,128]{2,1,0:T(8,128)}, bf16[256,4,128]{2,1,0:T(4,128)(2,1)}) custom-call(bf16[4,256,1024]{2,1,0:T(8,128)(2,1)} %bitcast.132, f32[32,128]{1,0:T(8,128)} %reshape.175.refs_1_.refs_10_, f32[256,128]{1,0:T(8,128)} %broadcast_in_dim.34.refs_2_.refs_11_.refs_6_, ...), custom_call_target="tpu_custom_call" | custom-call | flops 8000000000 | bytes 18235392 | tf_op jit(solution)/shard_map/pallas_call | solution.py:451
  62.2 2.5 copy.202
  64.8 6.2 %all-to-all-start.1 = ((bf16[256,4,128]{2,1,0:T(4,128)(2,1)}), bf16[256,4,128]{2,1,0:T(4,128)(2,1)S(1)}, u32[]{:S(2)}, u32[]{:S(2)}) async-start(bf16[256,4,128]{2,1,0:T(4,128)(2,1)} %get-tuple-element.87), calls=%async_computation.1 | async-start | bytes 524288 | tf_op jit(solution)/shard_map/all_to_all | solution.py:784
  72.4 14.4 %all-to-all-done.1.refs_0_ = bf16[256,4,128]{2,1,0:T(4,128)(2,1)S(1)} async-done(((bf16[256,4,128]{2,1,0:T(4,128)(2,1)}), bf16[256,4,128]{2,1,0:T(4,128)(2,1)S(1)}, u32[]{:S(2)}, u32[]{:S(2)}) %all-to-all-start.1) | async-done | bytes 262176 | tf_op jit(solution)/shard_map/all_to_all | solution.py:784
  87.5 2.2 shard_map.314
  89.7 4.4 all-to-all-start.2
  94.2 2.2 copy.203
  97.8 1.7 collective-permute-start.5
  100.2 3.0 all-to-all-done.2.refs_2_
  104.0 15.3 %shard_map.315 = (bf16[256,32,128]{2,1,0:T(8,128)(2,1)}, f32[256,32,128]{2,1,0:T(8,128)}, bf16[4,256,1024]{2,1,0:T(8,128)(2,1)}) custom-call(bf16[256,32,128]{2,1,0:T(8,128)(2,1)} %get-tuple-element.85.refs_0_.refs_1_.refs_3_, f32[256,32,128]{2,1,0:T(8,128)} %get-tuple-element.86.refs_1_, bf16[256,4,128]{2,1,0:T(4,128)(2,1)} %copy-done.33, ...), custom_call_target="tpu_custom_call" | custom-call | flops 14000000000 | bytes 24641536 | tf_op jit(solution)/shard_map/pallas_call | solution.py:451
  119.3 4.0 collective-permute-done.7.refs_7_
  123.3 30.8 %all_to_all.45 = bf16[4,256,1024]{2,1,0:T(8,128)(2,1)} all-to-all(bf16[4,256,1024]{2,1,0:T(8,128)(2,1)} %get-tuple-element.94), channel_id=1, replica_groups=mesh['seq'=8,'mp'=4] {'mp'}, dimensions={0} | all-to-all | bytes 4194304 | tf_op jit(solution)/shard_map/all_to_all | solution.py:877
  158.3 12.9 %shard_map.316 = (bf16[1024,1024]{1,0:T(8,128)(2,1)}, f32[1024,1024]{1,0:T(8,128)}, bf16[1024,1024]{1,0:T(8,128)(2,1)}, f32[1024,1024]{1,0:T(8,128)}, f32[1024,1024]{1,0:T(8,128)}, /*index=5*/f32[8,1024]{1,0:T(8,128)}) custom-call(s32[4]{0:T(128)} %pad_add_fusion.refs_0_, f32[1,1024]{1,0:T(1,128)} %fusion.19.refs_1_, bf16[1024,1024]{1,0:T(8,128)(2,1)} %bitcast.140, ...), custom_call_target="tpu_custom_call" | custom-call | flops 12000000000 | bytes 28872720 | tf_op jit(solution)/shard_map/pallas_call | solution.py:451
  172.6 36.3 %shard_map.317 = (f32[1024,1024]{1,0:T(8,128)}, f32[1024,1024]{1,0:T(8,128)}, bf16[2048,1024]{1,0:T(8,128)(2,1)}, bf16[2,1024,1024]{2,1,0:T(8,128)(2,1)}, f32[2048,128]{1,0:T(8,128)}) custom-call(bf16[1024,1024]{1,0:T(8,128)(2,1)} %get-tuple-element.95.refs_0_, bf16[1024,1024]{1,0:T(8,128)(2,1)} %get-tuple-element.96.refs_1_.refs_5_, ...), custom_call_target="tpu_custom_call" | custom-call | flops 38000001024 | bytes 35651584 | tf_op jit(solution)/shard_map/pallas_call | solution.py:451
  212.5 39.0 %shard_map.318 = (f32[1024,1024]{1,0:T(8,128)}, f32[1024,1024]{1,0:T(8,128)}, bf16[2048,1024]{1,0:T(8,128)(2,1)}, bf16[2,1024,1024]{2,1,0:T(8,128)(2,1)}, f32[2048,128]{1,0:T(8,128)}) custom-call(bf16[1024,1024]{1,0:T(8,128)(2,1)} %get-tuple-element.95.refs_0_, bf16[1024,1024]{1,0:T(8,128)(2,1)} %get-tuple-element.96.refs_1_.refs_5_, ...), custom_call_target="tpu_custom_call" | custom-call | flops 38000001024 | bytes 44040192 | tf_op jit(solution)/shard_map/pallas_call | solution.py:451
  253.1 5.6 add_convert_fusion
  261.8 1.8 collective-permute-start.16
  263.7 4.3 add_convert_fusion.1
  268.0 1.7 constant_dynamic-slice_fusion.6.refs_12_
  272.0 15.2 %shard_map.319 = (bf16[1024,1024]{1,0:T(8,128)(2,1)}, bf16[1024,1024]{1,0:T(8,128)(2,1)}, bf16[2048,1024]{1,0:T(8,128)(2,1)}, f32[4,4,256,128]{3,2,1,0:T(8,128)}) custom-call(s32[4]{0:T(128)} %pad_add_fusion.refs_0_, f32[1024,1024]{1,0:T(8,128)} %get-tuple-element.101.refs_1_, f32[1024,1024]{1,0:T(8,128)} %get-tuple-element.102.refs_2_.refs_3_, ...), custom_call_target="tpu_custom_call" | custom-call | flops 14000000000 | bytes 34111504 | tf_op jit(solution)/shard_map/pallas_call | solution.py:451
  288.3 12.4 %shard_map.320 = (bf16[2,1024,512]{2,1,0:T(8,128)(2,1)}, bf16[2,1024,512]{2,1,0:T(8,128)(2,1)}, bf16[1024,1024]{1,0:T(8,128)(2,1)}, f32[8,1024]{1,0:T(8,128)}) custom-call(s32[4]{0:T(128)} %pad_add_fusion.refs_0_, bf16[2048,1024]{1,0:T(8,128)(2,1)} %get-tuple-element.110.refs_1_, bf16[1024,1024]{1,0:T(8,128)(2,1)} %bitcast.141, ...), custom_call_target="tpu_custom_call" | custom-call | flops 10000000000 | bytes 21528592 | tf_op jit(solution)/shard_map/pallas_call | solution.py:451
  300.8 4.7 all-to-all-start.4
  305.5 2.2 reduce_sum.118
  309.2 2.7 pad_maximum_fusion.5
  312.5 3.4 add_convert_fusion.3
  318.3 2.6 add_convert_fusion.4
  324.8 6.5 %all-to-all-done.4.refs_0_ = bf16[4,256,1024]{2,1,0:T(8,128)(2,1)} async-done(((bf16[4,256,1024]{2,1,0:T(8,128)(2,1)}), bf16[4,256,1024]{2,1,0:T(8,128)(2,1)}, u32[]{:S(2)}, u32[]{:S(2)}) %all-to-all-start.4) | async-done | bytes 2097184 | tf_op jit(solution)/shard_map/all_to_all | solution.py:731
  331.2 12.5 %shard_map.321 = (bf16[256,32,128]{2,1,0:T(8,128)(2,1)}, f32[256,32,128]{2,1,0:T(8,128)}, bf16[256,4,128]{2,1,0:T(4,128)(2,1)}) custom-call(bf16[4,256,1024]{2,1,0:T(8,128)(2,1)} %all-to-all-done.4.refs_0_, bf16[256,32,128]{2,1,0:T(8,128)(2,1)} %get-tuple-element.115.refs_1_, bf16[256,128,128]{2,1,0:T(8,128)(2,1)} %get-tuple-element.89.refs_3_.refs_2_.refs_4_, ...), custom_call_target="tpu_custom_call" | custom-call | flops 10000000000 | bytes 20185088 | tf_op jit(solution)/shard_map/pallas_call | solution.py:451
  343.7 4.4 all-to-all-start.5
  348.1 2.8 add_convert_fusion.2
  352.0 4.8 all-to-all-done.5.refs_0_
  357.5 2.2 shard_map.322
  359.7 3.6 all-to-all-start.6
  364.0 2.0 collective-permute-start.22
  366.1 5.9 %all-to-all-done.6.refs_7_.refs_2_ = bf16[256,4,128]{2,1,0:T(4,128)(2,1)S(1)} async-done(((bf16[256,4,128]{2,1,0:T(4,128)(2,1)}), bf16[256,4,128]{2,1,0:T(4,128)(2,1)S(1)}, u32[]{:S(2)}, u32[]{:S(2)}) %all-to-all-start.6) | async-done | bytes 262176 | tf_op jit(solution)/shard_map/all_to_all | solution.py:794
  372.6 4.4 all-to-all-start.7
  377.1 2.1 add_convert_fusion.6
  380.1 1.9 collective-permute-start.21
  385.7 23.4 %shard_map.323.refs_15_ = f32[7,256,128]{2,1,0:T(8,128)} custom-call(bf16[256,32,128]{2,1,0:T(8,128)(2,1)} %get-tuple-element.120.refs_0_, bf16[256,32,128]{2,1,0:T(8,128)(2,1)} %get-tuple-element.85.refs_0_.refs_1_.refs_3_, f32[256,32,128]{2,1,0:T(8,128)} %get-tuple-element.122.refs_2_.refs_4_, f32[256,32,128]{2,1,0:T(8,128)} %get-tuple-element.121.refs_3_.refs_1_, ...), custom_call_target="tpu_custom_call" | custom-call | flops 20000000000 | bytes 21889024 | tf_op jit(solution)/shard_map/pallas_call | solution.py:451
  409.1 2.0 slice_bitcast_fusion.3
  419.1 1.9 collective-permute-start.24
  421.0 1.9 collective-permute-start.23
  422.9 13.9 %shard_map.324 = (bf16[4,128,1024]{2,1,0:T(8,128)(2,1)}, f32[4,128,128]{2,1,0:T(8,128)}, f32[32,128]{1,0:T(8,128)}, f32[128,128]{1,0:T(8,128)}) custom-call(bf16[256,32,128]{2,1,0:T(8,128)(2,1)} %get-tuple-element.120.refs_0_, f32[256,32,128]{2,1,0:T(8,128)} %get-tuple-element.121.refs_3_.refs_1_, bf16[256,4,128]{2,1,0:T(4,128)(2,1)} %copy-done.31, ...), custom_call_target="tpu_custom_call" | custom-call | flops 12000000000 | bytes 26181632 | tf_op jit(solution)/shard_map/pallas_call | solution.py:451
  437.9 2.0 add_convert_fusion.10.refs_13_
  441.0 14.0 %shard_map.326 = (bf16[4,128,1024]{2,1,0:T(8,128)(2,1)}, f32[4,128,128]{2,1,0:T(8,128)}, f32[32,128]{1,0:T(8,128)}, f32[128,128]{1,0:T(8,128)}) custom-call(bf16[256,32,128]{2,1,0:T(8,128)(2,1)} %get-tuple-element.120.refs_0_, f32[256,32,128]{2,1,0:T(8,128)} %get-tuple-element.121.refs_3_.refs_1_, bf16[256,4,128]{2,1,0:T(4,128)(2,1)} %copy-done.31, ...), custom_call_target="tpu_custom_call" | custom-call | flops 12000000000 | bytes 26181632 | tf_op jit(solution)/shard_map/pallas_call | solution.py:451
  461.3 1.9 collective-permute-start.32
  463.2 4.9 all-to-all-start.8
  469.0 10.8 %collective-permute-done.30 = f32[293,128]{1,0:T(8,128)S(1)} collective-permute-done((f32[293,128]{1,0:T(8,128)S(1)}, f32[293,128]{1,0:T(8,128)S(1)}, u32[]{:S(2)}, u32[]{:S(2)}) %collective-permute-start.30) | collective-permute-done | bytes 150048 | tf_op jit(solution)/shard_map/ppermute | solution.py:650
  479.8 4.7 collective-permute-start.31
  484.5 12.2 %shard_map.327 = f32[256,4,1024]{2,1,0:T(4,128)} custom-call(bf16[4,256,1024]{2,1,0:T(8,128)(2,1)} %bitcast.135, bf16[4,128,1024]{2,1,0:T(8,128)(2,1)} %get-tuple-element.128.refs_1_, bf16[4,128,1024]{2,1,0:T(8,128)(2,1)} %get-tuple-element.132.refs_2_, bf16[4,256,1024]{2,1,0:T(8,128)(2,1)} %all-to-all-done.7.refs_16_.refs_3_, f32[4,1024]{1,0:T(4,128)} %copy-done.36, ...), custom_call_target="tpu_custom_call" | custom-call | flops 8000000000 | bytes 10649600 | tf_op jit(solution)/shard_map/pallas_call | solution.py:451
  496.7 20.9 %collective-permute-done.31 = f32[293,128]{1,0:T(8,128)S(1)} collective-permute-done((f32[293,128]{1,0:T(8,128)S(1)}, f32[293,128]{1,0:T(8,128)S(1)}, u32[]{:S(2)}, u32[]{:S(2)}) %collective-permute-start.31) | collective-permute-done | bytes 150048 | tf_op jit(solution)/shard_map/ppermute | solution.py:650
  529.0 13.2 %collective-permute-done.33 = bf16[1,2,2,1,128,512]{5,4,3,2,1,0:T(8,128)(2,1)S(1)} collective-permute-done((bf16[1,2,2,1,128,512]{5,4,3,2,1,0:T(8,128)(2,1)S(1)}, bf16[1,2,2,1,128,512]{5,4,3,2,1,0:T(8,128)(2,1)S(1)}, u32[]{:S(2)}, u32[]{:S(2)}) %collective-permute-start.33) | collective-permute-done | bytes 524320 | tf_op jit(solution)/shard_map/ppermute | solution.py:650
  544.8 11.3 %collective-permute-done.34 = bf16[1,2,2,1,128,512]{5,4,3,2,1,0:T(8,128)(2,1)S(1)} collective-permute-done((bf16[1,2,2,1,128,512]{5,4,3,2,1,0:T(8,128)(2,1)S(1)}, bf16[1,2,2,1,128,512]{5,4,3,2,1,0:T(8,128)(2,1)S(1)}, u32[]{:S(2)}, u32[]{:S(2)}) %collective-permute-start.34) | collective-permute-done | bytes 524320 | tf_op jit(solution)/shard_map/ppermute | solution.py:650
  556.3 2.4 reshape.194
  558.7 4.3 shard_map.325
  563.0 2.7 fusion.28
  565.7 2.6 bitcast_convert_fusion
  568.3 2.6 bitcast_convert_fusion.1
  (298 shorter events, 77.6 us)
Async XLA Ops:
  10.7 38.8 %all-to-all-start = ((bf16[4,256,1024]{2,1,0:T(8,128)(2,1)}), bf16[4,256,1024]{2,1,0:T(8,128)(2,1)}, u32[]{:S(2)}, u32[]{:S(2)}) async-start(bf16[4,256,1024]{2,1,0:T(8,128)(2,1)} %bitcast.131), calls=%async_computation | async-start | bytes 4194304 | tf_op jit(solution)/shard_map/all_to_all | solution.py:758
  15.3 138.8 %all-gather.5.cloned.1.call-start = ((), (), s32[]{:S(2)}) async-start(), calls=%async_computation.9 | async-start | bytes 4718592 | tf_op jit(solution)/shard_map/all_gather | solution.py:847
  16.2 6.1 %copy-start.49 = (f32[6144]{0:T(1024)}, f32[6144]{0:T(1024)S(1)}, u32[]{:S(2)}) copy-start(f32[6144]{0:T(1024)S(1)} %constant_dynamic-update-slice_fusion.refs_5_) | copy-start | bytes 73732
  16.2 32.6 %collective-permute-start = (f32[6144]{0:T(1024)S(1)}, f32[6144]{0:T(1024)S(1)}, u32[]{:S(2)}, u32[]{:S(2)}) collective-permute-start(f32[6144]{0:T(1024)S(1)} %constant_dynamic-update-slice_fusion.refs_5_), channel_id=1, source_target_pairs={{0,2},{1,3},{2,0},{3,1},{4,6},{5,7},{6,4},{7,5},{8,10},{9,11},{10,... | collective-permute-start | bytes 73736 | tf_op jit(solution)/shard_map/ppermute | solution.py:650
  19.2 29.6 %collective-permute-start.1 = (f32[6144]{0:T(1024)S(1)}, f32[6144]{0:T(1024)S(1)}, u32[]{:S(2)}, u32[]{:S(2)}) collective-permute-start(f32[6144]{0:T(1024)S(1)} %constant_dynamic-update-slice_fusion.refs_5_), channel_id=1, source_target_pairs={{0,1},{1,0},{2,3},{3,2},{4,5},{5,4},{6,7},{7,6},{8,9},{9,8},{10,11... | collective-permute-start | bytes 73736 | tf_op jit(solution)/shard_map/ppermute | solution.py:650
  19.2 29.6 %collective-permute-start.2 = (f32[6144]{0:T(1024)S(1)}, f32[6144]{0:T(1024)S(1)}, u32[]{:S(2)}, u32[]{:S(2)}) collective-permute-start(f32[6144]{0:T(1024)S(1)} %constant_dynamic-update-slice_fusion.refs_5_), channel_id=1, source_target_pairs={{0,3},{1,2},{2,1},{3,0},{4,7},{5,6},{6,5},{7,4},{8,11},{9,10},{10,... | collective-permute-start | bytes 73736 | tf_op jit(solution)/shard_map/ppermute | solution.py:650
  22.3 131.9 %copy-start.14 = (bf16[1024,1024]{0,1:T(8,128)(2,1)}, bf16[1024,1024]{0,1:T(8,128)(2,1)S(1)}, u32[]{:S(2)}) copy-start(bf16[1024,1024]{0,1:T(8,128)(2,1)S(1)} %copy.201) | copy-start | bytes 6291460
  22.4 6.5 %copy-start.45 = (f32[256,32]{0,1:T(8,128)S(1)}, f32[256,32]{0,1:T(8,128)}, u32[]{:S(2)}) copy-start(f32[256,32]{0,1:T(8,128)} %param.25) | copy-start | bytes 98308
  22.4 7.2 %copy-start.40 = (f32[256]{0:T(256)S(1)}, f32[256]{0:T(256)}, u32[]{:S(2)}) copy-start(f32[256]{0:T(256)} %param.21) | copy-start | bytes 3076
  24.6 37.4 %collective-permute-start.10 = (bf16[2,128,1024]{2,1,0:T(8,128)(2,1)}, bf16[2,128,1024]{2,1,0:T(8,128)(2,1)}, u32[]{:S(2)}, u32[]{:S(2)}) collective-permute-start(bf16[2,128,1024]{2,1,0:T(8,128)(2,1)} %pad_maximum_fusion.refs_5_), channel_id=1, source_target_pairs={{0,2},{1,3},{2,0},{3,1},{4,6},{5,7},{6,4},{7,5},{8,10},{9,11},{10,... | collective-permute-start | bytes 1572872 | tf_op jit(solution)/shard_map/ppermute | solution.py:650
  30.4 19.1 %copy-start.54 = (f32[256]{0:T(256)S(1)}, f32[256]{0:T(256)}, u32[]{:S(2)}) copy-start(f32[256]{0:T(256)} %param.20) | copy-start | bytes 3076
  50.3 11.9 %copy-start.24 = (bf16[1024,2,256]{2,1,0:T(2,128)(2,1)S(1)}, bf16[1024,2,256]{2,1,0:T(2,128)(2,1)}, u32[]{:S(2)}) copy-start(bf16[1024,2,256]{2,1,0:T(2,128)(2,1)} %param.27) | copy-start | bytes 3145732
  62.1 24.7 %collective-permute-start.3 = (bf16[1024,1024]{1,0:T(8,128)(2,1)}, bf16[1024,1024]{1,0:T(8,128)(2,1)}, u32[]{:S(2)}, u32[]{:S(2)}) collective-permute-start(bf16[1024,1024]{1,0:T(8,128)(2,1)} %refs_4_.2), channel_id=1, source_target_pairs={{0,1},{1,0},{2,3},{3,2},{4,5},{5,4},{6,7},{7,6},{8,9},{9,8},{10,11... | collective-permute-start | bytes 6291464 | tf_op jit(solution)/shard_map/ppermute | solution.py:650
  64.7 29.4 %collective-permute-start.4 = (bf16[512,1024]{1,0:T(8,128)(2,1)}, bf16[512,1024]{1,0:T(8,128)(2,1)}, u32[]{:S(2)}, u32[]{:S(2)}) collective-permute-start(bf16[512,1024]{1,0:T(8,128)(2,1)} %bitcast.145), channel_id=1, source_target_pairs={{0,2},{1,3},{2,0},{3,1},{4,6},{5,7},{6,4},{7,5},{8,10},{9,11},{10,... | collective-permute-start | bytes 3145736 | tf_op jit(solution)/shard_map/ppermute | solution.py:650
  64.8 22.0 %all-to-all-start.1 = ((bf16[256,4,128]{2,1,0:T(4,128)(2,1)}), bf16[256,4,128]{2,1,0:T(4,128)(2,1)S(1)}, u32[]{:S(2)}, u32[]{:S(2)}) async-start(bf16[256,4,128]{2,1,0:T(4,128)(2,1)} %get-tuple-element.87), calls=%async_computation.1 | async-start | bytes 524288 | tf_op jit(solution)/shard_map/all_to_all | solution.py:784
  89.7 13.6 %all-to-all-start.2 = ((bf16[256,4,128]{2,1,0:T(4,128)(2,1)}), bf16[256,4,128]{2,1,0:T(4,128)(2,1)S(1)}, u32[]{:S(2)}, u32[]{:S(2)}) async-start(bf16[256,4,128]{2,1,0:T(4,128)(2,1)} %shard_map.314), calls=%async_computation.2 | async-start | bytes 524288 | tf_op jit(solution)/shard_map/all_to_all | solution.py:794
  94.1 29.2 %collective-permute-start.9 = (bf16[512,1024]{1,0:T(8,128)(2,1)}, bf16[512,1024]{1,0:T(8,128)(2,1)}, u32[]{:S(2)}, u32[]{:S(2)}) collective-permute-start(bf16[512,1024]{1,0:T(8,128)(2,1)} %collective-permute-done.4.refs_7_.refs_9_.refs_8_), channel_id=1, source_target_pairs={{0,1},{1,0},{2,3},{3,2},{4,5},{5,4},{6,7},{7,6},{8,9},{9,8},{10,11... | collective-permute-start | bytes 3145736 | tf_op jit(solution)/shard_map/ppermute | solution.py:650
  96.4 6.8 %copy-start.55 = (f32[256]{0:T(256)S(1)}, f32[256]{0:T(256)}, u32[]{:S(2)}) copy-start(f32[256]{0:T(256)} %param.26) | copy-start | bytes 3076
  97.8 21.4 %collective-permute-start.5 = (bf16[256,1024]{1,0:T(8,128)(2,1)}, bf16[256,1024]{1,0:T(8,128)(2,1)}, u32[]{:S(2)}, u32[]{:S(2)}) collective-permute-start(bf16[256,1024]{1,0:T(8,128)(2,1)} %get-tuple-element.266), channel_id=1, source_target_pairs={{0,2},{1,3},{2,0},{3,1},{4,6},{5,7},{6,4},{7,5},{8,10},{9,11},{10,... | collective-permute-start | bytes 1572872 | tf_op jit(solution)/shard_map/ppermute | solution.py:650
  99.6 19.7 %collective-permute-start.6 = (bf16[256,1024]{1,0:T(8,128)(2,1)}, bf16[256,1024]{1,0:T(8,128)(2,1)}, u32[]{:S(2)}, u32[]{:S(2)}) collective-permute-start(bf16[256,1024]{1,0:T(8,128)(2,1)} %get-tuple-element.265), channel_id=1, source_target_pairs={{0,1},{1,0},{2,3},{3,2},{4,5},{5,4},{6,7},{7,6},{8,9},{9,8},{10,11... | collective-permute-start | bytes 1572872 | tf_op jit(solution)/shard_map/ppermute | solution.py:650
  99.8 23.5 %collective-permute-start.7 = (bf16[256,1024]{1,0:T(8,128)(2,1)}, bf16[256,1024]{1,0:T(8,128)(2,1)}, u32[]{:S(2)}, u32[]{:S(2)}) collective-permute-start(bf16[256,1024]{1,0:T(8,128)(2,1)} %get-tuple-element.264), channel_id=1, source_target_pairs={{0,3},{1,2},{2,1},{3,0},{4,7},{5,6},{6,5},{7,4},{8,11},{9,10},{10,... | collective-permute-start | bytes 1572872 | tf_op jit(solution)/shard_map/ppermute | solution.py:650
  100.0 23.3 %collective-permute-start.8 = (bf16[512,1024]{1,0:T(8,128)(2,1)S(1)}, bf16[512,1024]{1,0:T(8,128)(2,1)}, u32[]{:S(2)}, u32[]{:S(2)}) collective-permute-start(bf16[512,1024]{1,0:T(8,128)(2,1)S(1)} %bitcast.148), channel_id=1, source_target_pairs={{0,1},{1,0},{2,3},{3,2},{4,5},{5,4},{6,7},{7,6},{8,9},{9,8},{10,11... | collective-permute-start | bytes 3145736 | tf_op jit(solution)/shard_map/ppermute | solution.py:650
  123.3 32.0 %copy-start.50 = (s32[4,1024]{1,0:T(4,128)S(1)}, s32[4,1024]{1,0:T(4,128)}, u32[]{:S(2)}) copy-start(s32[4,1024]{1,0:T(4,128)} %param.18) | copy-start | bytes 49156
  154.2 17.1 %collective-permute-start.12 = (bf16[8,2,128,1024]{3,2,1,0:T(8,128)(2,1)}, bf16[8,2,128,1024]{3,2,1,0:T(8,128)(2,1)}, u32[]{:S(2)}, u32[]{:S(2)}) collective-permute-start(bf16[8,2,128,1024]{3,2,1,0:T(8,128)(2,1)} %bitcast.174), channel_id=1, source_target_pairs={{0,1},{1,0},{2,3},{3,2},{4,5},{5,4},{6,7},{7,6},{8,9},{9,8},{10,11... | collective-permute-start | bytes 12582920 | tf_op jit(solution)/shard_map/ppermute | solution.py:650
  154.2 17.1 %collective-permute-start.11 = (bf16[1024,1024]{1,0:T(8,128)(2,1)S(1)}, bf16[1024,1024]{1,0:T(8,128)(2,1)}, u32[]{:S(2)}, u32[]{:S(2)}) collective-permute-start(bf16[1024,1024]{1,0:T(8,128)(2,1)S(1)} %bitcast.137), channel_id=1, source_target_pairs={{0,1},{1,0},{2,3},{3,2},{4,5},{5,4},{6,7},{7,6},{8,9},{9,8},{10,11... | collective-permute-start | bytes 6291464 | tf_op jit(solution)/shard_map/ppermute | solution.py:650
  208.9 44.2 %collective-permute-start.14 = (bf16[2,1024,1024]{2,1,0:T(8,128)(2,1)}, bf16[2,1024,1024]{2,1,0:T(8,128)(2,1)}, u32[]{:S(2)}, u32[]{:S(2)}) collective-permute-start(bf16[2,1024,1024]{2,1,0:T(8,128)(2,1)} %get-tuple-element.109), channel_id=1, source_target_pairs={{0,1},{1,0},{2,3},{3,2},{4,5},{5,4},{6,7},{7,6},{8,9},{9,8},{10,11... | collective-permute-start | bytes 12582920 | tf_op jit(solution)/shard_map/ppermute | solution.py:650
  209.1 54.6 %collective-permute-start.13 = (bf16[2048,1024]{1,0:T(8,128)(2,1)}, bf16[2048,1024]{1,0:T(8,128)(2,1)}, u32[]{:S(2)}, u32[]{:S(2)}) collective-permute-start(bf16[2048,1024]{1,0:T(8,128)(2,1)} %get-tuple-element.107), channel_id=1, source_target_pairs={{0,1},{1,0},{2,3},{3,2},{4,5},{5,4},{6,7},{7,6},{8,9},{9,8},{10,11... | collective-permute-start | bytes 12582920 | tf_op jit(solution)/shard_map/ppermute | solution.py:650
  261.8 50.6 %collective-permute-start.16 = (bf16[2,2,1,2,128,1024]{5,4,3,2,1,0:T(8,128)(2,1)}, bf16[2,2,1,2,128,1024]{5,4,3,2,1,0:T(8,128)(2,1)S(1)}, u32[]{:S(2)}, u32[]{:S(2)}) collective-permute-start(bf16[2,2,1,2,128,1024]{5,4,3,2,1,0:T(8,128)(2,1)} %constant_dynamic-slice_fusion.5.refs_13_), channel_id=1, source_target_pairs={{0,8},{4,12},{8,0},{12,4},{16,24},{20,28},{24,16},{28,20},{1,9},{5... | collective-permute-start | bytes 6291464 | tf_op jit(solution)/shard_map/ppermute | solution.py:650
  270.6 47.7 %collective-permute-start.15 = (bf16[2,2,2,1,128,1024]{5,4,3,2,1,0:T(8,128)(2,1)}, bf16[2,2,2,1,128,1024]{5,4,3,2,1,0:T(8,128)(2,1)}, u32[]{:S(2)}, u32[]{:S(2)}) collective-permute-start(bf16[2,2,2,1,128,1024]{5,4,3,2,1,0:T(8,128)(2,1)} %constant_dynamic-slice_fusion.6.refs_12_), channel_id=1, source_target_pairs={{0,4},{4,0},{8,12},{12,8},{16,20},{20,16},{24,28},{28,24},{1,5},{5... | collective-permute-start | bytes 6291464 | tf_op jit(solution)/shard_map/ppermute | solution.py:650
  300.7 30.5 %collective-permute-start.17 = (bf16[2,1024,512]{2,1,0:T(8,128)(2,1)}, bf16[2,1024,512]{2,1,0:T(8,128)(2,1)}, u32[]{:S(2)}, u32[]{:S(2)}) collective-permute-start(bf16[2,1024,512]{2,1,0:T(8,128)(2,1)} %get-tuple-element.116), channel_id=1, source_target_pairs={{0,1},{1,0},{2,3},{3,2},{4,5},{5,4},{6,7},{7,6},{8,9},{9,8},{10,11... | collective-permute-start | bytes 6291464 | tf_op jit(solution)/shard_map/ppermute | solution.py:650
  300.8 30.4 %all-to-all-start.4 = ((bf16[4,256,1024]{2,1,0:T(8,128)(2,1)}), bf16[4,256,1024]{2,1,0:T(8,128)(2,1)}, u32[]{:S(2)}, u32[]{:S(2)}) async-start(bf16[4,256,1024]{2,1,0:T(8,128)(2,1)} %bitcast.143), calls=%async_computation.4 | async-start | bytes 4194304 | tf_op jit(solution)/shard_map/all_to_all | solution.py:731
  312.0 51.3 %collective-permute-start.28 = (f32[2,2052]{1,0:T(2,128)S(1)}, f32[2,2052]{1,0:T(2,128)S(1)}, u32[]{:S(2)}, u32[]{:S(2)}) collective-permute-start(f32[2,2052]{1,0:T(2,128)S(1)} %pad_maximum_fusion.4), channel_id=1, source_target_pairs={{0,1},{1,0},{2,3},{3,2},{4,5},{5,4},{6,7},{7,6},{8,9},{9,8},{10,11... | collective-permute-start | bytes 49256 | tf_op jit(solution)/shard_map/ppermute | solution.py:650
  312.4 5.8 %copy-start.2 = (bf16[2048,1024]{1,0:T(8,128)(2,1)S(1)}, bf16[2048,1024]{1,0:T(8,128)(2,1)}, u32[]{:S(2)}) copy-start(bf16[2048,1024]{1,0:T(8,128)(2,1)} %copy-done.1) | copy-start | bytes 12582916
  315.9 61.2 %collective-permute-start.20 = (bf16[2,2,1,1,128,1024]{5,4,3,2,1,0:T(8,128)(2,1)S(1)}, bf16[2,2,1,1,128,1024]{5,4,3,2,1,0:T(8,128)(2,1)}, u32[]{:S(2)}, u32[]{:S(2)}) collective-permute-start(bf16[2,2,1,1,128,1024]{5,4,3,2,1,0:T(8,128)(2,1)S(1)} %constant_dynamic-slice_fusion.3.refs_3_), channel_id=1, source_target_pairs={{0,4},{4,0},{8,12},{12,8},{16,20},{20,16},{24,28},{28,24},{1,5},{5... | collective-permute-start | bytes 3145736 | tf_op jit(solution)/shard_map/ppermute | solution.py:650
  323.2 58.8 %collective-permute-start.18 = (bf16[2,2,1,1,128,1024]{5,4,3,2,1,0:T(8,128)(2,1)}, bf16[2,2,1,1,128,1024]{5,4,3,2,1,0:T(8,128)(2,1)}, u32[]{:S(2)}, u32[]{:S(2)}) collective-permute-start(bf16[2,2,1,1,128,1024]{5,4,3,2,1,0:T(8,128)(2,1)} %constant_dynamic-slice_fusion.4.refs_2_), channel_id=1, source_target_pairs={{0,8},{4,12},{8,0},{12,4},{16,24},{20,28},{24,16},{28,20},{1,9},{5... | collective-permute-start | bytes 3145736 | tf_op jit(solution)/shard_map/ppermute | solution.py:650
  343.7 13.1 %all-to-all-start.5 = ((bf16[256,4,128]{2,1,0:T(4,128)(2,1)}), bf16[256,4,128]{2,1,0:T(4,128)(2,1)S(1)}, u32[]{:S(2)}, u32[]{:S(2)}) async-start(bf16[256,4,128]{2,1,0:T(4,128)(2,1)} %get-tuple-element.117), calls=%async_computation.5 | async-start | bytes 524288 | tf_op jit(solution)/shard_map/all_to_all | solution.py:784
  359.7 12.2 %all-to-all-start.6 = ((bf16[256,4,128]{2,1,0:T(4,128)(2,1)}), bf16[256,4,128]{2,1,0:T(4,128)(2,1)S(1)}, u32[]{:S(2)}, u32[]{:S(2)}) async-start(bf16[256,4,128]{2,1,0:T(4,128)(2,1)} %shard_map.322), calls=%async_computation.6 | async-start | bytes 524288 | tf_op jit(solution)/shard_map/all_to_all | solution.py:794
  364.0 50.1 %collective-permute-start.22 = (bf16[2,2,2,1,128,512]{5,4,3,2,1,0:T(8,128)(2,1)}, bf16[2,2,2,1,128,512]{5,4,3,2,1,0:T(8,128)(2,1)}, u32[]{:S(2)}, u32[]{:S(2)}) collective-permute-start(bf16[2,2,2,1,128,512]{5,4,3,2,1,0:T(8,128)(2,1)} %constant_dynamic-slice_fusion.2.refs_4_), channel_id=1, source_target_pairs={{0,4},{4,0},{8,12},{12,8},{16,20},{20,16},{24,28},{28,24},{1,5},{5... | collective-permute-start | bytes 3145736 | tf_op jit(solution)/shard_map/ppermute | solution.py:650
  372.6 50.3 %all-to-all-start.7 = ((bf16[4,256,1024]{2,1,0:T(8,128)(2,1)}), bf16[4,256,1024]{2,1,0:T(8,128)(2,1)}, u32[]{:S(2)}, u32[]{:S(2)}) async-start(bf16[4,256,1024]{2,1,0:T(8,128)(2,1)} %bitcast.142), calls=%async_computation.7 | async-start | bytes 4194304 | tf_op jit(solution)/shard_map/all_to_all | solution.py:731
  377.1 185.9 %all-gather.7.cloned.1.call-start = ((), (), s32[]{:S(2)}) async-start(), calls=%async_computation.10 | async-start | bytes 4718592 | tf_op jit(solution)/shard_map/all_gather | solution.py:1108
  380.1 34.1 %collective-permute-start.21 = (bf16[1,2,1,1,128,1024]{5,4,3,2,1,0:T(8,128)(2,1)}, bf16[1,2,1,1,128,1024]{5,4,3,2,1,0:T(8,128)(2,1)S(1)}, u32[]{:S(2)}, u32[]{:S(2)}) collective-permute-start(bf16[1,2,1,1,128,1024]{5,4,3,2,1,0:T(8,128)(2,1)} %slice.409.refs_6_), channel_id=1, source_target_pairs={{0,2},{1,3},{2,0},{3,1},{4,6},{5,7},{6,4},{7,5},{8,10},{9,11},{10,... | collective-permute-start | bytes 1572872 | tf_op jit(solution)/shard_map/ppermute | solution.py:650
  384.6 29.6 %collective-permute-start.19 = (bf16[2,1,1,1,128,1024]{5,4,3,2,1,0:T(8,128)(2,1)}, bf16[2,1,1,1,128,1024]{5,4,3,2,1,0:T(8,128)(2,1)}, u32[]{:S(2)}, u32[]{:S(2)}) collective-permute-start(bf16[2,1,1,1,128,1024]{5,4,3,2,1,0:T(8,128)(2,1)} %constant_dynamic-slice_fusion.1.refs_5_), channel_id=1, source_target_pairs={{0,16},{4,20},{8,24},{12,28},{16,0},{20,4},{24,8},{28,12},{1,17},{... | collective-permute-start | bytes 1572872 | tf_op jit(solution)/shard_map/ppermute | solution.py:650
  385.7 26.4 %copy-start.7 = (f32[256,32]{1,0:T(8,128)S(1)}, f32[256,32]{1,0:T(8,128)}, u32[]{:S(2)}) copy-start(f32[256,32]{1,0:T(8,128)} %copy.197.refs_1_) | copy-start | bytes 98308
  385.7 26.4 %copy-start.8 = (f32[256,32]{1,0:T(8,128)S(1)}, f32[256,32]{1,0:T(8,128)}, u32[]{:S(2)}) copy-start(f32[256,32]{1,0:T(8,128)} %copy.198.refs_2_) | copy-start | bytes 98308
  385.7 26.4 %copy-start.41 = (f32[256]{0:T(256)S(1)}, f32[256]{0:T(256)}, u32[]{:S(2)}) copy-start(f32[256]{0:T(256)} %param.21) | copy-start | bytes 3076
  418.7 19.2 %collective-permute-start.25 = (bf16[1,2,2,1,128,512]{5,4,3,2,1,0:T(8,128)(2,1)}, bf16[1,2,2,1,128,512]{5,4,3,2,1,0:T(8,128)(2,1)}, u32[]{:S(2)}, u32[]{:S(2)}) collective-permute-start(bf16[1,2,2,1,128,512]{5,4,3,2,1,0:T(8,128)(2,1)} %slice.412.refs_14_), channel_id=1, source_target_pairs={{0,2},{1,3},{2,0},{3,1},{4,6},{5,7},{6,4},{7,5},{8,10},{9,11},{10,... | collective-permute-start | bytes 1572872 | tf_op jit(solution)/shard_map/ppermute | solution.py:650
  419.0 18.9 %copy-start.11 = (bf16[2,2,2,1,128,512]{5,4,3,2,1,0:T(8,128)(2,1)S(1)}, bf16[2,2,2,1,128,512]{5,4,3,2,1,0:T(8,128)(2,1)}, u32[]{:S(2)}) copy-start(bf16[2,2,2,1,128,512]{5,4,3,2,1,0:T(8,128)(2,1)} %copy-done.10) | copy-start | bytes 3145732
  419.1 17.8 %collective-permute-start.24 = (bf16[1,1,1,1,128,1024]{5,4,3,2,1,0:T(8,128)(2,1)S(1)}, bf16[1,1,1,1,128,1024]{5,4,3,2,1,0:T(8,128)(2,1)S(1)}, u32[]{:S(2)}, u32[]{:S(2)}) collective-permute-start(bf16[1,1,1,1,128,1024]{5,4,3,2,1,0:T(8,128)(2,1)S(1)} %constant_dynamic-slice_fusion.refs_13_), channel_id=1, source_target_pairs={{0,16},{4,20},{8,24},{12,28},{16,0},{20,4},{24,8},{28,12},{1,17},{... | collective-permute-start | bytes 786440 | tf_op jit(solution)/shard_map/ppermute | solution.py:650
  421.0 16.9 %collective-permute-start.23 = (bf16[1,1,1,1,128,1024]{5,4,3,2,1,0:T(8,128)(2,1)}, bf16[1,1,1,1,128,1024]{5,4,3,2,1,0:T(8,128)(2,1)S(1)}, u32[]{:S(2)}, u32[]{:S(2)}) collective-permute-start(bf16[1,1,1,1,128,1024]{5,4,3,2,1,0:T(8,128)(2,1)} %slice.410.refs_12_), channel_id=1, source_target_pairs={{0,2},{1,3},{2,0},{3,1},{4,6},{5,7},{6,4},{7,5},{8,10},{9,11},{10,... | collective-permute-start | bytes 786440 | tf_op jit(solution)/shard_map/ppermute | solution.py:650
  441.0 14.0 %copy-start.39 = (f32[128,128]{1,0:T(8,128)S(1)}, f32[128,128]{1,0:T(8,128)}, u32[]{:S(2)}) copy-start(f32[128,128]{1,0:T(8,128)} %get-tuple-element.136) | copy-start | bytes 196612
  441.0 15.1 %copy-start.38 = (f32[4104]{0:T(1024)S(1)}, f32[4104]{0:T(1024)}, u32[]{:S(2)}) copy-start(f32[4104]{0:T(1024)} %reshape.190) | copy-start | bytes 49252
  441.0 16.5 %copy-start.32 = (f32[4,128,128]{2,1,0:T(8,128)S(1)}, f32[4,128,128]{2,1,0:T(8,128)}, u32[]{:S(2)}) copy-start(f32[4,128,128]{2,1,0:T(8,128)} %get-tuple-element.134) | copy-start | bytes 786436
  458.2 9.9 %collective-permute-start.29 = (f32[293,128]{1,0:T(8,128)S(1)}, f32[293,128]{1,0:T(8,128)S(1)}, u32[]{:S(2)}, u32[]{:S(2)}) collective-permute-start(f32[293,128]{1,0:T(8,128)S(1)} %pad_maximum_fusion.2), channel_id=1, source_target_pairs={{0,4},{4,0},{8,12},{12,8},{16,20},{20,16},{24,28},{28,24},{1,5},{5... | collective-permute-start | bytes 450056 | tf_op jit(solution)/shard_map/ppermute | solution.py:650
  459.4 1.2 collective-permute-start.26
  460.6 7.4 %collective-permute-start.27 = (f32[32,128]{1,0:T(8,128)S(1)}, f32[32,128]{1,0:T(8,128)S(1)}, u32[]{:S(2)}, u32[]{:S(2)}) collective-permute-start(f32[32,128]{1,0:T(8,128)S(1)} %add.245), channel_id=1, source_target_pairs={{0,2},{1,3},{2,0},{3,1},{4,6},{5,7},{6,4},{7,5},{8,10},{9,11},{10,... | collective-permute-start | bytes 49160 | tf_op jit(solution)/shard_map/ppermute | solution.py:650
  461.3 60.8 %collective-permute-start.32 = (bf16[1,2,2,1,128,512]{5,4,3,2,1,0:T(8,128)(2,1)S(1)}, bf16[1,2,2,1,128,512]{5,4,3,2,1,0:T(8,128)(2,1)S(1)}, u32[]{:S(2)}, u32[]{:S(2)}) collective-permute-start(bf16[1,2,2,1,128,512]{5,4,3,2,1,0:T(8,128)(2,1)S(1)} %copy-done.16), channel_id=1, source_target_pairs={{0,16},{4,20},{8,24},{12,28},{16,0},{20,4},{24,8},{28,12},{1,17},{... | collective-permute-start | bytes 1572872 | tf_op jit(solution)/shard_map/ppermute | solution.py:650
  463.2 95.5 %all-to-all-start.8 = ((bf16[4,256,1024]{2,1,0:T(8,128)(2,1)}), bf16[4,256,1024]{2,1,0:T(8,128)(2,1)}, u32[]{:S(2)}, u32[]{:S(2)}) async-start(bf16[4,256,1024]{2,1,0:T(8,128)(2,1)} %bitcast.139), calls=%async_computation.8 | async-start | bytes 4194304 | tf_op jit(solution)/shard_map/all_to_all | solution.py:731
  468.1 11.6 %collective-permute-start.30 = (f32[293,128]{1,0:T(8,128)S(1)}, f32[293,128]{1,0:T(8,128)S(1)}, u32[]{:S(2)}, u32[]{:S(2)}) collective-permute-start(f32[293,128]{1,0:T(8,128)S(1)} %add.262), channel_id=1, source_target_pairs={{0,8},{4,12},{8,0},{12,4},{16,24},{20,28},{24,16},{28,20},{1,9},{5... | collective-permute-start | bytes 450056 | tf_op jit(solution)/shard_map/ppermute | solution.py:650
  479.8 37.7 %collective-permute-start.31 = (f32[293,128]{1,0:T(8,128)S(1)}, f32[293,128]{1,0:T(8,128)S(1)}, u32[]{:S(2)}, u32[]{:S(2)}) collective-permute-start(f32[293,128]{1,0:T(8,128)S(1)} %add.263), channel_id=1, source_target_pairs={{0,16},{4,20},{8,24},{12,28},{16,0},{20,4},{24,8},{28,12},{1,17},{... | collective-permute-start | bytes 450056 | tf_op jit(solution)/shard_map/ppermute | solution.py:650
  484.5 35.9 %copy-start.26 = (f32[256,32]{1,0:T(8,128)S(1)}, f32[256,32]{1,0:T(8,128)}, u32[]{:S(2)}) copy-start(f32[256,32]{1,0:T(8,128)} %copy.199.refs_3_) | copy-start | bytes 98308
  484.5 35.9 %copy-start.27 = (f32[256,32]{1,0:T(8,128)S(1)}, f32[256,32]{1,0:T(8,128)}, u32[]{:S(2)}) copy-start(f32[256,32]{1,0:T(8,128)} %copy.200.refs_4_) | copy-start | bytes 98308
  517.7 8.8 %collective-permute-start.35 = (f32[2052]{0:T(1024)S(1)}, f32[2052]{0:T(1024)S(1)}, u32[]{:S(2)}, u32[]{:S(2)}) collective-permute-start(f32[2052]{0:T(1024)S(1)} %slice.460), channel_id=1, source_target_pairs={{0,2},{1,3},{2,0},{3,1},{4,6},{5,7},{6,4},{7,5},{8,10},{9,11},{10,... | collective-permute-start | bytes 24632 | tf_op jit(solution)/shard_map/ppermute | solution.py:650
  522.2 20.0 %collective-permute-start.33 = (bf16[1,2,2,1,128,512]{5,4,3,2,1,0:T(8,128)(2,1)S(1)}, bf16[1,2,2,1,128,512]{5,4,3,2,1,0:T(8,128)(2,1)S(1)}, u32[]{:S(2)}, u32[]{:S(2)}) collective-permute-start(bf16[1,2,2,1,128,512]{5,4,3,2,1,0:T(8,128)(2,1)S(1)} %add_convert_fusion.9), channel_id=1, source_target_pairs={{0,8},{4,12},{8,0},{12,4},{16,24},{20,28},{24,16},{28,20},{1,9},{5... | collective-permute-start | bytes 1572872 | tf_op jit(solution)/shard_map/ppermute | solution.py:650
  542.3 13.8 %collective-permute-start.34 = (bf16[1,2,2,1,128,512]{5,4,3,2,1,0:T(8,128)(2,1)S(1)}, bf16[1,2,2,1,128,512]{5,4,3,2,1,0:T(8,128)(2,1)S(1)}, u32[]{:S(2)}, u32[]{:S(2)}) collective-permute-start(bf16[1,2,2,1,128,512]{5,4,3,2,1,0:T(8,128)(2,1)S(1)} %add_convert_fusion.8), channel_id=1, source_target_pairs={{0,4},{4,0},{8,12},{12,8},{16,20},{20,16},{24,28},{28,24},{1,5},{5... | collective-permute-start | bytes 1572872 | tf_op jit(solution)/shard_map/ppermute | solution.py:650
  (38 other events, 96.1 us)
Sparse Core Ops, SparseCore 0:
  62.2 79.6 all-gather.4
  441.1 92.0 all-gather.6

commit v5 on v4

--- a/solution.py
+++ b/solution.py
@@ -975,11 +975,27 @@
     cubes = split + (-1, D)
     first, second, third, rest = bits[0], bits[1], bits[2], bits[3:]
     upper_bit = 0
-    s_kept, s_sent, s_there = sent_down(added(shrink_near_g, core_shrink).reshape(cubes), first)
-    e_kept, e_sent, e_there = sent_down(added(expand_near_g, core_expand).reshape(split + (-1, hidden_own)), second)
-
     def onwards(kept, there, bit):
-        return sent_down(added(kept, there), bit)
+        if bit == upper_bit:
+            stays, sent = (added(kept[part_k], there[part_k]) for part_k in (slice(0, 1), slice(1, 2)))
+            return stays, sent, swap(sent, "mp", 2)
+        mine = (seq_me // bit) % 2
+        stays, sent = (
+            added(
+                lax.dynamic_slice_in_dim(kept, which, 1, axis_of(bit)),
+                lax.dynamic_slice_in_dim(there, which, 1, axis_of(bit)),
+            )
+            for which in (mine, 1 - mine)
+        )
+        return stays, sent, swap(sent, "seq", bit)
+
+    s_kept, s_sent, s_there = onwards(
+        shrink_near_g.reshape(cubes), core_shrink.reshape(cubes), first
+    )
+    wide_cubes = split + (-1, hidden_own)
+    e_kept, e_sent, e_there = onwards(
+        expand_near_g.reshape(wide_cubes), core_expand.reshape(wide_cubes), second
+    )
 
     sums_out = out((mp, 4, features, min(128, token_block)), f32)
     grad_lifted_one, grad_hidden, both_g, sums = by_tokens(
@@ -1107,7 +1123,9 @@
     both_parts = jnp.stack([s_all.reshape(-1, D), e_all.reshape(-1, hidden_own)])
     both_all = lax.all_gather(both_parts, "seq", axis=0)
     high = back(half, (both_parts, g_all, low[2]))
-    g_all = exchange(g_all, third, high[2])
+    there = [swap(g_all, "seq", mask) for mask in (second, third, second + third)]
+    there = after(there, high[2])
+    g_all = sum(v.astype(f32) for v in [g_all] + there).astype(bf16)
     result = returned(after(result, (own_hidden, low[2])))
     grad_first_gain = jnp.sum(jnp.concatenate([low[3], high[3]]), axis=1)
 
@@ -1182,9 +1200,10 @@
         axis=0,
     )
     for bit in bits:
+        if bit == third:
+            late = after(late, g_all)
         late = late + swap(late, "seq", bit)
-    g_all = exchange(g_all, second, grad_inputs)
-    g_all = up_step(g_all, first, late)
+    g_all = up_step(g_all, first, grad_inputs)
     result = result.reshape(contexts, features, local)
     (result,) = by_channel(
         turned_kernel, 2 * block, features, [(result, 1)], [(out(inputs.shape, bf16), 0)], 5

time: 588 us -> 576 us (0.980)
  waiting for transfers between devices: 98.1 us -> 81.6 us
  local copies, waits for them, and re-layouts: 59.3 us -> 47.4 us
  other arithmetic: 54.9 us -> 65 us
  starting transfers between devices: 72.7 us -> 79 us
    ppermute x36 -> x37, waiting for transfers between devices: 63.6 us -> 35.7 us  [swap(): return lax.ppermute(values, axis, [(i, i ^ bit) for i in range(size)])]
    convert_element_type x13 -> x11, other arithmetic: 27.6 us -> 36.4 us  [added(): return (a.astype(f32) + b.astype(f32)).astype(bf16)]
    all_gather x1, waiting for transfers between devices: 0.01 us -> 7.71 us  [shards(): both_all = lax.all_gather(both_parts, 'seq', axis=0)]
    ppermute x36 -> x37, starting transfers between devices: 35.5 us -> 42.5 us  [swap(): return lax.ppermute(values, axis, [(i, i ^ bit) for i in range(size)])]
    unnamed x132 -> x120, local copies, waits for them, and re-layouts: 16.1 us -> 12.3 us
  transfers between devices with their start and end apart: 46 -> 47, of which waited for: 13 -> 12; matrix products, arithmetic and copies ran while one was open for 16% -> 17% of each run, Pallas kernels for 36% -> 37%
where the time goes in v5:
time: 576 us; the launch traced here: 566 us
  Pallas kernels  246 us (43%)
  waiting for transfers between devices  81.6 us (14%)
  starting transfers between devices  79 us (14%)
  other arithmetic  65 us (11%)
  local copies, waits for them, and re-layouts  47.4 us (8%)
  blocking collectives  30.8 us (5%)
  between operations  16.5 us (3%)
    pallas_call x16, Pallas kernels, over_blocks(): pl.pallas_call(run, grid=(steps,), in_specs=[pl.BlockSpec(memory_space=pl...  246 us
    ppermute x37, starting transfers between devices, swap(): return lax.ppermute(values, axis, [(i, i ^ bit) for i in range(size)])  42.5 us
    convert_element_type x11, other arithmetic, added(): return (a.astype(f32) + b.astype(f32)).astype(bf16)  36.4 us
    ppermute x37, waiting for transfers between devices, swap(): return lax.ppermute(values, axis, [(i, i ^ bit) for i in range(size)])  35.7 us
    all_to_all x1, blocking collectives, shards(): lax.all_to_all(lifted_sent, 'mp', 0, 0, tiled=True).reshape(D, tokens)  30.8 us
    all_to_all x2, waiting for transfers between devices, handed(): terms = lax.all_to_all(ends, 'seq', 0, 0, tiled=True)  19.2 us
    all_to_all x3, starting transfers between devices, returned(): lax.all_to_all(values.reshape(mp, features, local), 'mp', 0, 0, tiled=True)  14 us
    unnamed x120, local copies, waits for them, and re-layouts  12.3 us
  transfers between devices with their start and end apart: 47, of which 12 were waited for; matrix products, arithmetic and copies ran while one was open for 17% of the time, Pallas kernels for 37%

profile of v5, /device:TPU:0, one launch (start us, length us, event | category | flops | bytes accessed | tf_op | source)
XLA Modules:
  0.0 566.0 jit_solution(2177984101890707010)
XLA Ops:
  7.2 3.5 copy.247
  10.7 4.6 all-to-all-start
  16.2 3.0 collective-permute-start
  19.4 2.9 copy.201
  24.6 1.9 collective-permute-start.10
  30.3 18.4 %shard_map.312 = (f32[256,8,128]{2,1,0:T(8,128)}, f32[256,2,128]{2,1,0:T(2,128)}, bf16[256,128,128]{2,1,0:T(8,128)(2,1)}, bf16[256,128,128]{2,1,0:T(8,128)(2,1)}, f32[256,128]{1,0:T(8,128)}) custom-call(f32[256,1]{1,0:T(8,128)} %copy.196.refs_0_, f32[256,32]{1,0:T(8,128)} %copy.197.refs_1_, f32[256,32]{1,0:T(8,128)} %copy.198.refs_2_, ...), custom_call_target="tpu_custom_call" | custom-call | flops 10000000000 | bytes 18351104 | tf_op jit(solution)/shard_map/pallas_call | solution.py:451
  50.2 11.8 %shard_map.313 = (bf16[256,32,128]{2,1,0:T(8,128)(2,1)}, f32[256,32,128]{2,1,0:T(8,128)}, bf16[256,4,128]{2,1,0:T(4,128)(2,1)}) custom-call(bf16[4,256,1024]{2,1,0:T(8,128)(2,1)} %bitcast.131, f32[32,128]{1,0:T(8,128)} %reshape.181.refs_1_.refs_10_, f32[256,128]{1,0:T(8,128)} %broadcast_in_dim.34.refs_2_.refs_11_.refs_6_, ...), custom_call_target="tpu_custom_call" | custom-call | flops 8000000000 | bytes 18235392 | tf_op jit(solution)/shard_map/pallas_call | solution.py:451
  62.1 2.6 copy.202
  64.7 6.2 %all-to-all-start.1 = ((bf16[256,4,128]{2,1,0:T(4,128)(2,1)}), bf16[256,4,128]{2,1,0:T(4,128)(2,1)S(1)}, u32[]{:S(2)}, u32[]{:S(2)}) async-start(bf16[256,4,128]{2,1,0:T(4,128)(2,1)} %get-tuple-element.89), calls=%async_computation.1 | async-start | bytes 524288 | tf_op jit(solution)/shard_map/all_to_all | solution.py:784
  72.3 14.4 %all-to-all-done.1.refs_0_ = bf16[256,4,128]{2,1,0:T(4,128)(2,1)S(1)} async-done(((bf16[256,4,128]{2,1,0:T(4,128)(2,1)}), bf16[256,4,128]{2,1,0:T(4,128)(2,1)S(1)}, u32[]{:S(2)}, u32[]{:S(2)}) %all-to-all-start.1) | async-done | bytes 262176 | tf_op jit(solution)/shard_map/all_to_all | solution.py:784
  87.5 2.2 shard_map.314
  89.7 4.4 all-to-all-start.2
  94.2 2.2 copy.203
  97.8 1.7 collective-permute-start.5
  100.2 3.1 all-to-all-done.2.refs_2_
  104.0 15.3 %shard_map.315 = (bf16[256,32,128]{2,1,0:T(8,128)(2,1)}, f32[256,32,128]{2,1,0:T(8,128)}, bf16[4,256,1024]{2,1,0:T(8,128)(2,1)}) custom-call(bf16[256,32,128]{2,1,0:T(8,128)(2,1)} %get-tuple-element.87.refs_0_.refs_1_.refs_3_, f32[256,32,128]{2,1,0:T(8,128)} %get-tuple-element.88.refs_1_, bf16[256,4,128]{2,1,0:T(4,128)(2,1)} %copy-done.27, ...), custom_call_target="tpu_custom_call" | custom-call | flops 14000000000 | bytes 24641536 | tf_op jit(solution)/shard_map/pallas_call | solution.py:451
  119.3 4.0 collective-permute-done.7.refs_7_
  123.3 30.8 %all_to_all.45 = bf16[4,256,1024]{2,1,0:T(8,128)(2,1)} all-to-all(bf16[4,256,1024]{2,1,0:T(8,128)(2,1)} %get-tuple-element.96), channel_id=1, replica_groups=mesh['seq'=8,'mp'=4] {'mp'}, dimensions={0} | all-to-all | bytes 4194304 | tf_op jit(solution)/shard_map/all_to_all | solution.py:877
  158.3 12.9 %shard_map.316 = (bf16[1024,1024]{1,0:T(8,128)(2,1)}, f32[1024,1024]{1,0:T(8,128)}, bf16[1024,1024]{1,0:T(8,128)(2,1)}, f32[1024,1024]{1,0:T(8,128)}, f32[1024,1024]{1,0:T(8,128)}, /*index=5*/f32[8,1024]{1,0:T(8,128)}) custom-call(s32[4]{0:T(128)} %pad_add_fusion.refs_0_, f32[1,1024]{1,0:T(1,128)} %fusion.19.refs_1_, bf16[1024,1024]{1,0:T(8,128)(2,1)} %bitcast.142, ...), custom_call_target="tpu_custom_call" | custom-call | flops 12000000000 | bytes 28872720 | tf_op jit(solution)/shard_map/pallas_call | solution.py:451
  172.5 36.3 %shard_map.317 = (f32[1024,1024]{1,0:T(8,128)}, f32[1024,1024]{1,0:T(8,128)}, bf16[2048,1024]{1,0:T(8,128)(2,1)}, bf16[2,1024,1024]{2,1,0:T(8,128)(2,1)}, f32[2048,128]{1,0:T(8,128)}) custom-call(bf16[1024,1024]{1,0:T(8,128)(2,1)} %get-tuple-element.97.refs_0_, bf16[1024,1024]{1,0:T(8,128)(2,1)} %get-tuple-element.98.refs_1_.refs_5_, ...), custom_call_target="tpu_custom_call" | custom-call | flops 38000001024 | bytes 35651584 | tf_op jit(solution)/shard_map/pallas_call | solution.py:451
  210.7 38.9 %shard_map.318 = (f32[1024,1024]{1,0:T(8,128)}, f32[1024,1024]{1,0:T(8,128)}, bf16[2048,1024]{1,0:T(8,128)(2,1)}, bf16[2,1024,1024]{2,1,0:T(8,128)(2,1)}, f32[2048,128]{1,0:T(8,128)}) custom-call(bf16[1024,1024]{1,0:T(8,128)(2,1)} %get-tuple-element.97.refs_0_, bf16[1024,1024]{1,0:T(8,128)(2,1)} %get-tuple-element.98.refs_1_.refs_5_, ...), custom_call_target="tpu_custom_call" | custom-call | flops 38000001024 | bytes 44040192 | tf_op jit(solution)/shard_map/pallas_call | solution.py:451
  249.7 7.9 %add_convert_fusion.1 = (bf16[2,2,1,2,128,1024]{5,4,3,2,1,0:T(8,128)(2,1)}, bf16[2,2,1,2,128,1024]{5,4,3,2,1,0:T(8,128)(2,1)}) fusion(bf16[2,2,2,2,128,1024]{5,4,3,2,1,0:T(8,128)(2,1)} %bitcast.28, s32[]{:T(128)S(6)} %select_n.121, bf16[2,2,2,2,128,1024]{5,4,3,2,1,0:T(8,128)(2,1)} %bitcast.136, s32[]{:T(128)S(6)} %select_n.119), kind=kLoop, calls=%fused_computation.1 | loop fusion | flops 8388608 | bytes 12582920 | tf_op jit(solution)/shard_map/convert_element_type | solution.py:654
  257.6 1.9 collective-permute-start.16
  259.5 5.8 %add_convert_fusion.2 = (bf16[2,2,2,1,128,1024]{5,4,3,2,1,0:T(8,128)(2,1)S(1)}, bf16[2,2,2,1,128,1024]{5,4,3,2,1,0:T(8,128)(2,1)}) fusion(bf16[2,2,2,2,128,1024]{5,4,3,2,1,0:T(8,128)(2,1)} %bitcast.26, s32[]{:T(128)S(6)} %select_n.120, bf16[2,2,2,2,128,1024]{5,4,3,2,1,0:T(8,128)(2,1)S(1)} %bitcast.135, s32[]{:T(128)S(6)} %select_n.116), kind=kLoop, calls=%fused_computation.2 | loop fusion | flops 8388608 | bytes 12582920 | tf_op jit(solution)/shard_map/convert_element_type | solution.py:654
  266.8 15.2 %shard_map.319 = (bf16[1024,1024]{1,0:T(8,128)(2,1)}, bf16[1024,1024]{1,0:T(8,128)(2,1)}, bf16[2048,1024]{1,0:T(8,128)(2,1)}, f32[4,4,256,128]{3,2,1,0:T(8,128)}) custom-call(s32[4]{0:T(128)} %pad_add_fusion.refs_0_, f32[1024,1024]{1,0:T(8,128)} %get-tuple-element.103.refs_1_, f32[1024,1024]{1,0:T(8,128)} %get-tuple-element.104.refs_2_.refs_3_, ...), custom_call_target="tpu_custom_call" | custom-call | flops 14000000000 | bytes 34111504 | tf_op jit(solution)/shard_map/pallas_call | solution.py:451
  283.0 12.5 %shard_map.320 = (bf16[2,1024,512]{2,1,0:T(8,128)(2,1)}, bf16[2,1024,512]{2,1,0:T(8,128)(2,1)}, bf16[1024,1024]{1,0:T(8,128)(2,1)}, f32[8,1024]{1,0:T(8,128)}) custom-call(s32[4]{0:T(128)} %pad_add_fusion.refs_0_, bf16[2048,1024]{1,0:T(8,128)(2,1)} %get-tuple-element.112.refs_1_, bf16[1024,1024]{1,0:T(8,128)(2,1)} %bitcast.143, ...), custom_call_target="tpu_custom_call" | custom-call | flops 10000000000 | bytes 21528592 | tf_op jit(solution)/shard_map/pallas_call | solution.py:451
  297.6 4.7 all-to-all-start.4
  303.7 2.7 pad_maximum_fusion.5
  306.4 2.2 reduce_sum.118
  309.2 4.2 add_convert_fusion.5
  314.0 3.8 add_convert_fusion.6
  318.0 10.0 %all-to-all-done.4.refs_0_ = bf16[4,256,1024]{2,1,0:T(8,128)(2,1)} async-done(((bf16[4,256,1024]{2,1,0:T(8,128)(2,1)}), bf16[4,256,1024]{2,1,0:T(8,128)(2,1)}, u32[]{:S(2)}, u32[]{:S(2)}) %all-to-all-start.4) | async-done | bytes 2097184 | tf_op jit(solution)/shard_map/all_to_all | solution.py:731
  328.0 12.4 %shard_map.321 = (bf16[256,32,128]{2,1,0:T(8,128)(2,1)}, f32[256,32,128]{2,1,0:T(8,128)}, bf16[256,4,128]{2,1,0:T(4,128)(2,1)}) custom-call(bf16[4,256,1024]{2,1,0:T(8,128)(2,1)} %all-to-all-done.4.refs_0_, bf16[256,32,128]{2,1,0:T(8,128)(2,1)} %get-tuple-element.117.refs_1_, bf16[256,128,128]{2,1,0:T(8,128)(2,1)} %get-tuple-element.91.refs_3_.refs_2_.refs_4_, ...), custom_call_target="tpu_custom_call" | custom-call | flops 10000000000 | bytes 20185088 | tf_op jit(solution)/shard_map/pallas_call | solution.py:451
  340.4 3.7 all-to-all-start.5
  344.1 2.8 add_convert_fusion
  348.0 4.8 all-to-all-done.5.refs_0_
  353.5 2.2 shard_map.322
  355.7 3.6 all-to-all-start.6
  360.0 2.0 collective-permute-start.22
  362.0 5.9 %all-to-all-done.6.refs_7_.refs_2_ = bf16[256,4,128]{2,1,0:T(4,128)(2,1)S(1)} async-done(((bf16[256,4,128]{2,1,0:T(4,128)(2,1)}), bf16[256,4,128]{2,1,0:T(4,128)(2,1)S(1)}, u32[]{:S(2)}, u32[]{:S(2)}) %all-to-all-start.6) | async-done | bytes 262176 | tf_op jit(solution)/shard_map/all_to_all | solution.py:794
  368.6 4.4 all-to-all-start.7
  373.1 2.5 add_convert_fusion.13
  375.6 1.9 collective-permute-start.21
  377.5 2.4 add_convert_fusion.15
  381.0 23.4 %shard_map.323.refs_15_ = f32[7,256,128]{2,1,0:T(8,128)} custom-call(bf16[256,32,128]{2,1,0:T(8,128)(2,1)} %get-tuple-element.122.refs_0_, bf16[256,32,128]{2,1,0:T(8,128)(2,1)} %get-tuple-element.87.refs_0_.refs_1_.refs_3_, f32[256,32,128]{2,1,0:T(8,128)} %get-tuple-element.124.refs_2_.refs_4_, f32[256,32,128]{2,1,0:T(8,128)} %get-tuple-element.123.refs_3_.refs_1_, ...), custom_call_target="tpu_custom_call" | custom-call | flops 20000000000 | bytes 21889024 | tf_op jit(solution)/shard_map/pallas_call | solution.py:451
  404.4 1.9 slice_bitcast_fusion.3
  410.0 2.0 add_convert_fusion.12.refs_14_
  412.4 1.7 add_convert_fusion.21.refs_13_
  415.2 1.7 add_convert_fusion.22.refs_12_
  416.9 1.8 collective-permute-start.23
  418.8 13.9 %shard_map.324 = (bf16[4,128,1024]{2,1,0:T(8,128)(2,1)}, f32[4,128,128]{2,1,0:T(8,128)}, f32[32,128]{1,0:T(8,128)}, f32[128,128]{1,0:T(8,128)}) custom-call(bf16[256,32,128]{2,1,0:T(8,128)(2,1)} %get-tuple-element.122.refs_0_, f32[256,32,128]{2,1,0:T(8,128)} %get-tuple-element.123.refs_3_.refs_1_, bf16[256,4,128]{2,1,0:T(4,128)(2,1)} %copy-done.25, ...), custom_call_target="tpu_custom_call" | custom-call | flops 12000000000 | bytes 26181632 | tf_op jit(solution)/shard_map/pallas_call | solution.py:451
  437.7 1.7 collective-permute-start.33
  441.6 14.0 %shard_map.326 = (bf16[4,128,1024]{2,1,0:T(8,128)(2,1)}, f32[4,128,128]{2,1,0:T(8,128)}, f32[32,128]{1,0:T(8,128)}, f32[128,128]{1,0:T(8,128)}) custom-call(bf16[256,32,128]{2,1,0:T(8,128)(2,1)} %get-tuple-element.122.refs_0_, f32[256,32,128]{2,1,0:T(8,128)} %get-tuple-element.123.refs_3_.refs_1_, bf16[256,4,128]{2,1,0:T(4,128)(2,1)} %copy-done.25, ...), custom_call_target="tpu_custom_call" | custom-call | flops 12000000000 | bytes 26181632 | tf_op jit(solution)/shard_map/pallas_call | solution.py:451
  461.7 4.9 all-to-all-start.8
  467.4 20.7 %collective-permute-done.30 = f32[293,128]{1,0:T(8,128)S(1)} collective-permute-done((f32[293,128]{1,0:T(8,128)S(1)}, f32[293,128]{1,0:T(8,128)S(1)}, u32[]{:S(2)}, u32[]{:S(2)}) %collective-permute-start.30) | collective-permute-done | bytes 150048 | tf_op jit(solution)/shard_map/ppermute | solution.py:650
  489.5 12.9 %collective-permute-start.34 = (f32[293,128]{1,0:T(8,128)S(1)}, f32[293,128]{1,0:T(8,128)S(1)}, u32[]{:S(2)}, u32[]{:S(2)}) collective-permute-start(f32[293,128]{1,0:T(8,128)S(1)} %add.314), channel_id=1, source_target_pairs={{0,16},{4,20},{8,24},{12,28},{16,0},{20,4},{24,8},{28,12},{1,17},{... | collective-permute-start | bytes 450056 | tf_op jit(solution)/shard_map/ppermute | solution.py:650
  502.5 12.1 %shard_map.327 = f32[256,4,1024]{2,1,0:T(4,128)} custom-call(bf16[4,256,1024]{2,1,0:T(8,128)(2,1)} %bitcast.134, bf16[4,128,1024]{2,1,0:T(8,128)(2,1)} %get-tuple-element.130.refs_1_, bf16[4,128,1024]{2,1,0:T(8,128)(2,1)} %get-tuple-element.134.refs_2_, bf16[4,256,1024]{2,1,0:T(8,128)(2,1)} %all-to-all-done.7.refs_16_.refs_3_, f32[4,1024]{1,0:T(4,128)} %copy-done.30, ...), custom_call_target="tpu_custom_call" | custom-call | flops 8000000000 | bytes 10649600 | tf_op jit(solution)/shard_map/pallas_call | solution.py:451
  527.4 8.8 %collective-permute-done.35 = bf16[1,2,2,1,128,512]{5,4,3,2,1,0:T(8,128)(2,1)S(1)} collective-permute-done((bf16[1,2,2,1,128,512]{5,4,3,2,1,0:T(8,128)(2,1)S(1)}, bf16[1,2,2,1,128,512]{5,4,3,2,1,0:T(8,128)(2,1)S(1)}, u32[]{:S(2)}, u32[]{:S(2)}) %collective-permute-start.35) | collective-permute-done | bytes 524320 | tf_op jit(solution)/shard_map/ppermute | solution.py:650
  536.4 2.4 reshape.202
  538.7 4.3 shard_map.325
  543.0 7.7 %all-gather.7.cloned.1.call-done = bf16[16,128,1024]{2,1,0:T(8,128)(2,1)} async-done(((bf16[2,128,1024]{2,1,0:T(8,128)(2,1)}), bf16[16,128,1024]{2,1,0:T(8,128)(2,1)}) %all-gather.7.cloned.1.call-update) | async-done | bytes 4194320 | tf_op jit(solution)/shard_map/all_gather | solution.py:1124
  550.8 2.7 fusion.28
  553.5 2.6 bitcast_convert_fusion
  556.1 2.6 bitcast_convert_fusion.1
  (278 shorter events, 65.2 us)
Async XLA Ops:
  10.7 38.7 %all-to-all-start = ((bf16[4,256,1024]{2,1,0:T(8,128)(2,1)}), bf16[4,256,1024]{2,1,0:T(8,128)(2,1)}, u32[]{:S(2)}, u32[]{:S(2)}) async-start(bf16[4,256,1024]{2,1,0:T(8,128)(2,1)} %bitcast.130), calls=%async_computation | async-start | bytes 4194304 | tf_op jit(solution)/shard_map/all_to_all | solution.py:758
  15.4 138.7 %all-gather.5.cloned.1.call-start = ((), (), s32[]{:S(2)}) async-start(), calls=%async_computation.9 | async-start | bytes 4718592 | tf_op jit(solution)/shard_map/all_gather | solution.py:847
  16.2 32.5 %collective-permute-start = (f32[6144]{0:T(1024)S(1)}, f32[6144]{0:T(1024)S(1)}, u32[]{:S(2)}, u32[]{:S(2)}) collective-permute-start(f32[6144]{0:T(1024)S(1)} %constant_dynamic-update-slice_fusion.refs_5_), channel_id=1, source_target_pairs={{0,2},{1,3},{2,0},{3,1},{4,6},{5,7},{6,4},{7,5},{8,10},{9,11},{10,... | collective-permute-start | bytes 73736 | tf_op jit(solution)/shard_map/ppermute | solution.py:650
  19.2 29.5 %collective-permute-start.1 = (f32[6144]{0:T(1024)S(1)}, f32[6144]{0:T(1024)S(1)}, u32[]{:S(2)}, u32[]{:S(2)}) collective-permute-start(f32[6144]{0:T(1024)S(1)} %constant_dynamic-update-slice_fusion.refs_5_), channel_id=1, source_target_pairs={{0,1},{1,0},{2,3},{3,2},{4,5},{5,4},{6,7},{7,6},{8,9},{9,8},{10,11... | collective-permute-start | bytes 73736 | tf_op jit(solution)/shard_map/ppermute | solution.py:650
  19.2 29.6 %collective-permute-start.2 = (f32[6144]{0:T(1024)S(1)}, f32[6144]{0:T(1024)S(1)}, u32[]{:S(2)}, u32[]{:S(2)}) collective-permute-start(f32[6144]{0:T(1024)S(1)} %constant_dynamic-update-slice_fusion.refs_5_), channel_id=1, source_target_pairs={{0,3},{1,2},{2,1},{3,0},{4,7},{5,6},{6,5},{7,4},{8,11},{9,10},{10,... | collective-permute-start | bytes 73736 | tf_op jit(solution)/shard_map/ppermute | solution.py:650
  22.3 131.8 %copy-start.5 = (bf16[1024,1024]{0,1:T(8,128)(2,1)}, bf16[1024,1024]{0,1:T(8,128)(2,1)S(1)}, u32[]{:S(2)}) copy-start(bf16[1024,1024]{0,1:T(8,128)(2,1)S(1)} %copy.201) | copy-start | bytes 6291460
  24.6 37.4 %collective-permute-start.10 = (bf16[2,128,1024]{2,1,0:T(8,128)(2,1)}, bf16[2,128,1024]{2,1,0:T(8,128)(2,1)}, u32[]{:S(2)}, u32[]{:S(2)}) collective-permute-start(bf16[2,128,1024]{2,1,0:T(8,128)(2,1)} %pad_maximum_fusion.refs_5_), channel_id=1, source_target_pairs={{0,2},{1,3},{2,0},{3,1},{4,6},{5,7},{6,4},{7,5},{8,10},{9,11},{10,... | collective-permute-start | bytes 1572872 | tf_op jit(solution)/shard_map/ppermute | solution.py:650
  30.3 19.2 %copy-start.48 = (f32[256]{0:T(256)S(1)}, f32[256]{0:T(256)}, u32[]{:S(2)}) copy-start(f32[256]{0:T(256)} %param.20) | copy-start | bytes 3076
  50.2 11.9 %copy-start.16 = (bf16[1024,2,256]{2,1,0:T(2,128)(2,1)S(1)}, bf16[1024,2,256]{2,1,0:T(2,128)(2,1)}, u32[]{:S(2)}) copy-start(bf16[1024,2,256]{2,1,0:T(2,128)(2,1)} %param.27) | copy-start | bytes 3145732
  62.0 24.8 %collective-permute-start.3 = (bf16[1024,1024]{1,0:T(8,128)(2,1)}, bf16[1024,1024]{1,0:T(8,128)(2,1)}, u32[]{:S(2)}, u32[]{:S(2)}) collective-permute-start(bf16[1024,1024]{1,0:T(8,128)(2,1)} %refs_4_.2), channel_id=1, source_target_pairs={{0,1},{1,0},{2,3},{3,2},{4,5},{5,4},{6,7},{7,6},{8,9},{9,8},{10,11... | collective-permute-start | bytes 6291464 | tf_op jit(solution)/shard_map/ppermute | solution.py:650
  64.6 29.5 %collective-permute-start.4 = (bf16[512,1024]{1,0:T(8,128)(2,1)}, bf16[512,1024]{1,0:T(8,128)(2,1)}, u32[]{:S(2)}, u32[]{:S(2)}) collective-permute-start(bf16[512,1024]{1,0:T(8,128)(2,1)} %bitcast.146), channel_id=1, source_target_pairs={{0,2},{1,3},{2,0},{3,1},{4,6},{5,7},{6,4},{7,5},{8,10},{9,11},{10,... | collective-permute-start | bytes 3145736 | tf_op jit(solution)/shard_map/ppermute | solution.py:650
  64.7 22.0 %all-to-all-start.1 = ((bf16[256,4,128]{2,1,0:T(4,128)(2,1)}), bf16[256,4,128]{2,1,0:T(4,128)(2,1)S(1)}, u32[]{:S(2)}, u32[]{:S(2)}) async-start(bf16[256,4,128]{2,1,0:T(4,128)(2,1)} %get-tuple-element.89), calls=%async_computation.1 | async-start | bytes 524288 | tf_op jit(solution)/shard_map/all_to_all | solution.py:784
  89.7 13.6 %all-to-all-start.2 = ((bf16[256,4,128]{2,1,0:T(4,128)(2,1)}), bf16[256,4,128]{2,1,0:T(4,128)(2,1)S(1)}, u32[]{:S(2)}, u32[]{:S(2)}) async-start(bf16[256,4,128]{2,1,0:T(4,128)(2,1)} %shard_map.314), calls=%async_computation.2 | async-start | bytes 524288 | tf_op jit(solution)/shard_map/all_to_all | solution.py:794
  94.1 29.2 %collective-permute-start.9 = (bf16[512,1024]{1,0:T(8,128)(2,1)}, bf16[512,1024]{1,0:T(8,128)(2,1)}, u32[]{:S(2)}, u32[]{:S(2)}) collective-permute-start(bf16[512,1024]{1,0:T(8,128)(2,1)} %collective-permute-done.4.refs_7_.refs_9_.refs_8_), channel_id=1, source_target_pairs={{0,1},{1,0},{2,3},{3,2},{4,5},{5,4},{6,7},{7,6},{8,9},{9,8},{10,11... | collective-permute-start | bytes 3145736 | tf_op jit(solution)/shard_map/ppermute | solution.py:650
  97.8 21.4 %collective-permute-start.5 = (bf16[256,1024]{1,0:T(8,128)(2,1)}, bf16[256,1024]{1,0:T(8,128)(2,1)}, u32[]{:S(2)}, u32[]{:S(2)}) collective-permute-start(bf16[256,1024]{1,0:T(8,128)(2,1)} %get-tuple-element.282), channel_id=1, source_target_pairs={{0,2},{1,3},{2,0},{3,1},{4,6},{5,7},{6,4},{7,5},{8,10},{9,11},{10,... | collective-permute-start | bytes 1572872 | tf_op jit(solution)/shard_map/ppermute | solution.py:650
  99.5 19.8 %collective-permute-start.6 = (bf16[256,1024]{1,0:T(8,128)(2,1)}, bf16[256,1024]{1,0:T(8,128)(2,1)}, u32[]{:S(2)}, u32[]{:S(2)}) collective-permute-start(bf16[256,1024]{1,0:T(8,128)(2,1)} %get-tuple-element.281), channel_id=1, source_target_pairs={{0,1},{1,0},{2,3},{3,2},{4,5},{5,4},{6,7},{7,6},{8,9},{9,8},{10,11... | collective-permute-start | bytes 1572872 | tf_op jit(solution)/shard_map/ppermute | solution.py:650
  99.7 23.6 %collective-permute-start.7 = (bf16[256,1024]{1,0:T(8,128)(2,1)}, bf16[256,1024]{1,0:T(8,128)(2,1)}, u32[]{:S(2)}, u32[]{:S(2)}) collective-permute-start(bf16[256,1024]{1,0:T(8,128)(2,1)} %get-tuple-element.280), channel_id=1, source_target_pairs={{0,3},{1,2},{2,1},{3,0},{4,7},{5,6},{6,5},{7,4},{8,11},{9,10},{10,... | collective-permute-start | bytes 1572872 | tf_op jit(solution)/shard_map/ppermute | solution.py:650
  100.0 23.3 %collective-permute-start.8 = (bf16[512,1024]{1,0:T(8,128)(2,1)S(1)}, bf16[512,1024]{1,0:T(8,128)(2,1)}, u32[]{:S(2)}, u32[]{:S(2)}) collective-permute-start(bf16[512,1024]{1,0:T(8,128)(2,1)S(1)} %bitcast.149), channel_id=1, source_target_pairs={{0,1},{1,0},{2,3},{3,2},{4,5},{5,4},{6,7},{7,6},{8,9},{9,8},{10,11... | collective-permute-start | bytes 3145736 | tf_op jit(solution)/shard_map/ppermute | solution.py:650
  123.3 31.9 %copy-start.44 = (s32[4,1024]{1,0:T(4,128)S(1)}, s32[4,1024]{1,0:T(4,128)}, u32[]{:S(2)}) copy-start(s32[4,1024]{1,0:T(4,128)} %param.18) | copy-start | bytes 49156
  154.1 17.1 %collective-permute-start.12 = (bf16[8,2,128,1024]{3,2,1,0:T(8,128)(2,1)}, bf16[8,2,128,1024]{3,2,1,0:T(8,128)(2,1)}, u32[]{:S(2)}, u32[]{:S(2)}) collective-permute-start(bf16[8,2,128,1024]{3,2,1,0:T(8,128)(2,1)} %bitcast.175), channel_id=1, source_target_pairs={{0,1},{1,0},{2,3},{3,2},{4,5},{5,4},{6,7},{7,6},{8,9},{9,8},{10,11... | collective-permute-start | bytes 12582920 | tf_op jit(solution)/shard_map/ppermute | solution.py:650
  154.1 17.1 %collective-permute-start.11 = (bf16[1024,1024]{1,0:T(8,128)(2,1)S(1)}, bf16[1024,1024]{1,0:T(8,128)(2,1)}, u32[]{:S(2)}, u32[]{:S(2)}) collective-permute-start(bf16[1024,1024]{1,0:T(8,128)(2,1)S(1)} %bitcast.138), channel_id=1, source_target_pairs={{0,1},{1,0},{2,3},{3,2},{4,5},{5,4},{6,7},{7,6},{8,9},{9,8},{10,11... | collective-permute-start | bytes 6291464 | tf_op jit(solution)/shard_map/ppermute | solution.py:650
  208.8 40.9 %collective-permute-start.14 = (bf16[2,1024,1024]{2,1,0:T(8,128)(2,1)}, bf16[2,1024,1024]{2,1,0:T(8,128)(2,1)}, u32[]{:S(2)}, u32[]{:S(2)}) collective-permute-start(bf16[2,1024,1024]{2,1,0:T(8,128)(2,1)} %get-tuple-element.111), channel_id=1, source_target_pairs={{0,1},{1,0},{2,3},{3,2},{4,5},{5,4},{6,7},{7,6},{8,9},{9,8},{10,11... | collective-permute-start | bytes 12582920 | tf_op jit(solution)/shard_map/ppermute | solution.py:650
  208.9 50.5 %collective-permute-start.13 = (bf16[2048,1024]{1,0:T(8,128)(2,1)}, bf16[2048,1024]{1,0:T(8,128)(2,1)}, u32[]{:S(2)}, u32[]{:S(2)}) collective-permute-start(bf16[2048,1024]{1,0:T(8,128)(2,1)} %get-tuple-element.109), channel_id=1, source_target_pairs={{0,1},{1,0},{2,3},{3,2},{4,5},{5,4},{6,7},{7,6},{8,9},{9,8},{10,11... | collective-permute-start | bytes 12582920 | tf_op jit(solution)/shard_map/ppermute | solution.py:650
  249.7 9.8 %copy-start.3 = (bf16[2048,1024]{1,0:T(8,128)(2,1)S(1)}, bf16[2048,1024]{1,0:T(8,128)(2,1)}, u32[]{:S(2)}) copy-start(bf16[2048,1024]{1,0:T(8,128)(2,1)} %get-tuple-element.108) | copy-start | bytes 12582916
  257.6 51.6 %collective-permute-start.16 = (bf16[2,2,1,2,128,1024]{5,4,3,2,1,0:T(8,128)(2,1)}, bf16[2,2,1,2,128,1024]{5,4,3,2,1,0:T(8,128)(2,1)}, u32[]{:S(2)}, u32[]{:S(2)}) collective-permute-start(bf16[2,2,1,2,128,1024]{5,4,3,2,1,0:T(8,128)(2,1)} %get-tuple-element.267.refs_13_), channel_id=1, source_target_pairs={{0,8},{4,12},{8,0},{12,4},{16,24},{20,28},{24,16},{28,20},{1,9},{5... | collective-permute-start | bytes 6291464 | tf_op jit(solution)/shard_map/ppermute | solution.py:650
  265.3 48.7 %collective-permute-start.15 = (bf16[2,2,2,1,128,1024]{5,4,3,2,1,0:T(8,128)(2,1)}, bf16[2,2,2,1,128,1024]{5,4,3,2,1,0:T(8,128)(2,1)}, u32[]{:S(2)}, u32[]{:S(2)}) collective-permute-start(bf16[2,2,2,1,128,1024]{5,4,3,2,1,0:T(8,128)(2,1)} %get-tuple-element.269.refs_12_), channel_id=1, source_target_pairs={{0,4},{4,0},{8,12},{12,8},{16,20},{20,16},{24,28},{28,24},{1,5},{5... | collective-permute-start | bytes 6291464 | tf_op jit(solution)/shard_map/ppermute | solution.py:650
  283.0 12.6 %copy-start.18 = (f32[2048,128]{1,0:T(8,128)S(1)}, f32[2048,128]{1,0:T(8,128)}, u32[]{:S(2)}) copy-start(f32[2048,128]{1,0:T(8,128)} %get-tuple-element.143) | copy-start | bytes 3145732
  295.5 32.5 %collective-permute-start.17 = (bf16[2,1024,512]{2,1,0:T(8,128)(2,1)}, bf16[2,1024,512]{2,1,0:T(8,128)(2,1)}, u32[]{:S(2)}, u32[]{:S(2)}) collective-permute-start(bf16[2,1024,512]{2,1,0:T(8,128)(2,1)} %get-tuple-element.118), channel_id=1, source_target_pairs={{0,1},{1,0},{2,3},{3,2},{4,5},{5,4},{6,7},{7,6},{8,9},{9,8},{10,11... | collective-permute-start | bytes 6291464 | tf_op jit(solution)/shard_map/ppermute | solution.py:650
  297.6 30.4 %all-to-all-start.4 = ((bf16[4,256,1024]{2,1,0:T(8,128)(2,1)}), bf16[4,256,1024]{2,1,0:T(8,128)(2,1)}, u32[]{:S(2)}, u32[]{:S(2)}) async-start(bf16[4,256,1024]{2,1,0:T(8,128)(2,1)} %bitcast.144), calls=%async_computation.4 | async-start | bytes 4194304 | tf_op jit(solution)/shard_map/all_to_all | solution.py:731
  308.7 50.5 %collective-permute-start.28 = (f32[2,2052]{1,0:T(2,128)S(1)}, f32[2,2052]{1,0:T(2,128)S(1)}, u32[]{:S(2)}, u32[]{:S(2)}) collective-permute-start(f32[2,2052]{1,0:T(2,128)S(1)} %pad_maximum_fusion.4), channel_id=1, source_target_pairs={{0,1},{1,0},{2,3},{3,2},{4,5},{5,4},{6,7},{7,6},{8,9},{9,8},{10,11... | collective-permute-start | bytes 49256 | tf_op jit(solution)/shard_map/ppermute | solution.py:650
  313.5 59.6 %collective-permute-start.20 = (bf16[2,2,1,1,128,1024]{5,4,3,2,1,0:T(8,128)(2,1)}, bf16[2,2,1,1,128,1024]{5,4,3,2,1,0:T(8,128)(2,1)}, u32[]{:S(2)}, u32[]{:S(2)}) collective-permute-start(bf16[2,2,1,1,128,1024]{5,4,3,2,1,0:T(8,128)(2,1)} %get-tuple-element.273.refs_3_), channel_id=1, source_target_pairs={{0,4},{4,0},{8,12},{12,8},{16,20},{20,16},{24,28},{28,24},{1,5},{5... | collective-permute-start | bytes 3145736 | tf_op jit(solution)/shard_map/ppermute | solution.py:650
  317.8 59.7 %collective-permute-start.18 = (bf16[2,2,1,1,128,1024]{5,4,3,2,1,0:T(8,128)(2,1)}, bf16[2,2,1,1,128,1024]{5,4,3,2,1,0:T(8,128)(2,1)}, u32[]{:S(2)}, u32[]{:S(2)}) collective-permute-start(bf16[2,2,1,1,128,1024]{5,4,3,2,1,0:T(8,128)(2,1)} %get-tuple-element.275.refs_2_), channel_id=1, source_target_pairs={{0,8},{4,12},{8,0},{12,4},{16,24},{20,28},{24,16},{28,20},{1,9},{5... | collective-permute-start | bytes 3145736 | tf_op jit(solution)/shard_map/ppermute | solution.py:650
  340.4 12.4 %all-to-all-start.5 = ((bf16[256,4,128]{2,1,0:T(4,128)(2,1)}), bf16[256,4,128]{2,1,0:T(4,128)(2,1)S(1)}, u32[]{:S(2)}, u32[]{:S(2)}) async-start(bf16[256,4,128]{2,1,0:T(4,128)(2,1)} %get-tuple-element.119), calls=%async_computation.5 | async-start | bytes 524288 | tf_op jit(solution)/shard_map/all_to_all | solution.py:784
  355.7 12.2 %all-to-all-start.6 = ((bf16[256,4,128]{2,1,0:T(4,128)(2,1)}), bf16[256,4,128]{2,1,0:T(4,128)(2,1)S(1)}, u32[]{:S(2)}, u32[]{:S(2)}) async-start(bf16[256,4,128]{2,1,0:T(4,128)(2,1)} %shard_map.322), calls=%async_computation.6 | async-start | bytes 524288 | tf_op jit(solution)/shard_map/all_to_all | solution.py:794
  360.0 49.4 %collective-permute-start.22 = (bf16[2,2,2,1,128,512]{5,4,3,2,1,0:T(8,128)(2,1)}, bf16[2,2,2,1,128,512]{5,4,3,2,1,0:T(8,128)(2,1)}, u32[]{:S(2)}, u32[]{:S(2)}) collective-permute-start(bf16[2,2,2,1,128,512]{5,4,3,2,1,0:T(8,128)(2,1)} %constant_dynamic-slice_fusion.refs_4_), channel_id=1, source_target_pairs={{0,4},{4,0},{8,12},{12,8},{16,20},{20,16},{24,28},{28,24},{1,5},{5... | collective-permute-start | bytes 3145736 | tf_op jit(solution)/shard_map/ppermute | solution.py:650
  368.6 50.2 %all-to-all-start.7 = ((bf16[4,256,1024]{2,1,0:T(8,128)(2,1)}), bf16[4,256,1024]{2,1,0:T(8,128)(2,1)}, u32[]{:S(2)}, u32[]{:S(2)}) async-start(bf16[4,256,1024]{2,1,0:T(8,128)(2,1)} %bitcast.141), calls=%async_computation.7 | async-start | bytes 4194304 | tf_op jit(solution)/shard_map/all_to_all | solution.py:731
  373.0 177.7 %all-gather.7.cloned.1.call-start = ((), (), s32[]{:S(2)}) async-start(), calls=%async_computation.10 | async-start | bytes 4718592 | tf_op jit(solution)/shard_map/all_gather | solution.py:1124
  375.6 36.8 %copy-start.8 = (bf16[1,2,1,1,128,1024]{5,4,3,2,1,0:T(8,128)(2,1)}, bf16[1,2,1,1,128,1024]{5,4,3,2,1,0:T(8,128)(2,1)S(1)}, u32[]{:S(2)}) copy-start(bf16[1,2,1,1,128,1024]{5,4,3,2,1,0:T(8,128)(2,1)S(1)} %get-tuple-element.276) | copy-start | bytes 1572868
  375.6 34.5 %collective-permute-start.21 = (bf16[1,2,1,1,128,1024]{5,4,3,2,1,0:T(8,128)(2,1)}, bf16[1,2,1,1,128,1024]{5,4,3,2,1,0:T(8,128)(2,1)}, u32[]{:S(2)}, u32[]{:S(2)}) collective-permute-start(bf16[1,2,1,1,128,1024]{5,4,3,2,1,0:T(8,128)(2,1)} %get-tuple-element.277.refs_6_), channel_id=1, source_target_pairs={{0,2},{1,3},{2,0},{3,1},{4,6},{5,7},{6,4},{7,5},{8,10},{9,11},{10,... | collective-permute-start | bytes 1572872 | tf_op jit(solution)/shard_map/ppermute | solution.py:650
  379.9 30.1 %collective-permute-start.19 = (bf16[2,1,1,1,128,1024]{5,4,3,2,1,0:T(8,128)(2,1)}, bf16[2,1,1,1,128,1024]{5,4,3,2,1,0:T(8,128)(2,1)}, u32[]{:S(2)}, u32[]{:S(2)}) collective-permute-start(bf16[2,1,1,1,128,1024]{5,4,3,2,1,0:T(8,128)(2,1)} %get-tuple-element.278.refs_5_), channel_id=1, source_target_pairs={{0,16},{4,20},{8,24},{12,28},{16,0},{20,4},{24,8},{28,12},{1,17},{... | collective-permute-start | bytes 1572872 | tf_op jit(solution)/shard_map/ppermute | solution.py:650
  381.0 26.4 %copy-start.1 = (f32[256,32]{1,0:T(8,128)S(1)}, f32[256,32]{1,0:T(8,128)}, u32[]{:S(2)}) copy-start(f32[256,32]{1,0:T(8,128)} %copy.197.refs_1_) | copy-start | bytes 98308
  381.0 26.4 %copy-start.2 = (f32[256,32]{1,0:T(8,128)S(1)}, f32[256,32]{1,0:T(8,128)}, u32[]{:S(2)}) copy-start(f32[256,32]{1,0:T(8,128)} %copy.198.refs_2_) | copy-start | bytes 98308
  381.0 26.4 %copy-start.35 = (f32[256]{0:T(256)S(1)}, f32[256]{0:T(256)}, u32[]{:S(2)}) copy-start(f32[256]{0:T(256)} %param.21) | copy-start | bytes 3076
  408.7 24.0 %copy-start.12 = (f32[256,32]{1,0:T(8,128)}, f32[256,32]{1,0:T(8,128)S(1)}, u32[]{:S(2)}) copy-start(f32[256,32]{1,0:T(8,128)S(1)} %get-tuple-element.264) | copy-start | bytes 98308
  408.7 24.0 %copy-start.14 = (f32[256,32]{1,0:T(8,128)}, f32[256,32]{1,0:T(8,128)S(1)}, u32[]{:S(2)}) copy-start(f32[256,32]{1,0:T(8,128)S(1)} %get-tuple-element.265) | copy-start | bytes 98308
  412.0 20.7 %collective-permute-start.25 = (bf16[1,2,2,1,128,512]{5,4,3,2,1,0:T(8,128)(2,1)}, bf16[1,2,2,1,128,512]{5,4,3,2,1,0:T(8,128)(2,1)}, u32[]{:S(2)}, u32[]{:S(2)}) collective-permute-start(bf16[1,2,2,1,128,512]{5,4,3,2,1,0:T(8,128)(2,1)} %add_convert_fusion.12.refs_14_), channel_id=1, source_target_pairs={{0,2},{1,3},{2,0},{3,1},{4,6},{5,7},{6,4},{7,5},{8,10},{9,11},{10,... | collective-permute-start | bytes 1572872 | tf_op jit(solution)/shard_map/ppermute | solution.py:650
  414.1 18.6 %collective-permute-start.24 = (bf16[1,1,1,1,128,1024]{5,4,3,2,1,0:T(8,128)(2,1)}, bf16[1,1,1,1,128,1024]{5,4,3,2,1,0:T(8,128)(2,1)S(1)}, u32[]{:S(2)}, u32[]{:S(2)}) collective-permute-start(bf16[1,1,1,1,128,1024]{5,4,3,2,1,0:T(8,128)(2,1)} %add_convert_fusion.21.refs_13_), channel_id=1, source_target_pairs={{0,16},{4,20},{8,24},{12,28},{16,0},{20,4},{24,8},{28,12},{1,17},{... | collective-permute-start | bytes 786440 | tf_op jit(solution)/shard_map/ppermute | solution.py:650
  416.9 15.8 %collective-permute-start.23 = (bf16[1,1,1,1,128,1024]{5,4,3,2,1,0:T(8,128)(2,1)}, bf16[1,1,1,1,128,1024]{5,4,3,2,1,0:T(8,128)(2,1)}, u32[]{:S(2)}, u32[]{:S(2)}) collective-permute-start(bf16[1,1,1,1,128,1024]{5,4,3,2,1,0:T(8,128)(2,1)} %add_convert_fusion.22.refs_12_), channel_id=1, source_target_pairs={{0,2},{1,3},{2,0},{3,1},{4,6},{5,7},{6,4},{7,5},{8,10},{9,11},{10,... | collective-permute-start | bytes 786440 | tf_op jit(solution)/shard_map/ppermute | solution.py:650
  434.9 53.3 %collective-permute-start.31 = (bf16[1,2,2,1,128,512]{5,4,3,2,1,0:T(8,128)(2,1)S(1)}, bf16[1,2,2,1,128,512]{5,4,3,2,1,0:T(8,128)(2,1)S(1)}, u32[]{:S(2)}, u32[]{:S(2)}) collective-permute-start(bf16[1,2,2,1,128,512]{5,4,3,2,1,0:T(8,128)(2,1)S(1)} %add_convert_fusion.10.refs_13_), channel_id=1, source_target_pairs={{0,8},{4,12},{8,0},{12,4},{16,24},{20,28},{24,16},{28,20},{1,9},{5... | collective-permute-start | bytes 1572872 | tf_op jit(solution)/shard_map/ppermute | solution.py:650
  436.1 52.1 %collective-permute-start.32 = (bf16[1,2,2,1,128,512]{5,4,3,2,1,0:T(8,128)(2,1)S(1)}, bf16[1,2,2,1,128,512]{5,4,3,2,1,0:T(8,128)(2,1)S(1)}, u32[]{:S(2)}, u32[]{:S(2)}) collective-permute-start(bf16[1,2,2,1,128,512]{5,4,3,2,1,0:T(8,128)(2,1)S(1)} %add_convert_fusion.10.refs_13_), channel_id=1, source_target_pairs={{0,16},{4,20},{8,24},{12,28},{16,0},{20,4},{24,8},{28,12},{1,17},{... | collective-permute-start | bytes 1572872 | tf_op jit(solution)/shard_map/ppermute | solution.py:650
  437.7 50.5 %collective-permute-start.33 = (bf16[1,2,2,1,128,512]{5,4,3,2,1,0:T(8,128)(2,1)S(1)}, bf16[1,2,2,1,128,512]{5,4,3,2,1,0:T(8,128)(2,1)}, u32[]{:S(2)}, u32[]{:S(2)}) collective-permute-start(bf16[1,2,2,1,128,512]{5,4,3,2,1,0:T(8,128)(2,1)S(1)} %add_convert_fusion.10.refs_13_), channel_id=1, source_target_pairs={{0,24},{4,28},{8,16},{12,20},{16,8},{20,12},{24,0},{28,4},{1,25},{... | collective-permute-start | bytes 1572872 | tf_op jit(solution)/shard_map/ppermute | solution.py:650
  441.6 14.0 %copy-start.33 = (f32[128,128]{1,0:T(8,128)S(1)}, f32[128,128]{1,0:T(8,128)}, u32[]{:S(2)}) copy-start(f32[128,128]{1,0:T(8,128)} %get-tuple-element.138) | copy-start | bytes 196612
  441.6 16.5 %copy-start.26 = (f32[4,128,128]{2,1,0:T(8,128)S(1)}, f32[4,128,128]{2,1,0:T(8,128)}, u32[]{:S(2)}) copy-start(f32[4,128,128]{2,1,0:T(8,128)} %get-tuple-element.136) | copy-start | bytes 786436
  458.8 7.8 %collective-permute-start.29 = (f32[293,128]{1,0:T(8,128)S(1)}, f32[293,128]{1,0:T(8,128)S(1)}, u32[]{:S(2)}, u32[]{:S(2)}) collective-permute-start(f32[293,128]{1,0:T(8,128)S(1)} %pad_maximum_fusion.2), channel_id=1, source_target_pairs={{0,4},{4,0},{8,12},{12,8},{16,20},{20,16},{24,28},{28,24},{1,5},{5... | collective-permute-start | bytes 450056 | tf_op jit(solution)/shard_map/ppermute | solution.py:650
  460.3 1.2 collective-permute-start.26
  461.5 5.1 collective-permute-start.27
  461.7 26.4 %copy-start.7 = (bf16[1,2,2,1,128,512]{5,4,3,2,1,0:T(8,128)(2,1)S(1)}, bf16[1,2,2,1,128,512]{5,4,3,2,1,0:T(8,128)(2,1)}, u32[]{:S(2)}) copy-start(bf16[1,2,2,1,128,512]{5,4,3,2,1,0:T(8,128)(2,1)} %copy-done.6) | copy-start | bytes 1572868
  461.7 77.0 %all-to-all-start.8 = ((bf16[4,256,1024]{2,1,0:T(8,128)(2,1)}), bf16[4,256,1024]{2,1,0:T(8,128)(2,1)}, u32[]{:S(2)}, u32[]{:S(2)}) async-start(bf16[4,256,1024]{2,1,0:T(8,128)(2,1)} %bitcast.140), calls=%async_computation.8 | async-start | bytes 4194304 | tf_op jit(solution)/shard_map/all_to_all | solution.py:731
  466.7 21.4 %collective-permute-start.30 = (f32[293,128]{1,0:T(8,128)S(1)}, f32[293,128]{1,0:T(8,128)S(1)}, u32[]{:S(2)}, u32[]{:S(2)}) collective-permute-start(f32[293,128]{1,0:T(8,128)S(1)} %add.313), channel_id=1, source_target_pairs={{0,8},{4,12},{8,0},{12,4},{16,24},{20,28},{24,16},{28,20},{1,9},{5... | collective-permute-start | bytes 450056 | tf_op jit(solution)/shard_map/ppermute | solution.py:650
  489.5 26.8 %collective-permute-start.34 = (f32[293,128]{1,0:T(8,128)S(1)}, f32[293,128]{1,0:T(8,128)S(1)}, u32[]{:S(2)}, u32[]{:S(2)}) collective-permute-start(f32[293,128]{1,0:T(8,128)S(1)} %add.314), channel_id=1, source_target_pairs={{0,16},{4,20},{8,24},{12,28},{16,0},{20,4},{24,8},{28,12},{1,17},{... | collective-permute-start | bytes 450056 | tf_op jit(solution)/shard_map/ppermute | solution.py:650
  502.5 15.4 %copy-start.19 = (f32[256,32]{1,0:T(8,128)S(1)}, f32[256,32]{1,0:T(8,128)}, u32[]{:S(2)}) copy-start(f32[256,32]{1,0:T(8,128)} %copy.199.refs_3_) | copy-start | bytes 98308
  502.5 15.4 %copy-start.20 = (f32[256,32]{1,0:T(8,128)S(1)}, f32[256,32]{1,0:T(8,128)}, u32[]{:S(2)}) copy-start(f32[256,32]{1,0:T(8,128)} %copy.200.refs_4_) | copy-start | bytes 98308
  514.5 21.6 %collective-permute-start.35 = (bf16[1,2,2,1,128,512]{5,4,3,2,1,0:T(8,128)(2,1)S(1)}, bf16[1,2,2,1,128,512]{5,4,3,2,1,0:T(8,128)(2,1)S(1)}, u32[]{:S(2)}, u32[]{:S(2)}) collective-permute-start(bf16[1,2,2,1,128,512]{5,4,3,2,1,0:T(8,128)(2,1)S(1)} %add_convert_fusion.9), channel_id=1, source_target_pairs={{0,4},{4,0},{8,12},{12,8},{16,20},{20,16},{24,28},{28,24},{1,5},{5... | collective-permute-start | bytes 1572872 | tf_op jit(solution)/shard_map/ppermute | solution.py:650
  516.4 7.3 %collective-permute-start.36 = (f32[2052]{0:T(1024)S(1)}, f32[2052]{0:T(1024)S(1)}, u32[]{:S(2)}, u32[]{:S(2)}) collective-permute-start(f32[2052]{0:T(1024)S(1)} %slice.481), channel_id=1, source_target_pairs={{0,2},{1,3},{2,0},{3,1},{4,6},{5,7},{6,4},{7,5},{8,10},{9,11},{10,... | collective-permute-start | bytes 24632 | tf_op jit(solution)/shard_map/ppermute | solution.py:650
  (33 other events, 104.3 us)
Sparse Core Ops, SparseCore 0:
  62.1 79.7 all-gather.4
  441.7 109.0 all-gather.6
